TPU v7x, 32 devices: a whole 2x2x4 slice. The times are simulated.
32 devices in a mesh: dp: 16 (over z, x, core), tensor: 2 (over y).
Axes of the slice: x: 2, y: 2, z: 4, core: 2. Of those that a mesh axis runs over, the one named last changes fastest.
Arguments:
- hidden_in: bfloat16 [16384, 1024], P('dp'), may hold values from -6 to 6
- cotangent: bfloat16 [16384, 1024], P('dp'), may hold values from -6 to 6
- qkv_weight: float32 [2, 1024, 3, 1024], P(None, 'dp', None, 'tensor'), may hold values from -0.1875 to 0.1875
- out_weight: float32 [2, 1024, 1024], P(None, 'tensor', 'dp'), may hold values from -1 to 1
- in_weight: float32 [2, 1024, 2, 2624], P(None, 'dp', None, 'tensor'), may hold values from -0.1875 to 0.1875
- down_weight: float32 [2, 2624, 1024], P(None, 'tensor', 'dp'), may hold values from -0.125 to 0.125
- norm_gains: float32 [2, 2, 1024], P(None, None, 'dp'), may hold values from 0.5 to 1.5
- qkv_moment_in: float32 [2, 1024, 3, 1024], P(None, 'dp', None, 'tensor'), may hold values from -40 to 40
- qkv_square_in: float32 [2, 1024, 3, 1024], P(None, 'dp', None, 'tensor'), may hold values from 81.92 to 327.68
- out_moment_in: float32 [2, 1024, 1024], P(None, 'tensor', 'dp'), may hold values from -8 to 8
- out_square_in: float32 [2, 1024, 1024], P(None, 'tensor', 'dp'), may hold values from 3.2768 to 13.1072
- in_moment_in: float32 [2, 1024, 2, 2624], P(None, 'dp', None, 'tensor'), may hold values from -32 to 32
- in_square_in: float32 [2, 1024, 2, 2624], P(None, 'dp', None, 'tensor'), may hold values from 54.0672 to 212.992
- down_moment_in: float32 [2, 2624, 1024], P(None, 'tensor', 'dp'), may hold values from -48 to 48
- down_square_in: float32 [2, 2624, 1024], P(None, 'tensor', 'dp'), may hold values from 119.6032 to 475.136
- gain_moment_in: float32 [2, 2, 1024], P(None, None, 'dp'), may hold values from -80 to 80
- gain_square_in: float32 [2, 2, 1024], P(None, None, 'dp'), may hold values from 327.68 to 1310.72
Outputs:
- hidden_out: bfloat16 [16384, 1024], P('dp')
- grad_in: float32 [16384, 1024], P('dp')
- qkv_moment: float32 [2, 1024, 3, 1024], P(None, 'dp', None, 'tensor')
- qkv_square: float32 [2, 1024, 3, 1024], P(None, 'dp', None, 'tensor')
- qkv_updated: float32 [2, 1024, 3, 1024], P(None, 'dp', None, 'tensor')
- out_moment: float32 [2, 1024, 1024], P(None, 'tensor', 'dp')
- out_square: float32 [2, 1024, 1024], P(None, 'tensor', 'dp')
- out_updated: float32 [2, 1024, 1024], P(None, 'tensor', 'dp')
- in_moment: float32 [2, 1024, 2, 2624], P(None, 'dp', None, 'tensor')
- in_square: float32 [2, 1024, 2, 2624], P(None, 'dp', None, 'tensor')
- in_updated: float32 [2, 1024, 2, 2624], P(None, 'dp', None, 'tensor')
- down_moment: float32 [2, 2624, 1024], P(None, 'tensor', 'dp')
- down_square: float32 [2, 2624, 1024], P(None, 'tensor', 'dp')
- down_updated: float32 [2, 2624, 1024], P(None, 'tensor', 'dp')
- gain_moment: float32 [2, 2, 1024], P(None, None, 'dp')
- gain_square: float32 [2, 2, 1024], P(None, None, 'dp')
- gain_updated: float32 [2, 2, 1024], P(None, None, 'dp')
All inputs are finite; a program needn't handle non-finite values.
Results may differ from a plain program's by a relative error of at most 0.034.
Values may be sent and summed in bfloat16 or wider, within the bound.
No kernel may reach another device: no remote copies, remote signals or barrier semaphores. Data moves between devices by JAX's collectives and lax.ppermute only.
A program may use at most 320 MiB of HBM per device.

v0:
```python
import jax
import jax.numpy as jnp
from jax import lax
from jax.sharding import PartitionSpec as P

HEAD_DIM = 64
HALF_WIN = 64
STEP = 10
SEQ_LEN = 1024


norm_eps = 1e-05
theta_local = 10000.0
theta_global = 160000.0
masked_score = -1e30
beta_one = 0.9
beta_two = 0.98
adam_eps = 1e-06
weight_decay = 1e-05
rate_qkv = 0.03
rate_out = 0.15
rate_inp = 0.03
rate_down = 0.02
rate_gain = 0.5


def layer_norm(values, gain):
    centred = values - jnp.mean(values, axis=-1, keepdims=True)
    spread = jnp.mean(centred * centred, axis=-1, keepdims=True)
    return centred * lax.rsqrt(spread + norm_eps) * gain


def rotary_tables(positions, rotary_base):
    inverse = rotary_base ** (-jnp.arange(0, HEAD_DIM, 2, dtype=jnp.float32) / HEAD_DIM)
    angles = positions.astype(jnp.float32)[:, None] * inverse[None, :]
    cosine = jnp.concatenate([jnp.cos(angles), jnp.cos(angles)], axis=-1)[:, None, :]
    sine_table = jnp.concatenate([jnp.sin(angles), jnp.sin(angles)], axis=-1)[:, None, :]
    return (cosine, sine_table)


def rotate(values, cosine, sine_table):
    half_dim = values.shape[-1] // 2
    turned = jnp.concatenate([-values[..., half_dim:], values[..., :half_dim]], axis=-1)
    return values * cosine + turned * sine_table


def gelu_gate(inner, gate_part):
    return jax.nn.gelu(inner, approximate=False) * gate_part


def row_total(partial_sum):
    summed = lax.psum(partial_sum.astype(jnp.bfloat16), "tensor").astype(jnp.float32)
    return summed


def grad_total(partial_sum):
    summed = lax.psum(partial_sum.astype(jnp.bfloat16), "tensor").astype(jnp.float32)
    return summed


def gather_weights(masters, layer_index):
    return (
        lax.all_gather(masters[0][layer_index].astype(jnp.bfloat16), "dp", axis=0, tiled=True),
        lax.all_gather(masters[1][layer_index].astype(jnp.bfloat16), "dp", axis=1, tiled=True),
        lax.all_gather(masters[2][layer_index].astype(jnp.bfloat16), "dp", axis=0, tiled=True),
        lax.all_gather(masters[3][layer_index].astype(jnp.bfloat16), "dp", axis=1, tiled=True),
        lax.all_gather(masters[4][layer_index].astype(jnp.bfloat16), "dp", axis=1, tiled=True),
    )


def band_view(heads, half_width):
    block = 2 * half_width
    seq_count, length = (heads.shape[0], heads.shape[1])
    count = length // block
    padded = jnp.pad(heads, ((0, 0), (half_width, half_width), (0, 0), (0, 0)))
    first = padded[:, :length].reshape(seq_count, count, block, heads.shape[2], heads.shape[3])
    second = padded[:, block:].reshape(seq_count, count, block, heads.shape[2], heads.shape[3])
    return jnp.concatenate([first, second], axis=2)


def band_fold(band, half_width, length):
    block = 2 * half_width
    seq_count = band.shape[0]
    first = band[:, :, :block].reshape(seq_count, length, band.shape[3], band.shape[4])
    second = band[:, :, block:].reshape(seq_count, length, band.shape[3], band.shape[4])
    padding = ((0, 0), (0, block), (0, 0), (0, 0))
    total = jnp.pad(first, padding) + jnp.pad(second, ((0, 0), (block, 0), (0, 0), (0, 0)))
    return total[:, half_width : half_width + length]


def band_mask(length, half_width):
    block = 2 * half_width
    count = length // block
    query_at = jnp.arange(block, dtype=jnp.int32)[None, :, None]
    key_at = jnp.arange(2 * block, dtype=jnp.int32)[None, None, :]
    start = jnp.arange(count, dtype=jnp.int32)[:, None, None] * block
    key_pos = start - half_width + key_at
    near = jnp.abs(query_at - key_at + half_width) <= half_width
    return near & (key_pos >= 0) & (key_pos < length)


def local_probability(queries, key_all):
    seq_count, length, heads_here, head_size = queries.shape
    block = 2 * HALF_WIN
    query_blocks = queries.reshape(seq_count, length // block, block, heads_here, head_size)
    key_band = band_view(key_all, HALF_WIN)
    scores = (
        jnp.einsum("sbqhd,sbkhd->sbhqk", query_blocks, key_band, preferred_element_type=jnp.float32)
        * 0.125
    )
    allowed = band_mask(length, HALF_WIN)[None, :, None]
    return (jnp.where(allowed, scores, masked_score), allowed, query_blocks, key_band)


def global_scores(queries, key_all):
    return (
        jnp.einsum("sqhd,skhd->shqk", queries, key_all, preferred_element_type=jnp.float32) * 0.125
    )


def attend_forward(queries, key_all, value_all, is_local):
    seq_count, length, heads_here, head_size = queries.shape
    if is_local:
        scores, allowed, query_blocks, key_band = local_probability(queries, key_all)
    else:
        scores = global_scores(queries, key_all)
    row_max = jnp.max(scores, axis=-1, keepdims=True)
    exponent = jnp.exp(scores - row_max)
    exp_total = jnp.sum(exponent, axis=-1, keepdims=True)
    probability = (exponent / exp_total).astype(jnp.bfloat16)
    if is_local:
        value_band = band_view(value_all, HALF_WIN)
        attended = jnp.einsum(
            "sbhqk,sbkhd->sbqhd", probability, value_band, preferred_element_type=jnp.float32
        )
    else:
        attended = jnp.einsum(
            "shqk,skhd->sqhd", probability, value_all, preferred_element_type=jnp.float32
        )
    return (
        attended.reshape(seq_count * length, heads_here * head_size),
        row_max + jnp.log(exp_total),
    )


def attend_backward(queries, key_all, value_all, log_total, d_attended, is_local):
    seq_count, length, heads_here, head_size = queries.shape
    if is_local:
        block = 2 * HALF_WIN
        scores, allowed, query_blocks, key_band = local_probability(queries, key_all)
        probability = jnp.where(allowed, jnp.exp(scores - log_total), 0.0)
        value_band = band_view(value_all, HALF_WIN)
        d_blocks = d_attended.reshape(seq_count, length // block, block, heads_here, head_size)
        d_value = band_fold(
            jnp.einsum(
                "sbhqk,sbqhd->sbkhd",
                probability.astype(jnp.bfloat16),
                d_blocks,
                preferred_element_type=jnp.float32,
            ),
            HALF_WIN,
            length,
        )
        d_probability = jnp.einsum(
            "sbqhd,sbkhd->sbhqk", d_blocks, value_band, preferred_element_type=jnp.float32
        )
        centre = jnp.sum(probability * d_probability, axis=-1, keepdims=True)
        d_scores = (probability * (d_probability - centre)).astype(jnp.bfloat16)
        d_queries = jnp.einsum(
            "sbhqk,sbkhd->sbqhd", d_scores, key_band, preferred_element_type=jnp.float32
        )
        d_queries = d_queries.reshape(seq_count, length, heads_here, head_size) * 0.125
        d_keys = (
            band_fold(
                jnp.einsum(
                    "sbhqk,sbqhd->sbkhd", d_scores, query_blocks, preferred_element_type=jnp.float32
                ),
                HALF_WIN,
                length,
            )
            * 0.125
        )
    else:
        d_heads = d_attended.reshape(seq_count, length, heads_here, head_size)
        probability = jnp.exp(global_scores(queries, key_all) - log_total)
        d_value = jnp.einsum(
            "shqk,sqhd->skhd",
            probability.astype(jnp.bfloat16),
            d_heads,
            preferred_element_type=jnp.float32,
        )
        d_probability = jnp.einsum(
            "sqhd,skhd->shqk", d_heads, value_all, preferred_element_type=jnp.float32
        )
        centre = jnp.sum(probability * d_probability, axis=-1, keepdims=True)
        d_scores = (probability * (d_probability - centre)).astype(jnp.bfloat16)
        d_queries = (
            jnp.einsum("shqk,skhd->sqhd", d_scores, key_all, preferred_element_type=jnp.float32)
            * 0.125
        )
        d_keys = (
            jnp.einsum("shqk,sqhd->skhd", d_scores, queries, preferred_element_type=jnp.float32)
            * 0.125
        )
    return (d_queries, d_keys, d_value)


def forward_layer(residual, lowered, weights, is_local):
    w_qkv, w_out, w_inp, w_down, gain_pair = weights
    row_count = lowered.shape[0]
    seq_count = row_count // SEQ_LEN
    local_width = w_qkv.shape[2]
    heads_here = local_width // HEAD_DIM
    positions = jnp.arange(SEQ_LEN, dtype=jnp.int32)
    cosine, sine_table = rotary_tables(positions, theta_local if is_local else theta_global)
    projected = jnp.einsum("td,dcn->tcn", lowered, w_qkv, preferred_element_type=jnp.float32)
    shape_four = (seq_count, SEQ_LEN, heads_here, HEAD_DIM)
    queries = rotate(projected[:, 0].reshape(shape_four), cosine, sine_table).astype(jnp.bfloat16)
    key_all = rotate(projected[:, 1].reshape(shape_four), cosine, sine_table).astype(jnp.bfloat16)
    value_all = projected[:, 2].astype(jnp.bfloat16).reshape(shape_four)
    attended, log_total = attend_forward(queries, key_all, value_all, is_local)
    attended = attended.astype(jnp.bfloat16)
    middle = residual + row_total(jnp.dot(attended, w_out, preferred_element_type=jnp.float32))
    lowered_two = layer_norm(middle, gain_pair[1].astype(jnp.float32)).astype(jnp.bfloat16)
    hidden = jnp.einsum("td,dcf->tcf", lowered_two, w_inp, preferred_element_type=jnp.float32)
    activated = gelu_gate(hidden[:, 0], hidden[:, 1]).astype(jnp.bfloat16)
    output = middle + row_total(jnp.dot(activated, w_down, preferred_element_type=jnp.float32))
    kept = (
        residual,
        middle,
        lowered,
        lowered_two,
        queries,
        key_all,
        value_all,
        log_total,
        attended,
        hidden,
        activated,
        cosine,
        sine_table,
    )
    return (output, kept)


def backward_layer(upstream, up_low, weights, kept, is_local):
    w_qkv, w_out, w_inp, w_down, gain_pair = weights
    (
        residual,
        middle,
        lowered,
        lowered_two,
        queries,
        key_all,
        value_all,
        log_total,
        attended,
        hidden,
        activated,
        cosine,
        sine_table,
    ) = kept
    row_count = lowered.shape[0]
    local_width = w_qkv.shape[2]
    d_activated = jnp.einsum("td,fd->tf", up_low, w_down, preferred_element_type=jnp.float32)
    grad_down = jnp.einsum("tf,td->fd", activated, up_low, preferred_element_type=jnp.float32)
    unused, pullback = jax.vjp(gelu_gate, hidden[:, 0], hidden[:, 1])
    d_inner, d_gate = pullback(d_activated)
    d_hidden = jnp.stack([d_inner, d_gate], axis=1).astype(jnp.bfloat16)
    grad_inp = jnp.einsum("td,tcf->dcf", lowered_two, d_hidden, preferred_element_type=jnp.float32)
    d_normed_two = grad_total(
        jnp.einsum("tcf,dcf->td", d_hidden, w_inp, preferred_element_type=jnp.float32)
    )
    unused, pullback = jax.vjp(layer_norm, middle, gain_pair[1].astype(jnp.float32))
    d_mid_norm, d_gain_two = pullback(d_normed_two)
    d_middle = upstream + d_mid_norm
    d_branch = d_middle.astype(jnp.bfloat16)
    d_attended = jnp.einsum(
        "td,nd->tn", d_branch, w_out, preferred_element_type=jnp.float32
    ).astype(jnp.bfloat16)
    grad_out = jnp.einsum("tn,td->nd", attended, d_branch, preferred_element_type=jnp.float32)
    d_queries, d_keys, d_value = attend_backward(
        queries, key_all, value_all, log_total, d_attended, is_local
    )

    def turn(heads_in):
        return rotate(heads_in, cosine, sine_table)

    unused, pullback = jax.vjp(turn, d_queries)
    d_query_raw = pullback(d_queries)[0].reshape(row_count, local_width)
    d_key_raw = pullback(d_keys)[0].reshape(row_count, local_width)
    d_projected = jnp.stack(
        [d_query_raw, d_key_raw, d_value.reshape(row_count, local_width)], axis=1
    ).astype(jnp.bfloat16)
    grad_qkv = jnp.einsum("td,tcn->dcn", lowered, d_projected, preferred_element_type=jnp.float32)
    d_normed = grad_total(
        jnp.einsum("tcn,dcn->td", d_projected, w_qkv, preferred_element_type=jnp.float32)
    )
    unused, pullback = jax.vjp(layer_norm, residual, gain_pair[0].astype(jnp.float32))
    d_in_norm, d_gain_one = pullback(d_normed)
    gain_grads = jnp.stack([d_gain_one, d_gain_two])
    gradients = (grad_qkv, grad_out, grad_inp, grad_down, gain_grads)
    return (d_middle + d_in_norm, gradients)


def adam_update(weight, moment, square, gradient, step_rate, decay_here):
    moment_new = beta_one * moment + (1.0 - beta_one) * gradient
    square_new = beta_two * square + (1.0 - beta_two) * gradient * gradient
    moment_hat = moment_new / (1.0 - beta_one**STEP)
    square_hat = square_new / (1.0 - beta_two**STEP)
    updated = weight - step_rate * (
        moment_hat / (jnp.sqrt(square_hat) + adam_eps) + decay_here * weight
    )
    return (moment_new, square_new, updated)


def per_device(
    hidden_in,
    cotangent,
    qkv_weight,
    out_weight,
    in_weight,
    down_weight,
    norm_gains,
    qkv_moment_in,
    qkv_square_in,
    out_moment_in,
    out_square_in,
    in_moment_in,
    in_square_in,
    down_moment_in,
    down_square_in,
    gain_moment_in,
    gain_square_in,
):
    masters = (qkv_weight, out_weight, in_weight, down_weight, norm_gains)
    first_weights = gather_weights(masters, 0)
    inputs = hidden_in.astype(jnp.float32)
    lowered_first = layer_norm(inputs, first_weights[4][0].astype(jnp.float32)).astype(jnp.bfloat16)
    middle, kept_first = forward_layer(inputs, lowered_first, first_weights, True)
    second_weights = gather_weights(masters, 1)
    lowered_second = layer_norm(middle, second_weights[4][0].astype(jnp.float32)).astype(
        jnp.bfloat16
    )
    output, kept_second = forward_layer(middle, lowered_second, second_weights, False)
    d_middle, grads_second = backward_layer(
        cotangent.astype(jnp.float32), cotangent, second_weights, kept_second, False
    )
    d_values, grads_first = backward_layer(
        d_middle, d_middle.astype(jnp.bfloat16), first_weights, kept_first, True
    )
    reduced = (
        lax.psum_scatter(grads_first[0], "dp", scatter_dimension=0, tiled=True),
        lax.psum_scatter(grads_first[1], "dp", scatter_dimension=1, tiled=True),
        lax.psum_scatter(grads_first[2], "dp", scatter_dimension=0, tiled=True),
        lax.psum_scatter(grads_first[3], "dp", scatter_dimension=1, tiled=True),
        lax.psum_scatter(grads_first[4], "dp", scatter_dimension=1, tiled=True),
        lax.psum_scatter(grads_second[0], "dp", scatter_dimension=0, tiled=True),
        lax.psum_scatter(grads_second[1], "dp", scatter_dimension=1, tiled=True),
        lax.psum_scatter(grads_second[2], "dp", scatter_dimension=0, tiled=True),
        lax.psum_scatter(grads_second[3], "dp", scatter_dimension=1, tiled=True),
        lax.psum_scatter(grads_second[4], "dp", scatter_dimension=1, tiled=True),
    )
    reduced_first = reduced[:5]
    reduced_second = reduced[5:]
    g_qkv = jnp.stack([reduced_first[0], reduced_second[0]])
    g_out = jnp.stack([reduced_first[1], reduced_second[1]])
    g_inp = jnp.stack([reduced_first[2], reduced_second[2]])
    g_down = jnp.stack([reduced_first[3], reduced_second[3]])
    g_gain = jnp.stack([reduced_first[4], reduced_second[4]])
    qkv_m, qkv_s, qkv_w = adam_update(
        qkv_weight, qkv_moment_in, qkv_square_in, g_qkv, rate_qkv, weight_decay
    )
    out_m, out_s, out_w = adam_update(
        out_weight, out_moment_in, out_square_in, g_out, rate_out, weight_decay
    )
    inp_m, inp_s, inp_w = adam_update(
        in_weight, in_moment_in, in_square_in, g_inp, rate_inp, weight_decay
    )
    down_m, down_s, down_w = adam_update(
        down_weight, down_moment_in, down_square_in, g_down, rate_down, weight_decay
    )
    gain_m, gain_s, gain_w = adam_update(
        norm_gains, gain_moment_in, gain_square_in, g_gain, rate_gain, 0.0
    )
    final_out, final_grad = (output.astype(jnp.bfloat16), d_values)
    return (
        final_out,
        final_grad,
        qkv_m,
        qkv_s,
        qkv_w,
        out_m,
        out_s,
        out_w,
        inp_m,
        inp_s,
        inp_w,
        down_m,
        down_s,
        down_w,
        gain_m,
        gain_s,
        gain_w,
    )


def solution(mesh):
    return jax.shard_map(
        per_device,
        mesh=mesh,
        in_specs=(
            P("dp", None),
            P("dp", None),
            P(None, "dp", None, "tensor"),
            P(None, "tensor", "dp"),
            P(None, "dp", None, "tensor"),
            P(None, "tensor", "dp"),
            P(None, None, "dp"),
            P(None, "dp", None, "tensor"),
            P(None, "dp", None, "tensor"),
            P(None, "tensor", "dp"),
            P(None, "tensor", "dp"),
            P(None, "dp", None, "tensor"),
            P(None, "dp", None, "tensor"),
            P(None, "tensor", "dp"),
            P(None, "tensor", "dp"),
            P(None, None, "dp"),
            P(None, None, "dp"),
        ),
        out_specs=(
            P("dp", None),
            P("dp", None),
            P(None, "dp", None, "tensor"),
            P(None, "dp", None, "tensor"),
            P(None, "dp", None, "tensor"),
            P(None, "tensor", "dp"),
            P(None, "tensor", "dp"),
            P(None, "tensor", "dp"),
            P(None, "dp", None, "tensor"),
            P(None, "dp", None, "tensor"),
            P(None, "dp", None, "tensor"),
            P(None, "tensor", "dp"),
            P(None, "tensor", "dp"),
            P(None, "tensor", "dp"),
            P(None, None, "dp"),
            P(None, None, "dp"),
            P(None, None, "dp"),
        ),
        check_vma=False,
    )
```

profile of v0, /device:TPU:1, one launch (start us, length us, event | category | flops | bytes accessed | tf_op | source)
XLA Modules:
  0.0 2051.7 jit_solution(8636964310211172565)
XLA Ops:
  15.0 24.9 %all-gather = bf16[1,2,1024]{1,0,2:T(2,128)(2,1)S(1)} all-gather(bf16[1,2,64]{1,0,2:T(2,128)(2,1)S(1)} %get-tuple-element.184), channel_id=2, replica_groups=mesh['dp'=16,'tensor'=2] {'dp'}, dimensions={2}, use_global_device_ids=true | all-gather | bytes 4352 | tf_op jit(solution)/shard_map/all_gather | solution.py:67
  83.6 15.9 all-gather.21.cloned.1.call-done
  107.1 57.8 %all-reduce.23.cloned.1.call-done = bf16[1024,1024]{1,0:T(8,128)(2,1)} async-done(((bf16[1024,1024]{1,0:T(8,128)(2,1)}), bf16[1024,1024]{1,0:T(8,128)(2,1)}) %all-reduce.23.cloned.1.call-update) | async-done | bytes 2097168 | tf_op jit(solution)/shard_map/psum | solution.py:52
  168.3 59.1 %all-gather.23.cloned.1.call-done = bf16[1,1024,2,1312]{3,2,0,1:T(2,128)(2,1)} async-done(((bf16[1,64,2,1312]{3,2,0,1:T(2,128)(2,1)}), bf16[1,1024,2,1312]{3,2,0,1:T(2,128)(2,1)}) %all-gather.23.cloned.1.call-update) | async-done | bytes 5373968 | tf_op jit(solution)/shard_map/all_gather | solution.py:65
  227.4 15.3 copy.154
  283.7 20.4 all-gather.5
  311.4 30.4 %all-reduce.25.cloned.1.call-done = bf16[1024,1024]{1,0:T(8,128)(2,1)} async-done(((bf16[1024,1024]{1,0:T(8,128)(2,1)}), bf16[1024,1024]{1,0:T(8,128)(2,1)}) %all-reduce.25.cloned.1.call-update) | async-done | bytes 2097168 | tf_op jit(solution)/shard_map/psum | solution.py:52
  347.5 42.7 %all-gather.27.cloned.1.call-done = bf16[1,1024,3,512]{3,1,2,0:T(8,128)(2,1)} async-done(((bf16[1,64,3,512]{3,1,2,0:T(8,128)(2,1)}), bf16[1,1024,3,512]{3,1,2,0:T(8,128)(2,1)}) %all-gather.27.cloned.1.call-update) | async-done | bytes 3145744 | tf_op jit(solution)/shard_map/all_gather | solution.py:63
  413.6 13.7 fusion
  427.3 14.1 fusion.146
  445.8 30.1 %all-gather.33.cloned.1.call-done = bf16[1,1312,1024]{1,2,0:T(8,128)(2,1)} async-done(((bf16[1,1312,64]{1,2,0:T(8,128)(2,1)}), bf16[1,1312,1024]{1,2,0:T(8,128)(2,1)}) %all-gather.33.cloned.1.call-update) | async-done | bytes 2686992 | tf_op jit(solution)/shard_map/all_gather | solution.py:66
  482.9 53.1 %all-gather.31.cloned.1.call-done = bf16[1,1024,2,1312]{3,2,0,1:T(2,128)(2,1)} async-done(((bf16[1,64,2,1312]{3,2,0,1:T(2,128)(2,1)}), bf16[1,1024,2,1312]{3,2,0,1:T(2,128)(2,1)}) %all-gather.31.cloned.1.call-update) | async-done | bytes 5373968 | tf_op jit(solution)/shard_map/all_gather | solution.py:65
  536.0 15.0 copy.157
  551.0 49.0 %all-reduce.27.cloned.1.call-done = bf16[1024,1024]{1,0:T(8,128)(2,1)} async-done(((bf16[1024,1024]{1,0:T(8,128)(2,1)}), bf16[1024,1024]{1,0:T(8,128)(2,1)}) %all-reduce.27.cloned.1.call-update) | async-done | bytes 2097168 | tf_op jit(solution)/shard_map/psum | solution.py:52
  610.5 13.6 fusion.104
  639.5 63.0 %all-reduce.29.cloned.1.call-done = bf16[1024,1024]{1,0:T(8,128)(2,1)} async-done(((bf16[1024,1024]{1,0:T(8,128)(2,1)}), bf16[1024,1024]{1,0:T(8,128)(2,1)}) %all-reduce.29.cloned.1.call-update) | async-done | bytes 2097168 | tf_op jit(solution)/shard_map/psum | solution.py:57
  712.8 13.7 fusion.143
  726.5 22.4 %multiply_reduce_fusion = (f32[8,1024]{1,0:T(8,128)S(1)}, f32[8,1024,1024]{1,2,0:T(8,128)}) fusion(f32[8,1024,1024]{1,2,0:T(8,128)} %get-tuple-element.198, f32[8,1024]{1,0:T(8,128)S(1)} %log_add_fusion.1, bf16[1024,8,64]{0,2,1:T(8,128)(2,1)S(1)} %bitcast.470, bf16[1024,8,64]{0,2,1:T(8,128)(2,1)S(1)} %bitcast.472), kind=kOutput, calls=%fused_computation.1 | convolution fusion | flops 1107288064 | bytes 69271552 | tf_op jit(solution)/shard_map/sqhd,skhd->shqk/dot_general | solution.py:192
  750.2 28.4 %multiply_convert_fusion = bf16[8,1024,1024]{1,2,0:T(8,128)(2,1)} fusion(f32[8,1024,1024]{1,2,0:T(8,128)} %get-tuple-element.200, f32[8,1024,1024]{1,2,0:T(8,128)} %get-tuple-element.198, f32[8,1024]{1,0:T(8,128)S(1)} %get-tuple-element.199, f32[8,1024]{1,0:T(8,128)S(1)} %log_add_fusion.1), kind=kLoop, calls=%fused_computation | loop fusion | flops 41943040 | bytes 83951616 | tf_op jit(solution)/shard_map/convert_element_type | solution.py:196
  812.0 63.0 %all-reduce.31.cloned.1.call-done = bf16[1024,1024]{1,0:T(8,128)(2,1)} async-done(((bf16[1024,1024]{1,0:T(8,128)(2,1)}), bf16[1024,1024]{1,0:T(8,128)(2,1)}) %all-reduce.31.cloned.1.call-update) | async-done | bytes 2097168 | tf_op jit(solution)/shard_map/psum | solution.py:57
  914.0 55.4 %all-reduce.33.cloned.1.call-done = bf16[1024,1024]{1,0:T(8,128)(2,1)} async-done(((bf16[1024,1024]{1,0:T(8,128)(2,1)}), bf16[1024,1024]{1,0:T(8,128)(2,1)}) %all-reduce.33.cloned.1.call-update) | async-done | bytes 2097168 | tf_op jit(solution)/shard_map/psum | solution.py:57
  1042.8 15.6 add_convert_fusion.2
  1082.7 96.8 %all-reduce.35.cloned.1.call-done = (bf16[1024,1024]{1,0:T(8,128)(2,1)}, bf16[1024,1024]{1,0:T(8,128)(2,1)}) async-done(((bf16[1024,1024]{1,0:T(8,128)(2,1)}, bf16[1024,1024]{1,0:T(8,128)(2,1)}), (bf16[1024,1024]{1,0:T(8,128)(2,1)}, bf16[1024,1024]{1,0:T(8,128)(2,1)})) %all-reduce.35.cloned.1.call-update) | async-done | bytes 4194320 | tf_op jit(solution)/shard_map/psum | solution.py:52
  1250.7 51.6 %reduce-scatter.21.cloned.1.call-done = f32[512,64]{0,1:T(8,128)} async-done(((f32[512,1024]{0,1:T(8,128)}), f32[512,64]{0,1:T(8,128)}) %reduce-scatter.21.cloned.1.call-update) | async-done | bytes 131088 | tf_op jit(solution)/shard_map/reduce_scatter | solution.py:359
  1302.3 64.7 %reduce-scatter.19.cloned.1.call-done = f32[512,64]{0,1:T(8,128)} async-done(((f32[512,1024]{0,1:T(8,128)}), f32[512,64]{0,1:T(8,128)}) %reduce-scatter.19.cloned.1.call-update) | async-done | bytes 131088 | tf_op jit(solution)/shard_map/reduce_scatter | solution.py:354
  1377.6 47.9 %reduce-scatter.31.cloned.1.call-done = f32[64,2]{1,0:T(8,128)} async-done(((f32[1024,2]{1,0:T(8,128)}), f32[64,2]{1,0:T(8,128)}) %reduce-scatter.31.cloned.1.call-update) | async-done | bytes 528
  1427.0 84.8 %reduce-scatter.29.cloned.1.call-done = f32[1312,64]{0,1:T(8,128)} async-done(((f32[1312,1024]{0,1:T(8,128)}), f32[1312,64]{0,1:T(8,128)}) %reduce-scatter.29.cloned.1.call-update) | async-done | bytes 335888 | tf_op jit(solution)/shard_map/reduce_scatter | solution.py:361
  1511.7 85.2 %reduce-scatter.27.cloned.1.call-done = f32[1312,64]{0,1:T(8,128)} async-done(((f32[1312,1024]{0,1:T(8,128)}), f32[1312,64]{0,1:T(8,128)}) %reduce-scatter.27.cloned.1.call-update) | async-done | bytes 335888 | tf_op jit(solution)/shard_map/reduce_scatter | solution.py:356
  1600.2 85.4 %reduce-scatter.17.cloned.1.call-done = f32[64,3,512]{2,0,1:T(8,128)} async-done(((f32[1024,3,512]{2,0,1:T(8,128)}), f32[64,3,512]{2,0,1:T(8,128)}) %reduce-scatter.17.cloned.1.call-update) | async-done | bytes 393232 | tf_op jit(solution)/shard_map/reduce_scatter | solution.py:358
  1685.6 88.4 %reduce-scatter.15.cloned.1.call-done = f32[64,3,512]{2,0,1:T(8,128)} async-done(((f32[1024,3,512]{2,0,1:T(8,128)}), f32[64,3,512]{2,0,1:T(8,128)}) %reduce-scatter.15.cloned.1.call-update) | async-done | bytes 393232 | tf_op jit(solution)/shard_map/reduce_scatter | solution.py:353
  1777.5 127.0 %reduce-scatter.25.cloned.1.call-done = f32[64,2,1312]{2,0,1:T(8,128)} async-done(((f32[1024,2,1312]{2,0,1:T(8,128)}), f32[64,2,1312]{2,0,1:T(8,128)}) %reduce-scatter.25.cloned.1.call-update) | async-done | bytes 671760 | tf_op jit(solution)/shard_map/reduce_scatter | solution.py:360
  1904.5 130.2 %reduce-scatter.23.cloned.1.call-done = f32[64,2,1312]{2,0,1:T(8,128)} async-done(((f32[1024,2,1312]{2,0,1:T(8,128)}), f32[64,2,1312]{2,0,1:T(8,128)}) %reduce-scatter.23.cloned.1.call-update) | async-done | bytes 671760 | tf_op jit(solution)/shard_map/reduce_scatter | solution.py:355
  (443 shorter events, 456.5 us)
Async XLA Ops:
  7.2 52.7 %all-gather.19.cloned.1.call-start = ((), (), s32[]{:S(2)}) async-start(), calls=%async_computation.24 | async-start | bytes 3342336 | tf_op jit(solution)/shard_map/all_gather | solution.py:63
  9.4 90.1 %all-gather.21.cloned.1.call-start = ((), (), s32[]{:S(2)}) async-start(), calls=%async_computation.25 | async-start | bytes 1114112 | tf_op jit(solution)/shard_map/all_gather | solution.py:64
  11.1 153.9 %all-reduce.23.cloned.1.call-start = ((), (), s32[]{:S(2)}) async-start(), calls=%async_computation.10 | async-start | bytes 4194304 | tf_op jit(solution)/shard_map/psum | solution.py:52
  46.2 196.5 %copy-start.73 = (f32[1024]{0:T(1024)}, f32[1024]{0:T(1024)S(1)}, u32[]{:S(2)}) copy-start(f32[1024]{0:T(1024)S(1)} %get-tuple-element.95) | copy-start | bytes 12292
  103.4 124.0 %all-gather.23.cloned.1.call-start = ((), (), s32[]{:S(2)}) async-start(), calls=%async_computation.26 | async-start | bytes 6127616 | tf_op jit(solution)/shard_map/all_gather | solution.py:65
  106.2 167.2 %all-gather.25.cloned.1.call-start = ((), (), s32[]{:S(2)}) async-start(), calls=%async_computation.27 | async-start | bytes 3063808 | tf_op jit(solution)/shard_map/all_gather | solution.py:66
  107.1 234.7 %all-reduce.25.cloned.1.call-start = ((), (), s32[]{:S(2)}) async-start(), calls=%async_computation.11 | async-start | bytes 4194304 | tf_op jit(solution)/shard_map/psum | solution.py:52
  280.8 109.4 %all-gather.27.cloned.1.call-start = ((), (), s32[]{:S(2)}) async-start(), calls=%async_computation.28 | async-start | bytes 3342336 | tf_op jit(solution)/shard_map/all_gather | solution.py:63
  281.6 159.9 %all-gather.29.cloned.1.call-start = ((), (), s32[]{:S(2)}) async-start(), calls=%async_computation.29 | async-start | bytes 1114112 | tf_op jit(solution)/shard_map/all_gather | solution.py:64
  282.3 193.6 %all-gather.33.cloned.1.call-start = ((), (), s32[]{:S(2)}) async-start(), calls=%async_computation.31 | async-start | bytes 3063808 | tf_op jit(solution)/shard_map/all_gather | solution.py:66
  283.1 253.0 %all-gather.31.cloned.1.call-start = ((), (), s32[]{:S(2)}) async-start(), calls=%async_computation.30 | async-start | bytes 6127616 | tf_op jit(solution)/shard_map/all_gather | solution.py:65
  283.7 316.4 %all-reduce.27.cloned.1.call-start = ((), (), s32[]{:S(2)}) async-start(), calls=%async_computation.12 | async-start | bytes 4194304 | tf_op jit(solution)/shard_map/psum | solution.py:52
  310.4 397.1 %copy-start.85 = (f32[1024]{0:T(1024)}, f32[1024]{0:T(1024)S(1)}, u32[]{:S(2)}) copy-start(f32[1024]{0:T(1024)S(1)} %get-tuple-element.93) | copy-start | bytes 12292
  445.8 256.7 %all-reduce.29.cloned.1.call-start = ((), (), s32[]{:S(2)}) async-start(), calls=%async_computation.13 | async-start | bytes 4194304 | tf_op jit(solution)/shard_map/psum | solution.py:57
  639.4 235.5 %all-reduce.31.cloned.1.call-start = ((), (), s32[]{:S(2)}) async-start(), calls=%async_computation.14 | async-start | bytes 4194304 | tf_op jit(solution)/shard_map/psum | solution.py:57
  811.9 157.4 %all-reduce.33.cloned.1.call-start = ((), (), s32[]{:S(2)}) async-start(), calls=%async_computation.15 | async-start | bytes 4194304 | tf_op jit(solution)/shard_map/psum | solution.py:57
  906.3 273.2 %all-reduce.35.cloned.1.call-start = ((), (), s32[]{:S(2)}) async-start(), calls=%async_computation.34 | async-start | bytes 8388608 | tf_op jit(solution)/shard_map/psum | solution.py:52
  1071.1 178.7 %reduce-scatter.33.cloned.1.call-start = ((), (), s32[]{:S(2)}) async-start(), calls=%async_computation.33 | async-start | bytes 557056
  1072.8 229.5 %reduce-scatter.21.cloned.1.call-start = ((), (), s32[]{:S(2)}) async-start(), calls=%async_computation.19 | async-start | bytes 2228224 | tf_op jit(solution)/shard_map/reduce_scatter | solution.py:359
  1077.5 289.4 %reduce-scatter.19.cloned.1.call-start = ((), (), s32[]{:S(2)}) async-start(), calls=%async_computation.18 | async-start | bytes 2228224 | tf_op jit(solution)/shard_map/reduce_scatter | solution.py:354
  1082.6 342.9 %reduce-scatter.31.cloned.1.call-start = ((), (), s32[]{:S(2)}) async-start(), calls=%async_computation.32 | async-start | bytes 557056
  1186.1 325.7 %reduce-scatter.29.cloned.1.call-start = ((), (), s32[]{:S(2)}) async-start(), calls=%async_computation.23 | async-start | bytes 6127616 | tf_op jit(solution)/shard_map/reduce_scatter | solution.py:361
  1194.5 402.4 %reduce-scatter.27.cloned.1.call-start = ((), (), s32[]{:S(2)}) async-start(), calls=%async_computation.22 | async-start | bytes 6127616 | tf_op jit(solution)/shard_map/reduce_scatter | solution.py:356
  1203.6 482.0 %reduce-scatter.17.cloned.1.call-start = ((), (), s32[]{:S(2)}) async-start(), calls=%async_computation.17 | async-start | bytes 6684672 | tf_op jit(solution)/shard_map/reduce_scatter | solution.py:358
  1214.0 560.0 %reduce-scatter.15.cloned.1.call-start = ((), (), s32[]{:S(2)}) async-start(), calls=%async_computation.16 | async-start | bytes 6684672 | tf_op jit(solution)/shard_map/reduce_scatter | solution.py:353
  1223.2 681.4 %reduce-scatter.25.cloned.1.call-start = ((), (), s32[]{:S(2)}) async-start(), calls=%async_computation.21 | async-start | bytes 12255232 | tf_op jit(solution)/shard_map/reduce_scatter | solution.py:360
  1236.7 798.0 %reduce-scatter.23.cloned.1.call-start = ((), (), s32[]{:S(2)}) async-start(), calls=%async_computation.20 | async-start | bytes 12255232 | tf_op jit(solution)/shard_map/reduce_scatter | solution.py:355
  1249.7 117.2 %copy-start.58 = (f32[2,512,64]{1,2,0:T(8,128)S(1)}, f32[2,512,64]{1,2,0:T(8,128)}, u32[]{:S(2)}) copy-start(f32[2,512,64]{1,2,0:T(8,128)} %param.27) | copy-start | bytes 786436
  1249.7 117.2 %copy-start.59 = (f32[2,512,64]{1,2,0:T(8,128)S(1)}, f32[2,512,64]{1,2,0:T(8,128)}, u32[]{:S(2)}) copy-start(f32[2,512,64]{1,2,0:T(8,128)} %param.26) | copy-start | bytes 786436
  1374.1 222.8 %copy-start.39 = (f32[2,1312,64]{1,2,0:T(8,128)S(1)}, f32[2,1312,64]{1,2,0:T(8,128)}, u32[]{:S(2)}) copy-start(f32[2,1312,64]{1,2,0:T(8,128)} %param.22) | copy-start | bytes 2015236
  1377.6 396.4 %copy-start.37 = (f32[2,64,3,512]{3,1,2,0:T(8,128)S(1)}, f32[2,64,3,512]{3,1,2,0:T(8,128)}, u32[]{:S(2)}) copy-start(f32[2,64,3,512]{3,1,2,0:T(8,128)} %param.19) | copy-start | bytes 2359300
  1596.9 437.8 %copy-start.36 = (f32[2,64,2,1312]{3,2,1,0:T(2,128)S(1)}, f32[2,64,2,1312]{3,2,1,0:T(2,128)}, u32[]{:S(2)}) copy-start(f32[2,64,2,1312]{3,2,1,0:T(2,128)} %param.21) | copy-start | bytes 4030468
  (106 other events, 2567.3 us)
Sparse Core Ops, SparseCore 0:
  10.8 49.0 all-gather.18
  62.6 36.8 all-gather.20
  103.5 61.4 all-reduce.22
  167.9 59.4 all-gather.22
  230.4 42.9 all-gather.24
  281.0 60.7 all-reduce.24
  344.6 45.6 all-gather.26
  393.0 36.7 all-gather.28
  432.6 43.2 all-gather.32
  478.6 57.3 all-gather.30
  538.9 61.0 all-reduce.26
  639.6 62.9 all-reduce.28
  812.0 62.8 all-reduce.30
  906.4 62.9 all-reduce.32
  1071.2 108.2 all-reduce.34
  1183.9 53.8 reduce-scatter.32
  1241.4 60.8 reduce-scatter.20
  1306.4 60.5 reduce-scatter.18
  1371.1 54.3 reduce-scatter.30
  1429.8 81.9 reduce-scatter.28
  1516.1 80.7 reduce-scatter.26
  1601.3 84.2 reduce-scatter.16
  1689.6 84.3 reduce-scatter.14
  1778.5 125.9 reduce-scatter.24
  1908.6 126.0 reduce-scatter.22
where the time goes:
time: 2060 us; the launch traced here: 2050 us
  waiting for transfers between devices  1400 us (68%)
  matrix products  286 us (14%)
  other arithmetic  210 us (10%)
  local copies, waits for them, and re-layouts  93.5 us (5%)
  blocking collectives  45.3 us (2%)
    psum x4, waiting for transfers between devices, row_total(): lax.psum(partial_sum.astype(jnp.bfloat16), 'tensor').astype(jnp.float32)  234 us
    psum x3, waiting for transfers between devices, grad_total(): lax.psum(partial_sum.astype(jnp.bfloat16), 'tensor').astype(jnp.float32)  181 us
    reduce_scatter x1, waiting for transfers between devices, per_device(): lax.psum_scatter(grads_first[2], 'dp', scatter_dimension=0, tiled=True)  130 us
    reduce_scatter x1, waiting for transfers between devices, per_device(): lax.psum_scatter(grads_second[2], 'dp', scatter_dimension=0, tiled=True)  127 us
    all_gather x2, waiting for transfers between devices, gather_weights(): lax.all_gather(masters[2][layer_index].astype(jnp.bfloat16), 'dp', axis=0...  112 us
    reduce_scatter x1, waiting for transfers between devices, per_device(): lax.psum_scatter(grads_first[0], 'dp', scatter_dimension=0, tiled=True)  88.4 us
    reduce_scatter x1, waiting for transfers between devices, per_device(): lax.psum_scatter(grads_second[0], 'dp', scatter_dimension=0, tiled=True)  85.4 us
    reduce_scatter x1, waiting for transfers between devices, per_device(): lax.psum_scatter(grads_first[3], 'dp', scatter_dimension=1, tiled=True)  85.2 us
  transfers between devices with their start and end apart: 25, of which 23 were waited for; matrix products, arithmetic and copies ran while one was open for 13% of the time, Pallas kernels for 0%

commit v1 on v0

v1 whole, which is shorter than its diff:
```python
import jax
import jax.numpy as jnp
from jax import lax
from jax.sharding import Mesh, PartitionSpec as P

HEAD_DIM = 64
HALF_WIN = 64
STEP = 10
SEQ_LEN = 1024


norm_eps = 1e-05
theta_local = 10000.0
theta_global = 160000.0
masked_score = -1e30
beta_one = 0.9
beta_two = 0.98
adam_eps = 1e-06
weight_decay = 1e-05
rate_qkv = 0.03
rate_out = 0.15
rate_inp = 0.03
rate_down = 0.02
rate_gain = 0.5

every_axis = ("chip", "core", "tensor")
chip_axes = ("chip", "tensor")


def swap_pairs(chips):
    pairs = []
    for chip in range(chips):
        for core in range(2):
            for row in range(2):
                pairs.append((chip * 4 + core * 2 + row, chip * 4 + row * 2 + core))
    return pairs


def result_pairs(chips):
    return [(chip * 4 + c * 3, chip * 4 + c * 2 + 1 - c) for chip in range(chips) for c in range(2)]


def role_swap(values, chips):
    return lax.ppermute(values, every_axis, swap_pairs(chips))


def core_swap(values):
    return lax.ppermute(values, "core", [(0, 1), (1, 0)])


def core_total(partial_sum):
    own = partial_sum.astype(jnp.bfloat16)
    return own.astype(jnp.float32) + core_swap(own).astype(jnp.float32)


def layer_norm(values, gain):
    centred = values - jnp.mean(values, axis=-1, keepdims=True)
    spread = jnp.mean(centred * centred, axis=-1, keepdims=True)
    return centred * lax.rsqrt(spread + norm_eps) * gain


def rotary_tables(positions, rotary_base):
    inverse = rotary_base ** (-jnp.arange(0, HEAD_DIM, 2, dtype=jnp.float32) / HEAD_DIM)
    angles = positions.astype(jnp.float32)[:, None] * inverse[None, :]
    cosine = jnp.concatenate([jnp.cos(angles), jnp.cos(angles)], axis=-1)[:, None, :]
    sine_table = jnp.concatenate([jnp.sin(angles), jnp.sin(angles)], axis=-1)[:, None, :]
    return (cosine, sine_table)


def rotate(values, cosine, sine_table):
    half_dim = values.shape[-1] // 2
    turned = jnp.concatenate([-values[..., half_dim:], values[..., :half_dim]], axis=-1)
    return values * cosine + turned * sine_table


def gelu_gate(inner, gate_part):
    return jax.nn.gelu(inner, approximate=False) * gate_part


def gather_rows(shard, chips):
    return lax.all_gather(role_swap(shard, chips), chip_axes, axis=0, tiled=True)


def scatter_rows(gradient, chips):
    shard = lax.psum_scatter(
        gradient.astype(jnp.bfloat16), chip_axes, scatter_dimension=0, tiled=True
    )
    return role_swap(shard, chips).astype(jnp.float32)


def gather_weights(masters, layer, chips):
    qkv, out, inp, down, gains = [m[layer] for m in masters]
    rows = qkv.shape[0]
    qkv_rows = jnp.concatenate(
        [qkv.reshape(rows, -1), jnp.pad(gains.T, ((0, 0), (0, 126)))], axis=1
    ).astype(jnp.bfloat16)
    qkv_all = gather_rows(qkv_rows, chips)
    width = qkv.shape[1] * qkv.shape[2]
    return (
        qkv_all[:, :width],
        gather_rows(out.T.astype(jnp.bfloat16), chips),
        gather_rows(inp[:, 0].astype(jnp.bfloat16), chips),
        gather_rows(inp[:, 1].astype(jnp.bfloat16), chips),
        gather_rows(down.T.astype(jnp.bfloat16), chips),
        qkv_all[:, width : width + 2].T.astype(jnp.float32),
    )


def band_view(heads, half_width):
    block = 2 * half_width
    seq_count, length = (heads.shape[0], heads.shape[1])
    count = length // block
    padded = jnp.pad(heads, ((0, 0), (half_width, half_width), (0, 0), (0, 0)))
    first = padded[:, :length].reshape(seq_count, count, block, heads.shape[2], heads.shape[3])
    second = padded[:, block:].reshape(seq_count, count, block, heads.shape[2], heads.shape[3])
    return jnp.concatenate([first, second], axis=2)


def band_fold(band, half_width, length):
    block = 2 * half_width
    seq_count = band.shape[0]
    first = band[:, :, :block].reshape(seq_count, length, band.shape[3], band.shape[4])
    second = band[:, :, block:].reshape(seq_count, length, band.shape[3], band.shape[4])
    padding = ((0, 0), (0, block), (0, 0), (0, 0))
    total = jnp.pad(first, padding) + jnp.pad(second, ((0, 0), (block, 0), (0, 0), (0, 0)))
    return total[:, half_width : half_width + length]


def band_mask(length, half_width):
    block = 2 * half_width
    count = length // block
    query_at = jnp.arange(block, dtype=jnp.int32)[None, :, None]
    key_at = jnp.arange(2 * block, dtype=jnp.int32)[None, None, :]
    start = jnp.arange(count, dtype=jnp.int32)[:, None, None] * block
    key_pos = start - half_width + key_at
    near = jnp.abs(query_at - key_at + half_width) <= half_width
    return near & (key_pos >= 0) & (key_pos < length)


def local_probability(queries, key_all):
    seq_count, length, heads_here, head_size = queries.shape
    block = 2 * HALF_WIN
    query_blocks = queries.reshape(seq_count, length // block, block, heads_here, head_size)
    key_band = band_view(key_all, HALF_WIN)
    scores = (
        jnp.einsum("sbqhd,sbkhd->sbhqk", query_blocks, key_band, preferred_element_type=jnp.float32)
        * 0.125
    )
    allowed = band_mask(length, HALF_WIN)[None, :, None]
    return (jnp.where(allowed, scores, masked_score), allowed, query_blocks, key_band)


def global_scores(queries, key_all):
    return (
        jnp.einsum("sqhd,skhd->shqk", queries, key_all, preferred_element_type=jnp.float32) * 0.125
    )


def attend_forward(queries, key_all, value_all, is_local):
    seq_count, length, heads_here, head_size = queries.shape
    if is_local:
        scores, allowed, query_blocks, key_band = local_probability(queries, key_all)
    else:
        scores = global_scores(queries, key_all)
    row_max = jnp.max(scores, axis=-1, keepdims=True)
    exponent = jnp.exp(scores - row_max)
    exp_total = jnp.sum(exponent, axis=-1, keepdims=True)
    probability = (exponent / exp_total).astype(jnp.bfloat16)
    if is_local:
        value_band = band_view(value_all, HALF_WIN)
        attended = jnp.einsum(
            "sbhqk,sbkhd->sbqhd", probability, value_band, preferred_element_type=jnp.float32
        )
    else:
        attended = jnp.einsum(
            "shqk,skhd->sqhd", probability, value_all, preferred_element_type=jnp.float32
        )
    return (
        attended.reshape(seq_count * length, heads_here * head_size),
        row_max + jnp.log(exp_total),
    )


def attend_backward(queries, key_all, value_all, log_total, d_attended, is_local):
    seq_count, length, heads_here, head_size = queries.shape
    if is_local:
        block = 2 * HALF_WIN
        scores, allowed, query_blocks, key_band = local_probability(queries, key_all)
        probability = jnp.where(allowed, jnp.exp(scores - log_total), 0.0)
        value_band = band_view(value_all, HALF_WIN)
        d_blocks = d_attended.reshape(seq_count, length // block, block, heads_here, head_size)
        d_value = band_fold(
            jnp.einsum(
                "sbhqk,sbqhd->sbkhd",
                probability.astype(jnp.bfloat16),
                d_blocks,
                preferred_element_type=jnp.float32,
            ),
            HALF_WIN,
            length,
        )
        d_probability = jnp.einsum(
            "sbqhd,sbkhd->sbhqk", d_blocks, value_band, preferred_element_type=jnp.float32
        )
        centre = jnp.sum(probability * d_probability, axis=-1, keepdims=True)
        d_scores = (probability * (d_probability - centre)).astype(jnp.bfloat16)
        d_queries = jnp.einsum(
            "sbhqk,sbkhd->sbqhd", d_scores, key_band, preferred_element_type=jnp.float32
        )
        d_queries = d_queries.reshape(seq_count, length, heads_here, head_size) * 0.125
        d_keys = (
            band_fold(
                jnp.einsum(
                    "sbhqk,sbqhd->sbkhd", d_scores, query_blocks, preferred_element_type=jnp.float32
                ),
                HALF_WIN,
                length,
            )
            * 0.125
        )
    else:
        d_heads = d_attended.reshape(seq_count, length, heads_here, head_size)
        probability = jnp.exp(global_scores(queries, key_all) - log_total)
        d_value = jnp.einsum(
            "shqk,sqhd->skhd",
            probability.astype(jnp.bfloat16),
            d_heads,
            preferred_element_type=jnp.float32,
        )
        d_probability = jnp.einsum(
            "sqhd,skhd->shqk", d_heads, value_all, preferred_element_type=jnp.float32
        )
        centre = jnp.sum(probability * d_probability, axis=-1, keepdims=True)
        d_scores = (probability * (d_probability - centre)).astype(jnp.bfloat16)
        d_queries = (
            jnp.einsum("shqk,skhd->sqhd", d_scores, key_all, preferred_element_type=jnp.float32)
            * 0.125
        )
        d_keys = (
            jnp.einsum("shqk,sqhd->skhd", d_scores, queries, preferred_element_type=jnp.float32)
            * 0.125
        )
    return (d_queries, d_keys, d_value)


def product(left, right, contract):
    return lax.dot_general(
        left, right, ((contract[:1], contract[1:]), ((), ())), preferred_element_type=jnp.float32
    )


def forward_layer(residual, weights, is_local):
    w_qkv, w_out, w_inner, w_gate, w_down, gain_pair = weights
    lowered = layer_norm(residual, gain_pair[0]).astype(jnp.bfloat16)
    row_count = lowered.shape[0]
    seq_count = row_count // SEQ_LEN
    local_width = w_qkv.shape[1] // 3
    heads_here = local_width // HEAD_DIM
    positions = jnp.arange(SEQ_LEN, dtype=jnp.int32)
    cosine, sine_table = rotary_tables(positions, theta_local if is_local else theta_global)
    projected = product(lowered, w_qkv, (1, 0))
    shape_four = (seq_count, SEQ_LEN, heads_here, HEAD_DIM)
    raw = [projected[:, i * local_width : (i + 1) * local_width] for i in range(3)]
    queries = rotate(raw[0].reshape(shape_four), cosine, sine_table).astype(jnp.bfloat16)
    key_all = rotate(raw[1].reshape(shape_four), cosine, sine_table).astype(jnp.bfloat16)
    value_all = raw[2].astype(jnp.bfloat16).reshape(shape_four)
    attended, log_total = attend_forward(queries, key_all, value_all, is_local)
    attended = attended.astype(jnp.bfloat16)
    middle = residual + core_total(product(attended, w_out, (1, 1)))
    lowered_two = layer_norm(middle, gain_pair[1]).astype(jnp.bfloat16)
    inner = product(lowered_two, w_inner, (1, 0))
    gate_part = product(lowered_two, w_gate, (1, 0))
    activated = gelu_gate(inner, gate_part).astype(jnp.bfloat16)
    output = middle + core_total(product(activated, w_down, (1, 1)))
    kept = (
        residual,
        middle,
        lowered,
        lowered_two,
        queries,
        key_all,
        value_all,
        log_total,
        attended,
        inner,
        gate_part,
        activated,
        cosine,
        sine_table,
    )
    return (output, kept)


def backward_layer(upstream, weights, kept, is_local, chips):
    w_qkv, w_out, w_inner, w_gate, w_down, gain_pair = weights
    (
        residual,
        middle,
        lowered,
        lowered_two,
        queries,
        key_all,
        value_all,
        log_total,
        attended,
        inner,
        gate_part,
        activated,
        cosine,
        sine_table,
    ) = kept
    row_count = lowered.shape[0]
    local_width = w_qkv.shape[1] // 3
    up_low = upstream.astype(jnp.bfloat16)
    d_activated = product(up_low, w_down, (1, 0))
    grad_down = scatter_rows(product(up_low, activated, (0, 0)), chips)
    unused, pullback = jax.vjp(gelu_gate, inner, gate_part)
    d_inner, d_gate = [v.astype(jnp.bfloat16) for v in pullback(d_activated)]
    grad_inner = scatter_rows(product(lowered_two, d_inner, (0, 0)), chips)
    grad_gate = scatter_rows(product(lowered_two, d_gate, (0, 0)), chips)
    d_normed_two = core_total(
        product(d_inner, w_inner, (1, 1)) + product(d_gate, w_gate, (1, 1))
    )
    unused, pullback = jax.vjp(layer_norm, middle, gain_pair[1])
    d_mid_norm, d_gain_two = pullback(d_normed_two)
    d_middle = upstream + d_mid_norm
    d_branch = d_middle.astype(jnp.bfloat16)
    d_attended = product(d_branch, w_out, (1, 0)).astype(jnp.bfloat16)
    grad_out = scatter_rows(product(d_branch, attended, (0, 0)), chips)
    d_queries, d_keys, d_value = attend_backward(
        queries, key_all, value_all, log_total, d_attended, is_local
    )

    def turn(heads_in):
        return rotate(heads_in, cosine, sine_table)

    unused, pullback = jax.vjp(turn, d_queries)
    d_query_raw = pullback(d_queries)[0].reshape(row_count, local_width)
    d_key_raw = pullback(d_keys)[0].reshape(row_count, local_width)
    d_projected = jnp.concatenate(
        [d_query_raw, d_key_raw, d_value.reshape(row_count, local_width)], axis=1
    ).astype(jnp.bfloat16)
    d_normed = core_total(product(d_projected, w_qkv, (1, 1)))
    unused, pullback = jax.vjp(layer_norm, residual, gain_pair[0])
    d_in_norm, d_gain_one = pullback(d_normed)
    gains = jnp.pad(jnp.stack([d_gain_one, d_gain_two], axis=1), ((0, 0), (0, 126)))
    grad_qkv = scatter_rows(
        jnp.concatenate([product(lowered, d_projected, (0, 0)), gains], axis=1), chips
    )
    rows = grad_qkv.shape[0]
    width = 3 * local_width
    gradients = (
        grad_qkv[:, :width].reshape(rows, 3, local_width),
        grad_out.T,
        jnp.stack([grad_inner, grad_gate], axis=1),
        grad_down.T,
        grad_qkv[:, width : width + 2].T,
    )
    return (d_middle + d_in_norm, gradients)


def adam_update(weight, moment, square, gradient, step_rate, decay_here):
    moment_new = beta_one * moment + (1.0 - beta_one) * gradient
    square_new = beta_two * square + (1.0 - beta_two) * gradient * gradient
    moment_hat = moment_new / (1.0 - beta_one**STEP)
    square_hat = square_new / (1.0 - beta_two**STEP)
    updated = weight - step_rate * (
        moment_hat / (jnp.sqrt(square_hat) + adam_eps) + decay_here * weight
    )
    return (moment_new, square_new, updated)


def per_device(chips, hidden_in, cotangent, *state):
    masters = state[:5]
    moments = state[5:]
    same = lax.axis_index("core") == lax.axis_index("tensor")

    def chip_sequence(values):
        return jnp.where(same, values, core_swap(values)).astype(jnp.float32)

    def own_sequence(values):
        return jnp.where(same, values, lax.ppermute(values, every_axis, result_pairs(chips)))

    inputs = chip_sequence(hidden_in)
    upstream = chip_sequence(cotangent)
    first_weights = gather_weights(masters, 0, chips)
    second_weights = gather_weights(masters, 1, chips)
    middle, kept_first = forward_layer(inputs, first_weights, True)
    output, kept_second = forward_layer(middle, second_weights, False)
    final_out = own_sequence(output.astype(jnp.bfloat16))
    d_middle, grads_second = backward_layer(upstream, second_weights, kept_second, False, chips)
    d_values, grads_first = backward_layer(d_middle, first_weights, kept_first, True, chips)
    final_grad = own_sequence(d_values.astype(jnp.bfloat16)).astype(jnp.float32)
    rates = (rate_qkv, rate_out, rate_inp, rate_down, rate_gain)
    results = [final_out, final_grad]
    for i, rate in enumerate(rates):
        gradient = jnp.stack([grads_first[i], grads_second[i]])
        decay = 0.0 if i == 4 else weight_decay
        results += adam_update(
            masters[i], moments[2 * i], moments[2 * i + 1], gradient, rate, decay
        )
    return tuple(results)


def solution(mesh):
    chips = mesh.shape["dp"] // 2
    fine = Mesh(mesh.devices.reshape(chips, 2, mesh.shape["tensor"]), every_axis)
    dp = ("chip", "core")
    tokens = P(dp, None)
    first = P(None, dp, None, "tensor")
    second = P(None, "tensor", dp)
    gain = P(None, None, dp)
    weights = (first, second, first, second, gain)
    pairs = tuple(s for s in weights for unused in range(2))
    triples = tuple(s for s in weights for unused in range(3))

    def body(*arguments):
        return per_device(chips, *arguments)

    return jax.shard_map(
        body,
        mesh=fine,
        in_specs=(tokens, tokens) + weights + pairs,
        out_specs=(tokens, tokens) + triples,
        check_vma=False,
    )
```

time: 2060 us -> 1600 us (0.78)
  waiting for transfers between devices: 1400 us -> 858 us
  starting transfers between devices: 1.66 us -> 118 us
  blocking collectives: 45.3 us -> 0 us
    psum x7 -> x0, waiting for transfers between devices: 416 us -> none  [the longest x4 234 us: row_total(): lax.psum(partial_sum.astype(jnp.bfloat16), 'tensor').astype(jnp.float32)]
    reduce_scatter x8 -> x10, waiting for transfers between devices: 717 us -> 376 us  [scatter_rows(): lax.psum_scatter(gradient.astype(jnp.bfloat16), chip_axes, scatter_dimens...]
    all_gather x8 -> x10, waiting for transfers between devices: 215 us -> 401 us  [gather_rows(): lax.all_gather(role_swap(shard, chips), chip_axes, axis=0, tiled=True)]
    ppermute x0 -> x32, starting transfers between devices: none -> 116 us  [the longest x20 105 us: role_swap(): return lax.ppermute(values, every_axis, swap_pairs(chips))]
    ppermute x0 -> x32, waiting for transfers between devices: none -> 80.3 us  [the longest x2 43.6 us: own_sequence(): lax.ppermute(values, every_axis, result_pairs(chips))]
    unnamed x27 -> x20, waiting for transfers between devices: 50.9 us -> 0.33 us
    all_gather x2 -> x0, blocking collectives: 45.3 us -> none  [gather_weights(): lax.all_gather(masters[4][layer_index].astype(jnp.bfloat16), 'dp', axis=1...]
    all_gather x2 -> x0, local copies, waits for them, and re-layouts: 30.3 us -> none  [gather_weights(): lax.all_gather(masters[2][layer_index].astype(jnp.bfloat16), 'dp', axis=0...]
  transfers between devices with their start and end apart: 25 -> 52, of which waited for: 23 -> 28; matrix products, arithmetic and copies ran while one was open for 13% -> 33% of each run, Pallas kernels for 0% -> 0%
where the time goes in v1:
time: 1600 us; the launch traced here: 1590 us
  waiting for transfers between devices  858 us (54%)
  matrix products  301 us (19%)
  other arithmetic  207 us (13%)
  starting transfers between devices  118 us (7%)
  local copies, waits for them, and re-layouts  88.2 us (6%)
  between operations  17.1 us (1%)
    all_gather x10, waiting for transfers between devices, gather_rows(): lax.all_gather(role_swap(shard, chips), chip_axes, axis=0, tiled=True)  401 us
    reduce_scatter x10, waiting for transfers between devices, scatter_rows(): lax.psum_scatter(gradient.astype(jnp.bfloat16), chip_axes, scatter_dimens...  376 us
    dot_general x30, matrix products, product(): lax.dot_general(left, right, ((contract[:1], contract[1:]), ((), ())), pr...  194 us
    ppermute x20, starting transfers between devices, role_swap(): return lax.ppermute(values, every_axis, swap_pairs(chips))  105 us
    unnamed x281, local copies, waits for them, and re-layouts  50 us
    ppermute x2, waiting for transfers between devices, own_sequence(): lax.ppermute(values, every_axis, result_pairs(chips))  43.6 us
  transfers between devices with their start and end apart: 52, of which 28 were waited for; matrix products, arithmetic and copies ran while one was open for 33% of the time, Pallas kernels for 0%

profile of v1, /device:TPU:1, one launch (start us, length us, event | category | flops | bytes accessed | tf_op | source)
XLA Modules:
  0.0 1588.7 jit_solution(1038281591264968271)
XLA Ops:
  68.8 20.0 %all-gather.11.cloned.1.call-done = bf16[1024,1664]{1,0:T(8,128)(2,1)} async-done(((bf16[64,1664]{1,0:T(8,128)(2,1)}), bf16[1024,1664]{1,0:T(8,128)(2,1)}) %all-gather.11.cloned.1.call-update) | async-done | bytes 3407888 | tf_op jit(solution)/shard_map/all_gather | solution.py:81
  128.7 16.5 %all-gather.13.cloned.1.call-done = bf16[1024,512]{1,0:T(8,128)(2,1)} async-done(((bf16[64,512]{1,0:T(8,128)(2,1)}), bf16[1024,512]{1,0:T(8,128)(2,1)}) %all-gather.13.cloned.1.call-update) | async-done | bytes 1048592 | tf_op jit(solution)/shard_map/all_gather | solution.py:81
  171.8 41.0 %all-gather.15.cloned.1.call-done = bf16[1024,1312]{1,0:T(8,128)(2,1)} async-done(((bf16[64,1312]{1,0:T(8,128)(2,1)}), bf16[1024,1312]{1,0:T(8,128)(2,1)}) %all-gather.15.cloned.1.call-update) | async-done | bytes 2686992 | tf_op jit(solution)/shard_map/all_gather | solution.py:81
  219.5 61.0 %all-gather.17.cloned.1.call-done = bf16[1024,1312]{1,0:T(8,128)(2,1)} async-done(((bf16[64,1312]{1,0:T(8,128)(2,1)}), bf16[1024,1312]{1,0:T(8,128)(2,1)}) %all-gather.17.cloned.1.call-update) | async-done | bytes 2686992 | tf_op jit(solution)/shard_map/all_gather | solution.py:81
  280.5 19.3 %multiply_convert_fusion.5 = (bf16[1024,1312]{0,1:T(8,128)(2,1)}, f32[1024,1312]{0,1:T(8,128)}, f32[1024,1312]{0,1:T(8,128)}) fusion(f32[1024,1312]{0,1:T(8,128)} %fusion.161, bf16[1024,1024]{0,1:T(8,128)(2,1)S(1)} %multiply_convert_fusion.8, bf16[1024,1312]{1,0:T(8,128)(2,1)} %all-gather.17.cloned.1.call-done), kind=kOutput, calls=%fused_computation.53 | convolution fusion | flops 2840133632 | bytes 23592960 | tf_op jit(solution)/shard_map/dot_general | solution.py:247
  299.8 48.8 %all-gather.19.cloned.1.call-done = bf16[1024,1312]{1,0:T(8,128)(2,1)} async-done(((bf16[64,1312]{1,0:T(8,128)(2,1)}), bf16[1024,1312]{1,0:T(8,128)(2,1)}) %all-gather.19.cloned.1.call-update) | async-done | bytes 2686992 | tf_op jit(solution)/shard_map/all_gather | solution.py:81
  367.9 53.5 %all-gather.21.cloned.1.call-done = bf16[1024,1664]{1,0:T(8,128)(2,1)} async-done(((bf16[64,1664]{1,0:T(8,128)(2,1)}), bf16[1024,1664]{1,0:T(8,128)(2,1)}) %all-gather.21.cloned.1.call-update) | async-done | bytes 3407888 | tf_op jit(solution)/shard_map/all_gather | solution.py:81
  447.2 13.2 multiply_reduce_fusion.1
  460.4 13.7 fusion
  476.4 13.2 fusion.78
  507.1 39.1 %all-gather.27.cloned.1.call-done = bf16[1024,1312]{1,0:T(8,128)(2,1)} async-done(((bf16[64,1312]{1,0:T(8,128)(2,1)}), bf16[1024,1312]{1,0:T(8,128)(2,1)}) %all-gather.27.cloned.1.call-update) | async-done | bytes 2686992 | tf_op jit(solution)/shard_map/all_gather | solution.py:81
  553.9 60.6 %all-gather.25.cloned.1.call-done = bf16[1024,1312]{1,0:T(8,128)(2,1)} async-done(((bf16[64,1312]{1,0:T(8,128)(2,1)}), bf16[1024,1312]{1,0:T(8,128)(2,1)}) %all-gather.25.cloned.1.call-update) | async-done | bytes 2686992 | tf_op jit(solution)/shard_map/all_gather | solution.py:81
  622.3 60.4 %all-gather.29.cloned.1.call-done = bf16[1024,1312]{1,0:T(8,128)(2,1)} async-done(((bf16[64,1312]{1,0:T(8,128)(2,1)}), bf16[1024,1312]{1,0:T(8,128)(2,1)}) %all-gather.29.cloned.1.call-update) | async-done | bytes 2686992 | tf_op jit(solution)/shard_map/all_gather | solution.py:81
  682.6 21.0 %add_convert_fusion.1 = (bf16[1024,1312]{0,1:T(8,128)(2,1)}, f32[1024,1312]{0,1:T(8,128)}, f32[1024,1312]{0,1:T(8,128)}) fusion(f32[1024,1312]{0,1:T(8,128)} %fusion.163, f32[1024,1312]{0,1:T(8,128)} %fusion.162, bf16[1024,1024]{0,1:T(8,128)(2,1)S(1)} %broadcast_select_fusion, bf16[1024,1312]{1,0:T(8,128)(2,1)} %all-gather.29.cloned.1.call-done), kind=kOutput, calls=%fused_computation.39 | convolution fusion | flops 2849538048 | bytes 28966912 | tf_op jit(solution)/shard_map/dot_general | solution.py:247
  703.6 12.5 multiply_convert_fusion.3
  762.0 22.9 %multiply_reduce_fusion = (f32[8,1024]{1,0:T(8,128)S(1)}, f32[8,1024,1024]{1,2,0:T(8,128)}) fusion(f32[8,1024,1024]{1,2,0:T(8,128)} %get-tuple-element.207, f32[8,1024]{1,0:T(8,128)S(1)} %log_add_fusion.1, bf16[1024,8,64]{0,2,1:T(8,128)(2,1)S(1)} %bitcast.286, bf16[1024,8,64]{0,2,1:T(8,128)(2,1)S(1)} %bitcast.289), kind=kOutput, calls=%fused_computation.1 | convolution fusion | flops 1107288064 | bytes 69271552 | tf_op jit(solution)/shard_map/sqhd,skhd->shqk/dot_general | solution.py:230
  784.9 28.4 %multiply_convert_fusion = bf16[8,1024,1024]{1,2,0:T(8,128)(2,1)} fusion(f32[8,1024,1024]{1,2,0:T(8,128)} %get-tuple-element.210, f32[8,1024,1024]{1,2,0:T(8,128)} %get-tuple-element.207, f32[8,1024]{1,0:T(8,128)S(1)} %get-tuple-element.209, f32[8,1024]{1,0:T(8,128)S(1)} %log_add_fusion.1), kind=kLoop, calls=%fused_computation | loop fusion | flops 41943040 | bytes 83951616 | tf_op jit(solution)/shard_map/convert_element_type | solution.py:234
  813.3 11.4 fusion.164
  837.2 15.0 fusion.75
  986.4 10.5 broadcast_multiply_fusion.1
  1001.6 16.5 %add_convert_fusion.7 = (bf16[1,1024,8,64]{1,0,3,2:T(2,128)(2,1)S(1)}, bf16[1,1024,8,64]{1,0,3,2:T(2,128)(2,1)S(1)}) fusion(f32[1,1024,8,32]{1,0,3,2:T(1,128)S(1)} %get-tuple-element.142, f32[1,1024,8,32]{1,0,3,2:T(1,128)S(1)} %get-tuple-element.141, f32[1,1024,8,64]{1,0,3,2:T(1,128)S(1)} %bitcast.264, f32[1024,64]{0,1:T(8,128)S(1)} %copy-done.53, ...), kind=kLoop, calls=%fused_computation.163 | loop fusion | flops 4718592 | bytes 12845056 | tf_op jit(solution)/shard_map/convert.43
  1040.4 43.6 %collective-permute-done.15 = bf16[1024,1024]{0,1:T(8,128)(2,1)S(1)} collective-permute-done((bf16[1024,1024]{0,1:T(8,128)(2,1)}, bf16[1024,1024]{0,1:T(8,128)(2,1)S(1)}, u32[]{:S(2)}, u32[]{:S(2)}) %collective-permute-start.15) | collective-permute-done | bytes 2097184 | tf_op jit(solution)/shard_map/ppermute | solution.py:382
  1109.6 30.7 %reduce-scatter.15.cloned.1.call-done = bf16[64,512]{1,0:T(8,128)(2,1)} async-done(((bf16[1024,512]{1,0:T(8,128)(2,1)}), bf16[64,512]{1,0:T(8,128)(2,1)}) %reduce-scatter.15.cloned.1.call-update) | async-done | bytes 65552 | tf_op jit(solution)/shard_map/reduce_scatter | solution.py:85
  1140.2 10.3 collective-permute-start.24
  1152.4 70.9 %reduce-scatter.19.cloned.1.call-done = bf16[64,1312]{1,0:T(8,128)(2,1)} async-done(((bf16[1024,1312]{1,0:T(8,128)(2,1)}), bf16[64,1312]{1,0:T(8,128)(2,1)}) %reduce-scatter.19.cloned.1.call-update) | async-done | bytes 167952 | tf_op jit(solution)/shard_map/reduce_scatter | solution.py:85
  1233.5 72.6 %reduce-scatter.21.cloned.1.call-done = bf16[64,1312]{1,0:T(8,128)(2,1)} async-done(((bf16[1024,1312]{1,0:T(8,128)(2,1)}), bf16[64,1312]{1,0:T(8,128)(2,1)}) %reduce-scatter.21.cloned.1.call-update) | async-done | bytes 167952 | tf_op jit(solution)/shard_map/reduce_scatter | solution.py:85
  1306.1 10.7 collective-permute-start.27
  1319.0 70.4 %reduce-scatter.27.cloned.1.call-done = bf16[64,1312]{1,0:T(8,128)(2,1)} async-done(((bf16[1024,1312]{1,0:T(8,128)(2,1)}), bf16[64,1312]{1,0:T(8,128)(2,1)}) %reduce-scatter.27.cloned.1.call-update) | async-done | bytes 167952 | tf_op jit(solution)/shard_map/reduce_scatter | solution.py:85
  1389.4 10.9 collective-permute-start.30
  1413.8 62.7 %reduce-scatter.13.cloned.1.call-done = bf16[64,1664]{1,0:T(8,128)(2,1)} async-done(((bf16[1024,1664]{1,0:T(8,128)(2,1)}), bf16[64,1664]{1,0:T(8,128)(2,1)}) %reduce-scatter.13.cloned.1.call-update) | async-done | bytes 213008 | tf_op jit(solution)/shard_map/reduce_scatter | solution.py:85
  1476.5 10.5 collective-permute-start.23
  1495.1 68.8 %reduce-scatter.11.cloned.1.call-done = bf16[64,1664]{1,0:T(8,128)(2,1)} async-done(((bf16[1024,1664]{1,0:T(8,128)(2,1)}), bf16[64,1664]{1,0:T(8,128)(2,1)}) %reduce-scatter.11.cloned.1.call-update) | async-done | bytes 213008 | tf_op jit(solution)/shard_map/reduce_scatter | solution.py:85
  (568 shorter events, 510.9 us)
Async XLA Ops:
  7.2 81.6 %all-gather.11.cloned.1.call-start = ((), (), s32[]{:S(2)}) async-start(), calls=%async_computation.10 | async-start | bytes 3620864 | tf_op jit(solution)/shard_map/all_gather | solution.py:81
  18.5 126.7 %all-gather.13.cloned.1.call-start = ((), (), s32[]{:S(2)}) async-start(), calls=%async_computation.11 | async-start | bytes 1114112 | tf_op jit(solution)/shard_map/all_gather | solution.py:81
  26.3 186.5 %all-gather.15.cloned.1.call-start = ((), (), s32[]{:S(2)}) async-start(), calls=%async_computation.12 | async-start | bytes 3063808 | tf_op jit(solution)/shard_map/all_gather | solution.py:81
  35.3 245.2 %all-gather.17.cloned.1.call-start = ((), (), s32[]{:S(2)}) async-start(), calls=%async_computation.13 | async-start | bytes 3063808 | tf_op jit(solution)/shard_map/all_gather | solution.py:81
  42.8 305.8 %all-gather.19.cloned.1.call-start = ((), (), s32[]{:S(2)}) async-start(), calls=%async_computation.14 | async-start | bytes 3063808 | tf_op jit(solution)/shard_map/all_gather | solution.py:81
  53.8 367.6 %all-gather.21.cloned.1.call-start = ((), (), s32[]{:S(2)}) async-start(), calls=%async_computation.15 | async-start | bytes 3620864 | tf_op jit(solution)/shard_map/all_gather | solution.py:81
  65.1 424.5 %all-gather.23.cloned.1.call-start = ((), (), s32[]{:S(2)}) async-start(), calls=%async_computation.16 | async-start | bytes 1114112 | tf_op jit(solution)/shard_map/all_gather | solution.py:81
  156.7 389.5 %all-gather.27.cloned.1.call-start = ((), (), s32[]{:S(2)}) async-start(), calls=%async_computation.18 | async-start | bytes 3063808 | tf_op jit(solution)/shard_map/all_gather | solution.py:81
  165.3 449.1 %all-gather.25.cloned.1.call-start = ((), (), s32[]{:S(2)}) async-start(), calls=%async_computation.17 | async-start | bytes 3063808 | tf_op jit(solution)/shard_map/all_gather | solution.py:81
  356.1 66.8 %collective-permute-start.7 = (bf16[1024,1024]{0,1:T(8,128)(2,1)}, bf16[1024,1024]{0,1:T(8,128)(2,1)}, u32[]{:S(2)}, u32[]{:S(2)}) collective-permute-start(bf16[1024,1024]{0,1:T(8,128)(2,1)} %convolution_convert_fusion.10), channel_id=1, source_target_pairs={{0,2},{2,0},{1,3},{3,1},{4,6},{6,4},{5,7},{7,5},{8,10},{10,8},{9,1... | collective-permute-start | bytes 6291464 | tf_op jit(solution)/shard_map/ppermute | solution.py:48
  361.0 134.5 %collective-permute-start.13 = (bf16[64,1312]{1,0:T(8,128)(2,1)}, bf16[64,1312]{1,0:T(8,128)(2,1)S(1)}, u32[]{:S(2)}, u32[]{:S(2)}) collective-permute-start(bf16[64,1312]{1,0:T(8,128)(2,1)} %get-tuple-element.169), channel_id=1, source_target_pairs={{0,0},{1,2},{2,1},{3,3},{4,4},{5,6},{6,5},{7,7},{8,8},{9,10},{10,9... | collective-permute-start | bytes 503816 | tf_op jit(solution)/shard_map/ppermute | solution.py:44
  366.0 130.7 %collective-permute-start.16 = (bf16[1024,1024]{0,1:T(8,128)(2,1)}, bf16[1024,1024]{0,1:T(8,128)(2,1)}, u32[]{:S(2)}, u32[]{:S(2)}) collective-permute-start(bf16[1024,1024]{0,1:T(8,128)(2,1)} %copy.219), channel_id=1, source_target_pairs={{0,2},{2,0},{1,3},{3,1},{4,6},{6,4},{5,7},{7,5},{8,10},{10,8},{9,1... | collective-permute-start | bytes 6291464 | tf_op jit(solution)/shard_map/ppermute | solution.py:48
  367.6 315.0 %all-gather.29.cloned.1.call-start = ((), (), s32[]{:S(2)}) async-start(), calls=%async_computation.19 | async-start | bytes 3063808 | tf_op jit(solution)/shard_map/all_gather | solution.py:81
  496.2 593.2 %reduce-scatter.17.cloned.1.call-start = ((), (), s32[]{:S(2)}) async-start(), calls=%async_computation.23 | async-start | bytes 1114112 | tf_op jit(solution)/shard_map/reduce_scatter | solution.py:85
  745.5 346.9 %reduce-scatter.23.cloned.1.call-start = ((), (), s32[]{:S(2)}) async-start(), calls=%async_computation.26 | async-start | bytes 3063808 | tf_op jit(solution)/shard_map/reduce_scatter | solution.py:85
  752.1 343.0 %reduce-scatter.25.cloned.1.call-start = ((), (), s32[]{:S(2)}) async-start(), calls=%async_computation.27 | async-start | bytes 3063808 | tf_op jit(solution)/shard_map/reduce_scatter | solution.py:85
  758.8 339.3 %reduce-scatter.29.cloned.1.call-start = ((), (), s32[]{:S(2)}) async-start(), calls=%async_computation.29 | async-start | bytes 3063808 | tf_op jit(solution)/shard_map/reduce_scatter | solution.py:85
  864.9 275.3 %reduce-scatter.15.cloned.1.call-start = ((), (), s32[]{:S(2)}) async-start(), calls=%async_computation.22 | async-start | bytes 1114112 | tf_op jit(solution)/shard_map/reduce_scatter | solution.py:85
  914.2 309.0 %reduce-scatter.19.cloned.1.call-start = ((), (), s32[]{:S(2)}) async-start(), calls=%async_computation.24 | async-start | bytes 3063808 | tf_op jit(solution)/shard_map/reduce_scatter | solution.py:85
  921.9 384.2 %reduce-scatter.21.cloned.1.call-start = ((), (), s32[]{:S(2)}) async-start(), calls=%async_computation.25 | async-start | bytes 3063808 | tf_op jit(solution)/shard_map/reduce_scatter | solution.py:85
  928.5 460.9 %reduce-scatter.27.cloned.1.call-start = ((), (), s32[]{:S(2)}) async-start(), calls=%async_computation.28 | async-start | bytes 3063808 | tf_op jit(solution)/shard_map/reduce_scatter | solution.py:85
  936.7 539.8 %reduce-scatter.13.cloned.1.call-start = ((), (), s32[]{:S(2)}) async-start(), calls=%async_computation.21 | async-start | bytes 3620864 | tf_op jit(solution)/shard_map/reduce_scatter | solution.py:85
  945.9 618.0 %reduce-scatter.11.cloned.1.call-start = ((), (), s32[]{:S(2)}) async-start(), calls=%async_computation.20 | async-start | bytes 3620864 | tf_op jit(solution)/shard_map/reduce_scatter | solution.py:85
  1039.1 44.9 %collective-permute-start.15 = (bf16[1024,1024]{0,1:T(8,128)(2,1)}, bf16[1024,1024]{0,1:T(8,128)(2,1)S(1)}, u32[]{:S(2)}, u32[]{:S(2)}) collective-permute-start(bf16[1024,1024]{0,1:T(8,128)(2,1)} %get-tuple-element.140), channel_id=1, source_target_pairs={{0,1},{3,2},{4,5},{7,6},{8,9},{11,10},{12,13},{15,14},{16,17},{19,... | collective-permute-start | bytes 6291464 | tf_op jit(solution)/shard_map/ppermute | solution.py:382
  1089.5 144.0 %collective-permute-start.25 = (bf16[64,512]{1,0:T(8,128)(2,1)}, bf16[64,512]{1,0:T(8,128)(2,1)}, u32[]{:S(2)}, u32[]{:S(2)}) collective-permute-start(bf16[64,512]{1,0:T(8,128)(2,1)} %reduce-scatter.17.cloned.1.call-done), channel_id=1, source_target_pairs={{0,0},{1,2},{2,1},{3,3},{4,4},{5,6},{6,5},{7,7},{8,8},{9,10},{10,9... | collective-permute-start | bytes 196616 | tf_op jit(solution)/shard_map/ppermute | solution.py:44
  1095.1 55.5 %collective-permute-start.29 = (bf16[64,1312]{1,0:T(8,128)(2,1)}, bf16[64,1312]{1,0:T(8,128)(2,1)}, u32[]{:S(2)}, u32[]{:S(2)}) collective-permute-start(bf16[64,1312]{1,0:T(8,128)(2,1)} %reduce-scatter.25.cloned.1.call-done), channel_id=1, source_target_pairs={{0,0},{1,2},{2,1},{3,3},{4,4},{5,6},{6,5},{7,7},{8,8},{9,10},{10,9... | collective-permute-start | bytes 503816 | tf_op jit(solution)/shard_map/ppermute | solution.py:44
  1098.0 313.1 %collective-permute-start.31 = (bf16[64,1312]{1,0:T(8,128)(2,1)}, bf16[64,1312]{1,0:T(8,128)(2,1)}, u32[]{:S(2)}, u32[]{:S(2)}) collective-permute-start(bf16[64,1312]{1,0:T(8,128)(2,1)} %reduce-scatter.29.cloned.1.call-done), channel_id=1, source_target_pairs={{0,0},{1,2},{2,1},{3,3},{4,4},{5,6},{6,5},{7,7},{8,8},{9,10},{10,9... | collective-permute-start | bytes 503816 | tf_op jit(solution)/shard_map/ppermute | solution.py:44
  1108.3 378.7 %collective-permute-start.21 = (bf16[1024,1024]{0,1:T(8,128)(2,1)}, bf16[1024,1024]{0,1:T(8,128)(2,1)S(1)}, u32[]{:S(2)}, u32[]{:S(2)}) collective-permute-start(bf16[1024,1024]{0,1:T(8,128)(2,1)} %add_convert_fusion.2), channel_id=1, source_target_pairs={{0,1},{3,2},{4,5},{7,6},{8,9},{11,10},{12,13},{15,14},{16,17},{19,... | collective-permute-start | bytes 6291464 | tf_op jit(solution)/shard_map/ppermute | solution.py:382
  1140.2 176.6 %collective-permute-start.24 = (bf16[64,512]{1,0:T(8,128)(2,1)}, bf16[64,512]{1,0:T(8,128)(2,1)}, u32[]{:S(2)}, u32[]{:S(2)}) collective-permute-start(bf16[64,512]{1,0:T(8,128)(2,1)} %reduce-scatter.15.cloned.1.call-done), channel_id=1, source_target_pairs={{0,0},{1,2},{2,1},{3,3},{4,4},{5,6},{6,5},{7,7},{8,8},{9,10},{10,9... | collective-permute-start | bytes 196616 | tf_op jit(solution)/shard_map/ppermute | solution.py:44
  1223.2 177.1 %collective-permute-start.26 = (bf16[64,1312]{1,0:T(8,128)(2,1)}, bf16[64,1312]{1,0:T(8,128)(2,1)}, u32[]{:S(2)}, u32[]{:S(2)}) collective-permute-start(bf16[64,1312]{1,0:T(8,128)(2,1)} %reduce-scatter.19.cloned.1.call-done), channel_id=1, source_target_pairs={{0,0},{1,2},{2,1},{3,3},{4,4},{5,6},{6,5},{7,7},{8,8},{9,10},{10,9... | collective-permute-start | bytes 503816 | tf_op jit(solution)/shard_map/ppermute | solution.py:44
  1306.1 94.2 %collective-permute-start.27 = (bf16[64,1312]{1,0:T(8,128)(2,1)}, bf16[64,1312]{1,0:T(8,128)(2,1)}, u32[]{:S(2)}, u32[]{:S(2)}) collective-permute-start(bf16[64,1312]{1,0:T(8,128)(2,1)} %reduce-scatter.21.cloned.1.call-done), channel_id=1, source_target_pairs={{0,0},{1,2},{2,1},{3,3},{4,4},{5,6},{6,5},{7,7},{8,8},{9,10},{10,9... | collective-permute-start | bytes 503816 | tf_op jit(solution)/shard_map/ppermute | solution.py:44
  1389.4 21.8 %collective-permute-start.30 = (bf16[64,1312]{1,0:T(8,128)(2,1)}, bf16[64,1312]{1,0:T(8,128)(2,1)S(1)}, u32[]{:S(2)}, u32[]{:S(2)}) collective-permute-start(bf16[64,1312]{1,0:T(8,128)(2,1)} %reduce-scatter.27.cloned.1.call-done), channel_id=1, source_target_pairs={{0,0},{1,2},{2,1},{3,3},{4,4},{5,6},{6,5},{7,7},{8,8},{9,10},{10,9... | collective-permute-start | bytes 503816 | tf_op jit(solution)/shard_map/ppermute | solution.py:44
  (151 other events, 2140.4 us)
Sparse Core Ops, SparseCore 0:
  18.6 70.1 all-gather.10
  91.5 53.5 all-gather.12
  148.0 64.8 all-gather.14
  215.5 64.8 all-gather.16
  283.7 64.8 all-gather.18
  351.9 69.4 all-gather.20
  424.2 53.5 all-gather.22
  481.2 64.9 all-gather.26
  549.5 64.8 all-gather.24
  617.7 64.8 all-gather.28
  745.6 65.1 reduce-scatter.16
  813.0 80.4 reduce-scatter.22
  896.0 81.7 reduce-scatter.24
  980.0 82.3 reduce-scatter.28
  1064.6 75.6 reduce-scatter.14
  1142.4 80.7 reduce-scatter.18
  1225.4 80.7 reduce-scatter.20
  1308.3 81.0 reduce-scatter.26
  1391.7 84.8 reduce-scatter.12
  1478.8 85.0 reduce-scatter.10

commit v2 on v1

--- a/solution.py
+++ b/solution.py
@@ -77,8 +77,72 @@
     return jax.nn.gelu(inner, approximate=False) * gate_part
 
 
+def group_bits(chips):
+    return chips.bit_length() - 1
+
+
+def bit_swap(values, bit, chips):
+    if bit < 0:
+        return lax.ppermute(values, "tensor", [(0, 1), (1, 0)])
+    return lax.ppermute(values, "chip", [(chip, chip ^ (1 << bit)) for chip in range(chips)])
+
+
+def own_bit(bit):
+    if bit < 0:
+        return lax.axis_index("tensor")
+    return (lax.axis_index("chip") >> bit) & 1
+
+
+def gather_bit(values, held, bit, chips):
+    place = len([b for b in held if b > bit])
+    other = bit_swap(values, bit, chips)
+    is_low = own_bit(bit) == 0
+    joined = jnp.stack(
+        [jnp.where(is_low, values, other), jnp.where(is_low, other, values)], axis=place
+    )
+    return joined, sorted(held + [bit], reverse=True)
+
+
+def reduce_bit(values, held, bit, chips):
+    place = held.index(bit)
+    mine = own_bit(bit)
+    kept = lax.dynamic_index_in_dim(values, mine, place, keepdims=False)
+    sent = lax.dynamic_index_in_dim(values, 1 - mine, place, keepdims=False)
+    other = bit_swap(sent, bit, chips)
+    total = (kept.astype(jnp.float32) + other.astype(jnp.float32)).astype(jnp.bfloat16)
+    return total, [b for b in held if b != bit]
+
+
+def gather_quick(shard, cut, chips):
+    values, held = shard, []
+    for bit in range(group_bits(chips) - 1, 0, -1):
+        values, held = gather_bit(values, held, bit, chips)
+    halves = []
+    for order, part in (((0, -1), values[..., :cut]), ((-1, 0), values[..., cut:])):
+        part_held = held
+        for bit in order:
+            part, part_held = gather_bit(part, part_held, bit, chips)
+        halves.append(part.reshape(-1, part.shape[-1]))
+    return halves
+
+
+def scatter_quick(halves, chips):
+    count = group_bits(chips)
+    parts = []
+    for order, part in (((-1, 0), halves[0]), ((0, -1), halves[1])):
+        held = list(range(count - 1, -2, -1))
+        values = part.astype(jnp.bfloat16).reshape([2] * len(held) + [-1, part.shape[-1]])
+        for bit in order:
+            values, held = reduce_bit(values, held, bit, chips)
+        parts.append(values)
+    values = jnp.concatenate(parts, axis=-1)
+    for bit in range(1, count):
+        values, held = reduce_bit(values, held, bit, chips)
+    return role_swap(values, chips).astype(jnp.float32)
+
+
 def gather_rows(shard, chips):
-    return lax.all_gather(role_swap(shard, chips), chip_axes, axis=0, tiled=True)
+    return lax.all_gather(shard, chip_axes, axis=0, tiled=True)
 
 
 def scatter_rows(gradient, chips):
@@ -88,21 +152,41 @@
     return role_swap(shard, chips).astype(jnp.float32)
 
 
-def gather_weights(masters, layer, chips):
+def padded_width(width):
+    return -(-width // 128) * 128
+
+
+def widen(values):
+    width = values.shape[1]
+    return jnp.pad(values, ((0, 0), (0, padded_width(width) - width)))
+
+
+def pack_shards(masters, layer):
     qkv, out, inp, down, gains = [m[layer] for m in masters]
-    rows = qkv.shape[0]
-    qkv_rows = jnp.concatenate(
-        [qkv.reshape(rows, -1), jnp.pad(gains.T, ((0, 0), (0, 126)))], axis=1
-    ).astype(jnp.bfloat16)
-    qkv_all = gather_rows(qkv_rows, chips)
-    width = qkv.shape[1] * qkv.shape[2]
+    quick = jnp.concatenate([qkv.reshape(qkv.shape[0], -1), widen(gains.T)], axis=1)
+    bulk = jnp.concatenate([out.T, widen(inp[:, 0]), widen(inp[:, 1]), down.T], axis=1)
+    return quick.astype(jnp.bfloat16), bulk.astype(jnp.bfloat16)
+
+
+def gather_weights(masters, quick, bulk, chips):
+    qkv, out, inp, down, gains = masters
+    width = qkv.shape[2] * qkv.shape[3]
+    cut = width // 2
+    first, second = gather_quick(quick, cut, chips)
+    bulk = gather_rows(bulk, chips)
+    heads, hidden = out.shape[1], down.shape[1]
+    step = padded_width(hidden)
+    start = heads
+    w_inner = bulk[:, start : start + hidden]
+    w_gate = bulk[:, start + step : start + step + hidden]
+    w_down = bulk[:, start + 2 * step :]
     return (
-        qkv_all[:, :width],
-        gather_rows(out.T.astype(jnp.bfloat16), chips),
-        gather_rows(inp[:, 0].astype(jnp.bfloat16), chips),
-        gather_rows(inp[:, 1].astype(jnp.bfloat16), chips),
-        gather_rows(down.T.astype(jnp.bfloat16), chips),
-        qkv_all[:, width : width + 2].T.astype(jnp.float32),
+        jnp.concatenate([first, second[:, :cut]], axis=1),
+        bulk[:, :heads],
+        w_inner,
+        w_gate,
+        w_down,
+        second[:, cut : cut + 2].T.astype(jnp.float32),
     )
 
 
@@ -313,11 +397,11 @@
     local_width = w_qkv.shape[1] // 3
     up_low = upstream.astype(jnp.bfloat16)
     d_activated = product(up_low, w_down, (1, 0))
-    grad_down = scatter_rows(product(up_low, activated, (0, 0)), chips)
+    grad_down = product(up_low, activated, (0, 0)).astype(jnp.bfloat16)
     unused, pullback = jax.vjp(gelu_gate, inner, gate_part)
     d_inner, d_gate = [v.astype(jnp.bfloat16) for v in pullback(d_activated)]
-    grad_inner = scatter_rows(product(lowered_two, d_inner, (0, 0)), chips)
-    grad_gate = scatter_rows(product(lowered_two, d_gate, (0, 0)), chips)
+    grad_inner = product(lowered_two, d_inner, (0, 0)).astype(jnp.bfloat16)
+    grad_gate = product(lowered_two, d_gate, (0, 0)).astype(jnp.bfloat16)
     d_normed_two = core_total(
         product(d_inner, w_inner, (1, 1)) + product(d_gate, w_gate, (1, 1))
     )
@@ -326,7 +410,15 @@
     d_middle = upstream + d_mid_norm
     d_branch = d_middle.astype(jnp.bfloat16)
     d_attended = product(d_branch, w_out, (1, 0)).astype(jnp.bfloat16)
-    grad_out = scatter_rows(product(d_branch, attended, (0, 0)), chips)
+    grad_out = product(d_branch, attended, (0, 0)).astype(jnp.bfloat16)
+    heads, hidden = grad_out.shape[1], grad_down.shape[1]
+    step = padded_width(hidden)
+    bulk = jnp.concatenate([grad_out, widen(grad_inner), widen(grad_gate), grad_down], axis=1)
+    d_attended, bulk = lax.optimization_barrier((d_attended, bulk))
+    bulk = scatter_rows(bulk, chips)
+    grad_inp = jnp.stack(
+        [bulk[:, heads : heads + hidden], bulk[:, heads + step : heads + step + hidden]], axis=1
+    )
     d_queries, d_keys, d_value = attend_backward(
         queries, key_all, value_all, log_total, d_attended, is_local
     )
@@ -343,18 +435,19 @@
     d_normed = core_total(product(d_projected, w_qkv, (1, 1)))
     unused, pullback = jax.vjp(layer_norm, residual, gain_pair[0])
     d_in_norm, d_gain_one = pullback(d_normed)
-    gains = jnp.pad(jnp.stack([d_gain_one, d_gain_two], axis=1), ((0, 0), (0, 126)))
-    grad_qkv = scatter_rows(
-        jnp.concatenate([product(lowered, d_projected, (0, 0)), gains], axis=1), chips
-    )
-    rows = grad_qkv.shape[0]
+    gains = widen(jnp.stack([d_gain_one, d_gain_two], axis=1)).astype(jnp.bfloat16)
     width = 3 * local_width
+    cut = width // 2
+    grad_qkv = product(lowered, d_projected, (0, 0)).astype(jnp.bfloat16)
+    quick = scatter_quick(
+        (grad_qkv[:, :cut], jnp.concatenate([grad_qkv[:, cut:], gains], axis=1)), chips
+    )
     gradients = (
-        grad_qkv[:, :width].reshape(rows, 3, local_width),
-        grad_out.T,
-        jnp.stack([grad_inner, grad_gate], axis=1),
-        grad_down.T,
-        grad_qkv[:, width : width + 2].T,
+        quick[:, :width].reshape(-1, 3, local_width),
+        bulk[:, :heads].T,
+        grad_inp,
+        bulk[:, heads + 2 * step :].T,
+        quick[:, width : width + 2].T,
     )
     return (d_middle + d_in_norm, gradients)
 
@@ -381,10 +474,16 @@
     def own_sequence(values):
         return jnp.where(same, values, lax.ppermute(values, every_axis, result_pairs(chips)))
 
+    quick_first, bulk_first = pack_shards(masters, 0)
+    quick_second, bulk_second = pack_shards(masters, 1)
+    quick_first = role_swap(quick_first, chips)
+    rest = role_swap(jnp.concatenate([bulk_first, bulk_second, quick_second], axis=1), chips)
+    cut = bulk_first.shape[1]
+    hidden_in, quick_first, rest = lax.optimization_barrier((hidden_in, quick_first, rest))
     inputs = chip_sequence(hidden_in)
     upstream = chip_sequence(cotangent)
-    first_weights = gather_weights(masters, 0, chips)
-    second_weights = gather_weights(masters, 1, chips)
+    first_weights = gather_weights(masters, quick_first, rest[:, :cut], chips)
+    second_weights = gather_weights(masters, rest[:, 2 * cut :], rest[:, cut : 2 * cut], chips)
     middle, kept_first = forward_layer(inputs, first_weights, True)
     output, kept_second = forward_layer(middle, second_weights, False)
     final_out = own_sequence(output.astype(jnp.bfloat16))

time: 1600 us -> 1110 us (0.69)
  waiting for transfers between devices: 858 us -> 352 us
  other arithmetic: 207 us -> 285 us
  starting transfers between devices: 118 us -> 66.5 us
  matrix products: 301 us -> 258 us
  local copies, waits for them, and re-layouts: 88.2 us -> 128 us
    all_gather x10 -> x2, waiting for transfers between devices: 401 us -> 23.6 us  [gather_rows(): return lax.all_gather(shard, chip_axes, axis=0, tiled=True)]
    reduce_scatter x10 -> x2, waiting for transfers between devices: 376 us -> 0.04 us  [scatter_rows(): lax.psum_scatter(gradient.astype(jnp.bfloat16), chip_axes, scatter_dimens...]
    ppermute x0 -> x24, waiting for transfers between devices: none -> 297 us  [the longest x8 175 us: bit_swap(): return lax.ppermute(values, 'tensor', [(0, 1), (1, 0)])]
    ppermute x20 -> x6, starting transfers between devices: 105 us -> 18.9 us  [role_swap(): return lax.ppermute(values, every_axis, swap_pairs(chips))]
    concatenate x4 -> x5, other arithmetic: 6.1 us -> 63.3 us  [the longest x2 61.5 us: backward_layer(): jnp.concatenate([grad_out, widen(grad_inner), widen(grad_gate), grad_down...]
    ppermute x2, waiting for transfers between devices: 43.6 us -> 0.01 us  [own_sequence(): lax.ppermute(values, every_axis, result_pairs(chips))]
    dot_general x30, matrix products: 194 us -> 151 us  [product(): lax.dot_general(left, right, ((contract[:1], contract[1:]), ((), ())), pr...]
    ppermute x0 -> x24, starting transfers between devices: none -> 27.9 us  [the longest x16 18.6 us: bit_swap(): lax.ppermute(values, 'chip', [(chip, chip ^ 1 << bit) for chip in range(c...]
  transfers between devices with their start and end apart: 52 -> 46, of which waited for: 28 -> 20; matrix products, arithmetic and copies ran while one was open for 33% -> 48% of each run, Pallas kernels for 0% -> 0%
where the time goes in v2:
time: 1110 us
  waiting for transfers between devices  352 us (32%)
  other arithmetic  285 us (26%)
  matrix products  258 us (23%)
  local copies, waits for them, and re-layouts  128 us (12%)
  starting transfers between devices  66.5 us (6%)
  between operations  16.9 us (2%)
    ppermute x8, waiting for transfers between devices, bit_swap(): return lax.ppermute(values, 'tensor', [(0, 1), (1, 0)])  175 us
    dot_general x30, matrix products, product(): lax.dot_general(left, right, ((contract[:1], contract[1:]), ((), ())), pr...  151 us
    ppermute x16, waiting for transfers between devices, bit_swap(): lax.ppermute(values, 'chip', [(chip, chip ^ 1 << bit) for chip in range(c...  122 us
    unnamed x318, local copies, waits for them, and re-layouts  68.6 us
    concatenate x2, other arithmetic, backward_layer(): jnp.concatenate([grad_out, widen(grad_inner), widen(grad_gate), grad_down...  61.5 us
    another operation x7, other arithmetic  33 us
    convert_element_type x2, other arithmetic, attend_backward(): d_scores = (probability * (d_probability - centre)).astype(jnp.bfloat16)  31.5 us
    ppermute x6, waiting for transfers between devices, role_swap(): return lax.ppermute(values, every_axis, swap_pairs(chips))  29.5 us
  transfers between devices with their start and end apart: 46, of which 20 were waited for; matrix products, arithmetic and copies ran while one was open for 48% of the time, Pallas kernels for 0%

profile of v2, /device:TPU:1, one launch (start us, length us, event | category | flops | bytes accessed | tf_op | source)
XLA Modules:
  0.0 1106.5 jit_solution(11324104185166013136)
XLA Ops:
  21.8 16.3 %collective-permute-done = bf16[64,1664]{1,0:T(8,128)(2,1)S(1)} collective-permute-done((bf16[64,1664]{1,0:T(8,128)(2,1)S(1)}, bf16[64,1664]{1,0:T(8,128)(2,1)S(1)}, u32[]{:S(2)}, u32[]{:S(2)}) %collective-permute-start) | collective-permute-done | bytes 213024 | tf_op jit(solution)/shard_map/ppermute | solution.py:44
  51.1 11.7 %collective-permute-done.4 = bf16[2,64,1664]{2,1,0:T(8,128)(2,1)S(1)} collective-permute-done((bf16[2,64,1664]{2,1,0:T(8,128)(2,1)S(1)}, bf16[2,64,1664]{2,1,0:T(8,128)(2,1)S(1)}, u32[]{:S(2)}, u32[]{:S(2)}) %collective-permute-start.4) | collective-permute-done | bytes 426016 | tf_op jit(solution)/shard_map/ppermute | solution.py:87
  70.5 9.2 collective-permute-start.2
  92.1 13.8 %collective-permute-done.8 = bf16[2,2,2,64,768]{4,3,0,1,2:T(8,128)(2,1)} collective-permute-done((bf16[2,2,2,64,768]{4,3,0,1,2:T(8,128)(2,1)}, bf16[2,2,2,64,768]{4,3,0,1,2:T(8,128)(2,1)}, u32[]{:S(2)}, u32[]{:S(2)}) %collective-permute-start.8) | collective-permute-done | bytes 786464 | tf_op jit(solution)/shard_map/ppermute | solution.py:86
  156.7 23.6 %all-gather.3.cloned.1.call-done = bf16[1024,4640]{1,0:T(8,128)(2,1)} async-done(((bf16[64,4640]{1,0:T(8,128)(2,1)}), bf16[1024,4640]{1,0:T(8,128)(2,1)}) %all-gather.3.cloned.1.call-update) | async-done | bytes 9502736 | tf_op jit(solution)/shard_map/all_gather | solution.py:145
  186.5 11.4 %collective-permute-done.12 = bf16[2,64,1664]{2,1,0:T(8,128)(2,1)S(1)} collective-permute-done((bf16[2,64,1664]{2,1,0:T(8,128)(2,1)S(1)}, bf16[2,64,1664]{2,1,0:T(8,128)(2,1)S(1)}, u32[]{:S(2)}, u32[]{:S(2)}) %collective-permute-start.12) | collective-permute-done | bytes 426016 | tf_op jit(solution)/shard_map/ppermute | solution.py:87
  221.1 16.7 %multiply_convert_fusion.5 = (bf16[1024,1312]{0,1:T(8,128)(2,1)S(1)}, f32[1024,1312]{0,1:T(8,128)}, f32[1024,1312]{0,1:T(8,128)}) fusion(f32[1024,1312]{0,1:T(8,128)S(1)} %fusion.69, bf16[1024,1024]{0,1:T(8,128)(2,1)S(1)} %multiply_convert_fusion.8, bf16[1024,4640]{1,0:T(8,128)(2,1)S(1)} %bitcast.460), kind=kOutput, calls=%fused_computation.66 | convolution fusion | flops 2840133632 | bytes 23789568 | tf_op jit(solution)/shard_map/dot_general | solution.py:331
  253.7 16.0 %collective-permute-done.14 = bf16[2,2,2,64,896]{4,3,0,1,2:T(8,128)(2,1)} collective-permute-done((bf16[2,2,2,64,896]{4,3,0,1,2:T(8,128)(2,1)}, bf16[2,2,2,64,896]{4,3,0,1,2:T(8,128)(2,1)}, u32[]{:S(2)}, u32[]{:S(2)}) %collective-permute-start.14) | collective-permute-done | bytes 917536 | tf_op jit(solution)/shard_map/ppermute | solution.py:87
  295.5 13.9 %multiply_reduce_fusion.1 = (f32[8,1024]{1,0:T(8,128)S(1)}, f32[8,1024,1024]{1,2,0:T(8,128)}) fusion(bf16[1024,8,64]{0,2,1:T(8,128)(2,1)S(1)} %get-tuple-element.212, bf16[1024,8,64]{0,2,1:T(8,128)(2,1)S(1)} %get-tuple-element.211), kind=kOutput, calls=%fused_computation.10 | convolution fusion | flops 1090510848 | bytes 35684352 | tf_op jit(solution)/shard_map/sqhd,skhd->shqk/dot_general | solution.py:239
  309.4 13.6 %fusion = f32[8,1024]{1,0:T(8,128)S(1)} fusion(f32[8,1024,1024]{1,2,0:T(8,128)} %get-tuple-element.257, f32[8,1024]{1,0:T(8,128)S(1)} %get-tuple-element.256), kind=kLoop, calls=%fused_computation.5 | loop fusion | flops 25157632 | bytes 33619968 | tf_op jit(solution)/shard_map/reduce_sum | solution.py:251
  322.9 13.2 %fusion.120 = bf16[8,64,1024]{2,1,0:T(8,128)(2,1)S(1)} fusion(bf16[1024,8,64]{0,2,1:T(8,128)(2,1)S(1)} %bitcast.420, f32[8,1024,1024]{1,2,0:T(8,128)} %get-tuple-element.257, f32[8,1024]{1,0:T(8,128)S(1)} %fusion, f32[8,1024]{1,0:T(8,128)S(1)} %get-tuple-element.256), kind=kOutput, calls=%fused_computation.231 | convolution fusion | flops 1107820544 | bytes 35717120 | tf_op jit(solution)/shard_map/shqk,skhd->sqhd/dot_general | solution.py:259
  358.0 18.4 %add_convert_fusion.1 = (bf16[1024,1312]{0,1:T(8,128)(2,1)}, f32[1024,1312]{0,1:T(8,128)}, f32[1024,1312]{0,1:T(8,128)}) fusion(f32[1024,1312]{0,1:T(8,128)S(1)} %fusion.53, f32[1024,1312]{0,1:T(8,128)S(1)} %fusion.57, bf16[1024,1024]{0,1:T(8,128)(2,1)S(1)} %broadcast_select_fusion, bf16[1024,4640]{1,0:T(8,128)(2,1)S(1)} %bitcast.462), kind=kOutput, calls=%fused_computation.52 | convolution fusion | flops 2849538048 | bytes 29163520 | tf_op jit(solution)/shard_map/dot_general | solution.py:331
  376.5 12.5 %multiply_convert_fusion.3 = (bf16[1024,1312]{0,1:T(8,128)(2,1)}, bf16[1024,1312]{0,1:T(8,128)(2,1)}) fusion(f32[1024,1312]{0,1:T(8,128)} %get-tuple-element.258, f32[1024,1312]{0,1:T(8,128)} %get-tuple-element.131, f32[1024,1312]{0,1:T(8,128)} %copy-done.44, f32[1024,1312]{0,1:T(8,128)} %copy-done.43), kind=kLoop, calls=%fused_computation.51 | loop fusion | flops 8060928 | bytes 26869760 | tf_op jit(solution)/shard_map/convert_element_type | solution.py:402
  426.0 30.8 %fusion.13 = bf16[1024,4640]{0,1:T(8,128)(2,1)} fusion(bf16[1024,1312]{0,1:T(8,128)(2,1)S(1)} %convolution_convert_fusion.6, bf16[1024,1312]{0,1:T(8,128)(2,1)S(1)} %convolution_convert_fusion.7, bf16[1024,1312]{0,1:T(8,128)(2,1)S(1)} %convolution_convert_fusion.5, bf16[1024,512]{0,1:T(8,128)(2,1)S(1)} %convolution_convert_fusion.12), kind=kLoop, calls=%fused_computation.22 | loop fusion | flops 76021760 | bytes 18612224 | tf_op jit(solution)/shard_map/concatenate | solution.py:416
  459.9 13.3 %copy.323 = bf16[1024,4640]{1,0:T(8,128)(2,1)} copy(bf16[1024,4640]{0,1:T(8,128)(2,1)} %fusion.13) | data formatting | bytes 19005440
  473.2 22.5 %multiply_reduce_fusion = (f32[8,1024]{1,0:T(8,128)S(1)}, f32[8,1024,1024]{1,2,0:T(8,128)}) fusion(f32[8,1024,1024]{1,2,0:T(8,128)} %get-tuple-element.257, f32[8,1024]{1,0:T(8,128)S(1)} %log_add_fusion.1, bf16[1024,8,64]{0,2,1:T(8,128)(2,1)S(1)} %bitcast.401, bf16[1024,8,64]{0,2,1:T(8,128)(2,1)S(1)} %bitcast.421), kind=kOutput, calls=%fused_computation.1 | convolution fusion | flops 1107288064 | bytes 69271552 | tf_op jit(solution)/shard_map/sqhd,skhd->shqk/dot_general | solution.py:314
  495.8 28.6 %multiply_convert_fusion = bf16[8,1024,1024]{1,2,0:T(8,128)(2,1)} fusion(f32[8,1024,1024]{1,2,0:T(8,128)} %get-tuple-element.260, f32[8,1024,1024]{1,2,0:T(8,128)} %get-tuple-element.257, f32[8,1024]{1,0:T(8,128)S(1)} %get-tuple-element.259, f32[8,1024]{1,0:T(8,128)S(1)} %log_add_fusion.1), kind=kLoop, calls=%fused_computation | loop fusion | flops 41943040 | bytes 83951616 | tf_op jit(solution)/shard_map/convert_element_type | solution.py:318
  524.4 11.5 %fusion.223 = f32[8,64,1024]{2,1,0:T(8,128)S(1)} fusion(bf16[1024,8,64]{0,2,1:T(8,128)(2,1)} %copy-done.26, bf16[8,1024,1024]{1,2,0:T(8,128)(2,1)} %multiply_convert_fusion), kind=kOutput, calls=%fused_computation.502 | convolution fusion | flops 1073741824 | bytes 19922944 | tf_op jit(solution)/shard_map/shqk,sqhd->skhd/dot_general | solution.py:324
  535.9 8.9 bitcast_multiply_fusion.2
  548.3 15.2 %fusion.117 = bf16[8,64,1024]{2,1,0:T(8,128)(2,1)} fusion(bf16[1024,8,64]{0,2,1:T(8,128)(2,1)S(1)} %bitcast.402, f32[8,1024,1024]{1,2,0:T(8,128)} %get-tuple-element.257, f32[8,1024]{1,0:T(8,128)S(1)} %log_add_fusion.1), kind=kOutput, calls=%fused_computation.226 | convolution fusion | flops 1099431936 | bytes 35684352 | tf_op jit(solution)/shard_map/shqk,sqhd->skhd/dot_general | solution.py:308
  578.5 51.9 %collective-permute-done.33 = bf16[2,2,2,64,768]{4,3,2,1,0:T(8,128)(2,1)S(1)} collective-permute-done((bf16[2,2,2,64,768]{4,3,2,1,0:T(8,128)(2,1)}, bf16[2,2,2,64,768]{4,3,2,1,0:T(8,128)(2,1)S(1)}, u32[]{:S(2)}, u32[]{:S(2)}) %collective-permute-start.33) | collective-permute-done | bytes 786464 | tf_op jit(solution)/shard_map/ppermute | solution.py:86
  650.6 12.0 %add_convert_fusion = (bf16[1024,1312]{0,1:T(8,128)(2,1)S(1)}, bf16[1024,1312]{0,1:T(8,128)(2,1)S(1)}) fusion(f32[1024,1312]{0,1:T(8,128)} %get-tuple-element.137, f32[1024,1312]{0,1:T(8,128)} %get-tuple-element.255, f32[1024,1312]{0,1:T(8,128)} %copy-done.137, bf16[1024,4640]{1,0:T(8,128)(2,1)} %all-gather.3.cloned.1.call-done, ...), kind=kOutput, calls=%fused_computation.50 | convolution fusion | flops 2776694784 | bytes 28573696 | tf_op jit(solution)/shard_map/dot_general | solution.py:331
  684.7 21.8 %collective-permute-done.35 = bf16[2,2,2,64,896]{4,3,2,1,0:T(8,128)(2,1)S(1)} collective-permute-done((bf16[2,2,2,64,896]{4,3,2,1,0:T(8,128)(2,1)S(1)}, bf16[2,2,2,64,896]{4,3,2,1,0:T(8,128)(2,1)S(1)}, u32[]{:S(2)}, u32[]{:S(2)}) %collective-permute-start.35) | collective-permute-done | bytes 917536 | tf_op jit(solution)/shard_map/ppermute | solution.py:87
  719.7 30.7 %fusion.16 = bf16[1024,4640]{0,1:T(8,128)(2,1)} fusion(bf16[1024,1312]{0,1:T(8,128)(2,1)S(1)} %convolution_convert_fusion.3, bf16[1024,1312]{0,1:T(8,128)(2,1)S(1)} %convolution_convert_fusion.4, bf16[1024,1312]{0,1:T(8,128)(2,1)S(1)} %convolution_convert_fusion.2, bf16[1024,512]{0,1:T(8,128)(2,1)S(1)} %convolution_convert_fusion.10), kind=kLoop, calls=%fused_computation.25 | loop fusion | flops 76021760 | bytes 18612224 | tf_op jit(solution)/shard_map/concatenate | solution.py:416
  764.4 13.1 %copy.321 = bf16[1024,4640]{1,0:T(8,128)(2,1)} copy(bf16[1024,4640]{0,1:T(8,128)(2,1)} %fusion.16) | data formatting | bytes 19005440
  777.5 10.3 fusion.78
  804.7 10.7 broadcast_multiply_fusion.1
  820.1 16.1 %add_convert_fusion.7 = (bf16[1,1024,8,64]{1,0,3,2:T(2,128)(2,1)S(1)}, bf16[1,1024,8,64]{1,0,3,2:T(2,128)(2,1)S(1)}) fusion(f32[1,1024,8,32]{1,0,3,2:T(1,128)S(1)} %get-tuple-element.160, f32[1,1024,8,32]{1,0,3,2:T(1,128)S(1)} %get-tuple-element.159, f32[1,1024,8,64]{1,0,3,2:T(1,128)S(1)} %bitcast.390, f32[1024,64]{0,1:T(8,128)S(1)} %copy-done.78, ...), kind=kLoop, calls=%fused_computation.195 | loop fusion | flops 4718592 | bytes 12845056 | tf_op jit(solution)/shard_map/convert.32
  856.1 47.8 %collective-permute-done.26 = bf16[2,2,2,64,768]{4,3,2,1,0:T(8,128)(2,1)} collective-permute-done((bf16[2,2,2,64,768]{4,3,2,1,0:T(8,128)(2,1)}, bf16[2,2,2,64,768]{4,3,2,1,0:T(8,128)(2,1)}, u32[]{:S(2)}, u32[]{:S(2)}) %collective-permute-start.26) | collective-permute-done | bytes 786464 | tf_op jit(solution)/shard_map/ppermute | solution.py:86
  923.2 31.5 %collective-permute-done.28 = bf16[2,2,2,64,896]{4,3,2,1,0:T(8,128)(2,1)S(1)} collective-permute-done((bf16[2,2,2,64,896]{4,3,2,1,0:T(8,128)(2,1)S(1)}, bf16[2,2,2,64,896]{4,3,2,1,0:T(8,128)(2,1)S(1)}, u32[]{:S(2)}, u32[]{:S(2)}) %collective-permute-start.28) | collective-permute-done | bytes 917536 | tf_op jit(solution)/shard_map/ppermute | solution.py:87
  966.2 61.3 %collective-permute-done.29 = bf16[2,2,64,896]{3,2,1,0:T(8,128)(2,1)S(1)} collective-permute-done((bf16[2,2,64,896]{3,2,1,0:T(8,128)(2,1)S(1)}, bf16[2,2,64,896]{3,2,1,0:T(8,128)(2,1)S(1)}, u32[]{:S(2)}, u32[]{:S(2)}) %collective-permute-start.29) | collective-permute-done | bytes 458784 | tf_op jit(solution)/shard_map/ppermute | solution.py:86
  1043.0 10.1 collective-permute-done.31
  (650 shorter events, 451.0 us)
Async XLA Ops:
  7.2 173.0 %all-gather.3.cloned.1.call-start = ((), (), s32[]{:S(2)}) async-start(), calls=%async_computation.2 | async-start | bytes 10305536 | tf_op jit(solution)/shard_map/all_gather | solution.py:145
  15.0 23.2 %collective-permute-start.1 = (bf16[64,10944]{1,0:T(8,128)(2,1)S(1)}, bf16[64,10944]{1,0:T(8,128)(2,1)S(1)}, u32[]{:S(2)}, u32[]{:S(2)}) collective-permute-start(bf16[64,10944]{1,0:T(8,128)(2,1)S(1)} %concatenate.118), channel_id=1, source_target_pairs={{0,0},{1,2},{2,1},{3,3},{4,4},{5,6},{6,5},{7,7},{8,8},{9,10},{10,9... | collective-permute-start | bytes 4202504 | tf_op jit(solution)/shard_map/ppermute | solution.py:44
  19.9 18.2 %collective-permute-start = (bf16[64,1664]{1,0:T(8,128)(2,1)S(1)}, bf16[64,1664]{1,0:T(8,128)(2,1)S(1)}, u32[]{:S(2)}, u32[]{:S(2)}) collective-permute-start(bf16[64,1664]{1,0:T(8,128)(2,1)S(1)} %fusion.171), channel_id=1, source_target_pairs={{0,0},{1,2},{2,1},{3,3},{4,4},{5,6},{6,5},{7,7},{8,8},{9,10},{10,9... | collective-permute-start | bytes 638984 | tf_op jit(solution)/shard_map/ppermute | solution.py:44
  39.6 296.6 %all-gather.5.cloned.1.call-start = ((), (), s32[]{:S(2)}) async-start(), calls=%async_computation.3 | async-start | bytes 10305536 | tf_op jit(solution)/shard_map/all_gather | solution.py:145
  63.6 16.0 %collective-permute-start.7 = (bf16[2,2,64,768]{3,2,0,1:T(8,128)(2,1)}, bf16[2,2,64,768]{3,2,0,1:T(8,128)(2,1)}, u32[]{:S(2)}, u32[]{:S(2)}) collective-permute-start(bf16[2,2,64,768]{3,2,0,1:T(8,128)(2,1)} %pad_maximum_fusion.29), channel_id=1, source_target_pairs={{0,4},{4,0},{8,12},{12,8},{16,20},{20,16},{24,28},{28,24},{1,5},{5... | collective-permute-start | bytes 1179656 | tf_op jit(solution)/shard_map/ppermute | solution.py:87
  70.5 43.4 %collective-permute-start.2 = (bf16[1024,1024]{0,1:T(8,128)(2,1)S(1)}, bf16[1024,1024]{0,1:T(8,128)(2,1)}, u32[]{:S(2)}, u32[]{:S(2)}) collective-permute-start(bf16[1024,1024]{0,1:T(8,128)(2,1)S(1)} %copy.258), channel_id=1, source_target_pairs={{0,2},{2,0},{1,3},{3,1},{4,6},{6,4},{5,7},{7,5},{8,10},{10,8},{9,1... | collective-permute-start | bytes 6291464 | tf_op jit(solution)/shard_map/ppermute | solution.py:48
  81.9 24.1 %collective-permute-start.8 = (bf16[2,2,2,64,768]{4,3,0,1,2:T(8,128)(2,1)}, bf16[2,2,2,64,768]{4,3,0,1,2:T(8,128)(2,1)}, u32[]{:S(2)}, u32[]{:S(2)}) collective-permute-start(bf16[2,2,2,64,768]{4,3,0,1,2:T(8,128)(2,1)} %pad_maximum_fusion.23), channel_id=1, source_target_pairs={{0,1},{1,0},{2,3},{3,2},{4,5},{5,4},{6,7},{7,6},{8,9},{9,8},{10,11... | collective-permute-start | bytes 2359304 | tf_op jit(solution)/shard_map/ppermute | solution.py:86
  84.8 26.6 %collective-permute-start.6 = (bf16[2,2,2,64,896]{4,3,0,1,2:T(8,128)(2,1)}, bf16[2,2,2,64,896]{4,3,0,1,2:T(8,128)(2,1)}, u32[]{:S(2)}, u32[]{:S(2)}) collective-permute-start(bf16[2,2,2,64,896]{4,3,0,1,2:T(8,128)(2,1)} %pad_maximum_fusion.21), channel_id=1, source_target_pairs={{0,4},{4,0},{8,12},{12,8},{16,20},{20,16},{24,28},{28,24},{1,5},{5... | collective-permute-start | bytes 2752520 | tf_op jit(solution)/shard_map/ppermute | solution.py:87
  88.3 96.9 %collective-permute-start.11 = (bf16[64,1664]{1,0:T(8,128)(2,1)}, bf16[64,1664]{1,0:T(8,128)(2,1)}, u32[]{:S(2)}, u32[]{:S(2)}) collective-permute-start(bf16[64,1664]{1,0:T(8,128)(2,1)} %slice.290), channel_id=1, source_target_pairs={{0,16},{4,20},{8,24},{12,28},{16,0},{20,4},{24,8},{28,12},{1,17},{... | collective-permute-start | bytes 638984 | tf_op jit(solution)/shard_map/ppermute | solution.py:87
  184.0 27.4 %collective-permute-start.9 = (bf16[1024,1024]{0,1:T(8,128)(2,1)}, bf16[1024,1024]{0,1:T(8,128)(2,1)}, u32[]{:S(2)}, u32[]{:S(2)}) collective-permute-start(bf16[1024,1024]{0,1:T(8,128)(2,1)} %convolution_convert_fusion.9), channel_id=1, source_target_pairs={{0,2},{2,0},{1,3},{3,1},{4,6},{6,4},{5,7},{7,5},{8,10},{10,8},{9,1... | collective-permute-start | bytes 6291464 | tf_op jit(solution)/shard_map/ppermute | solution.py:48
  199.3 866.4 %reduce-scatter.9.cloned.1.call-start = ((), (), s32[]{:S(2)}) async-start(), calls=%async_computation.5 | async-start | bytes 10305536 | tf_op jit(solution)/shard_map/reduce_scatter | solution.py:149
  199.4 45.0 %collective-permute-start.13 = (bf16[2,2,64,896]{3,2,0,1:T(8,128)(2,1)S(1)}, bf16[2,2,64,896]{3,2,0,1:T(8,128)(2,1)S(1)}, u32[]{:S(2)}, u32[]{:S(2)}) collective-permute-start(bf16[2,2,64,896]{3,2,0,1:T(8,128)(2,1)S(1)} %fusion.152), channel_id=1, source_target_pairs={{0,1},{1,0},{2,3},{3,2},{4,5},{5,4},{6,7},{7,6},{8,9},{9,8},{10,11... | collective-permute-start | bytes 1376264 | tf_op jit(solution)/shard_map/ppermute | solution.py:86
  210.2 41.9 %collective-permute-start.16 = (bf16[2,2,2,64,768]{4,3,0,1,2:T(8,128)(2,1)}, bf16[2,2,2,64,768]{4,3,0,1,2:T(8,128)(2,1)}, u32[]{:S(2)}, u32[]{:S(2)}) collective-permute-start(bf16[2,2,2,64,768]{4,3,0,1,2:T(8,128)(2,1)} %pad_maximum_fusion.24), channel_id=1, source_target_pairs={{0,1},{1,0},{2,3},{3,2},{4,5},{5,4},{6,7},{7,6},{8,9},{9,8},{10,11... | collective-permute-start | bytes 2359304 | tf_op jit(solution)/shard_map/ppermute | solution.py:86
  242.5 29.7 %collective-permute-start.10 = (bf16[1024,1024]{0,1:T(8,128)(2,1)}, bf16[1024,1024]{0,1:T(8,128)(2,1)}, u32[]{:S(2)}, u32[]{:S(2)}) collective-permute-start(bf16[1024,1024]{0,1:T(8,128)(2,1)} %fusion.97), channel_id=1, source_target_pairs={{0,2},{2,0},{1,3},{3,1},{4,6},{6,4},{5,7},{7,5},{8,10},{10,8},{9,1... | collective-permute-start | bytes 6291464 | tf_op jit(solution)/shard_map/ppermute | solution.py:48
  245.5 24.2 %collective-permute-start.14 = (bf16[2,2,2,64,896]{4,3,0,1,2:T(8,128)(2,1)}, bf16[2,2,2,64,896]{4,3,0,1,2:T(8,128)(2,1)}, u32[]{:S(2)}, u32[]{:S(2)}) collective-permute-start(bf16[2,2,2,64,896]{4,3,0,1,2:T(8,128)(2,1)} %pad_maximum_fusion.22), channel_id=1, source_target_pairs={{0,4},{4,0},{8,12},{12,8},{16,20},{20,16},{24,28},{28,24},{1,5},{5... | collective-permute-start | bytes 2752520 | tf_op jit(solution)/shard_map/ppermute | solution.py:87
  250.7 90.4 %collective-permute-start.20 = (bf16[1024,1024]{0,1:T(8,128)(2,1)}, bf16[1024,1024]{0,1:T(8,128)(2,1)}, u32[]{:S(2)}, u32[]{:S(2)}) collective-permute-start(bf16[1024,1024]{0,1:T(8,128)(2,1)} %copy.281), channel_id=1, source_target_pairs={{0,2},{2,0},{1,3},{3,1},{4,6},{6,4},{5,7},{7,5},{8,10},{10,8},{9,1... | collective-permute-start | bytes 6291464 | tf_op jit(solution)/shard_map/ppermute | solution.py:48
  400.8 16.2 %collective-permute-start.21 = (bf16[1024,1024]{0,1:T(8,128)(2,1)S(1)}, bf16[1024,1024]{0,1:T(8,128)(2,1)S(1)}, u32[]{:S(2)}, u32[]{:S(2)}) collective-permute-start(bf16[1024,1024]{0,1:T(8,128)(2,1)S(1)} %add_convert_fusion.4), channel_id=1, source_target_pairs={{0,2},{2,0},{1,3},{3,1},{4,6},{6,4},{5,7},{7,5},{8,10},{10,8},{9,1... | collective-permute-start | bytes 6291464 | tf_op jit(solution)/shard_map/ppermute | solution.py:48
  473.2 604.2 %reduce-scatter.7.cloned.1.call-start = ((), (), s32[]{:S(2)}) async-start(), calls=%async_computation.4 | async-start | bytes 10305536 | tf_op jit(solution)/shard_map/reduce_scatter | solution.py:149
  570.0 66.4 %collective-permute-start.22 = (bf16[1024,1024]{0,1:T(8,128)(2,1)S(1)}, bf16[1024,1024]{0,1:T(8,128)(2,1)}, u32[]{:S(2)}, u32[]{:S(2)}) collective-permute-start(bf16[1024,1024]{0,1:T(8,128)(2,1)S(1)} %fusion.104), channel_id=1, source_target_pairs={{0,2},{2,0},{1,3},{3,1},{4,6},{6,4},{5,7},{7,5},{8,10},{10,8},{9,1... | collective-permute-start | bytes 6291464 | tf_op jit(solution)/shard_map/ppermute | solution.py:48
  577.4 53.0 %collective-permute-start.33 = (bf16[2,2,2,64,768]{4,3,2,1,0:T(8,128)(2,1)}, bf16[2,2,2,64,768]{4,3,2,1,0:T(8,128)(2,1)S(1)}, u32[]{:S(2)}, u32[]{:S(2)}) collective-permute-start(bf16[2,2,2,64,768]{4,3,2,1,0:T(8,128)(2,1)} %dynamic-slice_bitcast_fusion.2), channel_id=1, source_target_pairs={{0,1},{1,0},{2,3},{3,2},{4,5},{5,4},{6,7},{7,6},{8,9},{9,8},{10,11... | collective-permute-start | bytes 2359304 | tf_op jit(solution)/shard_map/ppermute | solution.py:86
  633.4 219.4 %collective-permute-start.34 = (bf16[2,2,64,768]{3,2,1,0:T(8,128)(2,1)}, bf16[2,2,64,768]{3,2,1,0:T(8,128)(2,1)}, u32[]{:S(2)}, u32[]{:S(2)}) collective-permute-start(bf16[2,2,64,768]{3,2,1,0:T(8,128)(2,1)} %dynamic-slice_bitcast_fusion.6), channel_id=1, source_target_pairs={{0,4},{4,0},{8,12},{12,8},{16,20},{20,16},{24,28},{28,24},{1,5},{5... | collective-permute-start | bytes 1179656 | tf_op jit(solution)/shard_map/ppermute | solution.py:87
  673.6 36.1 %collective-permute-start.23 = (bf16[1024,1024]{0,1:T(8,128)(2,1)S(1)}, bf16[1024,1024]{0,1:T(8,128)(2,1)S(1)}, u32[]{:S(2)}, u32[]{:S(2)}) collective-permute-start(bf16[1024,1024]{0,1:T(8,128)(2,1)S(1)} %add_convert_fusion.3), channel_id=1, source_target_pairs={{0,2},{2,0},{1,3},{3,1},{4,6},{6,4},{5,7},{7,5},{8,10},{10,8},{9,1... | collective-permute-start | bytes 6291464 | tf_op jit(solution)/shard_map/ppermute | solution.py:48
  678.0 28.5 %collective-permute-start.35 = (bf16[2,2,2,64,896]{4,3,2,1,0:T(8,128)(2,1)S(1)}, bf16[2,2,2,64,896]{4,3,2,1,0:T(8,128)(2,1)S(1)}, u32[]{:S(2)}, u32[]{:S(2)}) collective-permute-start(bf16[2,2,2,64,896]{4,3,2,1,0:T(8,128)(2,1)S(1)} %dynamic-slice_bitcast_fusion), channel_id=1, source_target_pairs={{0,4},{4,0},{8,12},{12,8},{16,20},{20,16},{24,28},{28,24},{1,5},{5... | collective-permute-start | bytes 2752520 | tf_op jit(solution)/shard_map/ppermute | solution.py:87
  707.6 146.4 %collective-permute-start.36 = (bf16[2,2,64,896]{3,2,1,0:T(8,128)(2,1)}, bf16[2,2,64,896]{3,2,1,0:T(8,128)(2,1)}, u32[]{:S(2)}, u32[]{:S(2)}) collective-permute-start(bf16[2,2,64,896]{3,2,1,0:T(8,128)(2,1)} %dynamic-slice_bitcast_fusion.4), channel_id=1, source_target_pairs={{0,1},{1,0},{2,3},{3,2},{4,5},{5,4},{6,7},{7,6},{8,9},{9,8},{10,11... | collective-permute-start | bytes 1376264 | tf_op jit(solution)/shard_map/ppermute | solution.py:86
  842.9 64.1 %collective-permute-start.24 = (bf16[1024,1024]{0,1:T(8,128)(2,1)}, bf16[1024,1024]{0,1:T(8,128)(2,1)}, u32[]{:S(2)}, u32[]{:S(2)}) collective-permute-start(bf16[1024,1024]{0,1:T(8,128)(2,1)} %fusion.103), channel_id=1, source_target_pairs={{0,2},{2,0},{1,3},{3,1},{4,6},{6,4},{5,7},{7,5},{8,10},{10,8},{9,1... | collective-permute-start | bytes 6291464 | tf_op jit(solution)/shard_map/ppermute | solution.py:48
  850.9 53.0 %collective-permute-start.26 = (bf16[2,2,2,64,768]{4,3,2,1,0:T(8,128)(2,1)}, bf16[2,2,2,64,768]{4,3,2,1,0:T(8,128)(2,1)}, u32[]{:S(2)}, u32[]{:S(2)}) collective-permute-start(bf16[2,2,2,64,768]{4,3,2,1,0:T(8,128)(2,1)} %dynamic-slice_bitcast_fusion.3), channel_id=1, source_target_pairs={{0,1},{1,0},{2,3},{3,2},{4,5},{5,4},{6,7},{7,6},{8,9},{9,8},{10,11... | collective-permute-start | bytes 2359304 | tf_op jit(solution)/shard_map/ppermute | solution.py:86
  851.0 181.8 %collective-permute-start.19 = (bf16[1024,1024]{0,1:T(8,128)(2,1)}, bf16[1024,1024]{0,1:T(8,128)(2,1)}, u32[]{:S(2)}, u32[]{:S(2)}) collective-permute-start(bf16[1024,1024]{0,1:T(8,128)(2,1)} %get-tuple-element.154), channel_id=1, source_target_pairs={{0,1},{3,2},{4,5},{7,6},{8,9},{11,10},{12,13},{15,14},{16,17},{19,... | collective-permute-start | bytes 6291464 | tf_op jit(solution)/shard_map/ppermute | solution.py:475
  856.1 61.7 %collective-permute-start.37 = (bf16[2,64,1664]{2,1,0:T(8,128)(2,1)}, bf16[2,64,1664]{2,1,0:T(8,128)(2,1)}, u32[]{:S(2)}, u32[]{:S(2)}) collective-permute-start(bf16[2,64,1664]{2,1,0:T(8,128)(2,1)} %fusion.155), channel_id=1, source_target_pairs={{0,8},{4,12},{8,0},{12,4},{16,24},{20,28},{24,16},{28,20},{1,9},{5... | collective-permute-start | bytes 1277960 | tf_op jit(solution)/shard_map/ppermute | solution.py:87
  916.4 38.2 %collective-permute-start.28 = (bf16[2,2,2,64,896]{4,3,2,1,0:T(8,128)(2,1)S(1)}, bf16[2,2,2,64,896]{4,3,2,1,0:T(8,128)(2,1)S(1)}, u32[]{:S(2)}, u32[]{:S(2)}) collective-permute-start(bf16[2,2,2,64,896]{4,3,2,1,0:T(8,128)(2,1)S(1)} %dynamic-slice_bitcast_fusion.1), channel_id=1, source_target_pairs={{0,4},{4,0},{8,12},{12,8},{16,20},{20,16},{24,28},{28,24},{1,5},{5... | collective-permute-start | bytes 2752520 | tf_op jit(solution)/shard_map/ppermute | solution.py:87
  919.8 109.9 %collective-permute-start.38 = (bf16[64,1664]{1,0:T(8,128)(2,1)S(1)}, bf16[64,1664]{1,0:T(8,128)(2,1)S(1)}, u32[]{:S(2)}, u32[]{:S(2)}) collective-permute-start(bf16[64,1664]{1,0:T(8,128)(2,1)S(1)} %dynamic-slice_bitcast_fusion.8), channel_id=1, source_target_pairs={{0,16},{4,20},{8,24},{12,28},{16,0},{20,4},{24,8},{28,12},{1,17},{... | collective-permute-start | bytes 638984 | tf_op jit(solution)/shard_map/ppermute | solution.py:87
  954.9 72.5 %collective-permute-start.29 = (bf16[2,2,64,896]{3,2,1,0:T(8,128)(2,1)S(1)}, bf16[2,2,64,896]{3,2,1,0:T(8,128)(2,1)S(1)}, u32[]{:S(2)}, u32[]{:S(2)}) collective-permute-start(bf16[2,2,64,896]{3,2,1,0:T(8,128)(2,1)S(1)} %dynamic-slice_bitcast_fusion.5), channel_id=1, source_target_pairs={{0,1},{1,0},{2,3},{3,2},{4,5},{5,4},{6,7},{7,6},{8,9},{9,8},{10,11... | collective-permute-start | bytes 1376264 | tf_op jit(solution)/shard_map/ppermute | solution.py:86
  964.8 90.3 %collective-permute-start.25 = (bf16[1024,1024]{0,1:T(8,128)(2,1)}, bf16[1024,1024]{0,1:T(8,128)(2,1)}, u32[]{:S(2)}, u32[]{:S(2)}) collective-permute-start(bf16[1024,1024]{0,1:T(8,128)(2,1)} %add_convert_fusion.2), channel_id=1, source_target_pairs={{0,1},{3,2},{4,5},{7,6},{8,9},{11,10},{12,13},{15,14},{16,17},{19,... | collective-permute-start | bytes 6291464 | tf_op jit(solution)/shard_map/ppermute | solution.py:475
  (163 other events, 1690.1 us)
Sparse Core Ops, SparseCore 0:
  39.7 140.4 all-gather.2
  199.4 128.7 all-gather.4
  473.3 220.9 reduce-scatter.8
  777.6 245.8 reduce-scatter.6

commit v3 on v1

v3 whole, which is shorter than its diff:
```python
import functools

import jax
import jax.numpy as jnp
from jax import lax
from jax.experimental import pallas as pl
from jax.experimental.pallas import tpu as pltpu
from jax.sharding import Mesh, PartitionSpec as P

HEAD_DIM = 64
HALF_WIN = 64
STEP = 10
SEQ_LEN = 1024


norm_eps = 1e-05
theta_local = 10000.0
theta_global = 160000.0
masked_score = -1e30
beta_one = 0.9
beta_two = 0.98
adam_eps = 1e-06
weight_decay = 1e-05
rate_qkv = 0.03
rate_out = 0.15
rate_inp = 0.03
rate_down = 0.02
rate_gain = 0.5

kernel_vmem = 48 * 1024 * 1024
every_axis = ("chip", "core", "tensor")
chip_axes = ("chip", "tensor")


def swap_pairs(chips):
    pairs = []
    for chip in range(chips):
        for core in range(2):
            for row in range(2):
                pairs.append((chip * 4 + core * 2 + row, chip * 4 + row * 2 + core))
    return pairs


def result_pairs(chips):
    return [(chip * 4 + c * 3, chip * 4 + c * 2 + 1 - c) for chip in range(chips) for c in range(2)]


def role_swap(values, chips):
    return lax.ppermute(values, every_axis, swap_pairs(chips))


def core_swap(values):
    return lax.ppermute(values, "core", [(0, 1), (1, 0)])


def core_total(partial_sum):
    own = partial_sum.astype(jnp.bfloat16)
    return own.astype(jnp.float32) + core_swap(own).astype(jnp.float32)


def layer_norm(values, gain):
    centred = values - jnp.mean(values, axis=-1, keepdims=True)
    spread = jnp.mean(centred * centred, axis=-1, keepdims=True)
    return centred * lax.rsqrt(spread + norm_eps) * gain


def rotary_tables(rotary_base):
    positions = jnp.arange(SEQ_LEN, dtype=jnp.int32)
    inverse = rotary_base ** (-jnp.arange(0, HEAD_DIM, 2, dtype=jnp.float32) / HEAD_DIM)
    angles = positions.astype(jnp.float32)[:, None] * inverse[None, :]
    cosine, sine = jnp.cos(angles), jnp.sin(angles)
    return (
        jnp.concatenate([cosine] * 4, axis=-1),
        jnp.concatenate([-sine, sine, -sine, sine], axis=-1),
    )


def gelu_gate(inner, gate_part):
    return jax.nn.gelu(inner, approximate=False) * gate_part


def gather_rows(shard, chips):
    return lax.all_gather(shard, chip_axes, axis=0, tiled=True)


def scatter_rows(gradient, chips):
    shard = lax.psum_scatter(
        gradient.astype(jnp.bfloat16), chip_axes, scatter_dimension=0, tiled=True
    )
    return role_swap(shard, chips).astype(jnp.float32)


def padded_width(width):
    return -(-width // 128) * 128


def widen(values):
    width = values.shape[1]
    return jnp.pad(values, ((0, 0), (0, padded_width(width) - width)))


def layer_starts(masters):
    heads = masters[0].shape[3]
    step = padded_width(masters[2].shape[3])
    return (0, 3 * heads, 4 * heads, 4 * heads + 128, 4 * heads + 128 + step, 4 * heads + 128 + 2 * step)


def pair_major(values):
    rows, kinds, width = values.shape
    wide = 2 * HEAD_DIM
    return values.reshape(rows, kinds, width // wide, wide).swapaxes(1, 2).reshape(rows, -1)


def kind_major(values):
    rows, wide = values.shape[0], 2 * HEAD_DIM
    return values.reshape(rows, -1, 3, wide).swapaxes(1, 2).reshape(rows, 3, -1)


def pack_shards(masters, layer):
    qkv, out, inp, down, gains = [m[layer].astype(jnp.bfloat16) for m in masters]
    return jnp.concatenate(
        [pair_major(qkv), out.T, widen(gains.T), widen(inp[:, 0]), widen(inp[:, 1]), down.T], axis=1
    )


def unpack_weights(packed, starts, hidden):
    return (
        packed[:, : starts[1]],
        packed[:, starts[1] : starts[2]],
        packed[:, starts[3] : starts[3] + hidden],
        packed[:, starts[4] : starts[4] + hidden],
        packed[:, starts[5] :],
        packed[:, starts[2] : starts[2] + 2].T.astype(jnp.float32),
    )


def unpack_grads(packed, starts, hidden):
    inner = packed[:, starts[3] : starts[3] + hidden]
    gate = packed[:, starts[4] : starts[4] + hidden]
    return (
        kind_major(packed[:, : starts[1]]),
        packed[:, starts[1] : starts[2]].T,
        jnp.stack([inner, gate], axis=1),
        packed[:, starts[5] :].T,
        packed[:, starts[2] : starts[2] + 2].T,
    )


def rolled(values):
    lane = lax.broadcasted_iota(jnp.int32, values.shape, 1) % HEAD_DIM
    half = HEAD_DIM // 2
    width = values.shape[1]
    return jnp.where(
        lane < half, pltpu.roll(values, width - half, 1), pltpu.roll(values, half, 1)
    )


def pair_stack(values):
    lane = lax.broadcasted_iota(jnp.int32, values.shape, 1)
    nothing = jnp.zeros_like(values)
    return jnp.concatenate(
        [jnp.where(lane < HEAD_DIM, values, nothing), jnp.where(lane < HEAD_DIM, nothing, values)],
        axis=0,
    )


def pair_unstack(values):
    rows = values.shape[1] // 2
    return jnp.concatenate(
        [values[:HEAD_DIM, :rows], values[HEAD_DIM:, rows:]], axis=0
    ).T


def probability_block(keys_here, stacked, start, is_local, length):
    scores = (
        lax.dot_general(
            keys_here, stacked, (((1,), (1,)), ((), ())), preferred_element_type=jnp.float32
        )
        * 0.125
    )
    if is_local:
        rows = stacked.shape[0] // 2
        key_at = start - HALF_WIN + lax.broadcasted_iota(jnp.int32, scores.shape, 0)
        query_at = start + lax.broadcasted_iota(jnp.int32, scores.shape, 1) % rows
        allowed = (jnp.abs(query_at - key_at) <= HALF_WIN) & (key_at >= 0) & (key_at < length)
        scores = jnp.where(allowed, scores, masked_score)
    exponent = jnp.exp(scores - jnp.max(scores, axis=0, keepdims=True))
    return exponent * (1.0 / jnp.sum(exponent, axis=0, keepdims=True))


def attend_kernel(is_local, block, raw_ref, cos_ref, sin_ref, out_ref, keys, values_t):
    length = raw_ref.shape[0]
    pad = HALF_WIN if is_local else 0
    reach = block + 2 * HALF_WIN if is_local else length
    wide = 2 * HEAD_DIM
    raw_keys = raw_ref[:, wide : 2 * wide]
    rotated = (raw_keys * cos_ref[...] + rolled(raw_keys) * sin_ref[...]).astype(jnp.bfloat16)
    if is_local:
        keys[...] = jnp.zeros_like(keys)
        values_t[...] = jnp.zeros_like(values_t)
    keys[pl.ds(pad, length), :] = rotated
    values_t[:, pl.ds(pad, length)] = raw_ref[:, 2 * wide :].astype(jnp.bfloat16).T

    def step(i):
        start = pl.multiple_of(i * block, block)
        at = start if is_local else 0
        part = raw_ref[pl.ds(start, block), :wide]
        here = pl.ds(start, block)
        query = (part * cos_ref[here, :] + rolled(part) * sin_ref[here, :]).astype(jnp.bfloat16)
        probability = probability_block(
            keys[pl.ds(at, reach), :], pair_stack(query), start, is_local, length
        )
        mixed = jnp.dot(
            values_t[:, pl.ds(at, reach)],
            probability.astype(jnp.bfloat16),
            preferred_element_type=jnp.float32,
        )
        out_ref[here, :] = pair_unstack(mixed).astype(jnp.bfloat16)

    pl.loop(0, length // block, unroll=2)(step)


def attend_back_kernel(
    is_local, block, raw_ref, cos_ref, sin_ref, up_ref, out_ref, keys, keys_t, values, d_keys, d_values
):
    length = raw_ref.shape[0]
    pad = HALF_WIN if is_local else 0
    reach = block + 2 * HALF_WIN if is_local else length
    wide = 2 * HEAD_DIM
    raw_keys = raw_ref[:, wide : 2 * wide]
    rotated = (raw_keys * cos_ref[...] + rolled(raw_keys) * sin_ref[...]).astype(jnp.bfloat16)
    if is_local:
        keys[...] = jnp.zeros_like(keys)
        keys_t[...] = jnp.zeros_like(keys_t)
        values[...] = jnp.zeros_like(values)
    keys[pl.ds(pad, length), :] = rotated
    keys_t[:, pl.ds(pad, length)] = rotated.T
    values[pl.ds(pad, length), :] = raw_ref[:, 2 * wide :].astype(jnp.bfloat16)
    d_keys[...] = jnp.zeros_like(d_keys)
    d_values[...] = jnp.zeros_like(d_values)

    def step(i):
        start = pl.multiple_of(i * block, block)
        at = start if is_local else 0
        here = pl.ds(start, block)
        band = pl.ds(at, reach)
        part = raw_ref[here, :wide]
        query = (part * cos_ref[here, :] + rolled(part) * sin_ref[here, :]).astype(jnp.bfloat16)
        stacked = pair_stack(query)
        upstream = pair_stack(up_ref[here, :])
        probability = probability_block(keys[band, :], stacked, start, is_local, length)
        d_values[band, :] += jnp.dot(
            probability.astype(jnp.bfloat16), upstream, preferred_element_type=jnp.float32
        )
        d_probability = lax.dot_general(
            values[band, :], upstream, (((1,), (1,)), ((), ())), preferred_element_type=jnp.float32
        )
        centre = jnp.sum(probability * d_probability, axis=0, keepdims=True)
        d_scores = (probability * (d_probability - centre)).astype(jnp.bfloat16)
        d_keys[band, :] += jnp.dot(d_scores, stacked, preferred_element_type=jnp.float32)
        d_query = (
            pair_unstack(
                jnp.dot(keys_t[:, band], d_scores, preferred_element_type=jnp.float32)
            )
            * 0.125
        )
        out_ref[here, :wide] = (
            d_query * cos_ref[here, :] - rolled(d_query) * sin_ref[here, :]
        ).astype(jnp.bfloat16)

    pl.loop(0, length // block, unroll=2)(step)
    d_key = d_keys[pl.ds(pad, length), :] * 0.125
    out_ref[:, wide : 2 * wide] = (d_key * cos_ref[...] - rolled(d_key) * sin_ref[...]).astype(
        jnp.bfloat16
    )
    out_ref[:, 2 * wide :] = d_values[pl.ds(pad, length), :].astype(jnp.bfloat16)


def attend_specs(projected):
    rows, columns = projected.shape
    wide = 2 * HEAD_DIM
    raw = pl.BlockSpec((SEQ_LEN, 3 * wide), lambda s, j: (s, j))
    table = pl.BlockSpec((SEQ_LEN, wide), lambda s, j: (0, 0))
    narrow = pl.BlockSpec((SEQ_LEN, wide), lambda s, j: (s, j))
    grid = (rows // SEQ_LEN, columns // (3 * wide))
    return grid, raw, table, narrow


def attend_cost(projected, is_local, products):
    rows, columns = projected.shape
    reach = 4 * HALF_WIN if is_local else SEQ_LEN
    pairs = columns // (6 * HEAD_DIM)
    cells = rows * reach * pairs * 2
    return pl.CostEstimate(
        flops=cells * 8 * HEAD_DIM * products,
        bytes_accessed=projected.size * 8,
        transcendentals=cells,
    )


def attend_forward(projected, tables, is_local):
    rows, columns = projected.shape
    wide = 2 * HEAD_DIM
    grid, raw, table, narrow = attend_specs(projected)
    span = SEQ_LEN + 2 * HALF_WIN if is_local else SEQ_LEN
    return pl.pallas_call(
        functools.partial(attend_kernel, is_local, 128),
        out_shape=jax.ShapeDtypeStruct((rows, columns // 3), jnp.bfloat16),
        grid=grid,
        in_specs=[raw, table, table],
        out_specs=narrow,
        scratch_shapes=[
            pltpu.VMEM((span, wide), jnp.bfloat16),
            pltpu.VMEM((wide, span), jnp.bfloat16),
        ],
        compiler_params=pltpu.CompilerParams(vmem_limit_bytes=kernel_vmem),
        cost_estimate=attend_cost(projected, is_local, 2),
    )(projected, *tables)


def attend_backward(projected, tables, d_attended, is_local):
    rows, columns = projected.shape
    wide = 2 * HEAD_DIM
    grid, raw, table, narrow = attend_specs(projected)
    span = SEQ_LEN + 2 * HALF_WIN if is_local else SEQ_LEN
    return pl.pallas_call(
        functools.partial(attend_back_kernel, is_local, 128),
        out_shape=jax.ShapeDtypeStruct((rows, columns), jnp.bfloat16),
        grid=grid,
        in_specs=[raw, table, table, narrow],
        out_specs=raw,
        scratch_shapes=[
            pltpu.VMEM((span, wide), jnp.bfloat16),
            pltpu.VMEM((wide, span), jnp.bfloat16),
            pltpu.VMEM((span, wide), jnp.bfloat16),
            pltpu.VMEM((span, wide), jnp.float32),
            pltpu.VMEM((span, wide), jnp.float32),
        ],
        compiler_params=pltpu.CompilerParams(vmem_limit_bytes=kernel_vmem),
        cost_estimate=attend_cost(projected, is_local, 5),
    )(projected, *tables, d_attended)


def weight_grad_kernel(
    starts, lowered, branch, lowered_two, up, d_projected, attended, gains, d_inner, d_gate,
    activated, out_ref
):
    def put(left, right, start):
        width = right.shape[1]
        out_ref[:, start : start + width] = lax.dot_general(
            left, right[...], (((0,), (0,)), ((), ())), preferred_element_type=jnp.float32
        ).astype(jnp.bfloat16)

    put(lowered[...], d_projected, starts[0])
    put(branch[...], attended, starts[1])
    out_ref[:, starts[2] : starts[3]] = gains[...]
    normed = lowered_two[...]
    for right, start, stop in ((d_inner, starts[3], starts[4]), (d_gate, starts[4], starts[5])):
        put(normed, right, start)
        filled = start + right.shape[1]
        if filled < stop:
            out_ref[:, filled:stop] = jnp.zeros((out_ref.shape[0], stop - filled), jnp.bfloat16)
    put(up[...], activated, starts[5])


def weight_grads(starts, lefts, rights, gains):
    tokens, features = lefts[0].shape
    block = 256
    left = pl.BlockSpec((tokens, block), lambda i: (0, i))

    def whole(values):
        return pl.BlockSpec(values.shape, lambda i: (0, 0), pipeline_mode=pl.Buffered(1))

    total = starts[5] + rights[4].shape[1]
    d_projected, attended, d_inner, d_gate, activated = rights
    return pl.pallas_call(
        functools.partial(weight_grad_kernel, starts),
        out_shape=jax.ShapeDtypeStruct((features, total), jnp.bfloat16),
        grid=(features // block,),
        in_specs=[left] * 4
        + [
            whole(d_projected),
            whole(attended),
            pl.BlockSpec((block, gains.shape[1]), lambda i: (i, 0)),
            whole(d_inner),
            whole(d_gate),
            whole(activated),
        ],
        out_specs=pl.BlockSpec((block, total), lambda i: (i, 0)),
        compiler_params=pltpu.CompilerParams(vmem_limit_bytes=kernel_vmem),
        cost_estimate=pl.CostEstimate(
            flops=2 * tokens * features * total,
            bytes_accessed=2 * (4 * tokens * features + (tokens + features) * total),
            transcendentals=0,
        ),
    )(*lefts, d_projected, attended, gains, d_inner, d_gate, activated)


def product(left, right, contract):
    return lax.dot_general(
        left, right, ((contract[:1], contract[1:]), ((), ())), preferred_element_type=jnp.float32
    )


def forward_layer(residual, weights, tables, is_local):
    w_qkv, w_out, w_inner, w_gate, w_down, gain_pair = weights
    lowered = layer_norm(residual, gain_pair[0]).astype(jnp.bfloat16)
    projected = product(lowered, w_qkv, (1, 0))
    attended = attend_forward(projected, tables, is_local)
    middle = residual + core_total(product(attended, w_out, (1, 1)))
    lowered_two = layer_norm(middle, gain_pair[1]).astype(jnp.bfloat16)
    inner = product(lowered_two, w_inner, (1, 0))
    gate_part = product(lowered_two, w_gate, (1, 0))
    activated = gelu_gate(inner, gate_part).astype(jnp.bfloat16)
    output = middle + core_total(product(activated, w_down, (1, 1)))
    kept = (residual, middle, lowered, lowered_two, projected, attended, inner, gate_part, activated)
    return (output, kept)


def backward_layer(upstream, weights, tables, kept, is_local, starts):
    w_qkv, w_out, w_inner, w_gate, w_down, gain_pair = weights
    residual, middle, lowered, lowered_two, projected, attended, inner, gate_part, activated = kept
    up_low = upstream.astype(jnp.bfloat16)
    d_activated = product(up_low, w_down, (1, 0))
    unused, pullback = jax.vjp(gelu_gate, inner, gate_part)
    d_inner, d_gate = [v.astype(jnp.bfloat16) for v in pullback(d_activated)]
    d_normed_two = core_total(
        product(d_inner, w_inner, (1, 1)) + product(d_gate, w_gate, (1, 1))
    )
    unused, pullback = jax.vjp(layer_norm, middle, gain_pair[1])
    d_mid_norm, d_gain_two = pullback(d_normed_two)
    d_middle = upstream + d_mid_norm
    d_branch = d_middle.astype(jnp.bfloat16)
    d_attended = product(d_branch, w_out, (1, 0)).astype(jnp.bfloat16)
    d_projected = attend_backward(projected, tables, d_attended, is_local)
    d_normed = core_total(product(d_projected, w_qkv, (1, 1)))
    unused, pullback = jax.vjp(layer_norm, residual, gain_pair[0])
    d_in_norm, d_gain_one = pullback(d_normed)
    gains = widen(jnp.stack([d_gain_one, d_gain_two], axis=1)).astype(jnp.bfloat16)
    packed = weight_grads(
        starts,
        (lowered, d_branch, lowered_two, up_low),
        (d_projected, attended, d_inner, d_gate, activated),
        gains,
    )
    return (d_middle + d_in_norm, packed)


def adam_update(weight, moment, square, gradient, step_rate, decay_here):
    moment_new = beta_one * moment + (1.0 - beta_one) * gradient
    square_new = beta_two * square + (1.0 - beta_two) * gradient * gradient
    moment_hat = moment_new / (1.0 - beta_one**STEP)
    square_hat = square_new / (1.0 - beta_two**STEP)
    updated = weight - step_rate * (
        moment_hat / (jnp.sqrt(square_hat) + adam_eps) + decay_here * weight
    )
    return (moment_new, square_new, updated)


def per_device(chips, hidden_in, cotangent, *state):
    masters = state[:5]
    moments = state[5:]
    same = lax.axis_index("core") == lax.axis_index("tensor")

    def chip_sequence(values):
        return jnp.where(same, values, core_swap(values)).astype(jnp.float32)

    def own_sequence(values):
        return jnp.where(same, values, lax.ppermute(values, every_axis, result_pairs(chips)))

    starts = layer_starts(masters)
    hidden = masters[2].shape[3]
    local_tables = rotary_tables(theta_local)
    global_tables = rotary_tables(theta_global)
    shards = [role_swap(pack_shards(masters, layer), chips) for layer in range(2)]
    hidden_in, shards = lax.optimization_barrier((hidden_in, shards))
    weights = [unpack_weights(gather_rows(s, chips), starts, hidden) for s in shards]
    inputs = chip_sequence(hidden_in)
    upstream = chip_sequence(cotangent)
    middle, kept_first = forward_layer(inputs, weights[0], local_tables, True)
    output, kept_second = forward_layer(middle, weights[1], global_tables, False)
    final_out = own_sequence(output.astype(jnp.bfloat16))
    d_middle, packed = backward_layer(
        upstream, weights[1], global_tables, kept_second, False, starts
    )
    grads_second = unpack_grads(scatter_rows(packed, chips), starts, hidden)
    d_values, packed = backward_layer(d_middle, weights[0], local_tables, kept_first, True, starts)
    grads_first = unpack_grads(scatter_rows(packed, chips), starts, hidden)
    final_grad = own_sequence(d_values.astype(jnp.bfloat16)).astype(jnp.float32)
    rates = (rate_qkv, rate_out, rate_inp, rate_down, rate_gain)
    results = [final_out, final_grad]
    for i, rate in enumerate(rates):
        gradient = jnp.stack([grads_first[i], grads_second[i]])
        decay = 0.0 if i == 4 else weight_decay
        results += adam_update(
            masters[i], moments[2 * i], moments[2 * i + 1], gradient, rate, decay
        )
    return tuple(results)


def solution(mesh):
    chips = mesh.shape["dp"] // 2
    fine = Mesh(mesh.devices.reshape(chips, 2, mesh.shape["tensor"]), every_axis)
    dp = ("chip", "core")
    tokens = P(dp, None)
    first = P(None, dp, None, "tensor")
    second = P(None, "tensor", dp)
    gain = P(None, None, dp)
    weights = (first, second, first, second, gain)
    pairs = tuple(s for s in weights for unused in range(2))
    triples = tuple(s for s in weights for unused in range(3))

    def body(*arguments):
        return per_device(chips, *arguments)

    return jax.shard_map(
        body,
        mesh=fine,
        in_specs=(tokens, tokens) + weights + pairs,
        out_specs=(tokens, tokens) + triples,
        check_vma=False,
    )
```

time: 1600 us -> 1230 us (0.77)
  Pallas kernels: 0 us -> 182 us
  matrix products: 301 us -> 140 us
  other arithmetic: 207 us -> 82 us
  waiting for transfers between devices: 858 us -> 734 us
  starting transfers between devices: 118 us -> 19.7 us
  local copies, waits for them, and re-layouts: 88.2 us -> 46.1 us
    pallas_call x0 -> x6, Pallas kernels: none -> 182 us  [the longest x2 84.9 us: attend_backward(): pl.pallas_call(functools.partial(attend_back_kernel, is_local, 128), out_...]
    all_gather x10 -> x2, waiting for transfers between devices: 401 us -> 239 us  [gather_rows(): return lax.all_gather(shard, chip_axes, axis=0, tiled=True)]
    dot_general x12 -> x0, matrix products: 106 us -> none  [the longest x1 22.9 us: attend_backward(): jnp.einsum('sqhd,skhd->shqk', d_heads, value_all, preferred_element_type=...]
    ppermute x20 -> x4, starting transfers between devices: 105 us -> 12.1 us  [role_swap(): return lax.ppermute(values, every_axis, swap_pairs(chips))]
    dot_general x30 -> x20, matrix products: 194 us -> 140 us  [product(): lax.dot_general(left, right, ((contract[:1], contract[1:]), ((), ())), pr...]
    reduce_scatter x10 -> x2, waiting for transfers between devices: 376 us -> 430 us  [scatter_rows(): lax.psum_scatter(gradient.astype(jnp.bfloat16), chip_axes, scatter_dimens...]
    ppermute x2, waiting for transfers between devices: 43.6 us -> 4.23 us  [own_sequence(): lax.ppermute(values, every_axis, result_pairs(chips))]
    convert_element_type x7 -> x5, other arithmetic: 35.2 us -> 4.33 us  [the longest x2 1.97 us: unpack_weights(): packed[:, starts[2]:starts[2] + 2].T.astype(jnp.float32)]
  transfers between devices with their start and end apart: 52 -> 20, of which waited for: 28 -> 15; matrix products, arithmetic and copies ran while one was open for 33% -> 11% of each run, Pallas kernels for 0% -> 9%
where the time goes in v3:
time: 1230 us; the launch traced here: 1220 us
  waiting for transfers between devices  734 us (60%)
  Pallas kernels  182 us (15%)
  matrix products  140 us (11%)
  other arithmetic  82 us (7%)
  local copies, waits for them, and re-layouts  46.1 us (4%)
  starting transfers between devices  19.7 us (2%)
  between operations  15.8 us (1%)
    reduce_scatter x2, waiting for transfers between devices, scatter_rows(): lax.psum_scatter(gradient.astype(jnp.bfloat16), chip_axes, scatter_dimens...  430 us
    all_gather x2, waiting for transfers between devices, gather_rows(): return lax.all_gather(shard, chip_axes, axis=0, tiled=True)  239 us
    dot_general x20, matrix products, product(): lax.dot_general(left, right, ((contract[:1], contract[1:]), ((), ())), pr...  140 us
    pallas_call x2, Pallas kernels, attend_backward(): pl.pallas_call(functools.partial(attend_back_kernel, is_local, 128), out_...  84.9 us
    pallas_call x2, Pallas kernels, attend_forward(): pl.pallas_call(functools.partial(attend_kernel, is_local, 128), out_shape...  53.5 us
    pallas_call x2, Pallas kernels, weight_grads(): pl.pallas_call(functools.partial(weight_grad_kernel, starts), out_shape=j...  44 us
    ppermute x4, waiting for transfers between devices, role_swap(): return lax.ppermute(values, every_axis, swap_pairs(chips))  41.1 us
    unnamed x205, local copies, waits for them, and re-layouts  30.3 us
  transfers between devices with their start and end apart: 20, of which 15 were waited for; matrix products, arithmetic and copies ran while one was open for 11% of the time, Pallas kernels for 9%

profile of v3, /device:TPU:1, one launch (start us, length us, event | category | flops | bytes accessed | tf_op | source)
XLA Modules:
  0.0 1220.0 jit_solution(8832081740404673269)
XLA Ops:
  27.9 8.1 collective-permute-done.1
  36.0 8.9 collective-permute-done
  45.9 5.1 fusion.88
  55.8 147.0 %all-gather.3.cloned.1.call-done = bf16[1024,6304]{1,0:T(8,128)(2,1)} async-done(((bf16[64,6304]{1,0:T(8,128)(2,1)}), bf16[1024,6304]{1,0:T(8,128)(2,1)}) %all-gather.3.cloned.1.call-update) | async-done | bytes 12910608 | tf_op jit(solution)/shard_map/all_gather | solution.py:83
  205.6 7.9 fusion.32.raw_ref
  213.5 19.5 %shard_map.296.attended = bf16[1024,512]{1,0:T(8,128)(2,1)S(1)} custom-call(f32[1024,1536]{1,0:T(8,128)} %fusion.32.raw_ref, f32[1024,128]{1,0:T(8,128)S(1)} %get-tuple-element.195.cos_ref, f32[1024,128]{1,0:T(8,128)S(1)} %get-tuple-element.196.sin_ref), custom_call_target="tpu_custom_call" | custom-call | flops 2147483648 | bytes 12582912 | tf_op jit(solution)/shard_map/pallas_call | solution.py:306
  247.0 17.6 %multiply_convert_fusion.3 = (bf16[1024,1312]{1,0:T(8,128)(2,1)S(1)}, f32[1024,1312]{1,0:T(8,128)}, f32[1024,1312]{1,0:T(8,128)}) fusion(f32[1024,1312]{1,0:T(8,128)S(1)} %fusion.57, bf16[1024,1024]{1,0:T(8,128)(2,1)S(1)} %multiply_convert_fusion.6.lowered_two, bf16[1024,6304]{1,0:T(8,128)(2,1)S(1)} %bitcast.127), kind=kOutput, calls=%fused_computation.32 | convolution fusion | flops 2840133632 | bytes 24182784 | tf_op jit(solution)/shard_map/dot_general | solution.py:400
  269.8 91.7 %all-gather.5.cloned.1.call-done = bf16[1024,6304]{1,0:T(8,128)(2,1)} async-done(((bf16[64,6304]{1,0:T(8,128)(2,1)}), bf16[1024,6304]{1,0:T(8,128)(2,1)}) %all-gather.5.cloned.1.call-update) | async-done | bytes 12910608 | tf_op jit(solution)/shard_map/all_gather | solution.py:83
  368.0 7.8 fusion.28.raw_ref
  375.9 34.1 %shard_map.297.attended = bf16[1024,512]{1,0:T(8,128)(2,1)S(1)} custom-call(f32[1024,1536]{1,0:T(8,128)} %fusion.28.raw_ref, f32[1024,128]{1,0:T(8,128)S(1)} %get-tuple-element.197.cos_ref, f32[1024,128]{1,0:T(8,128)S(1)} %get-tuple-element.198.sin_ref), custom_call_target="tpu_custom_call" | custom-call | flops 8589934592 | bytes 12582912 | tf_op jit(solution)/shard_map/pallas_call | solution.py:306
  419.5 6.0 fusion.41
  425.5 5.2 fusion.45
  430.7 21.7 %add_convert_fusion.1 = (bf16[1024,1312]{1,0:T(8,128)(2,1)}, f32[1024,1312]{1,0:T(8,128)}, f32[1024,1312]{1,0:T(8,128)}) fusion(f32[1024,1312]{1,0:T(8,128)S(1)} %fusion.41, f32[1024,1312]{1,0:T(8,128)S(1)} %fusion.45, bf16[1024,1024]{1,0:T(8,128)(2,1)S(1)} %broadcast_select_fusion.up, bf16[1024,6304]{1,0:T(8,128)(2,1)} %all-gather.5.cloned.1.call-done), kind=kOutput, calls=%fused_computation.18 | convolution fusion | flops 2849538048 | bytes 29163520 | tf_op jit(solution)/shard_map/dot_general | solution.py:400
  452.4 8.5 multiply_convert_fusion.1
  460.9 7.9 fusion.39
  468.8 7.5 add_convert_fusion.4
  476.7 5.5 fusion.62
  495.8 55.4 %shard_map.298.d_projected = bf16[1024,1536]{1,0:T(8,128)(2,1)S(1)} custom-call(f32[1024,1536]{1,0:T(8,128)} %fusion.28.raw_ref, f32[1024,128]{1,0:T(8,128)S(1)} %get-tuple-element.197.cos_ref, f32[1024,128]{1,0:T(8,128)S(1)} %get-tuple-element.198.sin_ref, bf16[1024,512]{1,0:T(8,128)(2,1)S(1)} %convolution_convert_fusion.3.up_ref), custom_call_target="tpu_custom_call" | custom-call | flops 21474836480 | bytes 12582912 | tf_op jit(solution)/shard_map/pallas_call | solution.py:326
  551.2 6.7 fusion.68
  566.2 22.0 %shard_map.301 = bf16[1024,6304]{1,0:T(8,128)(2,1)} custom-call(bf16[1024,1024]{1,0:T(8,128)(2,1)S(1)} %copy-done.7, bf16[1024,1024]{1,0:T(8,128)(2,1)S(1)} %copy-done.9, bf16[1024,1024]{1,0:T(8,128)(2,1)} %copy-done.39, bf16[1024,1024]{1,0:T(8,128)(2,1)} %copy-done.26, bf16[1024,1536]{1,0:T(8,128)(2,1)} %copy-done.13, ...), custom_call_target="tpu_custom_call" | custom-call | flops 13220446208 | bytes 34209792 | tf_op jit(solution)/shard_map/pallas_call | solution.py:376
  589.8 4.6 fusion.106
  600.9 9.9 add_convert_fusion
  610.8 6.3 fusion.51
  617.2 5.7 add_convert_fusion.3
  636.2 29.5 %shard_map.299.d_projected = bf16[1024,1536]{1,0:T(8,128)(2,1)S(1)} custom-call(f32[1024,1536]{1,0:T(8,128)} %fusion.32.raw_ref, f32[1024,128]{1,0:T(8,128)S(1)} %copy-done.1, f32[1024,128]{1,0:T(8,128)S(1)} %copy-done.3, bf16[1024,512]{1,0:T(8,128)(2,1)S(1)} %convolution_convert_fusion.2.up_ref), custom_call_target="tpu_custom_call" | custom-call | flops 5368709120 | bytes 12582912 | tf_op jit(solution)/shard_map/pallas_call | solution.py:326
  665.8 6.7 fusion.65
  682.8 22.0 %shard_map.300 = bf16[1024,6304]{1,0:T(8,128)(2,1)} custom-call(bf16[1024,1024]{1,0:T(8,128)(2,1)S(1)} %copy-done.5, bf16[1024,1024]{1,0:T(8,128)(2,1)S(1)} %fusion.83.branch, bf16[1024,1024]{1,0:T(8,128)(2,1)} %copy-done.38, bf16[1024,1024]{1,0:T(8,128)(2,1)} %copy-done.45, bf16[1024,1536]{1,0:T(8,128)(2,1)} %copy-done.12, ...), custom_call_target="tpu_custom_call" | custom-call | flops 13220446208 | bytes 34209792 | tf_op jit(solution)/shard_map/pallas_call | solution.py:376
  706.3 6.7 add_convert_fusion.2
  714.5 180.0 %reduce-scatter.5.cloned.1.call-done = bf16[64,6304]{1,0:T(8,128)(2,1)} async-done(((bf16[1024,6304]{1,0:T(8,128)(2,1)}), bf16[64,6304]{1,0:T(8,128)(2,1)}) %reduce-scatter.5.cloned.1.call-update) | async-done | bytes 806928 | tf_op jit(solution)/shard_map/reduce_scatter | solution.py:87
  907.1 17.3 %collective-permute-done.15 = bf16[64,6304]{1,0:T(8,128)(2,1)S(1)} collective-permute-done((bf16[64,6304]{1,0:T(8,128)(2,1)}, bf16[64,6304]{1,0:T(8,128)(2,1)S(1)}, u32[]{:S(2)}, u32[]{:S(2)}) %collective-permute-start.15) | collective-permute-done | bytes 806944 | tf_op jit(solution)/shard_map/ppermute | solution.py:49
  925.4 250.0 %reduce-scatter.3.cloned.1.call-done = bf16[64,6304]{1,0:T(8,128)(2,1)} async-done(((bf16[1024,6304]{1,0:T(8,128)(2,1)}), bf16[64,6304]{1,0:T(8,128)(2,1)}) %reduce-scatter.3.cloned.1.call-update) | async-done | bytes 806928 | tf_op jit(solution)/shard_map/reduce_scatter | solution.py:87
  1182.4 6.9 collective-permute-done.14
  (353 shorter events, 164.8 us)
Async XLA Ops:
  7.2 195.6 %all-gather.3.cloned.1.call-start = ((), (), s32[]{:S(2)}) async-start(), calls=%async_computation.2 | async-start | bytes 13926400 | tf_op jit(solution)/shard_map/all_gather | solution.py:83
  15.1 30.6 %copy-start.43 = (bf16[1024,1024]{1,0:T(8,128)(2,1)S(1)}, bf16[1024,1024]{1,0:T(8,128)(2,1)}, u32[]{:S(2)}) copy-start(bf16[1024,1024]{1,0:T(8,128)(2,1)} %param.17) | copy-start | bytes 6291460
  21.5 14.5 %collective-permute-start.1 = (bf16[64,6304]{1,0:T(8,128)(2,1)S(1)}, bf16[64,6304]{1,0:T(8,128)(2,1)S(1)}, u32[]{:S(2)}, u32[]{:S(2)}) collective-permute-start(bf16[64,6304]{1,0:T(8,128)(2,1)S(1)} %get-tuple-element.170), channel_id=1, source_target_pairs={{0,0},{1,2},{2,1},{3,3},{4,4},{5,6},{6,5},{7,7},{8,8},{9,10},{10,9... | collective-permute-start | bytes 2420744 | tf_op jit(solution)/shard_map/ppermute | solution.py:49
  26.0 18.9 %collective-permute-start = (bf16[64,6304]{1,0:T(8,128)(2,1)}, bf16[64,6304]{1,0:T(8,128)(2,1)}, u32[]{:S(2)}, u32[]{:S(2)}) collective-permute-start(bf16[64,6304]{1,0:T(8,128)(2,1)} %get-tuple-element.171), channel_id=1, source_target_pairs={{0,0},{1,2},{2,1},{3,3},{4,4},{5,6},{6,5},{7,7},{8,8},{9,10},{10,9... | collective-permute-start | bytes 2420744 | tf_op jit(solution)/shard_map/ppermute | solution.py:49
  44.9 316.5 %all-gather.5.cloned.1.call-start = ((), (), s32[]{:S(2)}) async-start(), calls=%async_computation.3 | async-start | bytes 13926400 | tf_op jit(solution)/shard_map/all_gather | solution.py:83
  45.7 848.9 %reduce-scatter.5.cloned.1.call-start = ((), (), s32[]{:S(2)}) async-start(), calls=%async_computation.5 | async-start | bytes 13926400 | tf_op jit(solution)/shard_map/reduce_scatter | solution.py:87
  45.7 6.1 collective-permute-start.2
  51.8 161.7 %copy-start = (f32[1024,128]{1,0:T(8,128)}, f32[1024,128]{1,0:T(8,128)S(1)}, u32[]{:S(2)}) copy-start(f32[1024,128]{1,0:T(8,128)S(1)} %get-tuple-element.195.cos_ref) | copy-start | bytes 1572868
  51.9 161.7 %copy-start.2 = (f32[1024,128]{1,0:T(8,128)}, f32[1024,128]{1,0:T(8,128)S(1)}, u32[]{:S(2)}) copy-start(f32[1024,128]{1,0:T(8,128)S(1)} %get-tuple-element.196.sin_ref) | copy-start | bytes 1572868
  54.5 186.4 %copy-start.17 = (bf16[1024,1024]{1,0:T(8,128)(2,1)}, bf16[1024,1024]{1,0:T(8,128)(2,1)S(1)}, u32[]{:S(2)}) copy-start(bf16[1024,1024]{1,0:T(8,128)(2,1)S(1)} %get-tuple-element.154) | copy-start | bytes 6291460
  54.5 159.0 %copy-start.58 = (f32[1024]{0:T(1024)}, f32[1024]{0:T(1024)S(1)}, u32[]{:S(2)}) copy-start(f32[1024]{0:T(1024)S(1)} %broadcast_multiply_fusion.3) | copy-start | bytes 12292
  55.8 157.7 %copy-start.66 = (f32[1024]{0:T(1024)}, f32[1024]{0:T(1024)S(1)}, u32[]{:S(2)}) copy-start(f32[1024]{0:T(1024)S(1)} %fusion.91) | copy-start | bytes 12292
  204.3 38.1 %copy-start.68 = (f32[1024]{0:T(1024)}, f32[1024]{0:T(1024)S(1)}, u32[]{:S(2)}) copy-start(f32[1024]{0:T(1024)S(1)} %get-tuple-element.118) | copy-start | bytes 12292
  236.0 4.9 collective-permute-start.3
  247.0 17.6 %copy-start.85 = (f32[1024,1312]{1,0:T(8,128)}, f32[1024,1312]{1,0:T(8,128)S(1)}, u32[]{:S(2)}) copy-start(f32[1024,1312]{1,0:T(8,128)S(1)} %fusion.57) | copy-start | bytes 16121860
  268.3 94.6 %collective-permute-start.4 = (bf16[1024,1024]{1,0:T(8,128)(2,1)S(1)}, bf16[1024,1024]{1,0:T(8,128)(2,1)}, u32[]{:S(2)}, u32[]{:S(2)}) collective-permute-start(bf16[1024,1024]{1,0:T(8,128)(2,1)S(1)} %fusion.59), channel_id=1, source_target_pairs={{0,2},{2,0},{1,3},{3,1},{4,6},{6,4},{5,7},{7,5},{8,10},{10,8},{9,1... | collective-permute-start | bytes 6291464 | tf_op jit(solution)/shard_map/ppermute | solution.py:53
  268.7 144.9 %collective-permute-start.8 = (bf16[1024,1024]{1,0:T(8,128)(2,1)}, bf16[1024,1024]{1,0:T(8,128)(2,1)}, u32[]{:S(2)}, u32[]{:S(2)}) collective-permute-start(bf16[1024,1024]{1,0:T(8,128)(2,1)} %param.18), channel_id=1, source_target_pairs={{0,2},{2,0},{1,3},{3,1},{4,6},{6,4},{5,7},{7,5},{8,10},{10,8},{9,1... | collective-permute-start | bytes 6291464 | tf_op jit(solution)/shard_map/ppermute | solution.py:53
  366.6 195.7 %copy-start.16 = (f32[1024,1024]{1,0:T(8,128)}, f32[1024,1024]{1,0:T(8,128)S(1)}, u32[]{:S(2)}) copy-start(f32[1024,1024]{1,0:T(8,128)S(1)} %get-tuple-element.148) | copy-start | bytes 12582916
  412.5 4.9 collective-permute-start.5
  415.4 74.6 %copy-start.26 = (bf16[1024,1024]{1,0:T(8,128)(2,1)}, bf16[1024,1024]{1,0:T(8,128)(2,1)S(1)}, u32[]{:S(2)}) copy-start(bf16[1024,1024]{1,0:T(8,128)(2,1)S(1)} %broadcast_select_fusion.up) | copy-start | bytes 6291460
  430.7 21.8 %copy-start.33 = (f32[1024,1312]{1,0:T(8,128)}, f32[1024,1312]{1,0:T(8,128)S(1)}, u32[]{:S(2)}) copy-start(f32[1024,1312]{1,0:T(8,128)S(1)} %fusion.45) | copy-start | bytes 16121860
  476.3 6.1 collective-permute-start.9
  482.2 4.2 collective-permute-start.6
  558.0 4.2 collective-permute-start.10
  588.2 587.2 %reduce-scatter.3.cloned.1.call-start = ((), (), s32[]{:S(2)}) async-start(), calls=%async_computation.4 | async-start | bytes 13926400 | tf_op jit(solution)/shard_map/reduce_scatter | solution.py:87
  596.3 35.4 %copy-start.21 = (f32[1024,1024]{1,0:T(8,128)}, f32[1024,1024]{1,0:T(8,128)S(1)}, u32[]{:S(2)}) copy-start(f32[1024,1024]{1,0:T(8,128)S(1)} %get-tuple-element.138) | copy-start | bytes 12582916
  622.8 4.2 collective-permute-start.11
  672.6 4.2 collective-permute-start.12
  704.8 192.7 %collective-permute-start.7 = (bf16[1024,1024]{1,0:T(8,128)(2,1)}, bf16[1024,1024]{1,0:T(8,128)(2,1)}, u32[]{:S(2)}, u32[]{:S(2)}) collective-permute-start(bf16[1024,1024]{1,0:T(8,128)(2,1)} %get-tuple-element.159), channel_id=1, source_target_pairs={{0,1},{3,2},{4,5},{7,6},{8,9},{11,10},{12,13},{15,14},{16,17},{19,... | collective-permute-start | bytes 6291464 | tf_op jit(solution)/shard_map/ppermute | solution.py:469
  713.0 191.8 %collective-permute-start.13 = (bf16[1024,1024]{1,0:T(8,128)(2,1)}, bf16[1024,1024]{1,0:T(8,128)(2,1)S(1)}, u32[]{:S(2)}, u32[]{:S(2)}) collective-permute-start(bf16[1024,1024]{1,0:T(8,128)(2,1)} %add_convert_fusion.2), channel_id=1, source_target_pairs={{0,1},{3,2},{4,5},{7,6},{8,9},{11,10},{12,13},{15,14},{16,17},{19,... | collective-permute-start | bytes 6291464 | tf_op jit(solution)/shard_map/ppermute | solution.py:469
  894.6 29.8 %collective-permute-start.15 = (bf16[64,6304]{1,0:T(8,128)(2,1)}, bf16[64,6304]{1,0:T(8,128)(2,1)S(1)}, u32[]{:S(2)}, u32[]{:S(2)}) collective-permute-start(bf16[64,6304]{1,0:T(8,128)(2,1)} %reduce-scatter.5.cloned.1.call-done), channel_id=1, source_target_pairs={{0,0},{1,2},{2,1},{3,3},{4,4},{5,6},{6,5},{7,7},{8,8},{9,10},{10,9... | collective-permute-start | bytes 2420744 | tf_op jit(solution)/shard_map/ppermute | solution.py:49
  1175.4 13.9 %collective-permute-start.14 = (bf16[64,6304]{1,0:T(8,128)(2,1)}, bf16[64,6304]{1,0:T(8,128)(2,1)S(1)}, u32[]{:S(2)}, u32[]{:S(2)}) collective-permute-start(bf16[64,6304]{1,0:T(8,128)(2,1)} %reduce-scatter.3.cloned.1.call-done), channel_id=1, source_target_pairs={{0,0},{1,2},{2,1},{3,3},{4,4},{5,6},{6,5},{7,7},{8,8},{9,10},{10,9... | collective-permute-start | bytes 2420744 | tf_op jit(solution)/shard_map/ppermute | solution.py:49
  (84 other events, 474.3 us)
Sparse Core Ops, SparseCore 0:
  45.0 157.7 all-gather.2
  206.2 155.1 all-gather.4
  588.3 306.2 reduce-scatter.4
  896.8 278.6 reduce-scatter.2

commit v4 on v3

--- a/solution.py
+++ b/solution.py
@@ -79,15 +79,82 @@
     return jax.nn.gelu(inner, approximate=False) * gate_part
 
 
+def group_bits(chips):
+    return chips.bit_length() - 1
+
+
+def bit_swap(values, bit, chips):
+    if bit < 0:
+        return lax.ppermute(values, "tensor", [(0, 1), (1, 0)])
+    return lax.ppermute(values, "chip", [(chip, chip ^ (1 << bit)) for chip in range(chips)])
+
+
+def own_bit(bit):
+    if bit < 0:
+        return lax.axis_index("tensor")
+    return (lax.axis_index("chip") >> bit) & 1
+
+
+def gather_bit(values, held, bit, chips):
+    place = len([b for b in held if b > bit])
+    other = bit_swap(values, bit, chips)
+    is_low = own_bit(bit) == 0
+    joined = jnp.stack(
+        [jnp.where(is_low, values, other), jnp.where(is_low, other, values)], axis=place
+    )
+    return joined, sorted(held + [bit], reverse=True)
+
+
+def reduce_bit(values, held, bit, chips):
+    place = held.index(bit)
+    mine = own_bit(bit)
+    kept = lax.dynamic_index_in_dim(values, mine, place, keepdims=False)
+    sent = lax.dynamic_index_in_dim(values, 1 - mine, place, keepdims=False)
+    other = bit_swap(sent, bit, chips)
+    total = (kept.astype(jnp.float32) + other.astype(jnp.float32)).astype(jnp.bfloat16)
+    return total, [b for b in held if b != bit]
+
+
+def half_columns(values):
+    return values.shape[1] // 256 * 128
+
+
+def gather_quick(shard, chips):
+    values, held = shard, []
+    cut = half_columns(shard)
+    for bit in range(group_bits(chips) - 1, 0, -1):
+        values, held = gather_bit(values, held, bit, chips)
+    halves = []
+    for order, part in (((0, -1), values[..., :cut]), ((-1, 0), values[..., cut:])):
+        part_held = held
+        for bit in order:
+            part, part_held = gather_bit(part, part_held, bit, chips)
+        halves.append(part.reshape(-1, part.shape[-1]))
+    return jnp.concatenate(halves, axis=1)
+
+
+def scatter_quick(gradient, chips):
+    count = group_bits(chips)
+    cut = half_columns(gradient)
+    parts = []
+    for order, part in (((-1, 0), gradient[:, :cut]), ((0, -1), gradient[:, cut:])):
+        held = list(range(count - 1, -2, -1))
+        values = part.reshape([2] * len(held) + [-1, part.shape[-1]])
+        for bit in order:
+            values, held = reduce_bit(values, held, bit, chips)
+        parts.append(values)
+    values = jnp.concatenate(parts, axis=-1)
+    for bit in range(1, count):
+        values, held = reduce_bit(values, held, bit, chips)
+    return values
+
+
 def gather_rows(shard, chips):
     return lax.all_gather(shard, chip_axes, axis=0, tiled=True)
 
 
 def scatter_rows(gradient, chips):
-    shard = lax.psum_scatter(
-        gradient.astype(jnp.bfloat16), chip_axes, scatter_dimension=0, tiled=True
-    )
-    return role_swap(shard, chips).astype(jnp.float32)
+    return lax.psum_scatter(gradient, chip_axes, scatter_dimension=0, tiled=True)
 
 
 def padded_width(width):
@@ -123,14 +190,19 @@
     )
 
 
-def unpack_weights(packed, starts, hidden):
+def split_packed(packed, starts):
+    return packed[:, : starts[3]], packed[:, starts[3] :]
+
+
+def unpack_weights(heads_part, hidden_part, starts, hidden):
+    step = starts[4] - starts[3]
     return (
-        packed[:, : starts[1]],
-        packed[:, starts[1] : starts[2]],
-        packed[:, starts[3] : starts[3] + hidden],
-        packed[:, starts[4] : starts[4] + hidden],
-        packed[:, starts[5] :],
-        packed[:, starts[2] : starts[2] + 2].T.astype(jnp.float32),
+        heads_part[:, : starts[1]],
+        heads_part[:, starts[1] : starts[2]],
+        hidden_part[:, :hidden],
+        hidden_part[:, step : step + hidden],
+        hidden_part[:, 2 * step :],
+        heads_part[:, starts[2] : starts[2] + 2].T.astype(jnp.float32),
     )
 
 
@@ -341,59 +413,53 @@
     )(projected, *tables, d_attended)
 
 
-def weight_grad_kernel(
-    starts, lowered, branch, lowered_two, up, d_projected, attended, gains, d_inner, d_gate,
-    activated, out_ref
-):
-    def put(left, right, start):
-        width = right.shape[1]
-        out_ref[:, start : start + width] = lax.dot_general(
-            left, right[...], (((0,), (0,)), ((), ())), preferred_element_type=jnp.float32
-        ).astype(jnp.bfloat16)
-
-    put(lowered[...], d_projected, starts[0])
-    put(branch[...], attended, starts[1])
-    out_ref[:, starts[2] : starts[3]] = gains[...]
-    normed = lowered_two[...]
-    for right, start, stop in ((d_inner, starts[3], starts[4]), (d_gate, starts[4], starts[5])):
-        put(normed, right, start)
+def weight_grad_kernel(choice, starts, total, left_count, *refs):
+    lefts = [ref[...] for ref in refs[:left_count]]
+    rights, out_ref = refs[left_count:-1], refs[-1]
+    for right, which, start, stop in zip(rights, choice, starts, list(starts[1:]) + [total]):
         filled = start + right.shape[1]
+        if which is None:
+            out_ref[:, start:filled] = right[...]
+        else:
+            out_ref[:, start:filled] = lax.dot_general(
+                lefts[which],
+                right[...],
+                (((0,), (0,)), ((), ())),
+                preferred_element_type=jnp.float32,
+            ).astype(jnp.bfloat16)
         if filled < stop:
             out_ref[:, filled:stop] = jnp.zeros((out_ref.shape[0], stop - filled), jnp.bfloat16)
-    put(up[...], activated, starts[5])
-
-
-def weight_grads(starts, lefts, rights, gains):
+
+
+def weight_grads(lefts, rights, choice):
     tokens, features = lefts[0].shape
     block = 256
-    left = pl.BlockSpec((tokens, block), lambda i: (0, i))
-
-    def whole(values):
-        return pl.BlockSpec(values.shape, lambda i: (0, 0), pipeline_mode=pl.Buffered(1))
-
-    total = starts[5] + rights[4].shape[1]
-    d_projected, attended, d_inner, d_gate, activated = rights
+    starts, total = [], 0
+    for right in rights:
+        total = padded_width(total)
+        starts.append(total)
+        total += right.shape[1]
+    specs = [pl.BlockSpec((tokens, block), lambda i: (0, i))] * len(lefts)
+    for right, which in zip(rights, choice):
+        if which is None:
+            specs.append(pl.BlockSpec((block, right.shape[1]), lambda i: (i, 0)))
+        else:
+            specs.append(
+                pl.BlockSpec(right.shape, lambda i: (0, 0), pipeline_mode=pl.Buffered(1))
+            )
     return pl.pallas_call(
-        functools.partial(weight_grad_kernel, starts),
+        functools.partial(weight_grad_kernel, choice, tuple(starts), total, len(lefts)),
         out_shape=jax.ShapeDtypeStruct((features, total), jnp.bfloat16),
         grid=(features // block,),
-        in_specs=[left] * 4
-        + [
-            whole(d_projected),
-            whole(attended),
-            pl.BlockSpec((block, gains.shape[1]), lambda i: (i, 0)),
-            whole(d_inner),
-            whole(d_gate),
-            whole(activated),
-        ],
+        in_specs=specs,
         out_specs=pl.BlockSpec((block, total), lambda i: (i, 0)),
         compiler_params=pltpu.CompilerParams(vmem_limit_bytes=kernel_vmem),
         cost_estimate=pl.CostEstimate(
             flops=2 * tokens * features * total,
-            bytes_accessed=2 * (4 * tokens * features + (tokens + features) * total),
+            bytes_accessed=2 * (len(lefts) * tokens * features + (tokens + features) * total),
             transcendentals=0,
         ),
-    )(*lefts, d_projected, attended, gains, d_inner, d_gate, activated)
+    )(*lefts, *rights)
 
 
 def product(left, right, contract):
@@ -417,13 +483,14 @@
     return (output, kept)
 
 
-def backward_layer(upstream, weights, tables, kept, is_local, starts):
+def backward_layer(upstream, weights, tables, kept, is_local, scatter):
     w_qkv, w_out, w_inner, w_gate, w_down, gain_pair = weights
     residual, middle, lowered, lowered_two, projected, attended, inner, gate_part, activated = kept
     up_low = upstream.astype(jnp.bfloat16)
     d_activated = product(up_low, w_down, (1, 0))
     unused, pullback = jax.vjp(gelu_gate, inner, gate_part)
     d_inner, d_gate = [v.astype(jnp.bfloat16) for v in pullback(d_activated)]
+    hidden_grads = weight_grads((lowered_two, up_low), (d_inner, d_gate, activated), (0, 0, 1))
     d_normed_two = core_total(
         product(d_inner, w_inner, (1, 1)) + product(d_gate, w_gate, (1, 1))
     )
@@ -432,18 +499,17 @@
     d_middle = upstream + d_mid_norm
     d_branch = d_middle.astype(jnp.bfloat16)
     d_attended = product(d_branch, w_out, (1, 0)).astype(jnp.bfloat16)
+    d_attended, hidden_grads = lax.optimization_barrier((d_attended, hidden_grads))
+    hidden_grads = scatter(hidden_grads)
     d_projected = attend_backward(projected, tables, d_attended, is_local)
     d_normed = core_total(product(d_projected, w_qkv, (1, 1)))
     unused, pullback = jax.vjp(layer_norm, residual, gain_pair[0])
     d_in_norm, d_gain_one = pullback(d_normed)
     gains = widen(jnp.stack([d_gain_one, d_gain_two], axis=1)).astype(jnp.bfloat16)
-    packed = weight_grads(
-        starts,
-        (lowered, d_branch, lowered_two, up_low),
-        (d_projected, attended, d_inner, d_gate, activated),
-        gains,
-    )
-    return (d_middle + d_in_norm, packed)
+    head_grads = scatter(
+        weight_grads((lowered, d_branch), (d_projected, attended, gains), (0, 1, None))
+    )
+    return (d_middle + d_in_norm, (head_grads, hidden_grads))
 
 
 def adam_update(weight, moment, square, gradient, step_rate, decay_here):
@@ -472,20 +538,38 @@
     hidden = masters[2].shape[3]
     local_tables = rotary_tables(theta_local)
     global_tables = rotary_tables(theta_global)
-    shards = [role_swap(pack_shards(masters, layer), chips) for layer in range(2)]
-    hidden_in, shards = lax.optimization_barrier((hidden_in, shards))
-    weights = [unpack_weights(gather_rows(s, chips), starts, hidden) for s in shards]
+    packed = [pack_shards(masters, layer) for layer in range(2)]
+    heads_part = role_swap(packed[0][:, : starts[3]], chips)
+    hidden_part = role_swap(packed[0][:, starts[3] :], chips)
+    second = role_swap(packed[1], chips)
+    hidden_in, heads_part, hidden_part, second = lax.optimization_barrier(
+        (hidden_in, heads_part, hidden_part, second)
+    )
+    first = [gather_quick(part, chips) for part in (heads_part, hidden_part)]
+    weights = [
+        unpack_weights(first[0], first[1], starts, hidden),
+        unpack_weights(*split_packed(gather_rows(second, chips), starts), starts, hidden),
+    ]
     inputs = chip_sequence(hidden_in)
     upstream = chip_sequence(cotangent)
     middle, kept_first = forward_layer(inputs, weights[0], local_tables, True)
     output, kept_second = forward_layer(middle, weights[1], global_tables, False)
     final_out = own_sequence(output.astype(jnp.bfloat16))
-    d_middle, packed = backward_layer(
-        upstream, weights[1], global_tables, kept_second, False, starts
-    )
-    grads_second = unpack_grads(scatter_rows(packed, chips), starts, hidden)
-    d_values, packed = backward_layer(d_middle, weights[0], local_tables, kept_first, True, starts)
-    grads_first = unpack_grads(scatter_rows(packed, chips), starts, hidden)
+    by_call = functools.partial(scatter_rows, chips=chips)
+    by_steps = functools.partial(scatter_quick, chips=chips)
+    d_middle, shards_second = backward_layer(
+        upstream, weights[1], global_tables, kept_second, False, by_call
+    )
+    d_values, shards_first = backward_layer(
+        d_middle, weights[0], local_tables, kept_first, True, by_steps
+    )
+    shards_first = role_swap(jnp.concatenate(shards_first, axis=1), chips)
+    shards_first, shards_second = lax.optimization_barrier((shards_first, shards_second))
+    shards_second = role_swap(jnp.concatenate(shards_second, axis=1), chips)
+    grads_first, grads_second = [
+        unpack_grads(packed.astype(jnp.float32), starts, hidden)
+        for packed in (shards_first, shards_second)
+    ]
     final_grad = own_sequence(d_values.astype(jnp.bfloat16)).astype(jnp.float32)
     rates = (rate_qkv, rate_out, rate_inp, rate_down, rate_gain)
     results = [final_out, final_grad]

time: 1230 us -> 957 us (0.78)
  waiting for transfers between devices: 734 us -> 420 us
  starting transfers between devices: 19.7 us -> 46.5 us
  other arithmetic: 82 us -> 103 us
  matrix products: 140 us -> 127 us
    reduce_scatter x2, waiting for transfers between devices: 430 us -> 0.01 us  [scatter_rows(): lax.psum_scatter(gradient, chip_axes, scatter_dimension=0, tiled=True)]
    ppermute x0 -> x24, waiting for transfers between devices: none -> 383 us  [the longest x8 237 us: bit_swap(): return lax.ppermute(values, 'tensor', [(0, 1), (1, 0)])]
    all_gather x2 -> x1, waiting for transfers between devices: 239 us -> 0.02 us  [gather_rows(): return lax.all_gather(shard, chip_axes, axis=0, tiled=True)]
    ppermute x0 -> x24, starting transfers between devices: none -> 18.9 us  [the longest x16 9.87 us: bit_swap(): lax.ppermute(values, 'chip', [(chip, chip ^ 1 << bit) for chip in range(c...]
    ppermute x4 -> x5, waiting for transfers between devices: 41.1 us -> 26.5 us  [role_swap(): return lax.ppermute(values, every_axis, swap_pairs(chips))]
    dot_general x20, matrix products: 140 us -> 127 us  [product(): lax.dot_general(left, right, ((contract[:1], contract[1:]), ((), ())), pr...]
    pallas_call x2 -> x4, Pallas kernels: 44 us -> 49.2 us  [weight_grads(): pl.pallas_call(functools.partial(weight_grad_kernel, choice, tuple(starts...]
    unnamed x205 -> x214, local copies, waits for them, and re-layouts: 30.3 us -> 31.2 us
  transfers between devices with their start and end apart: 20 -> 44, of which waited for: 15 -> 23; matrix products, arithmetic and copies ran while one was open for 11% -> 17% of each run, Pallas kernels for 9% -> 13%
where the time goes in v4:
time: 957 us; the launch traced here: 952 us
  waiting for transfers between devices  420 us (44%)
  Pallas kernels  188 us (20%)
  matrix products  127 us (13%)
  other arithmetic  103 us (11%)
  local copies, waits for them, and re-layouts  51.8 us (5%)
  starting transfers between devices  46.5 us (5%)
  between operations  16.3 us (2%)
    ppermute x8, waiting for transfers between devices, bit_swap(): return lax.ppermute(values, 'tensor', [(0, 1), (1, 0)])  237 us
    ppermute x16, waiting for transfers between devices, bit_swap(): lax.ppermute(values, 'chip', [(chip, chip ^ 1 << bit) for chip in range(c...  146 us
    dot_general x20, matrix products, product(): lax.dot_general(left, right, ((contract[:1], contract[1:]), ((), ())), pr...  127 us
    pallas_call x2, Pallas kernels, attend_backward(): pl.pallas_call(functools.partial(attend_back_kernel, is_local, 128), out_...  84.7 us
    pallas_call x2, Pallas kernels, attend_forward(): pl.pallas_call(functools.partial(attend_kernel, is_local, 128), out_shape...  53.8 us
    pallas_call x4, Pallas kernels, weight_grads(): pl.pallas_call(functools.partial(weight_grad_kernel, choice, tuple(starts...  49.2 us
    unnamed x214, local copies, waits for them, and re-layouts  31.2 us
    ppermute x5, waiting for transfers between devices, role_swap(): return lax.ppermute(values, every_axis, swap_pairs(chips))  26.5 us
  transfers between devices with their start and end apart: 44, of which 23 were waited for; matrix products, arithmetic and copies ran while one was open for 17% of the time, Pallas kernels for 13%

profile of v4, /device:TPU:1, one launch (start us, length us, event | category | flops | bytes accessed | tf_op | source)
XLA Modules:
  0.0 952.5 jit_solution(10140036897781831112)
XLA Ops:
  25.6 13.1 %collective-permute-done = bf16[64,2176]{1,0:T(8,128)(2,1)S(1)} collective-permute-done((bf16[64,2176]{1,0:T(8,128)(2,1)S(1)}, bf16[64,2176]{1,0:T(8,128)(2,1)S(1)}, u32[]{:S(2)}, u32[]{:S(2)}) %collective-permute-start) | collective-permute-done | bytes 278560 | tf_op jit(solution)/shard_map/ppermute | solution.py:49
  53.5 12.9 %collective-permute-done.11 = bf16[64,4128]{1,0:T(8,128)(2,1)} collective-permute-done((bf16[64,4128]{1,0:T(8,128)(2,1)}, bf16[64,4128]{1,0:T(8,128)(2,1)}, u32[]{:S(2)}, u32[]{:S(2)}) %collective-permute-start.11) | collective-permute-done | bytes 528416 | tf_op jit(solution)/shard_map/ppermute | solution.py:89
  67.7 20.5 %collective-permute-done.5 = bf16[2,64,2176]{2,1,0:T(8,128)(2,1)S(1)} collective-permute-done((bf16[2,64,2176]{2,1,0:T(8,128)(2,1)S(1)}, bf16[2,64,2176]{2,1,0:T(8,128)(2,1)S(1)}, u32[]{:S(2)}, u32[]{:S(2)}) %collective-permute-start.5) | collective-permute-done | bytes 557088 | tf_op jit(solution)/shard_map/ppermute | solution.py:89
  89.8 7.0 collective-permute-done.8
  97.2 14.1 %collective-permute-done.6 = bf16[2,2,64,1152]{3,2,0,1:T(8,128)(2,1)S(1)} collective-permute-done((bf16[2,2,64,1152]{3,2,0,1:T(8,128)(2,1)S(1)}, bf16[2,2,64,1152]{3,2,0,1:T(8,128)(2,1)S(1)}, u32[]{:S(2)}, u32[]{:S(2)}) %collective-permute-start.6) | collective-permute-done | bytes 589856 | tf_op jit(solution)/shard_map/ppermute | solution.py:88
  111.9 33.9 %collective-permute-done.12 = bf16[2,64,4128]{2,1,0:T(8,128)(2,1)S(1)} collective-permute-done((bf16[2,64,4128]{2,1,0:T(8,128)(2,1)S(1)}, bf16[2,64,4128]{2,1,0:T(8,128)(2,1)S(1)}, u32[]{:S(2)}, u32[]{:S(2)}) %collective-permute-start.12) | collective-permute-done | bytes 1056800 | tf_op jit(solution)/shard_map/ppermute | solution.py:89
  163.8 19.5 %shard_map.296.refs_3_ = bf16[1024,512]{1,0:T(8,128)(2,1)S(1)} custom-call(f32[1024,1536]{1,0:T(8,128)} %fusion.73.raw_ref, f32[1024,128]{1,0:T(8,128)S(1)} %get-tuple-element.237.cos_ref, f32[1024,128]{1,0:T(8,128)S(1)} %get-tuple-element.238.sin_ref), custom_call_target="tpu_custom_call" | custom-call | flops 2147483648 | bytes 12582912 | tf_op jit(solution)/shard_map/pallas_call | solution.py:378
  186.8 6.8 collective-permute-done.13
  201.0 65.7 %collective-permute-done.14 = bf16[2,2,2,64,2048]{4,3,0,1,2:T(8,128)(2,1)S(1)} collective-permute-done((bf16[2,2,2,64,2048]{4,3,0,1,2:T(8,128)(2,1)S(1)}, bf16[2,2,2,64,2048]{4,3,0,1,2:T(8,128)(2,1)S(1)}, u32[]{:S(2)}, u32[]{:S(2)}) %collective-permute-start.14) | collective-permute-done | bytes 2097184 | tf_op jit(solution)/shard_map/ppermute | solution.py:88
  273.8 18.8 %multiply_convert_fusion.3 = (bf16[1024,1312]{1,0:T(8,128)(2,1)S(1)}, f32[1024,1312]{1,0:T(8,128)}, f32[1024,1312]{1,0:T(8,128)}) fusion(f32[1024,1312]{1,0:T(8,128)S(1)} %fusion.51, bf16[1024,1024]{1,0:T(8,128)(2,1)S(1)} %multiply_convert_fusion.6.refs_0_, bf16[1024,2080]{1,0:T(8,128)(2,1)S(1)} %bitcast.252, bf16[1024,2048]{1,0:T(8,128)(2,1)S(1)} %bitcast.259), kind=kOutput, calls=%fused_computation.32 | convolution fusion | flops 2845507584 | bytes 29360128 | tf_op jit(solution)/shard_map/dot_general | solution.py:466
  313.9 7.9 fusion.30.raw_ref
  321.8 34.3 %shard_map.297.refs_3_ = bf16[1024,512]{1,0:T(8,128)(2,1)S(1)} custom-call(f32[1024,1536]{1,0:T(8,128)} %fusion.30.raw_ref, f32[1024,128]{1,0:T(8,128)S(1)} %get-tuple-element.239.cos_ref, f32[1024,128]{1,0:T(8,128)S(1)} %get-tuple-element.240.sin_ref), custom_call_target="tpu_custom_call" | custom-call | flops 8589934592 | bytes 12582912 | tf_op jit(solution)/shard_map/pallas_call | solution.py:378
  376.5 21.1 %add_convert_fusion.1 = (bf16[1024,1312]{1,0:T(8,128)(2,1)}, f32[1024,1312]{1,0:T(8,128)}, f32[1024,1312]{1,0:T(8,128)}) fusion(f32[1024,1312]{1,0:T(8,128)S(1)} %fusion.39, f32[1024,1312]{1,0:T(8,128)S(1)} %fusion.43, bf16[1024,1024]{1,0:T(8,128)(2,1)S(1)} %broadcast_select_fusion.refs_1_, bf16[1024,6304]{1,0:T(8,128)(2,1)} %all-gather.2.cloned.1.call-done), kind=kOutput, calls=%fused_computation.18 | convolution fusion | flops 2849538048 | bytes 29163520 | tf_op jit(solution)/shard_map/dot_general | solution.py:466
  402.8 7.4 fusion.37
  410.2 6.5 add_convert_fusion.4
  417.1 6.4 fusion.61
  423.7 16.0 %shard_map.298 = bf16[1024,4128]{1,0:T(8,128)(2,1)} custom-call(bf16[1024,1024]{1,0:T(8,128)(2,1)S(1)} %multiply_convert_fusion.4.refs_0_, bf16[1024,1024]{1,0:T(8,128)(2,1)S(1)} %broadcast_select_fusion.refs_1_, bf16[1024,1312]{1,0:T(8,128)(2,1)} %get-tuple-element.159.refs_2_, bf16[1024,1312]{1,0:T(8,128)(2,1)} %copy-done.46, bf16[1024,1312]{1,0:T(8,128)(2,1)} %copy-done.47), custom_call_target="tpu_custom_call" | custom-call | flops 8657043456 | bytes 21102592 | tf_op jit(solution)/shard_map/pallas_call | solution.py:450
  456.5 55.0 %shard_map.299.refs_2_ = bf16[1024,1536]{1,0:T(8,128)(2,1)S(1)} custom-call(f32[1024,1536]{1,0:T(8,128)} %fusion.30.raw_ref, f32[1024,128]{1,0:T(8,128)S(1)} %get-tuple-element.239.cos_ref, f32[1024,128]{1,0:T(8,128)S(1)} %get-tuple-element.240.sin_ref, bf16[1024,512]{1,0:T(8,128)(2,1)S(1)} %convolution_convert_fusion.4.up_ref), custom_call_target="tpu_custom_call" | custom-call | flops 21474836480 | bytes 12582912 | tf_op jit(solution)/shard_map/pallas_call | solution.py:398
  511.6 6.7 fusion.64
  528.3 8.5 shard_map.303
  545.2 9.2 add_convert_fusion
  562.2 16.3 %shard_map.300 = bf16[1024,4128]{1,0:T(8,128)(2,1)} custom-call(bf16[1024,1024]{1,0:T(8,128)(2,1)S(1)} %copy-done.7, bf16[1024,1024]{1,0:T(8,128)(2,1)S(1)} %get-tuple-element.153.refs_1_, bf16[1024,1312]{1,0:T(8,128)(2,1)} %copy-done.97, bf16[1024,1312]{1,0:T(8,128)(2,1)} %copy-done.95, bf16[1024,1312]{1,0:T(8,128)(2,1)} %copy-done.98), custom_call_target="tpu_custom_call" | custom-call | flops 8657043456 | bytes 21102592 | tf_op jit(solution)/shard_map/pallas_call | solution.py:450
  587.4 29.7 %shard_map.301.refs_2_ = bf16[1024,1536]{1,0:T(8,128)(2,1)S(1)} custom-call(f32[1024,1536]{1,0:T(8,128)} %fusion.73.raw_ref, f32[1024,128]{1,0:T(8,128)S(1)} %copy-done.1, f32[1024,128]{1,0:T(8,128)S(1)} %copy-done.3, bf16[1024,512]{1,0:T(8,128)(2,1)S(1)} %convolution_convert_fusion.3.up_ref), custom_call_target="tpu_custom_call" | custom-call | flops 5368709120 | bytes 12582912 | tf_op jit(solution)/shard_map/pallas_call | solution.py:398
  646.1 8.5 shard_map.302
  658.2 82.8 %collective-permute-done.33 = bf16[2,2,2,64,2048]{4,3,0,1,2:T(8,128)(2,1)} collective-permute-done((bf16[2,2,2,64,2048]{4,3,0,1,2:T(8,128)(2,1)}, bf16[2,2,2,64,2048]{4,3,0,1,2:T(8,128)(2,1)}, u32[]{:S(2)}, u32[]{:S(2)}) %collective-permute-start.33) | collective-permute-done | bytes 2097184 | tf_op jit(solution)/shard_map/ppermute | solution.py:88
  752.3 14.0 %collective-permute-done.27 = bf16[2,2,2,64,1024]{4,3,0,1,2:T(8,128)(2,1)S(1)} collective-permute-done((bf16[2,2,2,64,1024]{4,3,0,1,2:T(8,128)(2,1)S(1)}, bf16[2,2,2,64,1024]{4,3,0,1,2:T(8,128)(2,1)S(1)}, u32[]{:S(2)}, u32[]{:S(2)}) %collective-permute-start.27) | collective-permute-done | bytes 1048608 | tf_op jit(solution)/shard_map/ppermute | solution.py:88
  773.2 17.7 %collective-permute-done.36 = bf16[2,2,64,2080]{3,2,0,1:T(8,128)(2,1)S(1)} collective-permute-done((bf16[2,2,64,2080]{3,2,0,1:T(8,128)(2,1)S(1)}, bf16[2,2,64,2080]{3,2,0,1:T(8,128)(2,1)S(1)}, u32[]{:S(2)}, u32[]{:S(2)}) %collective-permute-start.36) | collective-permute-done | bytes 1064992 | tf_op jit(solution)/shard_map/ppermute | solution.py:88
  794.0 43.0 %collective-permute-done.30 = bf16[2,2,64,1152]{3,2,0,1:T(8,128)(2,1)S(1)} collective-permute-done((bf16[2,2,64,1152]{3,2,0,1:T(8,128)(2,1)S(1)}, bf16[2,2,64,1152]{3,2,0,1:T(8,128)(2,1)S(1)}, u32[]{:S(2)}, u32[]{:S(2)}) %collective-permute-start.30) | collective-permute-done | bytes 589856 | tf_op jit(solution)/shard_map/ppermute | solution.py:88
  837.7 18.3 %collective-permute-done.31 = bf16[2,64,2176]{2,1,0:T(8,128)(2,1)S(1)} collective-permute-done((bf16[2,64,2176]{2,1,0:T(8,128)(2,1)S(1)}, bf16[2,64,2176]{2,1,0:T(8,128)(2,1)S(1)}, u32[]{:S(2)}, u32[]{:S(2)}) %collective-permute-start.31) | collective-permute-done | bytes 557088 | tf_op jit(solution)/shard_map/ppermute | solution.py:89
  858.6 24.5 %collective-permute-done.32 = bf16[64,2176]{1,0:T(8,128)(2,1)S(1)} collective-permute-done((bf16[64,2176]{1,0:T(8,128)(2,1)S(1)}, bf16[64,2176]{1,0:T(8,128)(2,1)S(1)}, u32[]{:S(2)}, u32[]{:S(2)}) %collective-permute-start.32) | collective-permute-done | bytes 278560 | tf_op jit(solution)/shard_map/ppermute | solution.py:89
  883.2 11.5 %collective-permute-done.38 = bf16[64,4128]{1,0:T(8,128)(2,1)S(1)} collective-permute-done((bf16[64,4128]{1,0:T(8,128)(2,1)S(1)}, bf16[64,4128]{1,0:T(8,128)(2,1)S(1)}, u32[]{:S(2)}, u32[]{:S(2)}) %collective-permute-start.38) | collective-permute-done | bytes 528416 | tf_op jit(solution)/shard_map/ppermute | solution.py:89
  916.1 8.6 collective-permute-done.40
  (481 shorter events, 269.8 us)
Async XLA Ops:
  7.2 301.8 %all-gather.2.cloned.1.call-start = ((), (), s32[]{:S(2)}) async-start(), calls=%async_computation.2 | async-start | bytes 13926400 | tf_op jit(solution)/shard_map/all_gather | solution.py:153
  14.8 23.9 %collective-permute-start.2 = (bf16[64,6304]{1,0:T(8,128)(2,1)}, bf16[64,6304]{1,0:T(8,128)(2,1)S(1)}, u32[]{:S(2)}, u32[]{:S(2)}) collective-permute-start(bf16[64,6304]{1,0:T(8,128)(2,1)} %fusion.103), channel_id=1, source_target_pairs={{0,0},{1,2},{2,1},{3,3},{4,4},{5,6},{6,5},{7,7},{8,8},{9,10},{10,9... | collective-permute-start | bytes 2420744 | tf_op jit(solution)/shard_map/ppermute | solution.py:49
  19.4 19.3 %collective-permute-start.1 = (bf16[64,4128]{1,0:T(8,128)(2,1)S(1)}, bf16[64,4128]{1,0:T(8,128)(2,1)}, u32[]{:S(2)}, u32[]{:S(2)}) collective-permute-start(bf16[64,4128]{1,0:T(8,128)(2,1)S(1)} %fusion.100), channel_id=1, source_target_pairs={{0,0},{1,2},{2,1},{3,3},{4,4},{5,6},{6,5},{7,7},{8,8},{9,10},{10,9... | collective-permute-start | bytes 1585160 | tf_op jit(solution)/shard_map/ppermute | solution.py:49
  47.5 18.9 %collective-permute-start.11 = (bf16[64,4128]{1,0:T(8,128)(2,1)}, bf16[64,4128]{1,0:T(8,128)(2,1)}, u32[]{:S(2)}, u32[]{:S(2)}) collective-permute-start(bf16[64,4128]{1,0:T(8,128)(2,1)} %collective-permute-done.1), channel_id=1, source_target_pairs={{0,16},{4,20},{8,24},{12,28},{16,0},{20,4},{24,8},{28,12},{1,17},{... | collective-permute-start | bytes 1585160 | tf_op jit(solution)/shard_map/ppermute | solution.py:89
  48.0 105.9 %collective-permute-start.3 = (bf16[1024,1024]{1,0:T(8,128)(2,1)}, bf16[1024,1024]{1,0:T(8,128)(2,1)S(1)}, u32[]{:S(2)}, u32[]{:S(2)}) collective-permute-start(bf16[1024,1024]{1,0:T(8,128)(2,1)} %param.17), channel_id=1, source_target_pairs={{0,2},{2,0},{1,3},{3,1},{4,6},{6,4},{5,7},{7,5},{8,10},{10,8},{9,1... | collective-permute-start | bytes 6291464 | tf_op jit(solution)/shard_map/ppermute | solution.py:53
  48.0 860.5 %reduce-scatter.3.cloned.1.call-start = ((), (), s32[]{:S(2)}) async-start(), calls=%async_computation.3 | async-start | bytes 4734976 | tf_op jit(solution)/shard_map/reduce_scatter | solution.py:157
  53.4 34.8 %collective-permute-start.5 = (bf16[2,64,2176]{2,1,0:T(8,128)(2,1)S(1)}, bf16[2,64,2176]{2,1,0:T(8,128)(2,1)S(1)}, u32[]{:S(2)}, u32[]{:S(2)}) collective-permute-start(bf16[2,64,2176]{2,1,0:T(8,128)(2,1)S(1)} %pad_maximum_fusion.19), channel_id=1, source_target_pairs={{0,8},{4,12},{8,0},{12,4},{16,24},{20,28},{24,16},{28,20},{1,9},{5... | collective-permute-start | bytes 1671176 | tf_op jit(solution)/shard_map/ppermute | solution.py:89
  89.5 21.8 %collective-permute-start.6 = (bf16[2,2,64,1152]{3,2,0,1:T(8,128)(2,1)S(1)}, bf16[2,2,64,1152]{3,2,0,1:T(8,128)(2,1)S(1)}, u32[]{:S(2)}, u32[]{:S(2)}) collective-permute-start(bf16[2,2,64,1152]{3,2,0,1:T(8,128)(2,1)S(1)} %fusion.92), channel_id=1, source_target_pairs={{0,1},{1,0},{2,3},{3,2},{4,5},{5,4},{6,7},{7,6},{8,9},{9,8},{10,11... | collective-permute-start | bytes 1769480 | tf_op jit(solution)/shard_map/ppermute | solution.py:88
  89.7 56.1 %collective-permute-start.12 = (bf16[2,64,4128]{2,1,0:T(8,128)(2,1)S(1)}, bf16[2,64,4128]{2,1,0:T(8,128)(2,1)S(1)}, u32[]{:S(2)}, u32[]{:S(2)}) collective-permute-start(bf16[2,64,4128]{2,1,0:T(8,128)(2,1)S(1)} %pad_maximum_fusion.13), channel_id=1, source_target_pairs={{0,8},{4,12},{8,0},{12,4},{16,24},{20,28},{24,16},{28,20},{1,9},{5... | collective-permute-start | bytes 3170312 | tf_op jit(solution)/shard_map/ppermute | solution.py:89
  97.1 58.3 %collective-permute-start.9 = (bf16[2,2,2,64,1024]{4,3,0,1,2:T(8,128)(2,1)S(1)}, bf16[2,2,2,64,1024]{4,3,0,1,2:T(8,128)(2,1)S(1)}, u32[]{:S(2)}, u32[]{:S(2)}) collective-permute-start(bf16[2,2,2,64,1024]{4,3,0,1,2:T(8,128)(2,1)S(1)} %pad_maximum_fusion.15), channel_id=1, source_target_pairs={{0,1},{1,0},{2,3},{3,2},{4,5},{5,4},{6,7},{7,6},{8,9},{9,8},{10,11... | collective-permute-start | bytes 3145736 | tf_op jit(solution)/shard_map/ppermute | solution.py:88
  111.6 44.6 %collective-permute-start.7 = (bf16[2,2,2,64,1152]{4,3,0,1,2:T(8,128)(2,1)S(1)}, bf16[2,2,2,64,1152]{4,3,0,1,2:T(8,128)(2,1)S(1)}, u32[]{:S(2)}, u32[]{:S(2)}) collective-permute-start(bf16[2,2,2,64,1152]{4,3,0,1,2:T(8,128)(2,1)S(1)} %pad_maximum_fusion.11), channel_id=1, source_target_pairs={{0,4},{4,0},{8,12},{12,8},{16,20},{20,16},{24,28},{28,24},{1,5},{5... | collective-permute-start | bytes 3538952 | tf_op jit(solution)/shard_map/ppermute | solution.py:89
  147.2 48.4 %collective-permute-start.15 = (bf16[2,2,64,2080]{3,2,0,1:T(8,128)(2,1)}, bf16[2,2,64,2080]{3,2,0,1:T(8,128)(2,1)}, u32[]{:S(2)}, u32[]{:S(2)}) collective-permute-start(bf16[2,2,64,2080]{3,2,0,1:T(8,128)(2,1)} %pad_maximum_fusion.12), channel_id=1, source_target_pairs={{0,1},{1,0},{2,3},{3,2},{4,5},{5,4},{6,7},{7,6},{8,9},{9,8},{10,11... | collective-permute-start | bytes 3194888 | tf_op jit(solution)/shard_map/ppermute | solution.py:88
  153.4 40.2 %collective-permute-start.13 = (bf16[2,2,64,2048]{3,2,0,1:T(8,128)(2,1)}, bf16[2,2,64,2048]{3,2,0,1:T(8,128)(2,1)}, u32[]{:S(2)}, u32[]{:S(2)}) collective-permute-start(bf16[2,2,64,2048]{3,2,0,1:T(8,128)(2,1)} %pad_maximum_fusion.14), channel_id=1, source_target_pairs={{0,4},{4,0},{8,12},{12,8},{16,20},{20,16},{24,28},{28,24},{1,5},{5... | collective-permute-start | bytes 3145736 | tf_op jit(solution)/shard_map/ppermute | solution.py:89
  195.5 71.2 %collective-permute-start.14 = (bf16[2,2,2,64,2048]{4,3,0,1,2:T(8,128)(2,1)S(1)}, bf16[2,2,2,64,2048]{4,3,0,1,2:T(8,128)(2,1)S(1)}, u32[]{:S(2)}, u32[]{:S(2)}) collective-permute-start(bf16[2,2,2,64,2048]{4,3,0,1,2:T(8,128)(2,1)S(1)} %pad_maximum_fusion.7), channel_id=1, source_target_pairs={{0,1},{1,0},{2,3},{3,2},{4,5},{5,4},{6,7},{7,6},{8,9},{9,8},{10,11... | collective-permute-start | bytes 6291464 | tf_op jit(solution)/shard_map/ppermute | solution.py:88
  197.5 73.9 %collective-permute-start.16 = (bf16[2,2,2,64,2080]{4,3,0,1,2:T(8,128)(2,1)S(1)}, bf16[2,2,2,64,2080]{4,3,0,1,2:T(8,128)(2,1)S(1)}, u32[]{:S(2)}, u32[]{:S(2)}) collective-permute-start(bf16[2,2,2,64,2080]{4,3,0,1,2:T(8,128)(2,1)S(1)} %pad_maximum_fusion.5), channel_id=1, source_target_pairs={{0,4},{4,0},{8,12},{12,8},{16,20},{20,16},{24,28},{28,24},{1,5},{5... | collective-permute-start | bytes 6389768 | tf_op jit(solution)/shard_map/ppermute | solution.py:89
  299.8 59.7 %collective-permute-start.21 = (bf16[1024,1024]{1,0:T(8,128)(2,1)S(1)}, bf16[1024,1024]{1,0:T(8,128)(2,1)}, u32[]{:S(2)}, u32[]{:S(2)}) collective-permute-start(bf16[1024,1024]{1,0:T(8,128)(2,1)S(1)} %copy-done.50), channel_id=1, source_target_pairs={{0,2},{2,0},{1,3},{3,1},{4,6},{6,4},{5,7},{7,5},{8,10},{10,8},{9,1... | collective-permute-start | bytes 6291464 | tf_op jit(solution)/shard_map/ppermute | solution.py:53
  416.7 22.9 %collective-permute-start.22 = (bf16[1024,1024]{1,0:T(8,128)(2,1)}, bf16[1024,1024]{1,0:T(8,128)(2,1)}, u32[]{:S(2)}, u32[]{:S(2)}) collective-permute-start(bf16[1024,1024]{1,0:T(8,128)(2,1)} %add_convert_fusion.4), channel_id=1, source_target_pairs={{0,2},{2,0},{1,3},{3,1},{4,6},{6,4},{5,7},{7,5},{8,10},{10,8},{9,1... | collective-permute-start | bytes 6291464 | tf_op jit(solution)/shard_map/ppermute | solution.py:53
  423.5 21.2 %collective-permute-start.19 = (bf16[1024,1024]{1,0:T(8,128)(2,1)}, bf16[1024,1024]{1,0:T(8,128)(2,1)}, u32[]{:S(2)}, u32[]{:S(2)}) collective-permute-start(bf16[1024,1024]{1,0:T(8,128)(2,1)} %fusion.61), channel_id=1, source_target_pairs={{0,2},{2,0},{1,3},{3,1},{4,6},{6,4},{5,7},{7,5},{8,10},{10,8},{9,1... | collective-permute-start | bytes 6291464 | tf_op jit(solution)/shard_map/ppermute | solution.py:53
  536.8 371.8 %reduce-scatter.5.cloned.1.call-start = ((), (), s32[]{:S(2)}) async-start(), calls=%async_computation.4 | async-start | bytes 9191424 | tf_op jit(solution)/shard_map/reduce_scatter | solution.py:157
  621.9 276.5 %collective-permute-start.20 = (bf16[1024,1024]{1,0:T(8,128)(2,1)}, bf16[1024,1024]{1,0:T(8,128)(2,1)}, u32[]{:S(2)}, u32[]{:S(2)}) collective-permute-start(bf16[1024,1024]{1,0:T(8,128)(2,1)} %get-tuple-element.181), channel_id=1, source_target_pairs={{0,1},{3,2},{4,5},{7,6},{8,9},{11,10},{12,13},{15,14},{16,17},{19,... | collective-permute-start | bytes 6291464 | tf_op jit(solution)/shard_map/ppermute | solution.py:535
  628.7 112.3 %collective-permute-start.33 = (bf16[2,2,2,64,2048]{4,3,0,1,2:T(8,128)(2,1)}, bf16[2,2,2,64,2048]{4,3,0,1,2:T(8,128)(2,1)}, u32[]{:S(2)}, u32[]{:S(2)}) collective-permute-start(bf16[2,2,2,64,2048]{4,3,0,1,2:T(8,128)(2,1)} %bitcast.243), channel_id=1, source_target_pairs={{0,1},{1,0},{2,3},{3,2},{4,5},{5,4},{6,7},{7,6},{8,9},{9,8},{10,11... | collective-permute-start | bytes 6291464 | tf_op jit(solution)/shard_map/ppermute | solution.py:88
  635.3 108.4 %collective-permute-start.35 = (bf16[2,2,2,64,2080]{4,3,0,1,2:T(8,128)(2,1)}, bf16[2,2,2,64,2080]{4,3,0,1,2:T(8,128)(2,1)}, u32[]{:S(2)}, u32[]{:S(2)}) collective-permute-start(bf16[2,2,2,64,2080]{4,3,0,1,2:T(8,128)(2,1)} %bitcast.242), channel_id=1, source_target_pairs={{0,4},{4,0},{8,12},{12,8},{16,20},{20,16},{24,28},{28,24},{1,5},{5... | collective-permute-start | bytes 6389768 | tf_op jit(solution)/shard_map/ppermute | solution.py:89
  656.7 109.5 %collective-permute-start.27 = (bf16[2,2,2,64,1024]{4,3,0,1,2:T(8,128)(2,1)S(1)}, bf16[2,2,2,64,1024]{4,3,0,1,2:T(8,128)(2,1)S(1)}, u32[]{:S(2)}, u32[]{:S(2)}) collective-permute-start(bf16[2,2,2,64,1024]{4,3,0,1,2:T(8,128)(2,1)S(1)} %bitcast.274), channel_id=1, source_target_pairs={{0,1},{1,0},{2,3},{3,2},{4,5},{5,4},{6,7},{7,6},{8,9},{9,8},{10,11... | collective-permute-start | bytes 3145736 | tf_op jit(solution)/shard_map/ppermute | solution.py:88
  657.6 133.6 %collective-permute-start.29 = (bf16[2,2,2,64,1152]{4,3,0,1,2:T(8,128)(2,1)S(1)}, bf16[2,2,2,64,1152]{4,3,0,1,2:T(8,128)(2,1)S(1)}, u32[]{:S(2)}, u32[]{:S(2)}) collective-permute-start(bf16[2,2,2,64,1152]{4,3,0,1,2:T(8,128)(2,1)S(1)} %bitcast.271), channel_id=1, source_target_pairs={{0,4},{4,0},{8,12},{12,8},{16,20},{20,16},{24,28},{28,24},{1,5},{5... | collective-permute-start | bytes 3538952 | tf_op jit(solution)/shard_map/ppermute | solution.py:89
  743.6 28.8 %collective-permute-start.34 = (bf16[2,2,64,2048]{3,2,0,1:T(8,128)(2,1)S(1)}, bf16[2,2,64,2048]{3,2,0,1:T(8,128)(2,1)S(1)}, u32[]{:S(2)}, u32[]{:S(2)}) collective-permute-start(bf16[2,2,64,2048]{3,2,0,1:T(8,128)(2,1)S(1)} %dynamic-slice_bitcast_fusion.1), channel_id=1, source_target_pairs={{0,4},{4,0},{8,12},{12,8},{16,20},{20,16},{24,28},{28,24},{1,5},{5... | collective-permute-start | bytes 3145736 | tf_op jit(solution)/shard_map/ppermute | solution.py:89
  746.3 44.6 %collective-permute-start.36 = (bf16[2,2,64,2080]{3,2,0,1:T(8,128)(2,1)S(1)}, bf16[2,2,64,2080]{3,2,0,1:T(8,128)(2,1)S(1)}, u32[]{:S(2)}, u32[]{:S(2)}) collective-permute-start(bf16[2,2,64,2080]{3,2,0,1:T(8,128)(2,1)S(1)} %dynamic-slice_bitcast_fusion), channel_id=1, source_target_pairs={{0,1},{1,0},{2,3},{3,2},{4,5},{5,4},{6,7},{7,6},{8,9},{9,8},{10,11... | collective-permute-start | bytes 3194888 | tf_op jit(solution)/shard_map/ppermute | solution.py:88
  766.2 135.3 %collective-permute-start.26 = (bf16[1024,1024]{1,0:T(8,128)(2,1)S(1)}, bf16[1024,1024]{1,0:T(8,128)(2,1)S(1)}, u32[]{:S(2)}, u32[]{:S(2)}) collective-permute-start(bf16[1024,1024]{1,0:T(8,128)(2,1)S(1)} %add_convert_fusion.2), channel_id=1, source_target_pairs={{0,1},{3,2},{4,5},{7,6},{8,9},{11,10},{12,13},{15,14},{16,17},{19,... | collective-permute-start | bytes 6291464 | tf_op jit(solution)/shard_map/ppermute | solution.py:535
  772.5 21.4 %collective-permute-start.28 = (bf16[2,2,64,1024]{3,2,0,1:T(8,128)(2,1)S(1)}, bf16[2,2,64,1024]{3,2,0,1:T(8,128)(2,1)S(1)}, u32[]{:S(2)}, u32[]{:S(2)}) collective-permute-start(bf16[2,2,64,1024]{3,2,0,1:T(8,128)(2,1)S(1)} %dynamic-slice_bitcast_fusion.4), channel_id=1, source_target_pairs={{0,4},{4,0},{8,12},{12,8},{16,20},{20,16},{24,28},{28,24},{1,5},{5... | collective-permute-start | bytes 1572872 | tf_op jit(solution)/shard_map/ppermute | solution.py:89
  791.6 45.5 %collective-permute-start.30 = (bf16[2,2,64,1152]{3,2,0,1:T(8,128)(2,1)S(1)}, bf16[2,2,64,1152]{3,2,0,1:T(8,128)(2,1)S(1)}, u32[]{:S(2)}, u32[]{:S(2)}) collective-permute-start(bf16[2,2,64,1152]{3,2,0,1:T(8,128)(2,1)S(1)} %dynamic-slice_bitcast_fusion.2), channel_id=1, source_target_pairs={{0,1},{1,0},{2,3},{3,2},{4,5},{5,4},{6,7},{7,6},{8,9},{9,8},{10,11... | collective-permute-start | bytes 1769480 | tf_op jit(solution)/shard_map/ppermute | solution.py:88
  791.7 45.6 %collective-permute-start.37 = (bf16[2,64,4128]{2,1,0:T(8,128)(2,1)S(1)}, bf16[2,64,4128]{2,1,0:T(8,128)(2,1)S(1)}, u32[]{:S(2)}, u32[]{:S(2)}) collective-permute-start(bf16[2,64,4128]{2,1,0:T(8,128)(2,1)S(1)} %fusion.77), channel_id=1, source_target_pairs={{0,8},{4,12},{8,0},{12,4},{16,24},{20,28},{24,16},{28,20},{1,9},{5... | collective-permute-start | bytes 3170312 | tf_op jit(solution)/shard_map/ppermute | solution.py:89
  856.1 27.0 %collective-permute-start.32 = (bf16[64,2176]{1,0:T(8,128)(2,1)S(1)}, bf16[64,2176]{1,0:T(8,128)(2,1)S(1)}, u32[]{:S(2)}, u32[]{:S(2)}) collective-permute-start(bf16[64,2176]{1,0:T(8,128)(2,1)S(1)} %dynamic-slice_bitcast_fusion.5), channel_id=1, source_target_pairs={{0,16},{4,20},{8,24},{12,28},{16,0},{20,4},{24,8},{28,12},{1,17},{... | collective-permute-start | bytes 835592 | tf_op jit(solution)/shard_map/ppermute | solution.py:89
  857.4 37.3 %collective-permute-start.38 = (bf16[64,4128]{1,0:T(8,128)(2,1)S(1)}, bf16[64,4128]{1,0:T(8,128)(2,1)S(1)}, u32[]{:S(2)}, u32[]{:S(2)}) collective-permute-start(bf16[64,4128]{1,0:T(8,128)(2,1)S(1)} %dynamic-slice_bitcast_fusion.3), channel_id=1, source_target_pairs={{0,16},{4,20},{8,24},{12,28},{16,0},{20,4},{24,8},{28,12},{1,17},{... | collective-permute-start | bytes 1585160 | tf_op jit(solution)/shard_map/ppermute | solution.py:89
  (118 other events, 1486.5 us)
Sparse Core Ops, SparseCore 0:
  48.2 227.2 all-gather.1
  536.9 105.3 reduce-scatter.2
  649.0 200.9 reduce-scatter.4

commit v5 on v4

--- a/solution.py
+++ b/solution.py
@@ -49,6 +49,11 @@
     return lax.ppermute(values, every_axis, swap_pairs(chips))
 
 
+def swap_after(values, earlier, chips):
+    width = values.shape[1]
+    return role_swap(jnp.concatenate([values, earlier[:, :128]], axis=1), chips)[:, :width]
+
+
 def core_swap(values):
     return lax.ppermute(values, "core", [(0, 1), (1, 0)])
 
@@ -105,14 +110,21 @@
     return joined, sorted(held + [bit], reverse=True)
 
 
-def reduce_bit(values, held, bit, chips):
+def exchange_bit(values, held, bit, chips):
     place = held.index(bit)
     mine = own_bit(bit)
     kept = lax.dynamic_index_in_dim(values, mine, place, keepdims=False)
     sent = lax.dynamic_index_in_dim(values, 1 - mine, place, keepdims=False)
-    other = bit_swap(sent, bit, chips)
-    total = (kept.astype(jnp.float32) + other.astype(jnp.float32)).astype(jnp.bfloat16)
-    return total, [b for b in held if b != bit]
+    return kept, bit_swap(sent, bit, chips), [b for b in held if b != bit]
+
+
+def add_halves(kept, other):
+    return (kept.astype(jnp.float32) + other.astype(jnp.float32)).astype(jnp.bfloat16)
+
+
+def reduce_bit(values, held, bit, chips):
+    kept, other, held = exchange_bit(values, held, bit, chips)
+    return add_halves(kept, other), held
 
 
 def half_columns(values):
@@ -133,18 +145,23 @@
     return jnp.concatenate(halves, axis=1)
 
 
-def scatter_quick(gradient, chips):
-    count = group_bits(chips)
+def quick_begin(gradient, chips):
+    held = list(range(group_bits(chips) - 1, -2, -1))
     cut = half_columns(gradient)
+    begun = []
+    for bit, part in ((-1, gradient[:, :cut]), (0, gradient[:, cut:])):
+        values = part.reshape([2] * len(held) + [-1, part.shape[-1]])
+        begun.append(exchange_bit(values, held, bit, chips))
+    return begun
+
+
+def quick_finish(begun, chips):
     parts = []
-    for order, part in (((-1, 0), gradient[:, :cut]), ((0, -1), gradient[:, cut:])):
-        held = list(range(count - 1, -2, -1))
-        values = part.reshape([2] * len(held) + [-1, part.shape[-1]])
-        for bit in order:
-            values, held = reduce_bit(values, held, bit, chips)
+    for bit, (kept, other, held) in zip((0, -1), begun):
+        values, held = reduce_bit(add_halves(kept, other), held, bit, chips)
         parts.append(values)
     values = jnp.concatenate(parts, axis=-1)
-    for bit in range(1, count):
+    for bit in range(1, group_bits(chips)):
         values, held = reduce_bit(values, held, bit, chips)
     return values
 
@@ -244,11 +261,8 @@
 
 
 def probability_block(keys_here, stacked, start, is_local, length):
-    scores = (
-        lax.dot_general(
-            keys_here, stacked, (((1,), (1,)), ((), ())), preferred_element_type=jnp.float32
-        )
-        * 0.125
+    scores = lax.dot_general(
+        keys_here, stacked, (((1,), (1,)), ((), ())), preferred_element_type=jnp.float32
     )
     if is_local:
         rows = stacked.shape[0] // 2
@@ -278,7 +292,9 @@
         at = start if is_local else 0
         part = raw_ref[pl.ds(start, block), :wide]
         here = pl.ds(start, block)
-        query = (part * cos_ref[here, :] + rolled(part) * sin_ref[here, :]).astype(jnp.bfloat16)
+        query = (part * cos_ref[here, :] + rolled(part) * sin_ref[here, :]).astype(
+            jnp.bfloat16
+        ) * jnp.bfloat16(0.125)
         probability = probability_block(
             keys[pl.ds(at, reach), :], pair_stack(query), start, is_local, length
         )
@@ -292,9 +308,8 @@
     pl.loop(0, length // block, unroll=2)(step)
 
 
-def attend_back_kernel(
-    is_local, block, raw_ref, cos_ref, sin_ref, up_ref, out_ref, keys, keys_t, values, d_keys, d_values
-):
+def attend_back_kernel(is_local, block, raw_ref, cos_ref, sin_ref, up_ref, *refs):
+    out_ref, keys, keys_t, values, d_keys, d_values = refs[-6:]
     length = raw_ref.shape[0]
     pad = HALF_WIN if is_local else 0
     reach = block + 2 * HALF_WIN if is_local else length
@@ -306,7 +321,7 @@
         keys_t[...] = jnp.zeros_like(keys_t)
         values[...] = jnp.zeros_like(values)
     keys[pl.ds(pad, length), :] = rotated
-    keys_t[:, pl.ds(pad, length)] = rotated.T
+    keys_t[:, pl.ds(pad, length)] = (rotated * jnp.bfloat16(0.125)).T
     values[pl.ds(pad, length), :] = raw_ref[:, 2 * wide :].astype(jnp.bfloat16)
     d_keys[...] = jnp.zeros_like(d_keys)
     d_values[...] = jnp.zeros_like(d_values)
@@ -317,7 +332,9 @@
         here = pl.ds(start, block)
         band = pl.ds(at, reach)
         part = raw_ref[here, :wide]
-        query = (part * cos_ref[here, :] + rolled(part) * sin_ref[here, :]).astype(jnp.bfloat16)
+        query = (part * cos_ref[here, :] + rolled(part) * sin_ref[here, :]).astype(
+            jnp.bfloat16
+        ) * jnp.bfloat16(0.125)
         stacked = pair_stack(query)
         upstream = pair_stack(up_ref[here, :])
         probability = probability_block(keys[band, :], stacked, start, is_local, length)
@@ -330,32 +347,30 @@
         centre = jnp.sum(probability * d_probability, axis=0, keepdims=True)
         d_scores = (probability * (d_probability - centre)).astype(jnp.bfloat16)
         d_keys[band, :] += jnp.dot(d_scores, stacked, preferred_element_type=jnp.float32)
-        d_query = (
-            pair_unstack(
-                jnp.dot(keys_t[:, band], d_scores, preferred_element_type=jnp.float32)
-            )
-            * 0.125
+        d_query = pair_unstack(
+            jnp.dot(keys_t[:, band], d_scores, preferred_element_type=jnp.float32)
         )
         out_ref[here, :wide] = (
             d_query * cos_ref[here, :] - rolled(d_query) * sin_ref[here, :]
         ).astype(jnp.bfloat16)
 
     pl.loop(0, length // block, unroll=2)(step)
-    d_key = d_keys[pl.ds(pad, length), :] * 0.125
+    d_key = d_keys[pl.ds(pad, length), :]
     out_ref[:, wide : 2 * wide] = (d_key * cos_ref[...] - rolled(d_key) * sin_ref[...]).astype(
         jnp.bfloat16
     )
     out_ref[:, 2 * wide :] = d_values[pl.ds(pad, length), :].astype(jnp.bfloat16)
 
 
-def attend_specs(projected):
+def attend_specs(projected, part=0, parts=1):
     rows, columns = projected.shape
     wide = 2 * HEAD_DIM
-    raw = pl.BlockSpec((SEQ_LEN, 3 * wide), lambda s, j: (s, j))
+    pairs = columns // (3 * wide) // parts
+    skipped = part * pairs
+    raw = pl.BlockSpec((SEQ_LEN, 3 * wide), lambda s, j: (s, j + skipped))
     table = pl.BlockSpec((SEQ_LEN, wide), lambda s, j: (0, 0))
-    narrow = pl.BlockSpec((SEQ_LEN, wide), lambda s, j: (s, j))
-    grid = (rows // SEQ_LEN, columns // (3 * wide))
-    return grid, raw, table, narrow
+    narrow = pl.BlockSpec((SEQ_LEN, wide), lambda s, j: (s, j + skipped))
+    return (rows // SEQ_LEN, pairs), raw, table, narrow
 
 
 def attend_cost(projected, is_local, products):
@@ -390,17 +405,17 @@
     )(projected, *tables)
 
 
-def attend_backward(projected, tables, d_attended, is_local):
+def attend_backward(projected, tables, d_attended, is_local, part, after=()):
     rows, columns = projected.shape
     wide = 2 * HEAD_DIM
-    grid, raw, table, narrow = attend_specs(projected)
+    grid, raw, table, narrow = attend_specs(projected, part, 2)
     span = SEQ_LEN + 2 * HALF_WIN if is_local else SEQ_LEN
     return pl.pallas_call(
         functools.partial(attend_back_kernel, is_local, 128),
-        out_shape=jax.ShapeDtypeStruct((rows, columns), jnp.bfloat16),
+        out_shape=jax.ShapeDtypeStruct((rows, columns // 2), jnp.bfloat16),
         grid=grid,
-        in_specs=[raw, table, table, narrow],
-        out_specs=raw,
+        in_specs=[raw, table, table, narrow] + [pl.BlockSpec(memory_space=pl.ANY)] * len(after),
+        out_specs=pl.BlockSpec((SEQ_LEN, 3 * wide), lambda s, j: (s, j)),
         scratch_shapes=[
             pltpu.VMEM((span, wide), jnp.bfloat16),
             pltpu.VMEM((wide, span), jnp.bfloat16),
@@ -409,8 +424,8 @@
             pltpu.VMEM((span, wide), jnp.float32),
         ],
         compiler_params=pltpu.CompilerParams(vmem_limit_bytes=kernel_vmem),
-        cost_estimate=attend_cost(projected, is_local, 5),
-    )(projected, *tables, d_attended)
+        cost_estimate=attend_cost(projected, is_local, 2),
+    )(projected, *tables, d_attended, *after)
 
 
 def weight_grad_kernel(choice, starts, total, left_count, *refs):
@@ -483,7 +498,7 @@
     return (output, kept)
 
 
-def backward_layer(upstream, weights, tables, kept, is_local, scatter):
+def backward_layer(upstream, weights, tables, kept, is_local, begin, after):
     w_qkv, w_out, w_inner, w_gate, w_down, gain_pair = weights
     residual, middle, lowered, lowered_two, projected, attended, inner, gate_part, activated = kept
     up_low = upstream.astype(jnp.bfloat16)
@@ -500,16 +515,22 @@
     d_branch = d_middle.astype(jnp.bfloat16)
     d_attended = product(d_branch, w_out, (1, 0)).astype(jnp.bfloat16)
     d_attended, hidden_grads = lax.optimization_barrier((d_attended, hidden_grads))
-    hidden_grads = scatter(hidden_grads)
-    d_projected = attend_backward(projected, tables, d_attended, is_local)
-    d_normed = core_total(product(d_projected, w_qkv, (1, 1)))
+    hidden_begun = begin(hidden_grads)
+    d_first = attend_backward(projected, tables, d_attended, is_local, 0)
+    d_second = attend_backward(
+        projected, tables, d_attended, is_local, 1, after(hidden_begun)
+    )
+    cut = d_first.shape[1]
+    d_normed = core_total(
+        product(d_first, w_qkv[:, :cut], (1, 1)) + product(d_second, w_qkv[:, cut:], (1, 1))
+    )
     unused, pullback = jax.vjp(layer_norm, residual, gain_pair[0])
     d_in_norm, d_gain_one = pullback(d_normed)
     gains = widen(jnp.stack([d_gain_one, d_gain_two], axis=1)).astype(jnp.bfloat16)
-    head_grads = scatter(
-        weight_grads((lowered, d_branch), (d_projected, attended, gains), (0, 1, None))
-    )
-    return (d_middle + d_in_norm, (head_grads, hidden_grads))
+    head_grads = weight_grads(
+        (lowered, d_branch), (d_first, d_second, attended, gains), (0, 0, 1, None)
+    )
+    return (d_middle + d_in_norm, (begin(head_grads), hidden_begun))
 
 
 def adam_update(weight, moment, square, gradient, step_rate, decay_here):
@@ -531,46 +552,60 @@
     def chip_sequence(values):
         return jnp.where(same, values, core_swap(values)).astype(jnp.float32)
 
-    def own_sequence(values):
-        return jnp.where(same, values, lax.ppermute(values, every_axis, result_pairs(chips)))
+    def arriving_sequence(values):
+        return lax.ppermute(values, every_axis, result_pairs(chips))
 
     starts = layer_starts(masters)
     hidden = masters[2].shape[3]
     local_tables = rotary_tables(theta_local)
     global_tables = rotary_tables(theta_global)
-    packed = [pack_shards(masters, layer) for layer in range(2)]
-    heads_part = role_swap(packed[0][:, : starts[3]], chips)
-    hidden_part = role_swap(packed[0][:, starts[3] :], chips)
-    second = role_swap(packed[1], chips)
-    hidden_in, heads_part, hidden_part, second = lax.optimization_barrier(
-        (hidden_in, heads_part, hidden_part, second)
-    )
-    first = [gather_quick(part, chips) for part in (heads_part, hidden_part)]
+    packed = [split_packed(pack_shards(masters, layer), starts) for layer in range(2)]
+    heads_first = role_swap(packed[0][0], chips)
+    hidden_first = swap_after(packed[0][1], heads_first, chips)
+    hidden_second = swap_after(packed[1][1], hidden_first, chips)
+    heads_second = swap_after(packed[1][0], hidden_second, chips)
+    heads_all = gather_quick(heads_first, chips)
     weights = [
-        unpack_weights(first[0], first[1], starts, hidden),
-        unpack_weights(*split_packed(gather_rows(second, chips), starts), starts, hidden),
+        unpack_weights(heads_all, gather_rows(hidden_first, chips), starts, hidden),
+        unpack_weights(
+            gather_quick(heads_second, chips), gather_rows(hidden_second, chips), starts, hidden
+        ),
     ]
     inputs = chip_sequence(hidden_in)
     upstream = chip_sequence(cotangent)
     middle, kept_first = forward_layer(inputs, weights[0], local_tables, True)
     output, kept_second = forward_layer(middle, weights[1], global_tables, False)
-    final_out = own_sequence(output.astype(jnp.bfloat16))
-    by_call = functools.partial(scatter_rows, chips=chips)
-    by_steps = functools.partial(scatter_quick, chips=chips)
-    d_middle, shards_second = backward_layer(
-        upstream, weights[1], global_tables, kept_second, False, by_call
-    )
-    d_values, shards_first = backward_layer(
-        d_middle, weights[0], local_tables, kept_first, True, by_steps
-    )
-    shards_first = role_swap(jnp.concatenate(shards_first, axis=1), chips)
-    shards_first, shards_second = lax.optimization_barrier((shards_first, shards_second))
-    shards_second = role_swap(jnp.concatenate(shards_second, axis=1), chips)
+    out_arrived = arriving_sequence(output.astype(jnp.bfloat16))
+    d_middle, (heads_second, hidden_second) = backward_layer(
+        upstream,
+        weights[1],
+        global_tables,
+        kept_second,
+        False,
+        functools.partial(scatter_rows, chips=chips),
+        lambda begun: (out_arrived,),
+    )
+    final_out = jnp.where(same, output.astype(jnp.bfloat16), out_arrived)
+    d_values, begun_first = backward_layer(
+        d_middle,
+        weights[0],
+        local_tables,
+        kept_first,
+        True,
+        functools.partial(quick_begin, chips=chips),
+        lambda begun: tuple(other for kept, other, held in begun),
+    )
+    heads_first, hidden_first = [quick_finish(begun, chips) for begun in begun_first]
+    shards_first = role_swap(jnp.concatenate([heads_first, hidden_first], axis=1), chips)
+    hidden_second = swap_after(hidden_second, shards_first, chips)
+    heads_second = swap_after(heads_second, hidden_second, chips)
+    shards_second = jnp.concatenate([heads_second, hidden_second], axis=1)
     grads_first, grads_second = [
         unpack_grads(packed.astype(jnp.float32), starts, hidden)
         for packed in (shards_first, shards_second)
     ]
-    final_grad = own_sequence(d_values.astype(jnp.bfloat16)).astype(jnp.float32)
+    d_low = d_values.astype(jnp.bfloat16)
+    final_grad = jnp.where(same, d_low, arriving_sequence(d_low)).astype(jnp.float32)
     rates = (rate_qkv, rate_out, rate_inp, rate_down, rate_gain)
     results = [final_out, final_grad]
     for i, rate in enumerate(rates):

time: 957 us -> 962 us (level)
  waiting for transfers between devices: 420 us -> 366 us
  starting transfers between devices: 46.5 us -> 72.6 us
  other arithmetic: 103 us -> 122 us
    ppermute x8, waiting for transfers between devices: 237 us -> 185 us  [bit_swap(): return lax.ppermute(values, 'tensor', [(0, 1), (1, 0)])]
    ppermute x16, waiting for transfers between devices: 146 us -> 120 us  [bit_swap(): lax.ppermute(values, 'chip', [(chip, chip ^ 1 << bit) for chip in range(c...]
    ppermute x16, starting transfers between devices: 9.87 us -> 30.8 us  [bit_swap(): lax.ppermute(values, 'chip', [(chip, chip ^ 1 << bit) for chip in range(c...]
    all_gather x1 -> x2, waiting for transfers between devices: 0.02 us -> 20.5 us  [gather_rows(): return lax.all_gather(shard, chip_axes, axis=0, tiled=True)]
    ppermute x5 -> x7, waiting for transfers between devices: 26.5 us -> 35.2 us  [role_swap(): return lax.ppermute(values, every_axis, swap_pairs(chips))]
    dot_general x20 -> x22, matrix products: 127 us -> 136 us  [product(): lax.dot_general(left, right, ((contract[:1], contract[1:]), ((), ())), pr...]
    unnamed x214 -> x269, local copies, waits for them, and re-layouts: 31.2 us -> 24.5 us
    ppermute x5 -> x7, starting transfers between devices: 17.2 us -> 21.4 us  [role_swap(): return lax.ppermute(values, every_axis, swap_pairs(chips))]
  transfers between devices with their start and end apart: 44 -> 47, of which waited for: 23 -> 23; matrix products, arithmetic and copies ran while one was open for 17% -> 21% of each run, Pallas kernels for 13% -> 17%
where the time goes in v5:
time: 962 us; the launch traced here: 958 us
  waiting for transfers between devices  366 us (38%)
  Pallas kernels  189 us (20%)
  matrix products  136 us (14%)
  other arithmetic  122 us (13%)
  starting transfers between devices  72.6 us (8%)
  local copies, waits for them, and re-layouts  56.1 us (6%)
  between operations  16.7 us (2%)
    ppermute x8, waiting for transfers between devices, bit_swap(): return lax.ppermute(values, 'tensor', [(0, 1), (1, 0)])  185 us
    dot_general x22, matrix products, product(): lax.dot_general(left, right, ((contract[:1], contract[1:]), ((), ())), pr...  136 us
    ppermute x16, waiting for transfers between devices, bit_swap(): lax.ppermute(values, 'chip', [(chip, chip ^ 1 << bit) for chip in range(c...  120 us
    pallas_call x4, Pallas kernels, attend_backward(): pl.pallas_call(functools.partial(attend_back_kernel, is_local, 128), out_...  87.8 us
    pallas_call x2, Pallas kernels, attend_forward(): pl.pallas_call(functools.partial(attend_kernel, is_local, 128), out_shape...  52.6 us
    pallas_call x4, Pallas kernels, weight_grads(): pl.pallas_call(functools.partial(weight_grad_kernel, choice, tuple(starts...  48.3 us
    ppermute x7, waiting for transfers between devices, role_swap(): return lax.ppermute(values, every_axis, swap_pairs(chips))  35.2 us
    ppermute x16, starting transfers between devices, bit_swap(): lax.ppermute(values, 'chip', [(chip, chip ^ 1 << bit) for chip in range(c...  30.8 us
  transfers between devices with their start and end apart: 47, of which 23 were waited for; matrix products, arithmetic and copies ran while one was open for 21% of the time, Pallas kernels for 17%

profile of v5, /device:TPU:1, one launch (start us, length us, event | category | flops | bytes accessed | tf_op | source)
XLA Modules:
  0.0 957.7 jit_solution(4383166772710763888)
XLA Ops:
  23.5 7.2 collective-permute-done.9
  46.7 12.5 %collective-permute-done.2 = bf16[64,2176]{1,0:T(8,128)(2,1)S(1)} collective-permute-done((bf16[64,2176]{1,0:T(8,128)(2,1)S(1)}, bf16[64,2176]{1,0:T(8,128)(2,1)S(1)}, u32[]{:S(2)}, u32[]{:S(2)}) %collective-permute-start.2) | collective-permute-done | bytes 278560 | tf_op jit(solution)/shard_map/ppermute | solution.py:94
  59.4 13.7 %collective-permute-start.3 = (bf16[2,64,2176]{2,1,0:T(8,128)(2,1)S(1)}, bf16[2,64,2176]{2,1,0:T(8,128)(2,1)S(1)}, u32[]{:S(2)}, u32[]{:S(2)}) collective-permute-start(bf16[2,64,2176]{2,1,0:T(8,128)(2,1)S(1)} %pad_maximum_fusion.15), channel_id=1, source_target_pairs={{0,8},{4,12},{8,0},{12,4},{16,24},{20,28},{24,16},{28,20},{1,9},{5... | collective-permute-start | bytes 1671176 | tf_op jit(solution)/shard_map/ppermute | solution.py:94
  73.2 8.7 collective-permute-start.14
  88.0 14.2 %collective-permute-done.3 = bf16[2,64,2176]{2,1,0:T(8,128)(2,1)S(1)} collective-permute-done((bf16[2,64,2176]{2,1,0:T(8,128)(2,1)S(1)}, bf16[2,64,2176]{2,1,0:T(8,128)(2,1)S(1)}, u32[]{:S(2)}, u32[]{:S(2)}) %collective-permute-start.3) | collective-permute-done | bytes 557088 | tf_op jit(solution)/shard_map/ppermute | solution.py:94
  102.2 18.5 %collective-permute-done.14 = bf16[2,64,2176]{2,1,0:T(8,128)(2,1)} collective-permute-done((bf16[2,64,2176]{2,1,0:T(8,128)(2,1)S(1)}, bf16[2,64,2176]{2,1,0:T(8,128)(2,1)}, u32[]{:S(2)}, u32[]{:S(2)}) %collective-permute-start.14) | collective-permute-done | bytes 557088 | tf_op jit(solution)/shard_map/ppermute | solution.py:94
  126.0 10.9 %collective-permute-done.6 = bf16[2,2,64,1024]{3,2,0,1:T(8,128)(2,1)S(1)} collective-permute-done((bf16[2,2,64,1024]{3,2,0,1:T(8,128)(2,1)S(1)}, bf16[2,2,64,1024]{3,2,0,1:T(8,128)(2,1)S(1)}, u32[]{:S(2)}, u32[]{:S(2)}) %collective-permute-start.6) | collective-permute-done | bytes 524320 | tf_op jit(solution)/shard_map/ppermute | solution.py:94
  142.8 43.9 %collective-permute-done.7 = bf16[2,2,2,64,1024]{4,3,0,1,2:T(8,128)(2,1)S(1)} collective-permute-done((bf16[2,2,2,64,1024]{4,3,0,1,2:T(8,128)(2,1)S(1)}, bf16[2,2,2,64,1024]{4,3,0,1,2:T(8,128)(2,1)S(1)}, u32[]{:S(2)}, u32[]{:S(2)}) %collective-permute-start.7) | collective-permute-done | bytes 1048608 | tf_op jit(solution)/shard_map/ppermute | solution.py:93
  197.0 19.3 %shard_map.296.refs_4_ = bf16[1024,512]{1,0:T(8,128)(2,1)S(1)} custom-call(f32[1024,1536]{1,0:T(8,128)} %fusion.32.raw_ref, f32[1024,128]{1,0:T(8,128)S(1)} %get-tuple-element.227.cos_ref, f32[1024,128]{1,0:T(8,128)S(1)} %get-tuple-element.228.sin_ref), custom_call_target="tpu_custom_call" | custom-call | flops 2147483648 | bytes 12582912 | tf_op jit(solution)/shard_map/pallas_call | solution.py:393
  226.8 10.7 %collective-permute-done.17 = bf16[2,2,64,1024]{3,2,0,1:T(8,128)(2,1)} collective-permute-done((bf16[2,2,64,1024]{3,2,0,1:T(8,128)(2,1)}, bf16[2,2,64,1024]{3,2,0,1:T(8,128)(2,1)}, u32[]{:S(2)}, u32[]{:S(2)}) %collective-permute-start.17) | collective-permute-done | bytes 524320 | tf_op jit(solution)/shard_map/ppermute | solution.py:94
  255.3 17.2 %multiply_convert_fusion.3 = (bf16[1024,1312]{1,0:T(8,128)(2,1)S(1)}, f32[1024,1312]{1,0:T(8,128)}, f32[1024,1312]{1,0:T(8,128)}) fusion(f32[1024,1312]{1,0:T(8,128)S(1)} %fusion.57, bf16[1024,1024]{1,0:T(8,128)(2,1)S(1)} %multiply_convert_fusion.6.refs_0_, bf16[1024,4128]{1,0:T(8,128)(2,1)S(1)} %copy-done.122), kind=kOutput, calls=%fused_computation.32 | convolution fusion | flops 2840133632 | bytes 24182784 | tf_op jit(solution)/shard_map/dot_general | solution.py:481
  294.1 33.3 %shard_map.297.refs_4_ = bf16[1024,512]{1,0:T(8,128)(2,1)S(1)} custom-call(f32[1024,1536]{1,0:T(8,128)} %fusion.29.raw_ref, f32[1024,128]{1,0:T(8,128)S(1)} %get-tuple-element.229.cos_ref, f32[1024,128]{1,0:T(8,128)S(1)} %get-tuple-element.230.sin_ref), custom_call_target="tpu_custom_call" | custom-call | flops 8589934592 | bytes 12582912 | tf_op jit(solution)/shard_map/pallas_call | solution.py:393
  337.7 20.4 %all-gather.5.cloned.1.call-done = bf16[1024,4128]{1,0:T(8,128)(2,1)} async-done(((bf16[64,4128]{1,0:T(8,128)(2,1)}), bf16[1024,4128]{1,0:T(8,128)(2,1)}) %all-gather.5.cloned.1.call-update) | async-done | bytes 8454160 | tf_op jit(solution)/shard_map/all_gather | solution.py:170
  367.6 19.6 %add_convert_fusion.1 = (bf16[1024,1312]{1,0:T(8,128)(2,1)}, f32[1024,1312]{1,0:T(8,128)}, f32[1024,1312]{1,0:T(8,128)}) fusion(f32[1024,1312]{1,0:T(8,128)S(1)} %fusion.41, f32[1024,1312]{1,0:T(8,128)S(1)} %fusion.45, bf16[1024,1024]{1,0:T(8,128)(2,1)S(1)} %broadcast_select_fusion.refs_1_, bf16[1024,4128]{1,0:T(8,128)(2,1)S(1)} %copy-done.123), kind=kOutput, calls=%fused_computation.18 | convolution fusion | flops 2849538048 | bytes 29949952 | tf_op jit(solution)/shard_map/dot_general | solution.py:481
  392.4 7.4 fusion.39
  414.2 15.9 %shard_map.298 = bf16[1024,4128]{1,0:T(8,128)(2,1)} custom-call(bf16[1024,1024]{1,0:T(8,128)(2,1)S(1)} %copy-done.8, bf16[1024,1024]{1,0:T(8,128)(2,1)S(1)} %broadcast_select_fusion.refs_1_, bf16[1024,1312]{1,0:T(8,128)(2,1)} %get-tuple-element.145.refs_2_, bf16[1024,1312]{1,0:T(8,128)(2,1)} %copy-done.69, bf16[1024,1312]{1,0:T(8,128)(2,1)} %copy-done.70), custom_call_target="tpu_custom_call" | custom-call | flops 8657043456 | bytes 21102592 | tf_op jit(solution)/shard_map/pallas_call | solution.py:465
  445.3 27.7 %shard_map.299.refs_2_ = bf16[1024,768]{1,0:T(8,128)(2,1)S(1)} custom-call(f32[1024,1536]{1,0:T(8,128)} %fusion.29.raw_ref, f32[1024,128]{1,0:T(8,128)S(1)} %get-tuple-element.229.cos_ref, f32[1024,128]{1,0:T(8,128)S(1)} %get-tuple-element.230.sin_ref, bf16[1024,512]{1,0:T(8,128)(2,1)S(1)} %convolution_convert_fusion.3.up_ref), custom_call_target="tpu_custom_call" | custom-call | flops 8589934592 | bytes 12582912 | tf_op jit(solution)/shard_map/pallas_call | solution.py:413
  478.8 28.5 %shard_map.300.refs_3_ = bf16[1024,768]{1,0:T(8,128)(2,1)S(1)} custom-call(f32[1024,1536]{1,0:T(8,128)} %fusion.29.raw_ref, f32[1024,128]{1,0:T(8,128)S(1)} %get-tuple-element.229.cos_ref, f32[1024,128]{1,0:T(8,128)S(1)} %get-tuple-element.230.sin_ref, bf16[1024,512]{1,0:T(8,128)(2,1)S(1)} %convolution_convert_fusion.3.up_ref, ...), custom_call_target="tpu_custom_call" | custom-call | flops 8589934592 | bytes 12582912 | tf_op jit(solution)/shard_map/pallas_call | solution.py:413
  531.4 6.9 fusion.47
  558.2 16.6 %shard_map.301 = bf16[1024,4128]{1,0:T(8,128)(2,1)} custom-call(bf16[1024,1024]{1,0:T(8,128)(2,1)S(1)} %copy-done.7, bf16[1024,1024]{1,0:T(8,128)(2,1)S(1)} %copy-done.10, bf16[1024,1312]{1,0:T(8,128)(2,1)} %get-tuple-element.157.refs_2_, bf16[1024,1312]{1,0:T(8,128)(2,1)} %get-tuple-element.158.refs_3_, bf16[1024,1312]{1,0:T(8,128)(2,1)} %copy-done.124), custom_call_target="tpu_custom_call" | custom-call | flops 8657043456 | bytes 21102592 | tf_op jit(solution)/shard_map/pallas_call | solution.py:465
  599.4 16.0 %shard_map.302.refs_2_ = bf16[1024,768]{1,0:T(8,128)(2,1)S(1)} custom-call(f32[1024,1536]{1,0:T(8,128)} %fusion.32.raw_ref, f32[1024,128]{1,0:T(8,128)S(1)} %copy-done.1, f32[1024,128]{1,0:T(8,128)S(1)} %copy-done.3, bf16[1024,512]{1,0:T(8,128)(2,1)S(1)} %convolution_convert_fusion.2.up_ref), custom_call_target="tpu_custom_call" | custom-call | flops 2147483648 | bytes 12582912 | tf_op jit(solution)/shard_map/pallas_call | solution.py:413
  619.3 34.9 %collective-permute-done.26 = bf16[2,2,2,64,2048]{4,3,0,1,2:T(8,128)(2,1)} collective-permute-done((bf16[2,2,2,64,2048]{4,3,0,1,2:T(8,128)(2,1)}, bf16[2,2,2,64,2048]{4,3,0,1,2:T(8,128)(2,1)}, u32[]{:S(2)}, u32[]{:S(2)}) %collective-permute-start.26) | collective-permute-done | bytes 2097184 | tf_op jit(solution)/shard_map/ppermute | solution.py:93
  667.0 15.5 %shard_map.303.refs_3_ = bf16[1024,768]{1,0:T(8,128)(2,1)S(1)} custom-call(f32[1024,1536]{1,0:T(8,128)} %fusion.32.raw_ref, f32[1024,128]{1,0:T(8,128)S(1)} %copy-done.1, f32[1024,128]{1,0:T(8,128)S(1)} %copy-done.3, bf16[1024,512]{1,0:T(8,128)(2,1)S(1)} %convolution_convert_fusion.2.up_ref, bf16[2,2,2,64,2048]{4,3,2,1,0:T(8,128)(2,1)S(1)} %copy.277.refs_0_, ...), custom_call_target="tpu_custom_call" | custom-call | flops 2147483648 | bytes 12582912 | tf_op jit(solution)/shard_map/pallas_call | solution.py:413
  688.8 7.8 shard_map.305
  711.9 7.9 shard_map.304
  731.0 62.1 %collective-permute-done.30 = bf16[2,2,2,64,1024]{4,3,0,1,2:T(8,128)(2,1)S(1)} collective-permute-done((bf16[2,2,2,64,1024]{4,3,0,1,2:T(8,128)(2,1)S(1)}, bf16[2,2,2,64,1024]{4,3,0,1,2:T(8,128)(2,1)S(1)}, u32[]{:S(2)}, u32[]{:S(2)}) %collective-permute-start.30) | collective-permute-done | bytes 1048608 | tf_op jit(solution)/shard_map/ppermute | solution.py:93
  798.2 13.6 %collective-permute-done.31 = bf16[2,2,64,1024]{3,2,0,1:T(8,128)(2,1)S(1)} collective-permute-done((bf16[2,2,64,1024]{3,2,0,1:T(8,128)(2,1)S(1)}, bf16[2,2,64,1024]{3,2,0,1:T(8,128)(2,1)S(1)}, u32[]{:S(2)}, u32[]{:S(2)}) %collective-permute-start.31) | collective-permute-done | bytes 524320 | tf_op jit(solution)/shard_map/ppermute | solution.py:94
  812.0 39.4 %collective-permute-done.33 = bf16[2,2,64,1152]{3,2,0,1:T(8,128)(2,1)S(1)} collective-permute-done((bf16[2,2,64,1152]{3,2,0,1:T(8,128)(2,1)S(1)}, bf16[2,2,64,1152]{3,2,0,1:T(8,128)(2,1)S(1)}, u32[]{:S(2)}, u32[]{:S(2)}) %collective-permute-start.33) | collective-permute-done | bytes 589856 | tf_op jit(solution)/shard_map/ppermute | solution.py:93
  853.4 23.0 %collective-permute-done.34 = bf16[2,64,2176]{2,1,0:T(8,128)(2,1)S(1)} collective-permute-done((bf16[2,64,2176]{2,1,0:T(8,128)(2,1)S(1)}, bf16[2,64,2176]{2,1,0:T(8,128)(2,1)S(1)}, u32[]{:S(2)}, u32[]{:S(2)}) %collective-permute-start.34) | collective-permute-done | bytes 557088 | tf_op jit(solution)/shard_map/ppermute | solution.py:94
  876.8 14.2 %collective-permute-done.35 = bf16[64,2176]{1,0:T(8,128)(2,1)S(1)} collective-permute-done((bf16[64,2176]{1,0:T(8,128)(2,1)S(1)}, bf16[64,2176]{1,0:T(8,128)(2,1)S(1)}, u32[]{:S(2)}, u32[]{:S(2)}) %collective-permute-start.35) | collective-permute-done | bytes 278560 | tf_op jit(solution)/shard_map/ppermute | solution.py:94
  897.0 7.9 collective-permute-done.40
  910.9 7.7 collective-permute-done.41
  (569 shorter events, 337.8 us)
Async XLA Ops:
  7.2 242.0 %all-gather.3.cloned.1.call-start = ((), (), s32[]{:S(2)}) async-start(), calls=%async_computation.2 | async-start | bytes 9191424 | tf_op jit(solution)/shard_map/all_gather | solution.py:170
  31.5 326.6 %all-gather.5.cloned.1.call-start = ((), (), s32[]{:S(2)}) async-start(), calls=%async_computation.3 | async-start | bytes 9191424 | tf_op jit(solution)/shard_map/all_gather | solution.py:170
  35.5 88.1 %collective-permute-start = (bf16[1024,1024]{1,0:T(8,128)(2,1)}, bf16[1024,1024]{1,0:T(8,128)(2,1)}, u32[]{:S(2)}, u32[]{:S(2)}) collective-permute-start(bf16[1024,1024]{1,0:T(8,128)(2,1)} %param.17), channel_id=1, source_target_pairs={{0,2},{2,0},{1,3},{3,1},{4,6},{6,4},{5,7},{7,5},{8,10},{10,8},{9,1... | collective-permute-start | bytes 6291464 | tf_op jit(solution)/shard_map/ppermute | solution.py:58
  36.2 23.0 %collective-permute-start.2 = (bf16[64,2176]{1,0:T(8,128)(2,1)S(1)}, bf16[64,2176]{1,0:T(8,128)(2,1)S(1)}, u32[]{:S(2)}, u32[]{:S(2)}) collective-permute-start(bf16[64,2176]{1,0:T(8,128)(2,1)S(1)} %collective-permute-done.1), channel_id=1, source_target_pairs={{0,16},{4,20},{8,24},{12,28},{16,0},{20,4},{24,8},{28,12},{1,17},{... | collective-permute-start | bytes 835592 | tf_op jit(solution)/shard_map/ppermute | solution.py:94
  43.1 16.2 %collective-permute-start.12 = (bf16[64,2304]{1,0:T(8,128)(2,1)S(1)}, bf16[64,2304]{1,0:T(8,128)(2,1)S(1)}, u32[]{:S(2)}, u32[]{:S(2)}) collective-permute-start(bf16[64,2304]{1,0:T(8,128)(2,1)S(1)} %fusion.108), channel_id=1, source_target_pairs={{0,0},{1,2},{2,1},{3,3},{4,4},{5,6},{6,5},{7,7},{8,8},{9,10},{10,9... | collective-permute-start | bytes 884744 | tf_op jit(solution)/shard_map/ppermute | solution.py:49
  59.4 42.8 %collective-permute-start.3 = (bf16[2,64,2176]{2,1,0:T(8,128)(2,1)S(1)}, bf16[2,64,2176]{2,1,0:T(8,128)(2,1)S(1)}, u32[]{:S(2)}, u32[]{:S(2)}) collective-permute-start(bf16[2,64,2176]{2,1,0:T(8,128)(2,1)S(1)} %pad_maximum_fusion.15), channel_id=1, source_target_pairs={{0,8},{4,12},{8,0},{12,4},{16,24},{20,28},{24,16},{28,20},{1,9},{5... | collective-permute-start | bytes 1671176 | tf_op jit(solution)/shard_map/ppermute | solution.py:94
  73.2 47.4 %collective-permute-start.14 = (bf16[2,64,2176]{2,1,0:T(8,128)(2,1)S(1)}, bf16[2,64,2176]{2,1,0:T(8,128)(2,1)}, u32[]{:S(2)}, u32[]{:S(2)}) collective-permute-start(bf16[2,64,2176]{2,1,0:T(8,128)(2,1)S(1)} %pad_maximum_fusion.16), channel_id=1, source_target_pairs={{0,8},{4,12},{8,0},{12,4},{16,24},{20,28},{24,16},{28,20},{1,9},{5... | collective-permute-start | bytes 1671176 | tf_op jit(solution)/shard_map/ppermute | solution.py:94
  123.4 18.3 %collective-permute-start.4 = (bf16[2,2,64,1152]{3,2,0,1:T(8,128)(2,1)S(1)}, bf16[2,2,64,1152]{3,2,0,1:T(8,128)(2,1)S(1)}, u32[]{:S(2)}, u32[]{:S(2)}) collective-permute-start(bf16[2,2,64,1152]{3,2,0,1:T(8,128)(2,1)S(1)} %fusion.98), channel_id=1, source_target_pairs={{0,1},{1,0},{2,3},{3,2},{4,5},{5,4},{6,7},{7,6},{8,9},{9,8},{10,11... | collective-permute-start | bytes 1769480 | tf_op jit(solution)/shard_map/ppermute | solution.py:93
  137.2 49.4 %collective-permute-start.7 = (bf16[2,2,2,64,1024]{4,3,0,1,2:T(8,128)(2,1)S(1)}, bf16[2,2,2,64,1024]{4,3,0,1,2:T(8,128)(2,1)S(1)}, u32[]{:S(2)}, u32[]{:S(2)}) collective-permute-start(bf16[2,2,2,64,1024]{4,3,0,1,2:T(8,128)(2,1)S(1)} %pad_maximum_fusion.11), channel_id=1, source_target_pairs={{0,1},{1,0},{2,3},{3,2},{4,5},{5,4},{6,7},{7,6},{8,9},{9,8},{10,11... | collective-permute-start | bytes 3145736 | tf_op jit(solution)/shard_map/ppermute | solution.py:93
  142.0 47.4 %collective-permute-start.5 = (bf16[2,2,2,64,1152]{4,3,0,1,2:T(8,128)(2,1)S(1)}, bf16[2,2,2,64,1152]{4,3,0,1,2:T(8,128)(2,1)S(1)}, u32[]{:S(2)}, u32[]{:S(2)}) collective-permute-start(bf16[2,2,2,64,1152]{4,3,0,1,2:T(8,128)(2,1)S(1)} %pad_maximum_fusion.9), channel_id=1, source_target_pairs={{0,4},{4,0},{8,12},{12,8},{16,20},{20,16},{24,28},{28,24},{1,5},{5... | collective-permute-start | bytes 3538952 | tf_op jit(solution)/shard_map/ppermute | solution.py:94
  218.9 24.5 %collective-permute-start.8 = (bf16[1024,1024]{1,0:T(8,128)(2,1)}, bf16[1024,1024]{1,0:T(8,128)(2,1)}, u32[]{:S(2)}, u32[]{:S(2)}) collective-permute-start(bf16[1024,1024]{1,0:T(8,128)(2,1)} %convolution_convert_fusion.1), channel_id=1, source_target_pairs={{0,2},{2,0},{1,3},{3,1},{4,6},{6,4},{5,7},{7,5},{8,10},{10,8},{9,1... | collective-permute-start | bytes 6291464 | tf_op jit(solution)/shard_map/ppermute | solution.py:58
  226.2 679.4 %reduce-scatter.5.cloned.1.call-start = ((), (), s32[]{:S(2)}) async-start(), calls=%async_computation.5 | async-start | bytes 9191424 | tf_op jit(solution)/shard_map/reduce_scatter | solution.py:174
  239.9 38.8 %collective-permute-start.18 = (bf16[2,2,2,64,1024]{4,3,0,1,2:T(8,128)(2,1)}, bf16[2,2,2,64,1024]{4,3,0,1,2:T(8,128)(2,1)}, u32[]{:S(2)}, u32[]{:S(2)}) collective-permute-start(bf16[2,2,2,64,1024]{4,3,0,1,2:T(8,128)(2,1)} %pad_maximum_fusion.12), channel_id=1, source_target_pairs={{0,1},{1,0},{2,3},{3,2},{4,5},{5,4},{6,7},{7,6},{8,9},{9,8},{10,11... | collective-permute-start | bytes 3145736 | tf_op jit(solution)/shard_map/ppermute | solution.py:93
  242.7 37.9 %collective-permute-start.16 = (bf16[2,2,2,64,1152]{4,3,0,1,2:T(8,128)(2,1)}, bf16[2,2,2,64,1152]{4,3,0,1,2:T(8,128)(2,1)}, u32[]{:S(2)}, u32[]{:S(2)}) collective-permute-start(bf16[2,2,2,64,1152]{4,3,0,1,2:T(8,128)(2,1)} %pad_maximum_fusion.10), channel_id=1, source_target_pairs={{0,4},{4,0},{8,12},{12,8},{16,20},{20,16},{24,28},{28,24},{1,5},{5... | collective-permute-start | bytes 3538952 | tf_op jit(solution)/shard_map/ppermute | solution.py:94
  277.7 51.5 %collective-permute-start.22 = (bf16[1024,1024]{1,0:T(8,128)(2,1)S(1)}, bf16[1024,1024]{1,0:T(8,128)(2,1)}, u32[]{:S(2)}, u32[]{:S(2)}) collective-permute-start(bf16[1024,1024]{1,0:T(8,128)(2,1)S(1)} %copy-done.73), channel_id=1, source_target_pairs={{0,2},{2,0},{1,3},{3,1},{4,6},{6,4},{5,7},{7,5},{8,10},{10,8},{9,1... | collective-permute-start | bytes 6291464 | tf_op jit(solution)/shard_map/ppermute | solution.py:58
  406.3 23.8 %collective-permute-start.23 = (bf16[1024,1024]{1,0:T(8,128)(2,1)}, bf16[1024,1024]{1,0:T(8,128)(2,1)}, u32[]{:S(2)}, u32[]{:S(2)}) collective-permute-start(bf16[1024,1024]{1,0:T(8,128)(2,1)} %add_convert_fusion.6), channel_id=1, source_target_pairs={{0,2},{2,0},{1,3},{3,1},{4,6},{6,4},{5,7},{7,5},{8,10},{10,8},{9,1... | collective-permute-start | bytes 6291464 | tf_op jit(solution)/shard_map/ppermute | solution.py:58
  414.2 21.0 %collective-permute-start.20 = (bf16[1024,1024]{1,0:T(8,128)(2,1)}, bf16[1024,1024]{1,0:T(8,128)(2,1)}, u32[]{:S(2)}, u32[]{:S(2)}) collective-permute-start(bf16[1024,1024]{1,0:T(8,128)(2,1)} %fusion.67), channel_id=1, source_target_pairs={{0,2},{2,0},{1,3},{3,1},{4,6},{6,4},{5,7},{7,5},{8,10},{10,8},{9,1... | collective-permute-start | bytes 6291464 | tf_op jit(solution)/shard_map/ppermute | solution.py:58
  440.0 38.7 %collective-permute-start.21 = (bf16[1024,1024]{1,0:T(8,128)(2,1)S(1)}, bf16[1024,1024]{1,0:T(8,128)(2,1)S(1)}, u32[]{:S(2)}, u32[]{:S(2)}) collective-permute-start(bf16[1024,1024]{1,0:T(8,128)(2,1)S(1)} %get-tuple-element.165), channel_id=1, source_target_pairs={{0,1},{3,2},{4,5},{7,6},{8,9},{11,10},{12,13},{15,14},{16,17},{19,... | collective-permute-start | bytes 6291464 | tf_op jit(solution)/shard_map/ppermute | solution.py:556
  515.7 402.9 %reduce-scatter.3.cloned.1.call-start = ((), (), s32[]{:S(2)}) async-start(), calls=%async_computation.4 | async-start | bytes 4734976 | tf_op jit(solution)/shard_map/reduce_scatter | solution.py:174
  556.1 18.7 %collective-permute-start.25 = (bf16[1024,1024]{1,0:T(8,128)(2,1)}, bf16[1024,1024]{1,0:T(8,128)(2,1)}, u32[]{:S(2)}, u32[]{:S(2)}) collective-permute-start(bf16[1024,1024]{1,0:T(8,128)(2,1)} %add_convert_fusion.4), channel_id=1, source_target_pairs={{0,2},{2,0},{1,3},{3,1},{4,6},{6,4},{5,7},{7,5},{8,10},{10,8},{9,1... | collective-permute-start | bytes 6291464 | tf_op jit(solution)/shard_map/ppermute | solution.py:58
  593.0 61.1 %collective-permute-start.26 = (bf16[2,2,2,64,2048]{4,3,0,1,2:T(8,128)(2,1)}, bf16[2,2,2,64,2048]{4,3,0,1,2:T(8,128)(2,1)}, u32[]{:S(2)}, u32[]{:S(2)}) collective-permute-start(bf16[2,2,2,64,2048]{4,3,0,1,2:T(8,128)(2,1)} %bitcast.241), channel_id=1, source_target_pairs={{0,1},{1,0},{2,3},{3,2},{4,5},{5,4},{6,7},{7,6},{8,9},{9,8},{10,11... | collective-permute-start | bytes 6291464 | tf_op jit(solution)/shard_map/ppermute | solution.py:93
  598.5 61.9 %collective-permute-start.27 = (bf16[2,2,2,64,2080]{4,3,0,1,2:T(8,128)(2,1)}, bf16[2,2,2,64,2080]{4,3,0,1,2:T(8,128)(2,1)}, u32[]{:S(2)}, u32[]{:S(2)}) collective-permute-start(bf16[2,2,2,64,2080]{4,3,0,1,2:T(8,128)(2,1)} %bitcast.240), channel_id=1, source_target_pairs={{0,4},{4,0},{8,12},{12,8},{16,20},{20,16},{24,28},{28,24},{1,5},{5... | collective-permute-start | bytes 6389768 | tf_op jit(solution)/shard_map/ppermute | solution.py:94
  657.8 38.8 %collective-permute-start.36 = (bf16[2,2,64,2048]{3,2,0,1:T(8,128)(2,1)}, bf16[2,2,64,2048]{3,2,0,1:T(8,128)(2,1)}, u32[]{:S(2)}, u32[]{:S(2)}) collective-permute-start(bf16[2,2,64,2048]{3,2,0,1:T(8,128)(2,1)} %dynamic-slice_bitcast_fusion.1), channel_id=1, source_target_pairs={{0,4},{4,0},{8,12},{12,8},{16,20},{20,16},{24,28},{28,24},{1,5},{5... | collective-permute-start | bytes 3145736 | tf_op jit(solution)/shard_map/ppermute | solution.py:94
  662.7 36.0 %collective-permute-start.37 = (bf16[2,2,64,2080]{3,2,0,1:T(8,128)(2,1)S(1)}, bf16[2,2,64,2080]{3,2,0,1:T(8,128)(2,1)}, u32[]{:S(2)}, u32[]{:S(2)}) collective-permute-start(bf16[2,2,64,2080]{3,2,0,1:T(8,128)(2,1)S(1)} %dynamic-slice_bitcast_fusion), channel_id=1, source_target_pairs={{0,1},{1,0},{2,3},{3,2},{4,5},{5,4},{6,7},{7,6},{8,9},{9,8},{10,11... | collective-permute-start | bytes 3194888 | tf_op jit(solution)/shard_map/ppermute | solution.py:93
  703.1 93.6 %collective-permute-start.38 = (bf16[2,64,4128]{2,1,0:T(8,128)(2,1)}, bf16[2,64,4128]{2,1,0:T(8,128)(2,1)}, u32[]{:S(2)}, u32[]{:S(2)}) collective-permute-start(bf16[2,64,4128]{2,1,0:T(8,128)(2,1)} %fusion.85), channel_id=1, source_target_pairs={{0,8},{4,12},{8,0},{12,4},{16,24},{20,28},{24,16},{28,20},{1,9},{5... | collective-permute-start | bytes 3170312 | tf_op jit(solution)/shard_map/ppermute | solution.py:94
  721.8 71.4 %collective-permute-start.30 = (bf16[2,2,2,64,1024]{4,3,0,1,2:T(8,128)(2,1)S(1)}, bf16[2,2,2,64,1024]{4,3,0,1,2:T(8,128)(2,1)S(1)}, u32[]{:S(2)}, u32[]{:S(2)}) collective-permute-start(bf16[2,2,2,64,1024]{4,3,0,1,2:T(8,128)(2,1)S(1)} %bitcast.277), channel_id=1, source_target_pairs={{0,1},{1,0},{2,3},{3,2},{4,5},{5,4},{6,7},{7,6},{8,9},{9,8},{10,11... | collective-permute-start | bytes 3145736 | tf_op jit(solution)/shard_map/ppermute | solution.py:93
  722.5 71.2 %collective-permute-start.32 = (bf16[2,2,2,64,1152]{4,3,0,1,2:T(8,128)(2,1)S(1)}, bf16[2,2,2,64,1152]{4,3,0,1,2:T(8,128)(2,1)S(1)}, u32[]{:S(2)}, u32[]{:S(2)}) collective-permute-start(bf16[2,2,2,64,1152]{4,3,0,1,2:T(8,128)(2,1)S(1)} %bitcast.274), channel_id=1, source_target_pairs={{0,4},{4,0},{8,12},{12,8},{16,20},{20,16},{24,28},{28,24},{1,5},{5... | collective-permute-start | bytes 3538952 | tf_op jit(solution)/shard_map/ppermute | solution.py:94
  729.7 164.9 %collective-permute-start.29 = (bf16[1024,1024]{1,0:T(8,128)(2,1)S(1)}, bf16[1024,1024]{1,0:T(8,128)(2,1)S(1)}, u32[]{:S(2)}, u32[]{:S(2)}) collective-permute-start(bf16[1024,1024]{1,0:T(8,128)(2,1)S(1)} %add_convert_fusion.2), channel_id=1, source_target_pairs={{0,1},{3,2},{4,5},{7,6},{8,9},{11,10},{12,13},{15,14},{16,17},{19,... | collective-permute-start | bytes 6291464 | tf_op jit(solution)/shard_map/ppermute | solution.py:556
  793.6 18.2 %collective-permute-start.31 = (bf16[2,2,64,1024]{3,2,0,1:T(8,128)(2,1)S(1)}, bf16[2,2,64,1024]{3,2,0,1:T(8,128)(2,1)S(1)}, u32[]{:S(2)}, u32[]{:S(2)}) collective-permute-start(bf16[2,2,64,1024]{3,2,0,1:T(8,128)(2,1)S(1)} %dynamic-slice_bitcast_fusion.4), channel_id=1, source_target_pairs={{0,4},{4,0},{8,12},{12,8},{16,20},{20,16},{24,28},{28,24},{1,5},{5... | collective-permute-start | bytes 1572872 | tf_op jit(solution)/shard_map/ppermute | solution.py:94
  794.0 57.4 %collective-permute-start.33 = (bf16[2,2,64,1152]{3,2,0,1:T(8,128)(2,1)S(1)}, bf16[2,2,64,1152]{3,2,0,1:T(8,128)(2,1)S(1)}, u32[]{:S(2)}, u32[]{:S(2)}) collective-permute-start(bf16[2,2,64,1152]{3,2,0,1:T(8,128)(2,1)S(1)} %dynamic-slice_bitcast_fusion.2), channel_id=1, source_target_pairs={{0,1},{1,0},{2,3},{3,2},{4,5},{5,4},{6,7},{7,6},{8,9},{9,8},{10,11... | collective-permute-start | bytes 1769480 | tf_op jit(solution)/shard_map/ppermute | solution.py:93
  851.7 24.8 %collective-permute-start.34 = (bf16[2,64,2176]{2,1,0:T(8,128)(2,1)S(1)}, bf16[2,64,2176]{2,1,0:T(8,128)(2,1)S(1)}, u32[]{:S(2)}, u32[]{:S(2)}) collective-permute-start(bf16[2,64,2176]{2,1,0:T(8,128)(2,1)S(1)} %fusion.102), channel_id=1, source_target_pairs={{0,8},{4,12},{8,0},{12,4},{16,24},{20,28},{24,16},{28,20},{1,9},{5... | collective-permute-start | bytes 1671176 | tf_op jit(solution)/shard_map/ppermute | solution.py:94
  851.8 24.9 %collective-permute-start.39 = (bf16[64,4128]{1,0:T(8,128)(2,1)S(1)}, bf16[64,4128]{1,0:T(8,128)(2,1)S(1)}, u32[]{:S(2)}, u32[]{:S(2)}) collective-permute-start(bf16[64,4128]{1,0:T(8,128)(2,1)S(1)} %dynamic-slice_bitcast_fusion.3), channel_id=1, source_target_pairs={{0,16},{4,20},{8,24},{12,28},{16,0},{20,4},{24,8},{28,12},{1,17},{... | collective-permute-start | bytes 1585160 | tf_op jit(solution)/shard_map/ppermute | solution.py:94
  (152 other events, 1728.7 us)
Sparse Core Ops, SparseCore 0:
  31.6 181.4 all-gather.2
  226.3 131.7 all-gather.4
  515.9 176.5 reduce-scatter.4
  696.7 129.8 reduce-scatter.2

commit v6 on v5

--- a/solution.py
+++ b/solution.py
@@ -50,8 +50,9 @@
 
 
 def swap_after(values, earlier, chips):
-    width = values.shape[1]
-    return role_swap(jnp.concatenate([values, earlier[:, :128]], axis=1), chips)[:, :width]
+    rows, width = values.shape
+    rider = jnp.broadcast_to(earlier[:1, :128], (rows, 128))
+    return role_swap(jnp.concatenate([values, rider], axis=1), chips)[:, :width]
 
 
 def core_swap(values):
@@ -136,42 +137,44 @@
     cut = half_columns(shard)
     for bit in range(group_bits(chips) - 1, 0, -1):
         values, held = gather_bit(values, held, bit, chips)
+    token = corner(values)
     halves = []
     for order, part in (((0, -1), values[..., :cut]), ((-1, 0), values[..., cut:])):
         part_held = held
         for bit in order:
             part, part_held = gather_bit(part, part_held, bit, chips)
         halves.append(part.reshape(-1, part.shape[-1]))
-    return jnp.concatenate(halves, axis=1)
-
-
-def quick_begin(gradient, chips):
+    return jnp.concatenate(halves, axis=1), token
+
+
+def corner(values):
+    return values[(0,) * (values.ndim - 2)][:16, :128]
+
+
+def quick_scatter(gradient, chips, results):
     held = list(range(group_bits(chips) - 1, -2, -1))
     cut = half_columns(gradient)
     begun = []
     for bit, part in ((-1, gradient[:, :cut]), (0, gradient[:, cut:])):
         values = part.reshape([2] * len(held) + [-1, part.shape[-1]])
         begun.append(exchange_bit(values, held, bit, chips))
-    return begun
-
-
-def quick_finish(begun, chips):
-    parts = []
-    for bit, (kept, other, held) in zip((0, -1), begun):
-        values, held = reduce_bit(add_halves(kept, other), held, bit, chips)
-        parts.append(values)
-    values = jnp.concatenate(parts, axis=-1)
+    yield tuple(corner(other) for kept, other, held in begun)
+    begun = [
+        exchange_bit(add_halves(kept, other), held, bit, chips)
+        for bit, (kept, other, held) in zip((0, -1), begun)
+    ]
+    yield tuple(corner(other) for kept, other, held in begun)
+    held = begun[0][2]
+    values = jnp.concatenate([add_halves(kept, other) for kept, other, unused in begun], axis=-1)
     for bit in range(1, group_bits(chips)):
-        values, held = reduce_bit(values, held, bit, chips)
-    return values
+        kept, other, held = exchange_bit(values, held, bit, chips)
+        yield (corner(other),)
+        values = add_halves(kept, other)
+    results.append(values)
 
 
 def gather_rows(shard, chips):
     return lax.all_gather(shard, chip_axes, axis=0, tiled=True)
-
-
-def scatter_rows(gradient, chips):
-    return lax.psum_scatter(gradient, chip_axes, scatter_dimension=0, tiled=True)
 
 
 def padded_width(width):
@@ -211,15 +214,17 @@
     return packed[:, : starts[3]], packed[:, starts[3] :]
 
 
-def unpack_weights(heads_part, hidden_part, starts, hidden):
+def unpack_hidden(packed, starts, hidden):
     step = starts[4] - starts[3]
+    last = 2 * step
+    return packed[:, :hidden], packed[:, step : step + hidden], packed[:, last : last + hidden]
+
+
+def unpack_heads(packed, starts):
     return (
-        heads_part[:, : starts[1]],
-        heads_part[:, starts[1] : starts[2]],
-        hidden_part[:, :hidden],
-        hidden_part[:, step : step + hidden],
-        hidden_part[:, 2 * step :],
-        heads_part[:, starts[2] : starts[2] + 2].T.astype(jnp.float32),
+        packed[:, : starts[1]],
+        packed[:, starts[1] : starts[2]],
+        packed[:, starts[2] : starts[2] + 2].T.astype(jnp.float32),
     )
 
 
@@ -430,7 +435,7 @@
 
 def weight_grad_kernel(choice, starts, total, left_count, *refs):
     lefts = [ref[...] for ref in refs[:left_count]]
-    rights, out_ref = refs[left_count:-1], refs[-1]
+    rights, out_ref = refs[left_count : left_count + len(choice)], refs[-1]
     for right, which, start, stop in zip(rights, choice, starts, list(starts[1:]) + [total]):
         filled = start + right.shape[1]
         if which is None:
@@ -446,7 +451,7 @@
             out_ref[:, filled:stop] = jnp.zeros((out_ref.shape[0], stop - filled), jnp.bfloat16)
 
 
-def weight_grads(lefts, rights, choice):
+def weight_grads(lefts, rights, choice, after=()):
     tokens, features = lefts[0].shape
     block = 256
     starts, total = [], 0
@@ -462,6 +467,7 @@
             specs.append(
                 pl.BlockSpec(right.shape, lambda i: (0, 0), pipeline_mode=pl.Buffered(1))
             )
+    specs += [pl.BlockSpec(memory_space=pl.ANY)] * len(after)
     return pl.pallas_call(
         functools.partial(weight_grad_kernel, choice, tuple(starts), total, len(lefts)),
         out_shape=jax.ShapeDtypeStruct((features, total), jnp.bfloat16),
@@ -474,7 +480,7 @@
             bytes_accessed=2 * (len(lefts) * tokens * features + (tokens + features) * total),
             transcendentals=0,
         ),
-    )(*lefts, *rights)
+    )(*lefts, *rights, *after)
 
 
 def product(left, right, contract):
@@ -484,7 +490,7 @@
 
 
 def forward_layer(residual, weights, tables, is_local):
-    w_qkv, w_out, w_inner, w_gate, w_down, gain_pair = weights
+    w_qkv, w_out, gain_pair, w_inner, w_gate, w_down = weights
     lowered = layer_norm(residual, gain_pair[0]).astype(jnp.bfloat16)
     projected = product(lowered, w_qkv, (1, 0))
     attended = attend_forward(projected, tables, is_local)
@@ -498,14 +504,16 @@
     return (output, kept)
 
 
-def backward_layer(upstream, weights, tables, kept, is_local, begin, after):
-    w_qkv, w_out, w_inner, w_gate, w_down, gain_pair = weights
+def backward_layer(upstream, weights, tables, kept, is_local, begin, slots):
+    w_qkv, w_out, gain_pair, w_inner, w_gate, w_down = weights
     residual, middle, lowered, lowered_two, projected, attended, inner, gate_part, activated = kept
     up_low = upstream.astype(jnp.bfloat16)
     d_activated = product(up_low, w_down, (1, 0))
     unused, pullback = jax.vjp(gelu_gate, inner, gate_part)
     d_inner, d_gate = [v.astype(jnp.bfloat16) for v in pullback(d_activated)]
-    hidden_grads = weight_grads((lowered_two, up_low), (d_inner, d_gate, activated), (0, 0, 1))
+    hidden_grads = weight_grads(
+        (lowered_two, up_low), (d_inner, d_gate, activated), (0, 0, 1), slots[0]()
+    )
     d_normed_two = core_total(
         product(d_inner, w_inner, (1, 1)) + product(d_gate, w_gate, (1, 1))
     )
@@ -516,9 +524,9 @@
     d_attended = product(d_branch, w_out, (1, 0)).astype(jnp.bfloat16)
     d_attended, hidden_grads = lax.optimization_barrier((d_attended, hidden_grads))
     hidden_begun = begin(hidden_grads)
-    d_first = attend_backward(projected, tables, d_attended, is_local, 0)
+    d_first = attend_backward(projected, tables, d_attended, is_local, 0, slots[1]())
     d_second = attend_backward(
-        projected, tables, d_attended, is_local, 1, after(hidden_begun)
+        projected, tables, d_attended, is_local, 1, slots[2]() + next(hidden_begun)
     )
     cut = d_first.shape[1]
     d_normed = core_total(
@@ -528,7 +536,10 @@
     d_in_norm, d_gain_one = pullback(d_normed)
     gains = widen(jnp.stack([d_gain_one, d_gain_two], axis=1)).astype(jnp.bfloat16)
     head_grads = weight_grads(
-        (lowered, d_branch), (d_first, d_second, attended, gains), (0, 0, 1, None)
+        (lowered, d_branch),
+        (d_first, d_second, attended, gains),
+        (0, 0, 1, None),
+        slots[3](hidden_begun),
     )
     return (d_middle + d_in_norm, (begin(head_grads), hidden_begun))
 
@@ -560,46 +571,60 @@
     local_tables = rotary_tables(theta_local)
     global_tables = rotary_tables(theta_global)
     packed = [split_packed(pack_shards(masters, layer), starts) for layer in range(2)]
-    heads_first = role_swap(packed[0][0], chips)
-    hidden_first = swap_after(packed[0][1], heads_first, chips)
-    hidden_second = swap_after(packed[1][1], hidden_first, chips)
-    heads_second = swap_after(packed[1][0], hidden_second, chips)
-    heads_all = gather_quick(heads_first, chips)
-    weights = [
-        unpack_weights(heads_all, gather_rows(hidden_first, chips), starts, hidden),
-        unpack_weights(
-            gather_quick(heads_second, chips), gather_rows(hidden_second, chips), starts, hidden
-        ),
-    ]
+    heads_all, token = gather_quick(role_swap(packed[0][0], chips), chips)
+    hidden_both = jnp.concatenate([widen(packed[0][1]), packed[1][1]], axis=1)
+    hidden_both = gather_rows(swap_after(hidden_both, token, chips), chips)
+    cut = padded_width(packed[0][1].shape[1])
+    hidden_first = unpack_hidden(hidden_both[:, :cut], starts, hidden)
+    hidden_second = unpack_hidden(hidden_both[:, cut:], starts, hidden)
     inputs = chip_sequence(hidden_in)
     upstream = chip_sequence(cotangent)
+    weights = [unpack_heads(heads_all, starts) + hidden_first]
     middle, kept_first = forward_layer(inputs, weights[0], local_tables, True)
+    heads_second = swap_after(packed[1][0], kept_first[5], chips)
+    heads_second = gather_quick(heads_second, chips)[0]
+    weights.append(unpack_heads(heads_second, starts) + hidden_second)
     output, kept_second = forward_layer(middle, weights[1], global_tables, False)
     out_arrived = arriving_sequence(output.astype(jnp.bfloat16))
-    d_middle, (heads_second, hidden_second) = backward_layer(
+    results = []
+
+    def begin(gradient):
+        results.append([])
+        return quick_scatter(gradient, chips, results[-1])
+
+    def none(*unused):
+        return ()
+
+    d_middle, (heads_steps, hidden_steps) = backward_layer(
         upstream,
         weights[1],
         global_tables,
         kept_second,
         False,
-        functools.partial(scatter_rows, chips=chips),
-        lambda begun: (out_arrived,),
+        begin,
+        (none, none, lambda: (corner(out_arrived),), none),
     )
     final_out = jnp.where(same, output.astype(jnp.bfloat16), out_arrived)
+
+    def both():
+        return next(hidden_steps) + next(heads_steps)
+
     d_values, begun_first = backward_layer(
         d_middle,
         weights[0],
         local_tables,
         kept_first,
         True,
-        functools.partial(quick_begin, chips=chips),
-        lambda begun: tuple(other for kept, other, held in begun),
-    )
-    heads_first, hidden_first = [quick_finish(begun, chips) for begun in begun_first]
+        begin,
+        (both, both, both, lambda steps: next(heads_steps) + next(steps)),
+    )
+    for steps in (hidden_steps, heads_steps, begun_first[1], begun_first[0]):
+        for unused in steps:
+            pass
+    hidden_second, heads_second, hidden_first, heads_first = [r[0] for r in results]
     shards_first = role_swap(jnp.concatenate([heads_first, hidden_first], axis=1), chips)
-    hidden_second = swap_after(hidden_second, shards_first, chips)
-    heads_second = swap_after(heads_second, hidden_second, chips)
     shards_second = jnp.concatenate([heads_second, hidden_second], axis=1)
+    shards_second = role_swap(shards_second, chips)
     grads_first, grads_second = [
         unpack_grads(packed.astype(jnp.float32), starts, hidden)
         for packed in (shards_first, shards_second)

time: 962 us -> 982 us (1.021)
  local copies, waits for them, and re-layouts: 56.1 us -> 87.3 us
  starting transfers between devices: 72.6 us -> 62.4 us
    ppermute x8 -> x12, waiting for transfers between devices: 185 us -> 74.7 us  [bit_swap(): return lax.ppermute(values, 'tensor', [(0, 1), (1, 0)])]
    ppermute x16 -> x24, waiting for transfers between devices: 120 us -> 194 us  [bit_swap(): lax.ppermute(values, 'chip', [(chip, chip ^ 1 << bit) for chip in range(c...]
    ppermute x7 -> x5, waiting for transfers between devices: 35.2 us -> 57.2 us  [role_swap(): return lax.ppermute(values, every_axis, swap_pairs(chips))]
    ppermute x2, waiting for transfers between devices: 0.01 us -> 18 us  [arriving_sequence(): return lax.ppermute(values, every_axis, result_pairs(chips))]
    ppermute x16 -> x24, starting transfers between devices: 30.8 us -> 17.2 us  [bit_swap(): lax.ppermute(values, 'chip', [(chip, chip ^ 1 << bit) for chip in range(c...]
    convert_element_type x12 -> x24, other arithmetic: 12 us -> 22.5 us  [add_halves(): (kept.astype(jnp.float32) + other.astype(jnp.float32)).astype(jnp.bfloat16)]
    unnamed x269 -> x295, local copies, waits for them, and re-layouts: 24.5 us -> 32.5 us
    ppermute x7 -> x5, starting transfers between devices: 21.4 us -> 27.6 us  [role_swap(): return lax.ppermute(values, every_axis, swap_pairs(chips))]
  transfers between devices with their start and end apart: 47 -> 54, of which waited for: 23 -> 28; matrix products, arithmetic and copies ran while one was open for 21% -> 22% of each run, Pallas kernels for 17% -> 19%
where the time goes in v6:
time: 982 us; the launch traced here: 978 us
  waiting for transfers between devices  373 us (38%)
  Pallas kernels  187 us (19%)
  matrix products  138 us (14%)
  other arithmetic  113 us (12%)
  local copies, waits for them, and re-layouts  87.3 us (9%)
  starting transfers between devices  62.4 us (6%)
  between operations  17.4 us (2%)
    ppermute x24, waiting for transfers between devices, bit_swap(): lax.ppermute(values, 'chip', [(chip, chip ^ 1 << bit) for chip in range(c...  194 us
    dot_general x22, matrix products, product(): lax.dot_general(left, right, ((contract[:1], contract[1:]), ((), ())), pr...  138 us
    pallas_call x4, Pallas kernels, attend_backward(): pl.pallas_call(functools.partial(attend_back_kernel, is_local, 128), out_...  87 us
    ppermute x12, waiting for transfers between devices, bit_swap(): return lax.ppermute(values, 'tensor', [(0, 1), (1, 0)])  74.7 us
    ppermute x5, waiting for transfers between devices, role_swap(): return lax.ppermute(values, every_axis, swap_pairs(chips))  57.2 us
    pallas_call x2, Pallas kernels, attend_forward(): pl.pallas_call(functools.partial(attend_kernel, is_local, 128), out_shape...  52.6 us
    pallas_call x4, Pallas kernels, weight_grads(): pl.pallas_call(functools.partial(weight_grad_kernel, choice, tuple(starts...  47.4 us
    unnamed x295, local copies, waits for them, and re-layouts  32.5 us
  transfers between devices with their start and end apart: 54, of which 28 were waited for; matrix products, arithmetic and copies ran while one was open for 22% of the time, Pallas kernels for 19%

profile of v6, /device:TPU:1, one launch (start us, length us, event | category | flops | bytes accessed | tf_op | source)
XLA Modules:
  0.0 977.5 jit_solution(9248122352969015364)
XLA Ops:
  22.2 7.2 collective-permute-done.2
  30.8 10.8 %collective-permute-done.3 = bf16[2,64,2176]{2,1,0:T(8,128)(2,1)S(1)} collective-permute-done((bf16[2,64,2176]{2,1,0:T(8,128)(2,1)S(1)}, bf16[2,64,2176]{2,1,0:T(8,128)(2,1)S(1)}, u32[]{:S(2)}, u32[]{:S(2)}) %collective-permute-start.3) | collective-permute-done | bytes 557088 | tf_op jit(solution)/shard_map/ppermute | solution.py:95
  44.9 14.5 %collective-permute-done.9 = bf16[64,8480]{1,0:T(8,128)(2,1)S(1)} collective-permute-done((bf16[64,8480]{1,0:T(8,128)(2,1)S(1)}, bf16[64,8480]{1,0:T(8,128)(2,1)S(1)}, u32[]{:S(2)}, u32[]{:S(2)}) %collective-permute-start.9) | collective-permute-done | bytes 1085472 | tf_op jit(solution)/shard_map/ppermute | solution.py:49
  89.3 20.9 %collective-permute-done.7 = bf16[2,2,2,64,1024]{4,3,0,1,2:T(8,128)(2,1)S(1)} collective-permute-done((bf16[2,2,2,64,1024]{4,3,0,1,2:T(8,128)(2,1)S(1)}, bf16[2,2,2,64,1024]{4,3,0,1,2:T(8,128)(2,1)S(1)}, u32[]{:S(2)}, u32[]{:S(2)}) %collective-permute-start.7) | collective-permute-done | bytes 1048608 | tf_op jit(solution)/shard_map/ppermute | solution.py:94
  118.4 19.3 %shard_map.296.refs_4_ = bf16[1024,512]{1,0:T(8,128)(2,1)S(1)} custom-call(f32[1024,1536]{1,0:T(8,128)} %fusion.34.raw_ref, f32[1024,128]{1,0:T(8,128)S(1)} %get-tuple-element.233.cos_ref, f32[1024,128]{1,0:T(8,128)S(1)} %get-tuple-element.234.sin_ref), custom_call_target="tpu_custom_call" | custom-call | flops 2147483648 | bytes 12582912 | tf_op jit(solution)/shard_map/pallas_call | solution.py:398
  137.7 16.2 %collective-permute-start.11 = (bf16[64,2304]{1,0:T(8,128)(2,1)S(1)}, bf16[64,2304]{1,0:T(8,128)(2,1)S(1)}, u32[]{:S(2)}, u32[]{:S(2)}) collective-permute-start(bf16[64,2304]{1,0:T(8,128)(2,1)S(1)} %fusion.133), channel_id=1, source_target_pairs={{0,0},{1,2},{2,1},{3,3},{4,4},{5,6},{6,5},{7,7},{8,8},{9,10},{10,9... | collective-permute-start | bytes 884744 | tf_op jit(solution)/shard_map/ppermute | solution.py:49
  158.6 16.6 %collective-permute-done.12 = bf16[64,2176]{1,0:T(8,128)(2,1)S(1)} collective-permute-done((bf16[64,2176]{1,0:T(8,128)(2,1)S(1)}, bf16[64,2176]{1,0:T(8,128)(2,1)S(1)}, u32[]{:S(2)}, u32[]{:S(2)}) %collective-permute-start.12) | collective-permute-done | bytes 278560 | tf_op jit(solution)/shard_map/ppermute | solution.py:95
  176.9 53.1 %collective-permute-done.13 = bf16[2,64,2176]{2,1,0:T(8,128)(2,1)S(1)} collective-permute-done((bf16[2,64,2176]{2,1,0:T(8,128)(2,1)S(1)}, bf16[2,64,2176]{2,1,0:T(8,128)(2,1)S(1)}, u32[]{:S(2)}, u32[]{:S(2)}) %collective-permute-start.13) | collective-permute-done | bytes 557088 | tf_op jit(solution)/shard_map/ppermute | solution.py:95
  230.5 18.3 %collective-permute-done.16 = bf16[2,2,64,1024]{3,2,0,1:T(8,128)(2,1)S(1)} collective-permute-done((bf16[2,2,64,1024]{3,2,0,1:T(8,128)(2,1)S(1)}, bf16[2,2,64,1024]{3,2,0,1:T(8,128)(2,1)S(1)}, u32[]{:S(2)}, u32[]{:S(2)}) %collective-permute-start.16) | collective-permute-done | bytes 524320 | tf_op jit(solution)/shard_map/ppermute | solution.py:95
  256.3 23.7 %all-gather.2.cloned.1.call-done = bf16[1024,8352]{1,0:T(8,128)(2,1)} async-done(((bf16[64,8352]{1,0:T(8,128)(2,1)}), bf16[1024,8352]{1,0:T(8,128)(2,1)}) %all-gather.2.cloned.1.call-update) | async-done | bytes 17104912 | tf_op jit(solution)/shard_map/all_gather | solution.py:177
  285.2 20.7 %multiply_convert_fusion.3 = (bf16[1024,1312]{1,0:T(8,128)(2,1)S(1)}, f32[1024,1312]{1,0:T(8,128)}, f32[1024,1312]{1,0:T(8,128)}) fusion(f32[1024,1312]{1,0:T(8,128)S(1)} %fusion.59, bf16[1024,1024]{1,0:T(8,128)(2,1)S(1)} %multiply_convert_fusion.6.refs_0_, bf16[1024,8352]{1,0:T(8,128)(2,1)} %all-gather.2.cloned.1.call-done), kind=kOutput, calls=%fused_computation.32 | convolution fusion | flops 2840133632 | bytes 23789568 | tf_op jit(solution)/shard_map/dot_general | solution.py:487
  331.3 33.3 %shard_map.297.refs_4_ = bf16[1024,512]{1,0:T(8,128)(2,1)S(1)} custom-call(f32[1024,1536]{1,0:T(8,128)} %fusion.31.raw_ref, f32[1024,128]{1,0:T(8,128)S(1)} %get-tuple-element.235.cos_ref, f32[1024,128]{1,0:T(8,128)S(1)} %get-tuple-element.236.sin_ref), custom_call_target="tpu_custom_call" | custom-call | flops 8589934592 | bytes 12582912 | tf_op jit(solution)/shard_map/pallas_call | solution.py:398
  384.2 21.2 %add_convert_fusion.1 = (bf16[1024,1312]{1,0:T(8,128)(2,1)}, f32[1024,1312]{1,0:T(8,128)S(1)}, f32[1024,1312]{1,0:T(8,128)}) fusion(f32[1024,1312]{1,0:T(8,128)S(1)} %fusion.43, f32[1024,1312]{1,0:T(8,128)S(1)} %fusion.47, bf16[1024,1024]{1,0:T(8,128)(2,1)S(1)} %broadcast_select_fusion.refs_1_, bf16[1024,8352]{1,0:T(8,128)(2,1)} %all-gather.2.cloned.1.call-done), kind=kOutput, calls=%fused_computation.18 | convolution fusion | flops 2849538048 | bytes 29163520 | tf_op jit(solution)/shard_map/dot_general | solution.py:487
  431.9 16.0 %shard_map.298 = bf16[1024,4128]{1,0:T(8,128)(2,1)} custom-call(bf16[1024,1024]{1,0:T(8,128)(2,1)S(1)} %copy-done.9, bf16[1024,1024]{1,0:T(8,128)(2,1)S(1)} %broadcast_select_fusion.refs_1_, bf16[1024,1312]{1,0:T(8,128)(2,1)} %get-tuple-element.145.refs_2_, bf16[1024,1312]{1,0:T(8,128)(2,1)} %copy-done.80, bf16[1024,1312]{1,0:T(8,128)(2,1)} %get-tuple-element.160.refs_4_), custom_call_target="tpu_custom_call" | custom-call | flops 8657043456 | bytes 21102592 | tf_op jit(solution)/shard_map/pallas_call | solution.py:471
  479.0 27.9 %shard_map.299.refs_2_ = bf16[1024,768]{1,0:T(8,128)(2,1)S(1)} custom-call(f32[1024,1536]{1,0:T(8,128)} %fusion.31.raw_ref, f32[1024,128]{1,0:T(8,128)S(1)} %get-tuple-element.235.cos_ref, f32[1024,128]{1,0:T(8,128)S(1)} %get-tuple-element.236.sin_ref, bf16[1024,512]{1,0:T(8,128)(2,1)S(1)} %copy-done.21), custom_call_target="tpu_custom_call" | custom-call | flops 8589934592 | bytes 12582912 | tf_op jit(solution)/shard_map/pallas_call | solution.py:418
  510.7 7.9 collective-permute-done.23
  523.5 18.0 %collective-permute-done.20 = bf16[1024,1024]{1,0:T(8,128)(2,1)} collective-permute-done((bf16[1024,1024]{1,0:T(8,128)(2,1)S(1)}, bf16[1024,1024]{1,0:T(8,128)(2,1)}, u32[]{:S(2)}, u32[]{:S(2)}) %collective-permute-start.20) | collective-permute-done | bytes 2097184 | tf_op jit(solution)/shard_map/ppermute | solution.py:567
  549.5 27.9 %shard_map.300.refs_3_ = bf16[1024,768]{1,0:T(8,128)(2,1)S(1)} custom-call(f32[1024,1536]{1,0:T(8,128)} %fusion.31.raw_ref, f32[1024,128]{1,0:T(8,128)S(1)} %get-tuple-element.235.cos_ref, f32[1024,128]{1,0:T(8,128)S(1)} %get-tuple-element.236.sin_ref, bf16[1024,512]{1,0:T(8,128)(2,1)S(1)} %copy-done.21, bf16[16,128]{1,0:T(8,128)(2,1)S(1)} %slice.457.refs_0_, ...), custom_call_target="tpu_custom_call" | custom-call | flops 8589934592 | bytes 12582912 | tf_op jit(solution)/shard_map/pallas_call | solution.py:418
  594.1 7.7 shard_map.301
  644.7 24.3 %collective-permute-done.34 = bf16[64,4128]{1,0:T(8,128)(2,1)S(1)} collective-permute-done((bf16[64,4128]{1,0:T(8,128)(2,1)S(1)}, bf16[64,4128]{1,0:T(8,128)(2,1)S(1)}, u32[]{:S(2)}, u32[]{:S(2)}) %collective-permute-start.34) | collective-permute-done | bytes 528416 | tf_op jit(solution)/shard_map/ppermute | solution.py:95
  677.1 15.9 %shard_map.302 = bf16[1024,4128]{1,0:T(8,128)(2,1)} custom-call(bf16[1024,1024]{1,0:T(8,128)(2,1)S(1)} %copy-done.7, bf16[1024,1024]{1,0:T(8,128)(2,1)S(1)} %get-tuple-element.139.refs_1_, bf16[1024,1312]{1,0:T(8,128)(2,1)} %copy-done.79, bf16[1024,1312]{1,0:T(8,128)(2,1)} %get-tuple-element.158.refs_3_, bf16[1024,1312]{1,0:T(8,128)(2,1)} %copy-done.137, ...), custom_call_target="tpu_custom_call" | custom-call | flops 8657043456 | bytes 21102592 | tf_op jit(solution)/shard_map/pallas_call | solution.py:471
  717.9 11.2 %collective-permute-done.40 = bf16[64,2176]{1,0:T(8,128)(2,1)S(1)} collective-permute-done((bf16[64,2176]{1,0:T(8,128)(2,1)S(1)}, bf16[64,2176]{1,0:T(8,128)(2,1)S(1)}, u32[]{:S(2)}, u32[]{:S(2)}) %collective-permute-start.40) | collective-permute-done | bytes 278560 | tf_op jit(solution)/shard_map/ppermute | solution.py:95
  731.7 15.6 %shard_map.303.refs_2_ = bf16[1024,768]{1,0:T(8,128)(2,1)S(1)} custom-call(f32[1024,1536]{1,0:T(8,128)} %fusion.34.raw_ref, f32[1024,128]{1,0:T(8,128)S(1)} %copy-done.1, f32[1024,128]{1,0:T(8,128)S(1)} %copy-done.3, bf16[1024,512]{1,0:T(8,128)(2,1)S(1)} %convolution_convert_fusion.2.up_ref, bf16[16,128]{1,0:T(8,128)(2,1)S(1)} %slice.473.refs_0_, ...), custom_call_target="tpu_custom_call" | custom-call | flops 2147483648 | bytes 12582912 | tf_op jit(solution)/shard_map/pallas_call | solution.py:418
  748.5 25.6 %collective-permute-done.52 = bf16[64,6304]{1,0:T(8,128)(2,1)S(1)} collective-permute-done((bf16[64,6304]{1,0:T(8,128)(2,1)S(1)}, bf16[64,6304]{1,0:T(8,128)(2,1)S(1)}, u32[]{:S(2)}, u32[]{:S(2)}) %collective-permute-start.52) | collective-permute-done | bytes 806944 | tf_op jit(solution)/shard_map/ppermute | solution.py:49
  788.3 15.6 %shard_map.304.refs_3_ = bf16[1024,768]{1,0:T(8,128)(2,1)S(1)} custom-call(f32[1024,1536]{1,0:T(8,128)} %fusion.34.raw_ref, f32[1024,128]{1,0:T(8,128)S(1)} %copy-done.1, f32[1024,128]{1,0:T(8,128)S(1)} %copy-done.3, bf16[1024,512]{1,0:T(8,128)(2,1)S(1)} %copy-done.5, bf16[16,128]{1,0:T(8,128)(2,1)S(1)} %slice.479.refs_0_, ...), custom_call_target="tpu_custom_call" | custom-call | flops 2147483648 | bytes 12582912 | tf_op jit(solution)/shard_map/pallas_call | solution.py:418
  826.2 7.7 shard_map.305
  844.6 16.1 %collective-permute-done.43 = bf16[2,2,2,64,1024]{4,3,0,1,2:T(8,128)(2,1)S(1)} collective-permute-done((bf16[2,2,2,64,1024]{4,3,0,1,2:T(8,128)(2,1)S(1)}, bf16[2,2,2,64,1024]{4,3,0,1,2:T(8,128)(2,1)S(1)}, u32[]{:S(2)}, u32[]{:S(2)}) %collective-permute-start.43) | collective-permute-done | bytes 1048608 | tf_op jit(solution)/shard_map/ppermute | solution.py:94
  866.9 7.2 collective-permute-done.44
  874.4 22.2 %collective-permute-done.46 = bf16[2,2,64,1152]{3,2,0,1:T(8,128)(2,1)S(1)} collective-permute-done((bf16[2,2,64,1152]{3,2,0,1:T(8,128)(2,1)S(1)}, bf16[2,2,64,1152]{3,2,0,1:T(8,128)(2,1)S(1)}, u32[]{:S(2)}, u32[]{:S(2)}) %collective-permute-start.46) | collective-permute-done | bytes 589856 | tf_op jit(solution)/shard_map/ppermute | solution.py:94
  898.6 22.6 %collective-permute-done.47 = bf16[2,64,2176]{2,1,0:T(8,128)(2,1)S(1)} collective-permute-done((bf16[2,64,2176]{2,1,0:T(8,128)(2,1)S(1)}, bf16[2,64,2176]{2,1,0:T(8,128)(2,1)S(1)}, u32[]{:S(2)}, u32[]{:S(2)}) %collective-permute-start.47) | collective-permute-done | bytes 557088 | tf_op jit(solution)/shard_map/ppermute | solution.py:95
  922.9 13.1 %collective-permute-done.48 = bf16[64,2176]{1,0:T(8,128)(2,1)S(1)} collective-permute-done((bf16[64,2176]{1,0:T(8,128)(2,1)S(1)}, bf16[64,2176]{1,0:T(8,128)(2,1)S(1)}, u32[]{:S(2)}, u32[]{:S(2)}) %collective-permute-start.48) | collective-permute-done | bytes 278560 | tf_op jit(solution)/shard_map/ppermute | solution.py:95
  941.8 8.0 collective-permute-done.51
  (665 shorter events, 373.7 us)
Async XLA Ops:
  7.2 272.7 %all-gather.2.cloned.1.call-start = ((), (), s32[]{:S(2)}) async-start(), calls=%async_computation | async-start | bytes 18382848 | tf_op jit(solution)/shard_map/all_gather | solution.py:177
  60.5 25.7 %collective-permute-start = (bf16[1024,1024]{1,0:T(8,128)(2,1)}, bf16[1024,1024]{1,0:T(8,128)(2,1)}, u32[]{:S(2)}, u32[]{:S(2)}) collective-permute-start(bf16[1024,1024]{1,0:T(8,128)(2,1)} %param.17), channel_id=1, source_target_pairs={{0,2},{2,0},{1,3},{3,1},{4,6},{6,4},{5,7},{7,5},{8,10},{10,8},{9,1... | collective-permute-start | bytes 6291464 | tf_op jit(solution)/shard_map/ppermute | solution.py:59
  80.2 30.0 %collective-permute-start.7 = (bf16[2,2,2,64,1024]{4,3,0,1,2:T(8,128)(2,1)S(1)}, bf16[2,2,2,64,1024]{4,3,0,1,2:T(8,128)(2,1)S(1)}, u32[]{:S(2)}, u32[]{:S(2)}) collective-permute-start(bf16[2,2,2,64,1024]{4,3,0,1,2:T(8,128)(2,1)S(1)} %pad_maximum_fusion.11), channel_id=1, source_target_pairs={{0,1},{1,0},{2,3},{3,2},{4,5},{5,4},{6,7},{7,6},{8,9},{9,8},{10,11... | collective-permute-start | bytes 3145736 | tf_op jit(solution)/shard_map/ppermute | solution.py:94
  86.1 24.6 %collective-permute-start.5 = (bf16[2,2,2,64,1152]{4,3,0,1,2:T(8,128)(2,1)S(1)}, bf16[2,2,2,64,1152]{4,3,0,1,2:T(8,128)(2,1)S(1)}, u32[]{:S(2)}, u32[]{:S(2)}) collective-permute-start(bf16[2,2,2,64,1152]{4,3,0,1,2:T(8,128)(2,1)S(1)} %pad_maximum_fusion.9), channel_id=1, source_target_pairs={{0,4},{4,0},{8,12},{12,8},{16,20},{20,16},{24,28},{28,24},{1,5},{5... | collective-permute-start | bytes 3538952 | tf_op jit(solution)/shard_map/ppermute | solution.py:95
  175.3 54.7 %collective-permute-start.13 = (bf16[2,64,2176]{2,1,0:T(8,128)(2,1)S(1)}, bf16[2,64,2176]{2,1,0:T(8,128)(2,1)S(1)}, u32[]{:S(2)}, u32[]{:S(2)}) collective-permute-start(bf16[2,64,2176]{2,1,0:T(8,128)(2,1)S(1)} %pad_maximum_fusion.17), channel_id=1, source_target_pairs={{0,8},{4,12},{8,0},{12,4},{16,24},{20,28},{24,16},{28,20},{1,9},{5... | collective-permute-start | bytes 1671176 | tf_op jit(solution)/shard_map/ppermute | solution.py:95
  176.7 76.0 %collective-permute-start.8 = (bf16[1024,1024]{1,0:T(8,128)(2,1)S(1)}, bf16[1024,1024]{1,0:T(8,128)(2,1)S(1)}, u32[]{:S(2)}, u32[]{:S(2)}) collective-permute-start(bf16[1024,1024]{1,0:T(8,128)(2,1)S(1)} %convolution_convert_fusion.1), channel_id=1, source_target_pairs={{0,2},{2,0},{1,3},{3,1},{4,6},{6,4},{5,7},{7,5},{8,10},{10,8},{9,1... | collective-permute-start | bytes 6291464 | tf_op jit(solution)/shard_map/ppermute | solution.py:59
  250.2 65.2 %collective-permute-start.17 = (bf16[2,2,2,64,1024]{4,3,0,1,2:T(8,128)(2,1)}, bf16[2,2,2,64,1024]{4,3,0,1,2:T(8,128)(2,1)}, u32[]{:S(2)}, u32[]{:S(2)}) collective-permute-start(bf16[2,2,2,64,1024]{4,3,0,1,2:T(8,128)(2,1)} %pad_maximum_fusion.12), channel_id=1, source_target_pairs={{0,1},{1,0},{2,3},{3,2},{4,5},{5,4},{6,7},{7,6},{8,9},{9,8},{10,11... | collective-permute-start | bytes 3145736 | tf_op jit(solution)/shard_map/ppermute | solution.py:94
  251.8 65.6 %collective-permute-start.15 = (bf16[2,2,2,64,1152]{4,3,0,1,2:T(8,128)(2,1)}, bf16[2,2,2,64,1152]{4,3,0,1,2:T(8,128)(2,1)}, u32[]{:S(2)}, u32[]{:S(2)}) collective-permute-start(bf16[2,2,2,64,1152]{4,3,0,1,2:T(8,128)(2,1)} %pad_maximum_fusion.10), channel_id=1, source_target_pairs={{0,4},{4,0},{8,12},{12,8},{16,20},{20,16},{24,28},{28,24},{1,5},{5... | collective-permute-start | bytes 3538952 | tf_op jit(solution)/shard_map/ppermute | solution.py:95
  314.5 51.9 %collective-permute-start.21 = (bf16[1024,1024]{1,0:T(8,128)(2,1)S(1)}, bf16[1024,1024]{1,0:T(8,128)(2,1)S(1)}, u32[]{:S(2)}, u32[]{:S(2)}) collective-permute-start(bf16[1024,1024]{1,0:T(8,128)(2,1)S(1)} %copy-done.84), channel_id=1, source_target_pairs={{0,2},{2,0},{1,3},{3,1},{4,6},{6,4},{5,7},{7,5},{8,10},{10,8},{9,1... | collective-permute-start | bytes 6291464 | tf_op jit(solution)/shard_map/ppermute | solution.py:59
  422.9 25.1 %collective-permute-start.22 = (bf16[1024,1024]{1,0:T(8,128)(2,1)}, bf16[1024,1024]{1,0:T(8,128)(2,1)}, u32[]{:S(2)}, u32[]{:S(2)}) collective-permute-start(bf16[1024,1024]{1,0:T(8,128)(2,1)} %add_convert_fusion.6), channel_id=1, source_target_pairs={{0,2},{2,0},{1,3},{3,1},{4,6},{6,4},{5,7},{7,5},{8,10},{10,8},{9,1... | collective-permute-start | bytes 6291464 | tf_op jit(solution)/shard_map/ppermute | solution.py:59
  468.8 49.7 %collective-permute-start.23 = (bf16[2,2,2,64,2048]{4,3,0,1,2:T(8,128)(2,1)}, bf16[2,2,2,64,2048]{4,3,0,1,2:T(8,128)(2,1)}, u32[]{:S(2)}, u32[]{:S(2)}) collective-permute-start(bf16[2,2,2,64,2048]{4,3,0,1,2:T(8,128)(2,1)} %bitcast.352), channel_id=1, source_target_pairs={{0,1},{1,0},{2,3},{3,2},{4,5},{5,4},{6,7},{7,6},{8,9},{9,8},{10,11... | collective-permute-start | bytes 6291464 | tf_op jit(solution)/shard_map/ppermute | solution.py:94
  476.8 68.4 %collective-permute-start.24 = (bf16[2,2,2,64,2080]{4,3,0,1,2:T(8,128)(2,1)}, bf16[2,2,2,64,2080]{4,3,0,1,2:T(8,128)(2,1)}, u32[]{:S(2)}, u32[]{:S(2)}) collective-permute-start(bf16[2,2,2,64,2080]{4,3,0,1,2:T(8,128)(2,1)} %bitcast.350), channel_id=1, source_target_pairs={{0,4},{4,0},{8,12},{12,8},{16,20},{20,16},{24,28},{28,24},{1,5},{5... | collective-permute-start | bytes 6389768 | tf_op jit(solution)/shard_map/ppermute | solution.py:95
  477.5 63.9 %collective-permute-start.20 = (bf16[1024,1024]{1,0:T(8,128)(2,1)S(1)}, bf16[1024,1024]{1,0:T(8,128)(2,1)}, u32[]{:S(2)}, u32[]{:S(2)}) collective-permute-start(bf16[1024,1024]{1,0:T(8,128)(2,1)S(1)} %copy-done.54), channel_id=1, source_target_pairs={{0,1},{3,2},{4,5},{7,6},{8,9},{11,10},{12,13},{15,14},{16,17},{19,... | collective-permute-start | bytes 6291464 | tf_op jit(solution)/shard_map/ppermute | solution.py:567
  523.1 61.7 %collective-permute-start.27 = (bf16[2,2,64,2048]{3,2,0,1:T(8,128)(2,1)}, bf16[2,2,64,2048]{3,2,0,1:T(8,128)(2,1)S(1)}, u32[]{:S(2)}, u32[]{:S(2)}) collective-permute-start(bf16[2,2,64,2048]{3,2,0,1:T(8,128)(2,1)} %dynamic-slice_bitcast_fusion.3), channel_id=1, source_target_pairs={{0,4},{4,0},{8,12},{12,8},{16,20},{20,16},{24,28},{28,24},{1,5},{5... | collective-permute-start | bytes 3145736 | tf_op jit(solution)/shard_map/ppermute | solution.py:95
  549.5 35.9 %collective-permute-start.28 = (bf16[2,2,64,2080]{3,2,0,1:T(8,128)(2,1)}, bf16[2,2,64,2080]{3,2,0,1:T(8,128)(2,1)S(1)}, u32[]{:S(2)}, u32[]{:S(2)}) collective-permute-start(bf16[2,2,64,2080]{3,2,0,1:T(8,128)(2,1)} %dynamic-slice_bitcast_fusion.1), channel_id=1, source_target_pairs={{0,1},{1,0},{2,3},{3,2},{4,5},{5,4},{6,7},{7,6},{8,9},{9,8},{10,11... | collective-permute-start | bytes 3194888 | tf_op jit(solution)/shard_map/ppermute | solution.py:94
  586.8 54.1 %collective-permute-start.31 = (bf16[2,64,4128]{2,1,0:T(8,128)(2,1)}, bf16[2,64,4128]{2,1,0:T(8,128)(2,1)}, u32[]{:S(2)}, u32[]{:S(2)}) collective-permute-start(bf16[2,64,4128]{2,1,0:T(8,128)(2,1)} %fusion.100), channel_id=1, source_target_pairs={{0,8},{4,12},{8,0},{12,4},{16,24},{20,28},{24,16},{28,20},{1,9},{5... | collective-permute-start | bytes 3170312 | tf_op jit(solution)/shard_map/ppermute | solution.py:95
  605.6 63.5 %collective-permute-start.29 = (bf16[2,2,2,64,1024]{4,3,0,1,2:T(8,128)(2,1)}, bf16[2,2,2,64,1024]{4,3,0,1,2:T(8,128)(2,1)}, u32[]{:S(2)}, u32[]{:S(2)}) collective-permute-start(bf16[2,2,2,64,1024]{4,3,0,1,2:T(8,128)(2,1)} %bitcast.356), channel_id=1, source_target_pairs={{0,1},{1,0},{2,3},{3,2},{4,5},{5,4},{6,7},{7,6},{8,9},{9,8},{10,11... | collective-permute-start | bytes 3145736 | tf_op jit(solution)/shard_map/ppermute | solution.py:94
  607.0 65.3 %collective-permute-start.30 = (bf16[2,2,2,64,1152]{4,3,0,1,2:T(8,128)(2,1)}, bf16[2,2,2,64,1152]{4,3,0,1,2:T(8,128)(2,1)}, u32[]{:S(2)}, u32[]{:S(2)}) collective-permute-start(bf16[2,2,2,64,1152]{4,3,0,1,2:T(8,128)(2,1)} %bitcast.354), channel_id=1, source_target_pairs={{0,4},{4,0},{8,12},{12,8},{16,20},{20,16},{24,28},{28,24},{1,5},{5... | collective-permute-start | bytes 3538952 | tf_op jit(solution)/shard_map/ppermute | solution.py:95
  640.4 53.2 %collective-permute-start.26 = (bf16[1024,1024]{1,0:T(8,128)(2,1)S(1)}, bf16[1024,1024]{1,0:T(8,128)(2,1)S(1)}, u32[]{:S(2)}, u32[]{:S(2)}) collective-permute-start(bf16[1024,1024]{1,0:T(8,128)(2,1)S(1)} %add_convert_fusion.4), channel_id=1, source_target_pairs={{0,2},{2,0},{1,3},{3,1},{4,6},{6,4},{5,7},{7,5},{8,10},{10,8},{9,1... | collective-permute-start | bytes 6291464 | tf_op jit(solution)/shard_map/ppermute | solution.py:59
  642.7 26.3 %collective-permute-start.34 = (bf16[64,4128]{1,0:T(8,128)(2,1)S(1)}, bf16[64,4128]{1,0:T(8,128)(2,1)S(1)}, u32[]{:S(2)}, u32[]{:S(2)}) collective-permute-start(bf16[64,4128]{1,0:T(8,128)(2,1)S(1)} %dynamic-slice_bitcast_fusion.7), channel_id=1, source_target_pairs={{0,16},{4,20},{8,24},{12,28},{16,0},{20,4},{24,8},{28,12},{1,17},{... | collective-permute-start | bytes 1585160 | tf_op jit(solution)/shard_map/ppermute | solution.py:95
  712.6 71.3 %collective-permute-start.37 = (bf16[2,2,2,64,2080]{4,3,1,0,2:T(8,128)(2,1)}, bf16[2,2,2,64,2080]{4,3,1,0,2:T(8,128)(2,1)}, u32[]{:S(2)}, u32[]{:S(2)}) collective-permute-start(bf16[2,2,2,64,2080]{4,3,1,0,2:T(8,128)(2,1)} %bitcast.349), channel_id=1, source_target_pairs={{0,4},{4,0},{8,12},{12,8},{16,20},{20,16},{24,28},{28,24},{1,5},{5... | collective-permute-start | bytes 6389768 | tf_op jit(solution)/shard_map/ppermute | solution.py:95
  717.8 60.5 %collective-permute-start.36 = (bf16[2,2,2,64,2048]{4,3,1,0,2:T(8,128)(2,1)}, bf16[2,2,2,64,2048]{4,3,1,0,2:T(8,128)(2,1)}, u32[]{:S(2)}, u32[]{:S(2)}) collective-permute-start(bf16[2,2,2,64,2048]{4,3,1,0,2:T(8,128)(2,1)} %bitcast.351), channel_id=1, source_target_pairs={{0,1},{1,0},{2,3},{3,2},{4,5},{5,4},{6,7},{7,6},{8,9},{9,8},{10,11... | collective-permute-start | bytes 6291464 | tf_op jit(solution)/shard_map/ppermute | solution.py:94
  729.2 45.0 %collective-permute-start.52 = (bf16[64,6304]{1,0:T(8,128)(2,1)S(1)}, bf16[64,6304]{1,0:T(8,128)(2,1)S(1)}, u32[]{:S(2)}, u32[]{:S(2)}) collective-permute-start(bf16[64,6304]{1,0:T(8,128)(2,1)S(1)} %pad_maximum_fusion.14), channel_id=1, source_target_pairs={{0,0},{1,2},{2,1},{3,3},{4,4},{5,6},{6,5},{7,7},{8,8},{9,10},{10,9... | collective-permute-start | bytes 2420744 | tf_op jit(solution)/shard_map/ppermute | solution.py:49
  783.4 25.5 %collective-permute-start.41 = (bf16[2,2,64,2048]{3,2,1,0:T(8,128)(2,1)}, bf16[2,2,64,2048]{3,2,1,0:T(8,128)(2,1)}, u32[]{:S(2)}, u32[]{:S(2)}) collective-permute-start(bf16[2,2,64,2048]{3,2,1,0:T(8,128)(2,1)} %dynamic-slice_bitcast_fusion.2), channel_id=1, source_target_pairs={{0,4},{4,0},{8,12},{12,8},{16,20},{20,16},{24,28},{28,24},{1,5},{5... | collective-permute-start | bytes 3145736 | tf_op jit(solution)/shard_map/ppermute | solution.py:95
  788.3 26.3 %collective-permute-start.42 = (bf16[2,2,64,2080]{3,2,1,0:T(8,128)(2,1)}, bf16[2,2,64,2080]{3,2,1,0:T(8,128)(2,1)}, u32[]{:S(2)}, u32[]{:S(2)}) collective-permute-start(bf16[2,2,64,2080]{3,2,1,0:T(8,128)(2,1)} %dynamic-slice_bitcast_fusion), channel_id=1, source_target_pairs={{0,1},{1,0},{2,3},{3,2},{4,5},{5,4},{6,7},{7,6},{8,9},{9,8},{10,11... | collective-permute-start | bytes 3194888 | tf_op jit(solution)/shard_map/ppermute | solution.py:94
  818.7 46.7 %collective-permute-start.49 = (bf16[2,64,4128]{2,1,0:T(8,128)(2,1)}, bf16[2,64,4128]{2,1,0:T(8,128)(2,1)}, u32[]{:S(2)}, u32[]{:S(2)}) collective-permute-start(bf16[2,64,4128]{2,1,0:T(8,128)(2,1)} %fusion.94), channel_id=1, source_target_pairs={{0,8},{4,12},{8,0},{12,4},{16,24},{20,28},{24,16},{28,20},{1,9},{5... | collective-permute-start | bytes 3170312 | tf_op jit(solution)/shard_map/ppermute | solution.py:95
  836.6 24.1 %collective-permute-start.43 = (bf16[2,2,2,64,1024]{4,3,0,1,2:T(8,128)(2,1)S(1)}, bf16[2,2,2,64,1024]{4,3,0,1,2:T(8,128)(2,1)S(1)}, u32[]{:S(2)}, u32[]{:S(2)}) collective-permute-start(bf16[2,2,2,64,1024]{4,3,0,1,2:T(8,128)(2,1)S(1)} %bitcast.398), channel_id=1, source_target_pairs={{0,1},{1,0},{2,3},{3,2},{4,5},{5,4},{6,7},{7,6},{8,9},{9,8},{10,11... | collective-permute-start | bytes 3145736 | tf_op jit(solution)/shard_map/ppermute | solution.py:94
  837.0 26.0 %collective-permute-start.45 = (bf16[2,2,2,64,1152]{4,3,0,1,2:T(8,128)(2,1)S(1)}, bf16[2,2,2,64,1152]{4,3,0,1,2:T(8,128)(2,1)S(1)}, u32[]{:S(2)}, u32[]{:S(2)}) collective-permute-start(bf16[2,2,2,64,1152]{4,3,0,1,2:T(8,128)(2,1)S(1)} %bitcast.395), channel_id=1, source_target_pairs={{0,4},{4,0},{8,12},{12,8},{16,20},{20,16},{24,28},{28,24},{1,5},{5... | collective-permute-start | bytes 3538952 | tf_op jit(solution)/shard_map/ppermute | solution.py:95
  843.3 96.3 %collective-permute-start.39 = (bf16[1024,1024]{1,0:T(8,128)(2,1)S(1)}, bf16[1024,1024]{1,0:T(8,128)(2,1)S(1)}, u32[]{:S(2)}, u32[]{:S(2)}) collective-permute-start(bf16[1024,1024]{1,0:T(8,128)(2,1)S(1)} %add_convert_fusion.2), channel_id=1, source_target_pairs={{0,1},{3,2},{4,5},{7,6},{8,9},{11,10},{12,13},{15,14},{16,17},{19,... | collective-permute-start | bytes 6291464 | tf_op jit(solution)/shard_map/ppermute | solution.py:567
  863.4 33.2 %collective-permute-start.46 = (bf16[2,2,64,1152]{3,2,0,1:T(8,128)(2,1)S(1)}, bf16[2,2,64,1152]{3,2,0,1:T(8,128)(2,1)S(1)}, u32[]{:S(2)}, u32[]{:S(2)}) collective-permute-start(bf16[2,2,64,1152]{3,2,0,1:T(8,128)(2,1)S(1)} %dynamic-slice_bitcast_fusion.4), channel_id=1, source_target_pairs={{0,1},{1,0},{2,3},{3,2},{4,5},{5,4},{6,7},{7,6},{8,9},{9,8},{10,11... | collective-permute-start | bytes 1769480 | tf_op jit(solution)/shard_map/ppermute | solution.py:94
  896.9 24.3 %collective-permute-start.47 = (bf16[2,64,2176]{2,1,0:T(8,128)(2,1)S(1)}, bf16[2,64,2176]{2,1,0:T(8,128)(2,1)S(1)}, u32[]{:S(2)}, u32[]{:S(2)}) collective-permute-start(bf16[2,64,2176]{2,1,0:T(8,128)(2,1)S(1)} %fusion.120), channel_id=1, source_target_pairs={{0,8},{4,12},{8,0},{12,4},{16,24},{20,28},{24,16},{28,20},{1,9},{5... | collective-permute-start | bytes 1671176 | tf_op jit(solution)/shard_map/ppermute | solution.py:95
  897.0 25.8 %collective-permute-start.50 = (bf16[64,4128]{1,0:T(8,128)(2,1)S(1)}, bf16[64,4128]{1,0:T(8,128)(2,1)S(1)}, u32[]{:S(2)}, u32[]{:S(2)}) collective-permute-start(bf16[64,4128]{1,0:T(8,128)(2,1)S(1)} %dynamic-slice_bitcast_fusion.6), channel_id=1, source_target_pairs={{0,16},{4,20},{8,24},{12,28},{16,0},{20,4},{24,8},{28,12},{1,17},{... | collective-permute-start | bytes 1585160 | tf_op jit(solution)/shard_map/ppermute | solution.py:95
  (175 other events, 1811.4 us)
Sparse Core Ops, SparseCore 0:
  60.6 219.2 all-gather.1

commit v7 on v6

--- a/solution.py
+++ b/solution.py
@@ -126,6 +126,10 @@
 def reduce_bit(values, held, bit, chips):
     kept, other, held = exchange_bit(values, held, bit, chips)
     return add_halves(kept, other), held
+
+
+def scatter_rows(gradient, chips):
+    return lax.psum_scatter(gradient, chip_axes, scatter_dimension=0, tiled=True)
 
 
 def half_columns(values):
@@ -310,7 +314,7 @@
         )
         out_ref[here, :] = pair_unstack(mixed).astype(jnp.bfloat16)
 
-    pl.loop(0, length // block, unroll=2)(step)
+    pl.loop(0, length // block, unroll=4 if is_local else 2)(step)
 
 
 def attend_back_kernel(is_local, block, raw_ref, cos_ref, sin_ref, up_ref, *refs):
@@ -359,7 +363,7 @@
             d_query * cos_ref[here, :] - rolled(d_query) * sin_ref[here, :]
         ).astype(jnp.bfloat16)
 
-    pl.loop(0, length // block, unroll=2)(step)
+    pl.loop(0, length // block, unroll=4 if is_local else 2)(step)
     d_key = d_keys[pl.ds(pad, length), :]
     out_ref[:, wide : 2 * wide] = (d_key * cos_ref[...] - rolled(d_key) * sin_ref[...]).astype(
         jnp.bfloat16
@@ -526,7 +530,7 @@
     hidden_begun = begin(hidden_grads)
     d_first = attend_backward(projected, tables, d_attended, is_local, 0, slots[1]())
     d_second = attend_backward(
-        projected, tables, d_attended, is_local, 1, slots[2]() + next(hidden_begun)
+        projected, tables, d_attended, is_local, 1, slots[2]()
     )
     cut = d_first.shape[1]
     d_normed = core_total(
@@ -587,6 +591,10 @@
     output, kept_second = forward_layer(middle, weights[1], global_tables, False)
     out_arrived = arriving_sequence(output.astype(jnp.bfloat16))
     results = []
+    by_call = []
+
+    def begin_call(gradient):
+        by_call.append((corner(gradient), scatter_rows(gradient, chips)))
 
     def begin(gradient):
         results.append([])
@@ -595,20 +603,17 @@
     def none(*unused):
         return ()
 
-    d_middle, (heads_steps, hidden_steps) = backward_layer(
+    d_middle, unused = backward_layer(
         upstream,
         weights[1],
         global_tables,
         kept_second,
         False,
-        begin,
+        begin_call,
         (none, none, lambda: (corner(out_arrived),), none),
     )
     final_out = jnp.where(same, output.astype(jnp.bfloat16), out_arrived)
-
-    def both():
-        return next(hidden_steps) + next(heads_steps)
-
+    hidden_second, heads_second = by_call
     d_values, begun_first = backward_layer(
         d_middle,
         weights[0],
@@ -616,15 +621,16 @@
         kept_first,
         True,
         begin,
-        (both, both, both, lambda steps: next(heads_steps) + next(steps)),
-    )
-    for steps in (hidden_steps, heads_steps, begun_first[1], begun_first[0]):
+        (lambda: (heads_second[0],), none, none, next),
+    )
+    for steps in (begun_first[1], begun_first[0]):
         for unused in steps:
             pass
-    hidden_second, heads_second, hidden_first, heads_first = [r[0] for r in results]
+    hidden_first, heads_first = [r[0] for r in results]
     shards_first = role_swap(jnp.concatenate([heads_first, hidden_first], axis=1), chips)
+    hidden_second = swap_after(hidden_second[1], shards_first, chips)
+    heads_second = swap_after(heads_second[1], hidden_second, chips)
     shards_second = jnp.concatenate([heads_second, hidden_second], axis=1)
-    shards_second = role_swap(shards_second, chips)
     grads_first, grads_second = [
         unpack_grads(packed.astype(jnp.float32), starts, hidden)
         for packed in (shards_first, shards_second)

time: 982 us -> 1010 us (1.029)
  waiting for transfers between devices: 373 us -> 446 us
  local copies, waits for them, and re-layouts: 87.3 us -> 56.1 us
    ppermute x12 -> x8, waiting for transfers between devices: 74.7 us -> 205 us  [bit_swap(): return lax.ppermute(values, 'tensor', [(0, 1), (1, 0)])]
    ppermute x5 -> x6, waiting for transfers between devices: 57.2 us -> 35.2 us  [role_swap(): return lax.ppermute(values, every_axis, swap_pairs(chips))]
    ppermute x24 -> x16, waiting for transfers between devices: 194 us -> 173 us  [bit_swap(): lax.ppermute(values, 'chip', [(chip, chip ^ 1 << bit) for chip in range(c...]
    ppermute x2, waiting for transfers between devices: 18 us -> 0.01 us  [arriving_sequence(): return lax.ppermute(values, every_axis, result_pairs(chips))]
    convert_element_type x24 -> x12, other arithmetic: 22.5 us -> 8.92 us  [add_halves(): (kept.astype(jnp.float32) + other.astype(jnp.float32)).astype(jnp.bfloat16)]
    ppermute x5 -> x6, starting transfers between devices: 27.6 us -> 36.3 us  [role_swap(): return lax.ppermute(values, every_axis, swap_pairs(chips))]
    unnamed x295 -> x219, local copies, waits for them, and re-layouts: 32.5 us -> 24.1 us
  transfers between devices with their start and end apart: 54 -> 45, of which waited for: 28 -> 25; matrix products, arithmetic and copies ran while one was open for 22% -> 19% of each run, Pallas kernels for 19% -> 18%
where the time goes in v7:
time: 1010 us
  waiting for transfers between devices  446 us (44%)
  Pallas kernels  181 us (18%)
  matrix products  132 us (13%)
  other arithmetic  114 us (11%)
  starting transfers between devices  61.6 us (6%)
  local copies, waits for them, and re-layouts  56.1 us (6%)
  between operations  16.4 us (2%)
    ppermute x8, waiting for transfers between devices, bit_swap(): return lax.ppermute(values, 'tensor', [(0, 1), (1, 0)])  205 us
    ppermute x16, waiting for transfers between devices, bit_swap(): lax.ppermute(values, 'chip', [(chip, chip ^ 1 << bit) for chip in range(c...  173 us
    dot_general x22, matrix products, product(): lax.dot_general(left, right, ((contract[:1], contract[1:]), ((), ())), pr...  132 us
    pallas_call x4, Pallas kernels, attend_backward(): pl.pallas_call(functools.partial(attend_back_kernel, is_local, 128), out_...  82.1 us
    pallas_call x2, Pallas kernels, attend_forward(): pl.pallas_call(functools.partial(attend_kernel, is_local, 128), out_shape...  50.3 us
    pallas_call x4, Pallas kernels, weight_grads(): pl.pallas_call(functools.partial(weight_grad_kernel, choice, tuple(starts...  48.7 us
    ppermute x6, starting transfers between devices, role_swap(): return lax.ppermute(values, every_axis, swap_pairs(chips))  36.3 us
    ppermute x6, waiting for transfers between devices, role_swap(): return lax.ppermute(values, every_axis, swap_pairs(chips))  35.2 us
  transfers between devices with their start and end apart: 45, of which 25 were waited for; matrix products, arithmetic and copies ran while one was open for 19% of the time, Pallas kernels for 18%

profile of v7, /device:TPU:1, one launch (start us, length us, event | category | flops | bytes accessed | tf_op | source)
XLA Modules:
  0.0 1007.2 jit_solution(13390482027270292438)
XLA Ops:
  23.7 7.2 collective-permute-done.2
  32.3 10.8 %collective-permute-done.3 = bf16[2,64,2176]{2,1,0:T(8,128)(2,1)S(1)} collective-permute-done((bf16[2,64,2176]{2,1,0:T(8,128)(2,1)S(1)}, bf16[2,64,2176]{2,1,0:T(8,128)(2,1)S(1)}, u32[]{:S(2)}, u32[]{:S(2)}) %collective-permute-start.3) | collective-permute-done | bytes 557088 | tf_op jit(solution)/shard_map/ppermute | solution.py:95
  47.8 14.7 %collective-permute-done.9 = bf16[64,8480]{1,0:T(8,128)(2,1)S(1)} collective-permute-done((bf16[64,8480]{1,0:T(8,128)(2,1)S(1)}, bf16[64,8480]{1,0:T(8,128)(2,1)S(1)}, u32[]{:S(2)}, u32[]{:S(2)}) %collective-permute-start.9) | collective-permute-done | bytes 1085472 | tf_op jit(solution)/shard_map/ppermute | solution.py:49
  75.0 7.5 collective-permute-done.6
  93.0 20.9 %collective-permute-done.7 = bf16[2,2,2,64,1024]{4,3,0,1,2:T(8,128)(2,1)S(1)} collective-permute-done((bf16[2,2,2,64,1024]{4,3,0,1,2:T(8,128)(2,1)S(1)}, bf16[2,2,2,64,1024]{4,3,0,1,2:T(8,128)(2,1)S(1)}, u32[]{:S(2)}, u32[]{:S(2)}) %collective-permute-start.7) | collective-permute-done | bytes 1048608 | tf_op jit(solution)/shard_map/ppermute | solution.py:94
  122.1 16.9 %shard_map.296.refs_4_ = bf16[1024,512]{1,0:T(8,128)(2,1)S(1)} custom-call(f32[1024,1536]{1,0:T(8,128)} %fusion.32.raw_ref, f32[1024,128]{1,0:T(8,128)S(1)} %get-tuple-element.223.cos_ref, f32[1024,128]{1,0:T(8,128)S(1)} %get-tuple-element.224.sin_ref), custom_call_target="tpu_custom_call" | custom-call | flops 2147483648 | bytes 12582912 | tf_op jit(solution)/shard_map/pallas_call | solution.py:402
  139.1 17.0 %collective-permute-start.11 = (bf16[64,2304]{1,0:T(8,128)(2,1)S(1)}, bf16[64,2304]{1,0:T(8,128)(2,1)S(1)}, u32[]{:S(2)}, u32[]{:S(2)}) collective-permute-start(bf16[64,2304]{1,0:T(8,128)(2,1)S(1)} %fusion.113), channel_id=1, source_target_pairs={{0,0},{1,2},{2,1},{3,3},{4,4},{5,6},{6,5},{7,7},{8,8},{9,10},{10,9... | collective-permute-start | bytes 884744 | tf_op jit(solution)/shard_map/ppermute | solution.py:49
  160.5 18.4 %collective-permute-done.12 = bf16[64,2176]{1,0:T(8,128)(2,1)S(1)} collective-permute-done((bf16[64,2176]{1,0:T(8,128)(2,1)S(1)}, bf16[64,2176]{1,0:T(8,128)(2,1)S(1)}, u32[]{:S(2)}, u32[]{:S(2)}) %collective-permute-start.12) | collective-permute-done | bytes 278560 | tf_op jit(solution)/shard_map/ppermute | solution.py:95
  180.6 53.0 %collective-permute-done.13 = bf16[2,64,2176]{2,1,0:T(8,128)(2,1)S(1)} collective-permute-done((bf16[2,64,2176]{2,1,0:T(8,128)(2,1)S(1)}, bf16[2,64,2176]{2,1,0:T(8,128)(2,1)S(1)}, u32[]{:S(2)}, u32[]{:S(2)}) %collective-permute-start.13) | collective-permute-done | bytes 557088 | tf_op jit(solution)/shard_map/ppermute | solution.py:95
  234.0 19.7 %collective-permute-done.16 = bf16[2,2,64,1024]{3,2,0,1:T(8,128)(2,1)S(1)} collective-permute-done((bf16[2,2,64,1024]{3,2,0,1:T(8,128)(2,1)S(1)}, bf16[2,2,64,1024]{3,2,0,1:T(8,128)(2,1)S(1)}, u32[]{:S(2)}, u32[]{:S(2)}) %collective-permute-start.16) | collective-permute-done | bytes 524320 | tf_op jit(solution)/shard_map/ppermute | solution.py:95
  261.3 27.7 %all-gather.2.cloned.1.call-done = bf16[1024,8352]{1,0:T(8,128)(2,1)} async-done(((bf16[64,8352]{1,0:T(8,128)(2,1)}), bf16[1024,8352]{1,0:T(8,128)(2,1)}) %all-gather.2.cloned.1.call-update) | async-done | bytes 17104912 | tf_op jit(solution)/shard_map/all_gather | solution.py:181
  294.2 20.5 %multiply_convert_fusion.3 = (bf16[1024,1312]{1,0:T(8,128)(2,1)S(1)}, f32[1024,1312]{1,0:T(8,128)}, f32[1024,1312]{1,0:T(8,128)}) fusion(f32[1024,1312]{1,0:T(8,128)S(1)} %fusion.57, bf16[1024,1024]{1,0:T(8,128)(2,1)S(1)} %multiply_convert_fusion.6.refs_0_, bf16[1024,8352]{1,0:T(8,128)(2,1)} %all-gather.2.cloned.1.call-done), kind=kOutput, calls=%fused_computation.32 | convolution fusion | flops 2840133632 | bytes 23789568 | tf_op jit(solution)/shard_map/dot_general | solution.py:491
  338.1 33.4 %shard_map.297.refs_4_ = bf16[1024,512]{1,0:T(8,128)(2,1)S(1)} custom-call(f32[1024,1536]{1,0:T(8,128)} %fusion.29.raw_ref, f32[1024,128]{1,0:T(8,128)S(1)} %get-tuple-element.225.cos_ref, f32[1024,128]{1,0:T(8,128)S(1)} %get-tuple-element.226.sin_ref), custom_call_target="tpu_custom_call" | custom-call | flops 8589934592 | bytes 12582912 | tf_op jit(solution)/shard_map/pallas_call | solution.py:402
  390.3 21.7 %add_convert_fusion.1 = (bf16[1024,1312]{1,0:T(8,128)(2,1)}, f32[1024,1312]{1,0:T(8,128)}, f32[1024,1312]{1,0:T(8,128)}) fusion(f32[1024,1312]{1,0:T(8,128)S(1)} %fusion.41, f32[1024,1312]{1,0:T(8,128)S(1)} %fusion.45, bf16[1024,1024]{1,0:T(8,128)(2,1)S(1)} %broadcast_select_fusion.refs_1_, bf16[1024,8352]{1,0:T(8,128)(2,1)} %all-gather.2.cloned.1.call-done), kind=kOutput, calls=%fused_computation.18 | convolution fusion | flops 2849538048 | bytes 29163520 | tf_op jit(solution)/shard_map/dot_general | solution.py:491
  417.1 7.4 fusion.39
  437.9 16.1 %shard_map.298 = bf16[1024,4128]{1,0:T(8,128)(2,1)} custom-call(bf16[1024,1024]{1,0:T(8,128)(2,1)S(1)} %multiply_convert_fusion.4.refs_0_, bf16[1024,1024]{1,0:T(8,128)(2,1)S(1)} %broadcast_select_fusion.refs_1_, bf16[1024,1312]{1,0:T(8,128)(2,1)} %get-tuple-element.145.refs_2_, bf16[1024,1312]{1,0:T(8,128)(2,1)} %copy-done.47, bf16[1024,1312]{1,0:T(8,128)(2,1)} %copy-done.48), custom_call_target="tpu_custom_call" | custom-call | flops 8657043456 | bytes 21102592 | tf_op jit(solution)/shard_map/pallas_call | solution.py:475
  473.0 27.9 %shard_map.299.refs_2_ = bf16[1024,768]{1,0:T(8,128)(2,1)S(1)} custom-call(f32[1024,1536]{1,0:T(8,128)} %fusion.29.raw_ref, f32[1024,128]{1,0:T(8,128)S(1)} %get-tuple-element.225.cos_ref, f32[1024,128]{1,0:T(8,128)S(1)} %get-tuple-element.226.sin_ref, bf16[1024,512]{1,0:T(8,128)(2,1)S(1)} %copy-done.16), custom_call_target="tpu_custom_call" | custom-call | flops 8589934592 | bytes 12582912 | tf_op jit(solution)/shard_map/pallas_call | solution.py:422
  503.4 27.9 %shard_map.300.refs_3_ = bf16[1024,768]{1,0:T(8,128)(2,1)S(1)} custom-call(f32[1024,1536]{1,0:T(8,128)} %fusion.29.raw_ref, f32[1024,128]{1,0:T(8,128)S(1)} %get-tuple-element.225.cos_ref, f32[1024,128]{1,0:T(8,128)S(1)} %get-tuple-element.226.sin_ref, bf16[1024,512]{1,0:T(8,128)(2,1)S(1)} %copy-done.16, bf16[16,128]{1,0:T(8,128)(2,1)S(1)} %slice.358.refs_0_), custom_call_target="tpu_custom_call" | custom-call | flops 8589934592 | bytes 12582912 | tf_op jit(solution)/shard_map/pallas_call | solution.py:422
  547.9 6.9 fusion.47
  575.9 8.0 shard_map.301
  586.2 16.4 %shard_map.302 = bf16[1024,4128]{1,0:T(8,128)(2,1)} custom-call(bf16[1024,1024]{1,0:T(8,128)(2,1)S(1)} %copy-done.5, bf16[1024,1024]{1,0:T(8,128)(2,1)S(1)} %copy-done.7, bf16[1024,1312]{1,0:T(8,128)(2,1)} %get-tuple-element.157.refs_2_, bf16[1024,1312]{1,0:T(8,128)(2,1)} %get-tuple-element.158.refs_3_, bf16[1024,1312]{1,0:T(8,128)(2,1)} %copy-done.97, ...), custom_call_target="tpu_custom_call" | custom-call | flops 8657043456 | bytes 21102592 | tf_op jit(solution)/shard_map/pallas_call | solution.py:475
  614.7 13.0 %shard_map.304.refs_3_ = bf16[1024,768]{1,0:T(8,128)(2,1)S(1)} custom-call(f32[1024,1536]{1,0:T(8,128)} %fusion.32.raw_ref, f32[1024,128]{1,0:T(8,128)S(1)} %copy-done.1, f32[1024,128]{1,0:T(8,128)S(1)} %copy-done.3, bf16[1024,512]{1,0:T(8,128)(2,1)S(1)} %convolution_convert_fusion.2.up_ref), custom_call_target="tpu_custom_call" | custom-call | flops 2147483648 | bytes 12582912 | tf_op jit(solution)/shard_map/pallas_call | solution.py:422
  627.7 13.3 %shard_map.303.refs_2_ = bf16[1024,768]{1,0:T(8,128)(2,1)S(1)} custom-call(f32[1024,1536]{1,0:T(8,128)} %fusion.32.raw_ref, f32[1024,128]{1,0:T(8,128)S(1)} %copy-done.1, f32[1024,128]{1,0:T(8,128)S(1)} %copy-done.3, bf16[1024,512]{1,0:T(8,128)(2,1)S(1)} %convolution_convert_fusion.2.up_ref), custom_call_target="tpu_custom_call" | custom-call | flops 2147483648 | bytes 12582912 | tf_op jit(solution)/shard_map/pallas_call | solution.py:422
  665.7 116.6 %collective-permute-done.27 = bf16[2,2,2,64,2048]{4,3,1,0,2:T(8,128)(2,1)} collective-permute-done((bf16[2,2,2,64,2048]{4,3,1,0,2:T(8,128)(2,1)}, bf16[2,2,2,64,2048]{4,3,1,0,2:T(8,128)(2,1)}, u32[]{:S(2)}, u32[]{:S(2)}) %collective-permute-start.27) | collective-permute-done | bytes 2097184 | tf_op jit(solution)/shard_map/ppermute | solution.py:94
  796.1 8.2 shard_map.305
  814.4 36.0 %collective-permute-done.29 = bf16[2,2,2,64,1024]{4,3,0,1,2:T(8,128)(2,1)S(1)} collective-permute-done((bf16[2,2,2,64,1024]{4,3,0,1,2:T(8,128)(2,1)S(1)}, bf16[2,2,2,64,1024]{4,3,0,1,2:T(8,128)(2,1)S(1)}, u32[]{:S(2)}, u32[]{:S(2)}) %collective-permute-start.29) | collective-permute-done | bytes 1048608 | tf_op jit(solution)/shard_map/ppermute | solution.py:94
  851.3 15.6 %collective-permute-done.36 = bf16[2,2,64,2080]{3,2,1,0:T(8,128)(2,1)S(1)} collective-permute-done((bf16[2,2,64,2080]{3,2,1,0:T(8,128)(2,1)S(1)}, bf16[2,2,64,2080]{3,2,1,0:T(8,128)(2,1)S(1)}, u32[]{:S(2)}, u32[]{:S(2)}) %collective-permute-start.36) | collective-permute-done | bytes 1064992 | tf_op jit(solution)/shard_map/ppermute | solution.py:94
  868.1 11.2 %collective-permute-done.32 = bf16[2,2,64,1152]{3,2,0,1:T(8,128)(2,1)S(1)} collective-permute-done((bf16[2,2,64,1152]{3,2,0,1:T(8,128)(2,1)S(1)}, bf16[2,2,64,1152]{3,2,0,1:T(8,128)(2,1)S(1)}, u32[]{:S(2)}, u32[]{:S(2)}) %collective-permute-start.32) | collective-permute-done | bytes 589856 | tf_op jit(solution)/shard_map/ppermute | solution.py:94
  879.6 8.4 collective-permute-done.37
  888.3 11.7 %collective-permute-done.33 = bf16[2,64,2176]{2,1,0:T(8,128)(2,1)S(1)} collective-permute-done((bf16[2,64,2176]{2,1,0:T(8,128)(2,1)S(1)}, bf16[2,64,2176]{2,1,0:T(8,128)(2,1)S(1)}, u32[]{:S(2)}, u32[]{:S(2)}) %collective-permute-start.33) | collective-permute-done | bytes 557088 | tf_op jit(solution)/shard_map/ppermute | solution.py:95
  902.7 24.6 %collective-permute-done.34 = bf16[64,2176]{1,0:T(8,128)(2,1)S(1)} collective-permute-done((bf16[64,2176]{1,0:T(8,128)(2,1)S(1)}, bf16[64,2176]{1,0:T(8,128)(2,1)S(1)}, u32[]{:S(2)}, u32[]{:S(2)}) %collective-permute-start.34) | collective-permute-done | bytes 278560 | tf_op jit(solution)/shard_map/ppermute | solution.py:95
  927.3 11.5 %collective-permute-done.38 = bf16[64,4128]{1,0:T(8,128)(2,1)S(1)} collective-permute-done((bf16[64,4128]{1,0:T(8,128)(2,1)S(1)}, bf16[64,4128]{1,0:T(8,128)(2,1)S(1)}, u32[]{:S(2)}, u32[]{:S(2)}) %collective-permute-start.38) | collective-permute-done | bytes 528416 | tf_op jit(solution)/shard_map/ppermute | solution.py:95
  (519 shorter events, 320.9 us)
Async XLA Ops:
  7.2 281.7 %all-gather.2.cloned.1.call-start = ((), (), s32[]{:S(2)}) async-start(), calls=%async_computation.2 | async-start | bytes 18382848 | tf_op jit(solution)/shard_map/all_gather | solution.py:181
  63.6 891.8 %reduce-scatter.5.cloned.1.call-start = ((), (), s32[]{:S(2)}) async-start(), calls=%async_computation.4 | async-start | bytes 9191424 | tf_op jit(solution)/shard_map/reduce_scatter | solution.py:132
  63.9 26.1 %collective-permute-start = (bf16[1024,1024]{1,0:T(8,128)(2,1)}, bf16[1024,1024]{1,0:T(8,128)(2,1)}, u32[]{:S(2)}, u32[]{:S(2)}) collective-permute-start(bf16[1024,1024]{1,0:T(8,128)(2,1)} %param.17), channel_id=1, source_target_pairs={{0,2},{2,0},{1,3},{3,1},{4,6},{6,4},{5,7},{7,5},{8,10},{10,8},{9,1... | collective-permute-start | bytes 6291464 | tf_op jit(solution)/shard_map/ppermute | solution.py:59
  64.9 17.7 %collective-permute-start.6 = (bf16[2,2,64,1024]{3,2,0,1:T(8,128)(2,1)}, bf16[2,2,64,1024]{3,2,0,1:T(8,128)(2,1)}, u32[]{:S(2)}, u32[]{:S(2)}) collective-permute-start(bf16[2,2,64,1024]{3,2,0,1:T(8,128)(2,1)} %pad_maximum_fusion.19), channel_id=1, source_target_pairs={{0,4},{4,0},{8,12},{12,8},{16,20},{20,16},{24,28},{28,24},{1,5},{5... | collective-permute-start | bytes 1572872 | tf_op jit(solution)/shard_map/ppermute | solution.py:95
  68.4 20.2 %collective-permute-start.4 = (bf16[2,2,64,1152]{3,2,0,1:T(8,128)(2,1)}, bf16[2,2,64,1152]{3,2,0,1:T(8,128)(2,1)}, u32[]{:S(2)}, u32[]{:S(2)}) collective-permute-start(bf16[2,2,64,1152]{3,2,0,1:T(8,128)(2,1)} %fusion.101), channel_id=1, source_target_pairs={{0,1},{1,0},{2,3},{3,2},{4,5},{5,4},{6,7},{7,6},{8,9},{9,8},{10,11... | collective-permute-start | bytes 1769480 | tf_op jit(solution)/shard_map/ppermute | solution.py:94
  83.9 30.0 %collective-permute-start.7 = (bf16[2,2,2,64,1024]{4,3,0,1,2:T(8,128)(2,1)S(1)}, bf16[2,2,2,64,1024]{4,3,0,1,2:T(8,128)(2,1)S(1)}, u32[]{:S(2)}, u32[]{:S(2)}) collective-permute-start(bf16[2,2,2,64,1024]{4,3,0,1,2:T(8,128)(2,1)S(1)} %pad_maximum_fusion.11), channel_id=1, source_target_pairs={{0,1},{1,0},{2,3},{3,2},{4,5},{5,4},{6,7},{7,6},{8,9},{9,8},{10,11... | collective-permute-start | bytes 3145736 | tf_op jit(solution)/shard_map/ppermute | solution.py:94
  89.9 24.6 %collective-permute-start.5 = (bf16[2,2,2,64,1152]{4,3,0,1,2:T(8,128)(2,1)S(1)}, bf16[2,2,2,64,1152]{4,3,0,1,2:T(8,128)(2,1)S(1)}, u32[]{:S(2)}, u32[]{:S(2)}) collective-permute-start(bf16[2,2,2,64,1152]{4,3,0,1,2:T(8,128)(2,1)S(1)} %pad_maximum_fusion.9), channel_id=1, source_target_pairs={{0,4},{4,0},{8,12},{12,8},{16,20},{20,16},{24,28},{28,24},{1,5},{5... | collective-permute-start | bytes 3538952 | tf_op jit(solution)/shard_map/ppermute | solution.py:95
  139.1 21.3 %collective-permute-start.11 = (bf16[64,2304]{1,0:T(8,128)(2,1)S(1)}, bf16[64,2304]{1,0:T(8,128)(2,1)S(1)}, u32[]{:S(2)}, u32[]{:S(2)}) collective-permute-start(bf16[64,2304]{1,0:T(8,128)(2,1)S(1)} %fusion.113), channel_id=1, source_target_pairs={{0,0},{1,2},{2,1},{3,3},{4,4},{5,6},{6,5},{7,7},{8,8},{9,10},{10,9... | collective-permute-start | bytes 884744 | tf_op jit(solution)/shard_map/ppermute | solution.py:49
  160.4 18.5 %collective-permute-start.12 = (bf16[64,2176]{1,0:T(8,128)(2,1)S(1)}, bf16[64,2176]{1,0:T(8,128)(2,1)S(1)}, u32[]{:S(2)}, u32[]{:S(2)}) collective-permute-start(bf16[64,2176]{1,0:T(8,128)(2,1)S(1)} %slice.345), channel_id=1, source_target_pairs={{0,16},{4,20},{8,24},{12,28},{16,0},{20,4},{24,8},{28,12},{1,17},{... | collective-permute-start | bytes 835592 | tf_op jit(solution)/shard_map/ppermute | solution.py:95
  179.0 54.5 %collective-permute-start.13 = (bf16[2,64,2176]{2,1,0:T(8,128)(2,1)S(1)}, bf16[2,64,2176]{2,1,0:T(8,128)(2,1)S(1)}, u32[]{:S(2)}, u32[]{:S(2)}) collective-permute-start(bf16[2,64,2176]{2,1,0:T(8,128)(2,1)S(1)} %pad_maximum_fusion.16), channel_id=1, source_target_pairs={{0,8},{4,12},{8,0},{12,4},{16,24},{20,28},{24,16},{28,20},{1,9},{5... | collective-permute-start | bytes 1671176 | tf_op jit(solution)/shard_map/ppermute | solution.py:95
  180.4 77.0 %collective-permute-start.8 = (bf16[1024,1024]{1,0:T(8,128)(2,1)S(1)}, bf16[1024,1024]{1,0:T(8,128)(2,1)S(1)}, u32[]{:S(2)}, u32[]{:S(2)}) collective-permute-start(bf16[1024,1024]{1,0:T(8,128)(2,1)S(1)} %convolution_convert_fusion.1), channel_id=1, source_target_pairs={{0,2},{2,0},{1,3},{3,1},{4,6},{6,4},{5,7},{7,5},{8,10},{10,8},{9,1... | collective-permute-start | bytes 6291464 | tf_op jit(solution)/shard_map/ppermute | solution.py:59
  233.8 19.9 %collective-permute-start.16 = (bf16[2,2,64,1024]{3,2,0,1:T(8,128)(2,1)S(1)}, bf16[2,2,64,1024]{3,2,0,1:T(8,128)(2,1)S(1)}, u32[]{:S(2)}, u32[]{:S(2)}) collective-permute-start(bf16[2,2,64,1024]{3,2,0,1:T(8,128)(2,1)S(1)} %pad_maximum_fusion.18), channel_id=1, source_target_pairs={{0,4},{4,0},{8,12},{12,8},{16,20},{20,16},{24,28},{28,24},{1,5},{5... | collective-permute-start | bytes 1572872 | tf_op jit(solution)/shard_map/ppermute | solution.py:95
  233.9 21.2 %collective-permute-start.14 = (bf16[2,2,64,1152]{3,2,0,1:T(8,128)(2,1)S(1)}, bf16[2,2,64,1152]{3,2,0,1:T(8,128)(2,1)S(1)}, u32[]{:S(2)}, u32[]{:S(2)}) collective-permute-start(bf16[2,2,64,1152]{3,2,0,1:T(8,128)(2,1)S(1)} %fusion.100), channel_id=1, source_target_pairs={{0,1},{1,0},{2,3},{3,2},{4,5},{5,4},{6,7},{7,6},{8,9},{9,8},{10,11... | collective-permute-start | bytes 1769480 | tf_op jit(solution)/shard_map/ppermute | solution.py:94
  255.1 67.8 %collective-permute-start.17 = (bf16[2,2,2,64,1024]{4,3,0,1,2:T(8,128)(2,1)}, bf16[2,2,2,64,1024]{4,3,0,1,2:T(8,128)(2,1)}, u32[]{:S(2)}, u32[]{:S(2)}) collective-permute-start(bf16[2,2,2,64,1024]{4,3,0,1,2:T(8,128)(2,1)} %pad_maximum_fusion.12), channel_id=1, source_target_pairs={{0,1},{1,0},{2,3},{3,2},{4,5},{5,4},{6,7},{7,6},{8,9},{9,8},{10,11... | collective-permute-start | bytes 3145736 | tf_op jit(solution)/shard_map/ppermute | solution.py:94
  256.4 68.3 %collective-permute-start.15 = (bf16[2,2,2,64,1152]{4,3,0,1,2:T(8,128)(2,1)}, bf16[2,2,2,64,1152]{4,3,0,1,2:T(8,128)(2,1)}, u32[]{:S(2)}, u32[]{:S(2)}) collective-permute-start(bf16[2,2,2,64,1152]{4,3,0,1,2:T(8,128)(2,1)} %pad_maximum_fusion.10), channel_id=1, source_target_pairs={{0,4},{4,0},{8,12},{12,8},{16,20},{20,16},{24,28},{28,24},{1,5},{5... | collective-permute-start | bytes 3538952 | tf_op jit(solution)/shard_map/ppermute | solution.py:95
  321.9 51.4 %collective-permute-start.21 = (bf16[1024,1024]{1,0:T(8,128)(2,1)}, bf16[1024,1024]{1,0:T(8,128)(2,1)}, u32[]{:S(2)}, u32[]{:S(2)}) collective-permute-start(bf16[1024,1024]{1,0:T(8,128)(2,1)} %param.18), channel_id=1, source_target_pairs={{0,2},{2,0},{1,3},{3,1},{4,6},{6,4},{5,7},{7,5},{8,10},{10,8},{9,1... | collective-permute-start | bytes 6291464 | tf_op jit(solution)/shard_map/ppermute | solution.py:59
  431.0 23.1 %collective-permute-start.22 = (bf16[1024,1024]{1,0:T(8,128)(2,1)}, bf16[1024,1024]{1,0:T(8,128)(2,1)}, u32[]{:S(2)}, u32[]{:S(2)}) collective-permute-start(bf16[1024,1024]{1,0:T(8,128)(2,1)} %add_convert_fusion.6), channel_id=1, source_target_pairs={{0,2},{2,0},{1,3},{3,1},{4,6},{6,4},{5,7},{7,5},{8,10},{10,8},{9,1... | collective-permute-start | bytes 6291464 | tf_op jit(solution)/shard_map/ppermute | solution.py:59
  437.8 21.3 %collective-permute-start.19 = (bf16[1024,1024]{1,0:T(8,128)(2,1)}, bf16[1024,1024]{1,0:T(8,128)(2,1)}, u32[]{:S(2)}, u32[]{:S(2)}) collective-permute-start(bf16[1024,1024]{1,0:T(8,128)(2,1)} %fusion.67), channel_id=1, source_target_pairs={{0,2},{2,0},{1,3},{3,1},{4,6},{6,4},{5,7},{7,5},{8,10},{10,8},{9,1... | collective-permute-start | bytes 6291464 | tf_op jit(solution)/shard_map/ppermute | solution.py:59
  464.9 37.8 %collective-permute-start.20 = (bf16[1024,1024]{1,0:T(8,128)(2,1)}, bf16[1024,1024]{1,0:T(8,128)(2,1)}, u32[]{:S(2)}, u32[]{:S(2)}) collective-permute-start(bf16[1024,1024]{1,0:T(8,128)(2,1)} %get-tuple-element.163), channel_id=1, source_target_pairs={{0,1},{3,2},{4,5},{7,6},{8,9},{11,10},{12,13},{15,14},{16,17},{19,... | collective-permute-start | bytes 6291464 | tf_op jit(solution)/shard_map/ppermute | solution.py:571
  471.7 496.4 %reduce-scatter.3.cloned.1.call-start = ((), (), s32[]{:S(2)}) async-start(), calls=%async_computation.3 | async-start | bytes 4734976 | tf_op jit(solution)/shard_map/reduce_scatter | solution.py:132
  572.6 30.0 %collective-permute-start.24 = (bf16[1024,1024]{1,0:T(8,128)(2,1)}, bf16[1024,1024]{1,0:T(8,128)(2,1)}, u32[]{:S(2)}, u32[]{:S(2)}) collective-permute-start(bf16[1024,1024]{1,0:T(8,128)(2,1)} %add_convert_fusion.4), channel_id=1, source_target_pairs={{0,2},{2,0},{1,3},{3,1},{4,6},{6,4},{5,7},{7,5},{8,10},{10,8},{9,1... | collective-permute-start | bytes 6291464 | tf_op jit(solution)/shard_map/ppermute | solution.py:59
  652.0 130.3 %collective-permute-start.27 = (bf16[2,2,2,64,2048]{4,3,1,0,2:T(8,128)(2,1)}, bf16[2,2,2,64,2048]{4,3,1,0,2:T(8,128)(2,1)}, u32[]{:S(2)}, u32[]{:S(2)}) collective-permute-start(bf16[2,2,2,64,2048]{4,3,1,0,2:T(8,128)(2,1)} %bitcast.253), channel_id=1, source_target_pairs={{0,1},{1,0},{2,3},{3,2},{4,5},{5,4},{6,7},{7,6},{8,9},{9,8},{10,11... | collective-permute-start | bytes 6291464 | tf_op jit(solution)/shard_map/ppermute | solution.py:94
  656.5 138.6 %collective-permute-start.28 = (bf16[2,2,2,64,2080]{4,3,2,1,0:T(8,128)(2,1)}, bf16[2,2,2,64,2080]{4,3,2,1,0:T(8,128)(2,1)}, u32[]{:S(2)}, u32[]{:S(2)}) collective-permute-start(bf16[2,2,2,64,2080]{4,3,2,1,0:T(8,128)(2,1)} %dynamic-slice_bitcast_fusion), channel_id=1, source_target_pairs={{0,4},{4,0},{8,12},{12,8},{16,20},{20,16},{24,28},{28,24},{1,5},{5... | collective-permute-start | bytes 6389768 | tf_op jit(solution)/shard_map/ppermute | solution.py:95
  788.3 24.5 %collective-permute-start.35 = (bf16[2,2,64,2048]{3,2,1,0:T(8,128)(2,1)S(1)}, bf16[2,2,64,2048]{3,2,1,0:T(8,128)(2,1)}, u32[]{:S(2)}, u32[]{:S(2)}) collective-permute-start(bf16[2,2,64,2048]{3,2,1,0:T(8,128)(2,1)S(1)} %dynamic-slice_bitcast_fusion.2), channel_id=1, source_target_pairs={{0,4},{4,0},{8,12},{12,8},{16,20},{20,16},{24,28},{28,24},{1,5},{5... | collective-permute-start | bytes 3145736 | tf_op jit(solution)/shard_map/ppermute | solution.py:95
  793.8 153.8 %collective-permute-start.26 = (bf16[1024,1024]{1,0:T(8,128)(2,1)S(1)}, bf16[1024,1024]{1,0:T(8,128)(2,1)S(1)}, u32[]{:S(2)}, u32[]{:S(2)}) collective-permute-start(bf16[1024,1024]{1,0:T(8,128)(2,1)S(1)} %add_convert_fusion.2), channel_id=1, source_target_pairs={{0,1},{3,2},{4,5},{7,6},{8,9},{11,10},{12,13},{15,14},{16,17},{19,... | collective-permute-start | bytes 6291464 | tf_op jit(solution)/shard_map/ppermute | solution.py:571
  806.2 44.2 %collective-permute-start.29 = (bf16[2,2,2,64,1024]{4,3,0,1,2:T(8,128)(2,1)S(1)}, bf16[2,2,2,64,1024]{4,3,0,1,2:T(8,128)(2,1)S(1)}, u32[]{:S(2)}, u32[]{:S(2)}) collective-permute-start(bf16[2,2,2,64,1024]{4,3,0,1,2:T(8,128)(2,1)S(1)} %bitcast.296), channel_id=1, source_target_pairs={{0,1},{1,0},{2,3},{3,2},{4,5},{5,4},{6,7},{7,6},{8,9},{9,8},{10,11... | collective-permute-start | bytes 3145736 | tf_op jit(solution)/shard_map/ppermute | solution.py:94
  810.8 56.2 %collective-permute-start.36 = (bf16[2,2,64,2080]{3,2,1,0:T(8,128)(2,1)S(1)}, bf16[2,2,64,2080]{3,2,1,0:T(8,128)(2,1)S(1)}, u32[]{:S(2)}, u32[]{:S(2)}) collective-permute-start(bf16[2,2,64,2080]{3,2,1,0:T(8,128)(2,1)S(1)} %dynamic-slice_bitcast_fusion.1), channel_id=1, source_target_pairs={{0,1},{1,0},{2,3},{3,2},{4,5},{5,4},{6,7},{7,6},{8,9},{9,8},{10,11... | collective-permute-start | bytes 3194888 | tf_op jit(solution)/shard_map/ppermute | solution.py:94
  812.0 55.2 %collective-permute-start.31 = (bf16[2,2,2,64,1152]{4,3,0,1,2:T(8,128)(2,1)S(1)}, bf16[2,2,2,64,1152]{4,3,0,1,2:T(8,128)(2,1)S(1)}, u32[]{:S(2)}, u32[]{:S(2)}) collective-permute-start(bf16[2,2,2,64,1152]{4,3,0,1,2:T(8,128)(2,1)S(1)} %bitcast.293), channel_id=1, source_target_pairs={{0,4},{4,0},{8,12},{12,8},{16,20},{20,16},{24,28},{28,24},{1,5},{5... | collective-permute-start | bytes 3538952 | tf_op jit(solution)/shard_map/ppermute | solution.py:95
  867.8 20.2 %collective-permute-start.37 = (bf16[2,64,4128]{2,1,0:T(8,128)(2,1)S(1)}, bf16[2,64,4128]{2,1,0:T(8,128)(2,1)S(1)}, u32[]{:S(2)}, u32[]{:S(2)}) collective-permute-start(bf16[2,64,4128]{2,1,0:T(8,128)(2,1)S(1)} %fusion.85), channel_id=1, source_target_pairs={{0,8},{4,12},{8,0},{12,4},{16,24},{20,28},{24,16},{28,20},{1,9},{5... | collective-permute-start | bytes 3170312 | tf_op jit(solution)/shard_map/ppermute | solution.py:95
  879.5 20.4 %collective-permute-start.33 = (bf16[2,64,2176]{2,1,0:T(8,128)(2,1)S(1)}, bf16[2,64,2176]{2,1,0:T(8,128)(2,1)S(1)}, u32[]{:S(2)}, u32[]{:S(2)}) collective-permute-start(bf16[2,64,2176]{2,1,0:T(8,128)(2,1)S(1)} %fusion.105), channel_id=1, source_target_pairs={{0,8},{4,12},{8,0},{12,4},{16,24},{20,28},{24,16},{28,20},{1,9},{5... | collective-permute-start | bytes 1671176 | tf_op jit(solution)/shard_map/ppermute | solution.py:95
  900.1 27.1 %collective-permute-start.34 = (bf16[64,2176]{1,0:T(8,128)(2,1)S(1)}, bf16[64,2176]{1,0:T(8,128)(2,1)S(1)}, u32[]{:S(2)}, u32[]{:S(2)}) collective-permute-start(bf16[64,2176]{1,0:T(8,128)(2,1)S(1)} %dynamic-slice_bitcast_fusion.6), channel_id=1, source_target_pairs={{0,16},{4,20},{8,24},{12,28},{16,0},{20,4},{24,8},{28,12},{1,17},{... | collective-permute-start | bytes 835592 | tf_op jit(solution)/shard_map/ppermute | solution.py:95
  900.2 38.5 %collective-permute-start.38 = (bf16[64,4128]{1,0:T(8,128)(2,1)S(1)}, bf16[64,4128]{1,0:T(8,128)(2,1)S(1)}, u32[]{:S(2)}, u32[]{:S(2)}) collective-permute-start(bf16[64,4128]{1,0:T(8,128)(2,1)S(1)} %dynamic-slice_bitcast_fusion.4), channel_id=1, source_target_pairs={{0,16},{4,20},{8,24},{12,28},{16,0},{20,4},{24,8},{28,12},{1,17},{... | collective-permute-start | bytes 1585160 | tf_op jit(solution)/shard_map/ppermute | solution.py:95
  (124 other events, 1474.5 us)
Sparse Core Ops, SparseCore 0:
  63.7 225.1 all-gather.1
  471.8 165.9 reduce-scatter.4
  652.4 137.9 reduce-scatter.2

commit v8 on v7

--- a/solution.py
+++ b/solution.py
@@ -133,7 +133,7 @@
 
 
 def half_columns(values):
-    return values.shape[1] // 256 * 128
+    return values.shape[1] * 3 // 7 // 128 * 128
 
 
 def gather_quick(shard, chips):
@@ -508,7 +508,7 @@
     return (output, kept)
 
 
-def backward_layer(upstream, weights, tables, kept, is_local, begin, slots):
+def backward_layer(upstream, weights, tables, kept, is_local, begin, slots, extra=()):
     w_qkv, w_out, gain_pair, w_inner, w_gate, w_down = weights
     residual, middle, lowered, lowered_two, projected, attended, inner, gate_part, activated = kept
     up_low = upstream.astype(jnp.bfloat16)
@@ -541,9 +541,9 @@
     gains = widen(jnp.stack([d_gain_one, d_gain_two], axis=1)).astype(jnp.bfloat16)
     head_grads = weight_grads(
         (lowered, d_branch),
-        (d_first, d_second, attended, gains),
-        (0, 0, 1, None),
-        slots[3](hidden_begun),
+        (d_first, d_second, attended, gains) + extra,
+        (0, 0, 1, None) + (None,) * len(extra),
+        slots[3](),
     )
     return (d_middle + d_in_norm, (begin(head_grads), hidden_begun))
 
@@ -591,10 +591,10 @@
     output, kept_second = forward_layer(middle, weights[1], global_tables, False)
     out_arrived = arriving_sequence(output.astype(jnp.bfloat16))
     results = []
-    by_call = []
-
-    def begin_call(gradient):
-        by_call.append((corner(gradient), scatter_rows(gradient, chips)))
+    seconds = []
+
+    def begin_second(gradient):
+        seconds.append(gradient)
 
     def begin(gradient):
         results.append([])
@@ -609,28 +609,35 @@
         global_tables,
         kept_second,
         False,
-        begin_call,
+        begin_second,
         (none, none, lambda: (corner(out_arrived),), none),
     )
     final_out = jnp.where(same, output.astype(jnp.bfloat16), out_arrived)
-    hidden_second, heads_second = by_call
-    d_values, begun_first = backward_layer(
+    hidden_second = scatter_rows(seconds[0], chips)
+    heads_second = seconds[1]
+
+    def reduced():
+        return (corner(hidden_second),)
+
+    d_values, (heads_steps, hidden_steps) = backward_layer(
         d_middle,
         weights[0],
         local_tables,
         kept_first,
         True,
         begin,
-        (lambda: (heads_second[0],), none, none, next),
-    )
-    for steps in (begun_first[1], begun_first[0]):
+        (lambda: (corner(heads_second),), reduced, reduced, none),
+        (heads_second,),
+    )
+    for steps in (hidden_steps, heads_steps):
         for unused in steps:
             pass
-    hidden_first, heads_first = [r[0] for r in results]
-    shards_first = role_swap(jnp.concatenate([heads_first, hidden_first], axis=1), chips)
-    hidden_second = swap_after(hidden_second[1], shards_first, chips)
-    heads_second = swap_after(heads_second[1], hidden_second, chips)
-    shards_second = jnp.concatenate([heads_second, hidden_second], axis=1)
+    hidden_first, heads_both = [r[0] for r in results]
+    shards = role_swap(jnp.concatenate([heads_both, hidden_first], axis=1), chips)
+    hidden_second = swap_after(hidden_second, d_values.astype(jnp.bfloat16), chips)
+    cut = heads_second.shape[1]
+    shards_first = jnp.concatenate([shards[:, :cut], shards[:, 2 * cut :]], axis=1)
+    shards_second = jnp.concatenate([shards[:, cut : 2 * cut], hidden_second], axis=1)
     grads_first, grads_second = [
         unpack_grads(packed.astype(jnp.float32), starts, hidden)
         for packed in (shards_first, shards_second)

time: 1010 us -> 915 us (0.906)
  waiting for transfers between devices: 446 us -> 366 us
    ppermute x8, waiting for transfers between devices: 205 us -> 78.7 us  [bit_swap(): return lax.ppermute(values, 'tensor', [(0, 1), (1, 0)])]
    reduce_scatter x2 -> x1, waiting for transfers between devices: 0.01 us -> 19.7 us  [scatter_rows(): lax.psum_scatter(gradient, chip_axes, scatter_dimension=0, tiled=True)]
    ppermute x16, waiting for transfers between devices: 173 us -> 191 us  [bit_swap(): lax.ppermute(values, 'chip', [(chip, chip ^ 1 << bit) for chip in range(c...]
    ppermute x6 -> x5, waiting for transfers between devices: 35.2 us -> 41.6 us  [role_swap(): return lax.ppermute(values, every_axis, swap_pairs(chips))]
    ppermute x6 -> x5, starting transfers between devices: 36.3 us -> 31.1 us  [role_swap(): return lax.ppermute(values, every_axis, swap_pairs(chips))]
    unnamed x219 -> x255, local copies, waits for them, and re-layouts: 24.1 us -> 19.9 us
  transfers between devices with their start and end apart: 45 -> 43, of which waited for: 25 -> 28; matrix products, arithmetic and copies ran while one was open for 19% -> 20% of each run, Pallas kernels for 18% -> 20%
where the time goes in v8:
time: 915 us; the launch traced here: 910 us
  waiting for transfers between devices  366 us (40%)
  Pallas kernels  183 us (20%)
  matrix products  133 us (15%)
  other arithmetic  105 us (11%)
  starting transfers between devices  58.5 us (6%)
  local copies, waits for them, and re-layouts  46.8 us (5%)
  between operations  16.9 us (2%)
    ppermute x16, waiting for transfers between devices, bit_swap(): lax.ppermute(values, 'chip', [(chip, chip ^ 1 << bit) for chip in range(c...  191 us
    dot_general x22, matrix products, product(): lax.dot_general(left, right, ((contract[:1], contract[1:]), ((), ())), pr...  133 us
    pallas_call x4, Pallas kernels, attend_backward(): pl.pallas_call(functools.partial(attend_back_kernel, is_local, 128), out_...  82.6 us
    ppermute x8, waiting for transfers between devices, bit_swap(): return lax.ppermute(values, 'tensor', [(0, 1), (1, 0)])  78.7 us
    pallas_call x2, Pallas kernels, attend_forward(): pl.pallas_call(functools.partial(attend_kernel, is_local, 128), out_shape...  50.3 us
    pallas_call x4, Pallas kernels, weight_grads(): pl.pallas_call(functools.partial(weight_grad_kernel, choice, tuple(starts...  50.3 us
    ppermute x5, waiting for transfers between devices, role_swap(): return lax.ppermute(values, every_axis, swap_pairs(chips))  41.6 us
    ppermute x5, starting transfers between devices, role_swap(): return lax.ppermute(values, every_axis, swap_pairs(chips))  31.1 us
  transfers between devices with their start and end apart: 43, of which 28 were waited for; matrix products, arithmetic and copies ran while one was open for 20% of the time, Pallas kernels for 20%

profile of v8, /device:TPU:1, one launch (start us, length us, event | category | flops | bytes accessed | tf_op | source)
XLA Modules:
  0.0 909.6 jit_solution(10280120873844605641)
XLA Ops:
  22.2 7.2 collective-permute-done.2
  30.8 10.8 %collective-permute-done.3 = bf16[2,64,2176]{2,1,0:T(8,128)(2,1)S(1)} collective-permute-done((bf16[2,64,2176]{2,1,0:T(8,128)(2,1)S(1)}, bf16[2,64,2176]{2,1,0:T(8,128)(2,1)S(1)}, u32[]{:S(2)}, u32[]{:S(2)}) %collective-permute-start.3) | collective-permute-done | bytes 557088 | tf_op jit(solution)/shard_map/ppermute | solution.py:95
  44.7 14.7 %collective-permute-done.9 = bf16[64,8480]{1,0:T(8,128)(2,1)S(1)} collective-permute-done((bf16[64,8480]{1,0:T(8,128)(2,1)S(1)}, bf16[64,8480]{1,0:T(8,128)(2,1)S(1)}, u32[]{:S(2)}, u32[]{:S(2)}) %collective-permute-start.9) | collective-permute-done | bytes 1085472 | tf_op jit(solution)/shard_map/ppermute | solution.py:49
  78.0 10.3 %collective-permute-done.4 = bf16[2,2,64,1280]{3,2,0,1:T(8,128)(2,1)} collective-permute-done((bf16[2,2,64,1280]{3,2,0,1:T(8,128)(2,1)}, bf16[2,2,64,1280]{3,2,0,1:T(8,128)(2,1)}, u32[]{:S(2)}, u32[]{:S(2)}) %collective-permute-start.4) | collective-permute-done | bytes 655392 | tf_op jit(solution)/shard_map/ppermute | solution.py:94
  92.8 15.6 %collective-permute-done.7 = bf16[2,2,2,64,896]{4,3,0,1,2:T(8,128)(2,1)S(1)} collective-permute-done((bf16[2,2,2,64,896]{4,3,0,1,2:T(8,128)(2,1)S(1)}, bf16[2,2,2,64,896]{4,3,0,1,2:T(8,128)(2,1)S(1)}, u32[]{:S(2)}, u32[]{:S(2)}) %collective-permute-start.7) | collective-permute-done | bytes 917536 | tf_op jit(solution)/shard_map/ppermute | solution.py:94
  109.0 14.9 %collective-permute-done.5 = bf16[2,2,2,64,1280]{4,3,0,1,2:T(8,128)(2,1)S(1)} collective-permute-done((bf16[2,2,2,64,1280]{4,3,0,1,2:T(8,128)(2,1)S(1)}, bf16[2,2,2,64,1280]{4,3,0,1,2:T(8,128)(2,1)S(1)}, u32[]{:S(2)}, u32[]{:S(2)}) %collective-permute-start.5) | collective-permute-done | bytes 1310752 | tf_op jit(solution)/shard_map/ppermute | solution.py:95
  131.3 16.9 %shard_map.296.refs_4_ = bf16[1024,512]{1,0:T(8,128)(2,1)S(1)} custom-call(f32[1024,1536]{1,0:T(8,128)} %fusion.34.raw_ref, f32[1024,128]{1,0:T(8,128)S(1)} %get-tuple-element.227.cos_ref, f32[1024,128]{1,0:T(8,128)S(1)} %get-tuple-element.228.sin_ref), custom_call_target="tpu_custom_call" | custom-call | flops 2147483648 | bytes 12582912 | tf_op jit(solution)/shard_map/pallas_call | solution.py:402
  148.4 14.2 %collective-permute-start.11 = (bf16[64,2304]{1,0:T(8,128)(2,1)S(1)}, bf16[64,2304]{1,0:T(8,128)(2,1)S(1)}, u32[]{:S(2)}, u32[]{:S(2)}) collective-permute-start(bf16[64,2304]{1,0:T(8,128)(2,1)S(1)} %fusion.113), channel_id=1, source_target_pairs={{0,0},{1,2},{2,1},{3,3},{4,4},{5,6},{6,5},{7,7},{8,8},{9,10},{10,9... | collective-permute-start | bytes 884744 | tf_op jit(solution)/shard_map/ppermute | solution.py:49
  167.5 13.9 %collective-permute-done.12 = bf16[64,2176]{1,0:T(8,128)(2,1)S(1)} collective-permute-done((bf16[64,2176]{1,0:T(8,128)(2,1)S(1)}, bf16[64,2176]{1,0:T(8,128)(2,1)S(1)}, u32[]{:S(2)}, u32[]{:S(2)}) %collective-permute-start.12) | collective-permute-done | bytes 278560 | tf_op jit(solution)/shard_map/ppermute | solution.py:95
  183.1 51.3 %collective-permute-done.13 = bf16[2,64,2176]{2,1,0:T(8,128)(2,1)S(1)} collective-permute-done((bf16[2,64,2176]{2,1,0:T(8,128)(2,1)S(1)}, bf16[2,64,2176]{2,1,0:T(8,128)(2,1)S(1)}, u32[]{:S(2)}, u32[]{:S(2)}) %collective-permute-start.13) | collective-permute-done | bytes 557088 | tf_op jit(solution)/shard_map/ppermute | solution.py:95
  234.9 21.0 %collective-permute-done.16 = bf16[2,2,64,896]{3,2,0,1:T(8,128)(2,1)S(1)} collective-permute-done((bf16[2,2,64,896]{3,2,0,1:T(8,128)(2,1)S(1)}, bf16[2,2,64,896]{3,2,0,1:T(8,128)(2,1)S(1)}, u32[]{:S(2)}, u32[]{:S(2)}) %collective-permute-start.16) | collective-permute-done | bytes 458784 | tf_op jit(solution)/shard_map/ppermute | solution.py:95
  266.2 29.6 %all-gather.2.cloned.1.call-done = bf16[1024,8352]{1,0:T(8,128)(2,1)} async-done(((bf16[64,8352]{1,0:T(8,128)(2,1)}), bf16[1024,8352]{1,0:T(8,128)(2,1)}) %all-gather.2.cloned.1.call-update) | async-done | bytes 17104912 | tf_op jit(solution)/shard_map/all_gather | solution.py:181
  301.0 20.5 %multiply_convert_fusion.3 = (bf16[1024,1312]{1,0:T(8,128)(2,1)S(1)}, f32[1024,1312]{1,0:T(8,128)}, f32[1024,1312]{1,0:T(8,128)}) fusion(f32[1024,1312]{1,0:T(8,128)S(1)} %fusion.61, bf16[1024,1024]{1,0:T(8,128)(2,1)S(1)} %multiply_convert_fusion.6.refs_0_, bf16[1024,8352]{1,0:T(8,128)(2,1)} %all-gather.2.cloned.1.call-done), kind=kOutput, calls=%fused_computation.32 | convolution fusion | flops 2840133632 | bytes 23789568 | tf_op jit(solution)/shard_map/dot_general | solution.py:491
  344.9 33.4 %shard_map.297.refs_4_ = bf16[1024,512]{1,0:T(8,128)(2,1)S(1)} custom-call(f32[1024,1536]{1,0:T(8,128)} %fusion.31.raw_ref, f32[1024,128]{1,0:T(8,128)S(1)} %get-tuple-element.229.cos_ref, f32[1024,128]{1,0:T(8,128)S(1)} %get-tuple-element.230.sin_ref), custom_call_target="tpu_custom_call" | custom-call | flops 8589934592 | bytes 12582912 | tf_op jit(solution)/shard_map/pallas_call | solution.py:402
  398.7 21.6 %add_convert_fusion.1 = (bf16[1024,1312]{1,0:T(8,128)(2,1)}, f32[1024,1312]{1,0:T(8,128)}, f32[1024,1312]{1,0:T(8,128)}) fusion(f32[1024,1312]{1,0:T(8,128)S(1)} %fusion.45, f32[1024,1312]{1,0:T(8,128)S(1)} %fusion.49, bf16[1024,1024]{1,0:T(8,128)(2,1)S(1)} %broadcast_select_fusion.refs_1_, bf16[1024,8352]{1,0:T(8,128)(2,1)} %all-gather.2.cloned.1.call-done), kind=kOutput, calls=%fused_computation.18 | convolution fusion | flops 2849538048 | bytes 29163520 | tf_op jit(solution)/shard_map/dot_general | solution.py:491
  425.3 7.4 fusion.43
  446.2 16.1 %shard_map.298 = bf16[1024,4128]{1,0:T(8,128)(2,1)} custom-call(bf16[1024,1024]{1,0:T(8,128)(2,1)S(1)} %multiply_convert_fusion.4.refs_0_, bf16[1024,1024]{1,0:T(8,128)(2,1)S(1)} %broadcast_select_fusion.refs_1_, bf16[1024,1312]{1,0:T(8,128)(2,1)} %get-tuple-element.145.refs_2_, bf16[1024,1312]{1,0:T(8,128)(2,1)} %copy-done.62, bf16[1024,1312]{1,0:T(8,128)(2,1)} %copy-done.63), custom_call_target="tpu_custom_call" | custom-call | flops 8657043456 | bytes 21102592 | tf_op jit(solution)/shard_map/pallas_call | solution.py:475
  481.3 27.9 %shard_map.299.refs_2_ = bf16[1024,768]{1,0:T(8,128)(2,1)S(1)} custom-call(f32[1024,1536]{1,0:T(8,128)} %fusion.31.raw_ref, f32[1024,128]{1,0:T(8,128)S(1)} %get-tuple-element.229.cos_ref, f32[1024,128]{1,0:T(8,128)S(1)} %get-tuple-element.230.sin_ref, bf16[1024,512]{1,0:T(8,128)(2,1)S(1)} %copy-done.20), custom_call_target="tpu_custom_call" | custom-call | flops 8589934592 | bytes 12582912 | tf_op jit(solution)/shard_map/pallas_call | solution.py:422
  511.8 27.9 %shard_map.300.refs_3_ = bf16[1024,768]{1,0:T(8,128)(2,1)S(1)} custom-call(f32[1024,1536]{1,0:T(8,128)} %fusion.31.raw_ref, f32[1024,128]{1,0:T(8,128)S(1)} %get-tuple-element.229.cos_ref, f32[1024,128]{1,0:T(8,128)S(1)} %get-tuple-element.230.sin_ref, bf16[1024,512]{1,0:T(8,128)(2,1)S(1)} %copy-done.20, bf16[16,128]{1,0:T(8,128)(2,1)S(1)} %slice.350.refs_0_), custom_call_target="tpu_custom_call" | custom-call | flops 8589934592 | bytes 12582912 | tf_op jit(solution)/shard_map/pallas_call | solution.py:422
  582.2 7.9 shard_map.301.refs_6_
  590.9 16.3 %shard_map.302 = bf16[1024,4128]{1,0:T(8,128)(2,1)} custom-call(bf16[1024,1024]{1,0:T(8,128)(2,1)S(1)} %copy-done.5, bf16[1024,1024]{1,0:T(8,128)(2,1)S(1)} %copy-done.7, bf16[1024,1312]{1,0:T(8,128)(2,1)} %get-tuple-element.157.refs_2_, bf16[1024,1312]{1,0:T(8,128)(2,1)} %get-tuple-element.158.refs_3_, bf16[1024,1312]{1,0:T(8,128)(2,1)} %copy-done.117, ...), custom_call_target="tpu_custom_call" | custom-call | flops 8657043456 | bytes 21102592 | tf_op jit(solution)/shard_map/pallas_call | solution.py:475
  630.0 19.7 %reduce-scatter.2.cloned.1.call-done = bf16[64,4128]{1,0:T(8,128)(2,1)} async-done(((bf16[1024,4128]{1,0:T(8,128)(2,1)}), bf16[64,4128]{1,0:T(8,128)(2,1)}) %reduce-scatter.2.cloned.1.call-update) | async-done | bytes 528400 | tf_op jit(solution)/shard_map/reduce_scatter | solution.py:132
  650.4 13.0 %shard_map.304.refs_3_ = bf16[1024,768]{1,0:T(8,128)(2,1)S(1)} custom-call(f32[1024,1536]{1,0:T(8,128)} %fusion.34.raw_ref, f32[1024,128]{1,0:T(8,128)S(1)} %copy-done.1, f32[1024,128]{1,0:T(8,128)S(1)} %copy-done.3, bf16[1024,512]{1,0:T(8,128)(2,1)S(1)} %convolution_convert_fusion.2.up_ref, bf16[16,128]{1,0:T(8,128)(2,1)S(1)} %slice.352.refs_0_), custom_call_target="tpu_custom_call" | custom-call | flops 2147483648 | bytes 12582912 | tf_op jit(solution)/shard_map/pallas_call | solution.py:422
  663.4 13.9 %shard_map.303.refs_2_ = bf16[1024,768]{1,0:T(8,128)(2,1)S(1)} custom-call(f32[1024,1536]{1,0:T(8,128)} %fusion.34.raw_ref, f32[1024,128]{1,0:T(8,128)S(1)} %copy-done.1, f32[1024,128]{1,0:T(8,128)S(1)} %copy-done.3, bf16[1024,512]{1,0:T(8,128)(2,1)S(1)} %convolution_convert_fusion.2.up_ref, bf16[16,128]{1,0:T(8,128)(2,1)S(1)} %slice.352.refs_0_), custom_call_target="tpu_custom_call" | custom-call | flops 2147483648 | bytes 12582912 | tf_op jit(solution)/shard_map/pallas_call | solution.py:422
  701.4 10.0 %shard_map.305 = bf16[1024,4352]{1,0:T(8,128)(2,1)} custom-call(bf16[1024,1024]{1,0:T(8,128)(2,1)} %copy-done.67, bf16[1024,1024]{1,0:T(8,128)(2,1)} %copy-done.66, bf16[1024,768]{1,0:T(8,128)(2,1)S(1)} %copy-done.11, bf16[1024,768]{1,0:T(8,128)(2,1)S(1)} %copy-done.9, bf16[1024,512]{1,0:T(8,128)(2,1)S(1)} %copy-done.13, bf16[1024,128]{1,0:T(8,128)(2,1)S(1)} %pad.41.refs_5_, ...), custom_call_target="tpu_custom_call" | custom-call | flops 9126805504 | bytes 22020096 | tf_op jit(solution)/shard_map/pallas_call | solution.py:475
  726.7 37.4 %collective-permute-done.27 = bf16[2,2,2,64,1792]{4,3,0,1,2:T(8,128)(2,1)S(1)} collective-permute-done((bf16[2,2,2,64,1792]{4,3,0,1,2:T(8,128)(2,1)S(1)}, bf16[2,2,2,64,1792]{4,3,0,1,2:T(8,128)(2,1)S(1)}, u32[]{:S(2)}, u32[]{:S(2)}) %collective-permute-start.27) | collective-permute-done | bytes 1835040 | tf_op jit(solution)/shard_map/ppermute | solution.py:94
  776.1 15.8 %collective-permute-done.28 = bf16[2,2,64,1792]{3,2,0,1:T(8,128)(2,1)S(1)} collective-permute-done((bf16[2,2,64,1792]{3,2,0,1:T(8,128)(2,1)S(1)}, bf16[2,2,64,1792]{3,2,0,1:T(8,128)(2,1)S(1)}, u32[]{:S(2)}, u32[]{:S(2)}) %collective-permute-start.28) | collective-permute-done | bytes 917536 | tf_op jit(solution)/shard_map/ppermute | solution.py:95
  792.2 7.0 collective-permute-done.30
  801.5 18.0 %collective-permute-done.31 = bf16[2,64,4352]{2,1,0:T(8,128)(2,1)S(1)} collective-permute-done((bf16[2,64,4352]{2,1,0:T(8,128)(2,1)S(1)}, bf16[2,64,4352]{2,1,0:T(8,128)(2,1)S(1)}, u32[]{:S(2)}, u32[]{:S(2)}) %collective-permute-start.31) | collective-permute-done | bytes 1114144 | tf_op jit(solution)/shard_map/ppermute | solution.py:95
  823.9 20.2 %collective-permute-done.32 = bf16[64,4352]{1,0:T(8,128)(2,1)S(1)} collective-permute-done((bf16[64,4352]{1,0:T(8,128)(2,1)S(1)}, bf16[64,4352]{1,0:T(8,128)(2,1)S(1)}, u32[]{:S(2)}, u32[]{:S(2)}) %collective-permute-start.32) | collective-permute-done | bytes 557088 | tf_op jit(solution)/shard_map/ppermute | solution.py:95
  844.3 8.4 collective-permute-start.39
  858.1 18.2 %collective-permute-done.40 = bf16[64,4256]{1,0:T(8,128)(2,1)S(1)} collective-permute-done((bf16[64,4256]{1,0:T(8,128)(2,1)S(1)}, bf16[64,4256]{1,0:T(8,128)(2,1)S(1)}, u32[]{:S(2)}, u32[]{:S(2)}) %collective-permute-start.40) | collective-permute-done | bytes 544800 | tf_op jit(solution)/shard_map/ppermute | solution.py:49
  (547 shorter events, 311.8 us)
Async XLA Ops:
  7.2 288.5 %all-gather.2.cloned.1.call-start = ((), (), s32[]{:S(2)}) async-start(), calls=%async_computation.1 | async-start | bytes 18382848 | tf_op jit(solution)/shard_map/all_gather | solution.py:181
  60.5 589.2 %reduce-scatter.2.cloned.1.call-start = ((), (), s32[]{:S(2)}) async-start(), calls=%async_computation.2 | async-start | bytes 9191424 | tf_op jit(solution)/shard_map/reduce_scatter | solution.py:132
  60.8 28.8 %collective-permute-start = (bf16[1024,1024]{1,0:T(8,128)(2,1)}, bf16[1024,1024]{1,0:T(8,128)(2,1)}, u32[]{:S(2)}, u32[]{:S(2)}) collective-permute-start(bf16[1024,1024]{1,0:T(8,128)(2,1)} %param.17), channel_id=1, source_target_pairs={{0,2},{2,0},{1,3},{3,1},{4,6},{6,4},{5,7},{7,5},{8,10},{10,8},{9,1... | collective-permute-start | bytes 6291464 | tf_op jit(solution)/shard_map/ppermute | solution.py:59
  65.3 22.9 %collective-permute-start.4 = (bf16[2,2,64,1280]{3,2,0,1:T(8,128)(2,1)}, bf16[2,2,64,1280]{3,2,0,1:T(8,128)(2,1)}, u32[]{:S(2)}, u32[]{:S(2)}) collective-permute-start(bf16[2,2,64,1280]{3,2,0,1:T(8,128)(2,1)} %fusion.105), channel_id=1, source_target_pairs={{0,1},{1,0},{2,3},{3,2},{4,5},{5,4},{6,7},{7,6},{8,9},{9,8},{10,11... | collective-permute-start | bytes 1966088 | tf_op jit(solution)/shard_map/ppermute | solution.py:94
  77.9 30.5 %collective-permute-start.7 = (bf16[2,2,2,64,896]{4,3,0,1,2:T(8,128)(2,1)S(1)}, bf16[2,2,2,64,896]{4,3,0,1,2:T(8,128)(2,1)S(1)}, u32[]{:S(2)}, u32[]{:S(2)}) collective-permute-start(bf16[2,2,2,64,896]{4,3,0,1,2:T(8,128)(2,1)S(1)} %pad_maximum_fusion.12), channel_id=1, source_target_pairs={{0,1},{1,0},{2,3},{3,2},{4,5},{5,4},{6,7},{7,6},{8,9},{9,8},{10,11... | collective-permute-start | bytes 2752520 | tf_op jit(solution)/shard_map/ppermute | solution.py:94
  89.6 34.3 %collective-permute-start.5 = (bf16[2,2,2,64,1280]{4,3,0,1,2:T(8,128)(2,1)S(1)}, bf16[2,2,2,64,1280]{4,3,0,1,2:T(8,128)(2,1)S(1)}, u32[]{:S(2)}, u32[]{:S(2)}) collective-permute-start(bf16[2,2,2,64,1280]{4,3,0,1,2:T(8,128)(2,1)S(1)} %pad_maximum_fusion.9), channel_id=1, source_target_pairs={{0,4},{4,0},{8,12},{12,8},{16,20},{20,16},{24,28},{28,24},{1,5},{5... | collective-permute-start | bytes 3932168 | tf_op jit(solution)/shard_map/ppermute | solution.py:95
  181.6 52.9 %collective-permute-start.13 = (bf16[2,64,2176]{2,1,0:T(8,128)(2,1)S(1)}, bf16[2,64,2176]{2,1,0:T(8,128)(2,1)S(1)}, u32[]{:S(2)}, u32[]{:S(2)}) collective-permute-start(bf16[2,64,2176]{2,1,0:T(8,128)(2,1)S(1)} %pad_maximum_fusion.16), channel_id=1, source_target_pairs={{0,8},{4,12},{8,0},{12,4},{16,24},{20,28},{24,16},{28,20},{1,9},{5... | collective-permute-start | bytes 1671176 | tf_op jit(solution)/shard_map/ppermute | solution.py:95
  182.9 79.4 %collective-permute-start.8 = (bf16[1024,1024]{1,0:T(8,128)(2,1)S(1)}, bf16[1024,1024]{1,0:T(8,128)(2,1)S(1)}, u32[]{:S(2)}, u32[]{:S(2)}) collective-permute-start(bf16[1024,1024]{1,0:T(8,128)(2,1)S(1)} %convolution_convert_fusion.1), channel_id=1, source_target_pairs={{0,2},{2,0},{1,3},{3,1},{4,6},{6,4},{5,7},{7,5},{8,10},{10,8},{9,1... | collective-permute-start | bytes 6291464 | tf_op jit(solution)/shard_map/ppermute | solution.py:59
  234.6 21.2 %collective-permute-start.16 = (bf16[2,2,64,896]{3,2,0,1:T(8,128)(2,1)S(1)}, bf16[2,2,64,896]{3,2,0,1:T(8,128)(2,1)S(1)}, u32[]{:S(2)}, u32[]{:S(2)}) collective-permute-start(bf16[2,2,64,896]{3,2,0,1:T(8,128)(2,1)S(1)} %pad_maximum_fusion.22), channel_id=1, source_target_pairs={{0,4},{4,0},{8,12},{12,8},{16,20},{20,16},{24,28},{28,24},{1,5},{5... | collective-permute-start | bytes 1376264 | tf_op jit(solution)/shard_map/ppermute | solution.py:95
  234.8 25.2 %collective-permute-start.14 = (bf16[2,2,64,1280]{3,2,0,1:T(8,128)(2,1)S(1)}, bf16[2,2,64,1280]{3,2,0,1:T(8,128)(2,1)S(1)}, u32[]{:S(2)}, u32[]{:S(2)}) collective-permute-start(bf16[2,2,64,1280]{3,2,0,1:T(8,128)(2,1)S(1)} %fusion.104), channel_id=1, source_target_pairs={{0,1},{1,0},{2,3},{3,2},{4,5},{5,4},{6,7},{7,6},{8,9},{9,8},{10,11... | collective-permute-start | bytes 1966088 | tf_op jit(solution)/shard_map/ppermute | solution.py:94
  257.3 72.4 %collective-permute-start.17 = (bf16[2,2,2,64,896]{4,3,0,1,2:T(8,128)(2,1)}, bf16[2,2,2,64,896]{4,3,0,1,2:T(8,128)(2,1)}, u32[]{:S(2)}, u32[]{:S(2)}) collective-permute-start(bf16[2,2,2,64,896]{4,3,0,1,2:T(8,128)(2,1)} %pad_maximum_fusion.13), channel_id=1, source_target_pairs={{0,1},{1,0},{2,3},{3,2},{4,5},{5,4},{6,7},{7,6},{8,9},{9,8},{10,11... | collective-permute-start | bytes 2752520 | tf_op jit(solution)/shard_map/ppermute | solution.py:94
  261.3 70.2 %collective-permute-start.15 = (bf16[2,2,2,64,1280]{4,3,0,1,2:T(8,128)(2,1)}, bf16[2,2,2,64,1280]{4,3,0,1,2:T(8,128)(2,1)}, u32[]{:S(2)}, u32[]{:S(2)}) collective-permute-start(bf16[2,2,2,64,1280]{4,3,0,1,2:T(8,128)(2,1)} %pad_maximum_fusion.10), channel_id=1, source_target_pairs={{0,4},{4,0},{8,12},{12,8},{16,20},{20,16},{24,28},{28,24},{1,5},{5... | collective-permute-start | bytes 3932168 | tf_op jit(solution)/shard_map/ppermute | solution.py:95
  328.7 52.9 %collective-permute-start.21 = (bf16[1024,1024]{1,0:T(8,128)(2,1)}, bf16[1024,1024]{1,0:T(8,128)(2,1)}, u32[]{:S(2)}, u32[]{:S(2)}) collective-permute-start(bf16[1024,1024]{1,0:T(8,128)(2,1)} %param.18), channel_id=1, source_target_pairs={{0,2},{2,0},{1,3},{3,1},{4,6},{6,4},{5,7},{7,5},{8,10},{10,8},{9,1... | collective-permute-start | bytes 6291464 | tf_op jit(solution)/shard_map/ppermute | solution.py:59
  439.2 23.0 %collective-permute-start.22 = (bf16[1024,1024]{1,0:T(8,128)(2,1)}, bf16[1024,1024]{1,0:T(8,128)(2,1)}, u32[]{:S(2)}, u32[]{:S(2)}) collective-permute-start(bf16[1024,1024]{1,0:T(8,128)(2,1)} %add_convert_fusion.6), channel_id=1, source_target_pairs={{0,2},{2,0},{1,3},{3,1},{4,6},{6,4},{5,7},{7,5},{8,10},{10,8},{9,1... | collective-permute-start | bytes 6291464 | tf_op jit(solution)/shard_map/ppermute | solution.py:59
  446.1 21.5 %collective-permute-start.19 = (bf16[1024,1024]{1,0:T(8,128)(2,1)}, bf16[1024,1024]{1,0:T(8,128)(2,1)}, u32[]{:S(2)}, u32[]{:S(2)}) collective-permute-start(bf16[1024,1024]{1,0:T(8,128)(2,1)} %fusion.68), channel_id=1, source_target_pairs={{0,2},{2,0},{1,3},{3,1},{4,6},{6,4},{5,7},{7,5},{8,10},{10,8},{9,1... | collective-permute-start | bytes 6291464 | tf_op jit(solution)/shard_map/ppermute | solution.py:59
  473.3 37.7 %collective-permute-start.20 = (bf16[1024,1024]{1,0:T(8,128)(2,1)}, bf16[1024,1024]{1,0:T(8,128)(2,1)}, u32[]{:S(2)}, u32[]{:S(2)}) collective-permute-start(bf16[1024,1024]{1,0:T(8,128)(2,1)} %get-tuple-element.165), channel_id=1, source_target_pairs={{0,1},{3,2},{4,5},{7,6},{8,9},{11,10},{12,13},{15,14},{16,17},{19,... | collective-permute-start | bytes 6291464 | tf_op jit(solution)/shard_map/ppermute | solution.py:571
  580.5 26.7 %collective-permute-start.24 = (bf16[1024,1024]{1,0:T(8,128)(2,1)}, bf16[1024,1024]{1,0:T(8,128)(2,1)}, u32[]{:S(2)}, u32[]{:S(2)}) collective-permute-start(bf16[1024,1024]{1,0:T(8,128)(2,1)} %add_convert_fusion.4), channel_id=1, source_target_pairs={{0,2},{2,0},{1,3},{3,1},{4,6},{6,4},{5,7},{7,5},{8,10},{10,8},{9,1... | collective-permute-start | bytes 6291464 | tf_op jit(solution)/shard_map/ppermute | solution.py:59
  624.7 58.1 %collective-permute-start.33 = (bf16[2,2,2,64,1664]{4,3,0,1,2:T(8,128)(2,1)}, bf16[2,2,2,64,1664]{4,3,0,1,2:T(8,128)(2,1)}, u32[]{:S(2)}, u32[]{:S(2)}) collective-permute-start(bf16[2,2,2,64,1664]{4,3,0,1,2:T(8,128)(2,1)} %bitcast.250), channel_id=1, source_target_pairs={{0,1},{1,0},{2,3},{3,2},{4,5},{5,4},{6,7},{7,6},{8,9},{9,8},{10,11... | collective-permute-start | bytes 5111816 | tf_op jit(solution)/shard_map/ppermute | solution.py:94
  629.2 62.6 %collective-permute-start.35 = (bf16[2,2,2,64,2464]{4,3,0,1,2:T(8,128)(2,1)}, bf16[2,2,2,64,2464]{4,3,0,1,2:T(8,128)(2,1)}, u32[]{:S(2)}, u32[]{:S(2)}) collective-permute-start(bf16[2,2,2,64,2464]{4,3,0,1,2:T(8,128)(2,1)} %bitcast.247), channel_id=1, source_target_pairs={{0,4},{4,0},{8,12},{12,8},{16,20},{20,16},{24,28},{28,24},{1,5},{5... | collective-permute-start | bytes 7569416 | tf_op jit(solution)/shard_map/ppermute | solution.py:95
  685.9 32.0 %collective-permute-start.34 = (bf16[2,2,64,1664]{3,2,0,1:T(8,128)(2,1)}, bf16[2,2,64,1664]{3,2,0,1:T(8,128)(2,1)}, u32[]{:S(2)}, u32[]{:S(2)}) collective-permute-start(bf16[2,2,64,1664]{3,2,0,1:T(8,128)(2,1)} %dynamic-slice_bitcast_fusion.3), channel_id=1, source_target_pairs={{0,4},{4,0},{8,12},{12,8},{16,20},{20,16},{24,28},{28,24},{1,5},{5... | collective-permute-start | bytes 2555912 | tf_op jit(solution)/shard_map/ppermute | solution.py:95
  695.6 29.3 %collective-permute-start.36 = (bf16[2,2,64,2464]{3,2,0,1:T(8,128)(2,1)}, bf16[2,2,64,2464]{3,2,0,1:T(8,128)(2,1)}, u32[]{:S(2)}, u32[]{:S(2)}) collective-permute-start(bf16[2,2,64,2464]{3,2,0,1:T(8,128)(2,1)} %dynamic-slice_bitcast_fusion), channel_id=1, source_target_pairs={{0,1},{1,0},{2,3},{3,2},{4,5},{5,4},{6,7},{7,6},{8,9},{9,8},{10,11... | collective-permute-start | bytes 3784712 | tf_op jit(solution)/shard_map/ppermute | solution.py:94
  713.9 50.2 %collective-permute-start.27 = (bf16[2,2,2,64,1792]{4,3,0,1,2:T(8,128)(2,1)S(1)}, bf16[2,2,2,64,1792]{4,3,0,1,2:T(8,128)(2,1)S(1)}, u32[]{:S(2)}, u32[]{:S(2)}) collective-permute-start(bf16[2,2,2,64,1792]{4,3,0,1,2:T(8,128)(2,1)S(1)} %bitcast.286), channel_id=1, source_target_pairs={{0,1},{1,0},{2,3},{3,2},{4,5},{5,4},{6,7},{7,6},{8,9},{9,8},{10,11... | collective-permute-start | bytes 5505032 | tf_op jit(solution)/shard_map/ppermute | solution.py:94
  716.6 55.7 %collective-permute-start.29 = (bf16[2,2,2,64,2560]{4,3,0,1,2:T(8,128)(2,1)S(1)}, bf16[2,2,2,64,2560]{4,3,0,1,2:T(8,128)(2,1)S(1)}, u32[]{:S(2)}, u32[]{:S(2)}) collective-permute-start(bf16[2,2,2,64,2560]{4,3,0,1,2:T(8,128)(2,1)S(1)} %bitcast.277), channel_id=1, source_target_pairs={{0,4},{4,0},{8,12},{12,8},{16,20},{20,16},{24,28},{28,24},{1,5},{5... | collective-permute-start | bytes 7864328 | tf_op jit(solution)/shard_map/ppermute | solution.py:95
  726.7 49.1 %collective-permute-start.37 = (bf16[2,64,4128]{2,1,0:T(8,128)(2,1)S(1)}, bf16[2,64,4128]{2,1,0:T(8,128)(2,1)S(1)}, u32[]{:S(2)}, u32[]{:S(2)}) collective-permute-start(bf16[2,64,4128]{2,1,0:T(8,128)(2,1)S(1)} %fusion.91), channel_id=1, source_target_pairs={{0,8},{4,12},{8,0},{12,4},{16,24},{20,28},{24,16},{28,20},{1,9},{5... | collective-permute-start | bytes 3170312 | tf_op jit(solution)/shard_map/ppermute | solution.py:95
  764.6 27.3 %collective-permute-start.28 = (bf16[2,2,64,1792]{3,2,0,1:T(8,128)(2,1)S(1)}, bf16[2,2,64,1792]{3,2,0,1:T(8,128)(2,1)S(1)}, u32[]{:S(2)}, u32[]{:S(2)}) collective-permute-start(bf16[2,2,64,1792]{3,2,0,1:T(8,128)(2,1)S(1)} %dynamic-slice_bitcast_fusion.2), channel_id=1, source_target_pairs={{0,4},{4,0},{8,12},{12,8},{16,20},{20,16},{24,28},{28,24},{1,5},{5... | collective-permute-start | bytes 2752520 | tf_op jit(solution)/shard_map/ppermute | solution.py:95
  773.1 26.1 %collective-permute-start.30 = (bf16[2,2,64,2560]{3,2,0,1:T(8,128)(2,1)S(1)}, bf16[2,2,64,2560]{3,2,0,1:T(8,128)(2,1)S(1)}, u32[]{:S(2)}, u32[]{:S(2)}) collective-permute-start(bf16[2,2,64,2560]{3,2,0,1:T(8,128)(2,1)S(1)} %dynamic-slice_bitcast_fusion.1), channel_id=1, source_target_pairs={{0,1},{1,0},{2,3},{3,2},{4,5},{5,4},{6,7},{7,6},{8,9},{9,8},{10,11... | collective-permute-start | bytes 3932168 | tf_op jit(solution)/shard_map/ppermute | solution.py:94
  776.1 25.3 %collective-permute-start.38 = (bf16[64,4128]{1,0:T(8,128)(2,1)S(1)}, bf16[64,4128]{1,0:T(8,128)(2,1)S(1)}, u32[]{:S(2)}, u32[]{:S(2)}) collective-permute-start(bf16[64,4128]{1,0:T(8,128)(2,1)S(1)} %dynamic-slice_bitcast_fusion.5), channel_id=1, source_target_pairs={{0,16},{4,20},{8,24},{12,28},{16,0},{20,4},{24,8},{28,12},{1,17},{... | collective-permute-start | bytes 1585160 | tf_op jit(solution)/shard_map/ppermute | solution.py:95
  799.7 19.8 %collective-permute-start.31 = (bf16[2,64,4352]{2,1,0:T(8,128)(2,1)S(1)}, bf16[2,64,4352]{2,1,0:T(8,128)(2,1)S(1)}, u32[]{:S(2)}, u32[]{:S(2)}) collective-permute-start(bf16[2,64,4352]{2,1,0:T(8,128)(2,1)S(1)} %fusion.86), channel_id=1, source_target_pairs={{0,8},{4,12},{8,0},{12,4},{16,24},{20,28},{24,16},{28,20},{1,9},{5... | collective-permute-start | bytes 3342344 | tf_op jit(solution)/shard_map/ppermute | solution.py:95
  819.8 24.3 %collective-permute-start.32 = (bf16[64,4352]{1,0:T(8,128)(2,1)S(1)}, bf16[64,4352]{1,0:T(8,128)(2,1)S(1)}, u32[]{:S(2)}, u32[]{:S(2)}) collective-permute-start(bf16[64,4352]{1,0:T(8,128)(2,1)S(1)} %dynamic-slice_bitcast_fusion.4), channel_id=1, source_target_pairs={{0,16},{4,20},{8,24},{12,28},{16,0},{20,4},{24,8},{28,12},{1,17},{... | collective-permute-start | bytes 1671176 | tf_op jit(solution)/shard_map/ppermute | solution.py:95
  822.3 54.0 %collective-permute-start.26 = (bf16[1024,1024]{1,0:T(8,128)(2,1)S(1)}, bf16[1024,1024]{1,0:T(8,128)(2,1)S(1)}, u32[]{:S(2)}, u32[]{:S(2)}) collective-permute-start(bf16[1024,1024]{1,0:T(8,128)(2,1)S(1)} %add_convert_fusion.2), channel_id=1, source_target_pairs={{0,1},{3,2},{4,5},{7,6},{8,9},{11,10},{12,13},{15,14},{16,17},{19,... | collective-permute-start | bytes 6291464 | tf_op jit(solution)/shard_map/ppermute | solution.py:571
  844.3 34.3 %collective-permute-start.39 = (bf16[64,8480]{1,0:T(8,128)(2,1)S(1)}, bf16[64,8480]{1,0:T(8,128)(2,1)S(1)}, u32[]{:S(2)}, u32[]{:S(2)}) collective-permute-start(bf16[64,8480]{1,0:T(8,128)(2,1)S(1)} %pad_maximum_fusion.11), channel_id=1, source_target_pairs={{0,0},{1,2},{2,1},{3,3},{4,4},{5,6},{6,5},{7,7},{8,8},{9,10},{10,9... | collective-permute-start | bytes 3256328 | tf_op jit(solution)/shard_map/ppermute | solution.py:49
  852.9 23.4 %collective-permute-start.40 = (bf16[64,4256]{1,0:T(8,128)(2,1)S(1)}, bf16[64,4256]{1,0:T(8,128)(2,1)S(1)}, u32[]{:S(2)}, u32[]{:S(2)}) collective-permute-start(bf16[64,4256]{1,0:T(8,128)(2,1)S(1)} %pad_maximum_fusion.17), channel_id=1, source_target_pairs={{0,0},{1,2},{2,1},{3,3},{4,4},{5,6},{6,5},{7,7},{8,8},{9,10},{10,9... | collective-permute-start | bytes 1634312 | tf_op jit(solution)/shard_map/ppermute | solution.py:49
  (142 other events, 1677.4 us)
Sparse Core Ops, SparseCore 0:
  60.6 235.0 all-gather.1
  480.2 169.3 reduce-scatter.1
